TPU v7x, 32 devices: a whole 2x2x4 slice. The times are simulated.
32 devices in a mesh: obs: 2 (over x), sub: 16 (over z, y, core).
Axes of the slice: x: 2, y: 2, z: 4, core: 2. Of those that a mesh axis runs over, the one named last changes fastest.
Arguments:
- visibilities: bfloat16 [2, 4, 4, 703, 3072], P(None, 'obs', None, None, 'sub'), parts along dimension 1, may hold values from -16 to 16
- delays: float32 [2, 4, 703], P(None, 'obs'), parts along dimension 1, may hold values from -1 to 1
- flags: int32 [4, 3072], P('obs', 'sub'), parts along dimension 0, may hold values 0 or 1
- windows: int32 [32], replicated, may hold values from 1 to 768, 3072 in all
- tracks: int32 [2, 4], P(None, 'obs'), parts along dimension 1, may hold values 0 or 1
Outputs:
- cleaned: bfloat16 [2, 4, 4, 703, 3072], P(None, 'obs', None, None, 'sub'), parts along dimension 1
- gains: float32 [2, 2, 4, 4, 38], P(None, None, 'obs'), parts along dimension 2
There are 2 independent parts, one for each index of `obs`. A program takes and returns all parts, laid end to end along the dimension named above; an argument that names none is the same for every part. Nothing has to cross between parts.
Inputs may be any that keep to these rules, and one draw needn't show every extreme that they name: The windows cover all 3072 channels.
All inputs are finite; a program needn't handle non-finite values. No bound on the sum of `flags` on one device may be relied on, other than what follows from the above.
Results may differ from a plain program's by a relative error of at most 0.001.
Values sent between devices are 32-bit elements; how exact they have to be, the bound alone decides.
No kernel may reach another device: no remote copies, remote signals or barrier semaphores. Data moves between devices by JAX's collectives and lax.ppermute only.
A program may use at most 128 MiB of HBM per device.

v0:
```python
import jax
import jax.numpy as jnp
import numpy as np
from jax import lax
from jax.experimental import pallas as pl
from jax.experimental.pallas import tpu as pltpu
from jax.sharding import PartitionSpec as P

STATIONS = 38
GITERS = 8
DAMPING = 1.0
STEPS_PER_TURN = 64.0
ROWS = 40
LANES = 384

F32 = jnp.float32
BF16 = jnp.bfloat16


def iota(shape, dim):
    return lax.broadcasted_iota(jnp.int32, shape, dim).astype(F32)


def sincos_turns(turns):
    half = (turns - jnp.floor(turns + 0.5)) * np.float32(np.pi)
    sq = half * half
    sin = np.float32(-1.0 / 39916800)
    for term in (1.0 / 362880, -1.0 / 5040, 1.0 / 120, -1.0 / 6, 1.0):
        sin = sin * sq + np.float32(term)
    sin = sin * half
    cos = np.float32(1.0 / 479001600)
    for term in (-1.0 / 3628800, 1.0 / 40320, -1.0 / 720, 1.0 / 24, -0.5, 1.0):
        cos = cos * sq + np.float32(term)
    return 1.0 - 2.0 * (sin * sin), 2.0 * (sin * cos)


def split_two(value):
    high = value.astype(BF16)
    low = (value - high.astype(F32)).astype(BF16)
    return high, low


def split_three(value):
    high = value.astype(BF16)
    rest = value - high.astype(F32)
    mid = rest.astype(BF16)
    low = (rest - mid.astype(F32)).astype(BF16)
    return high, mid, low


def dot(left, right):
    return jnp.dot(left, right, preferred_element_type=F32)


def phase_rows(delay, anchor, width):
    base = anchor + 8.0 * iota((width // 8, 1), 0)
    fine = iota((8, 1), 0)
    coarse_re, coarse_im = sincos_turns(delay * (base * np.float32(1.0 / STEPS_PER_TURN)))
    fine_re, fine_im = sincos_turns(delay * (fine * np.float32(1.0 / STEPS_PER_TURN)))
    return coarse_re, coarse_im, fine_re, fine_im


def spread(rows_ref, source, real, imag):
    for row in range(real.shape[0]):
        rows_ref[row, 2 * source:2 * source + 1, :] = real[row:row + 1]
        rows_ref[row, 2 * source + 1:2 * source + 2, :] = imag[row:row + 1]


def sums_kernel(width, me_ref, win_ref, flags_ref, delay_ref, vis_ref, y_ref,
                rows_s, member_s, alpha_s, window_s, coarse_s, fine_s, wave_s, mix_s, mexp_s, wt_s):
    time, part = pl.program_id(0), pl.program_id(1)
    me = me_ref[0]
    groups = flags_ref.shape[0]
    windows = win_ref.shape[1]
    anchor = me.astype(F32) * float(width)

    @pl.when((time == 0) & (part == 0))
    def prepare():
        win_row = win_ref[...].astype(F32)
        sub, lane = iota((windows, windows), 0), iota((windows, windows), 1)
        end_c = jnp.sum(jnp.where(lane <= sub, win_row, 0.0), axis=1, keepdims=True)
        start_c = jnp.sum(jnp.where(lane < sub, win_row, 0.0), axis=1, keepdims=True)
        win_c = end_c - start_c
        end_r = jnp.sum(jnp.where(sub <= lane, win_c, 0.0), axis=0, keepdims=True)
        start_r = jnp.sum(jnp.where(sub < lane, win_c, 0.0), axis=0, keepdims=True)
        group = iota((windows, groups), 1)
        low = group * float(width)
        first_hot = jnp.where((low <= start_c) & (start_c < low + float(width)), 1.0, 0.0)
        last_hot = jnp.where((low < end_c) & (end_c <= low + float(width)), 1.0, 0.0)
        first_g = jnp.sum(first_hot * group, axis=1, keepdims=True)
        last_g = jnp.sum(last_hot * group, axis=1, keepdims=True)
        full = jnp.where((group > first_g) & (group < last_g), 1.0, 0.0)
        pick = jnp.concatenate([first_hot, last_hot, full], axis=0).astype(BF16)
        place = iota((windows, width), 1)
        head_at = first_g * float(width) + place
        head_in = (head_at >= start_c) & (head_at < end_c)
        tail_in = (last_g > first_g) & (last_g * float(width) + place < end_c)
        channel = anchor + iota((width, windows), 0)
        member = (channel >= start_r) & (channel < end_r)
        diagonal = iota((width, width), 0) == iota((width, width), 1)
        window_s[0] = jnp.broadcast_to(first_g, (windows, 128))
        window_s[1] = jnp.broadcast_to(last_g, (windows, 128))
        for t in range(2):
            for g in range(groups):
                wt_s[t, g:g + 1, :] = 1.0 - flags_ref[lax.bitwise_xor(me, g), t:t + 1, :].astype(F32)
            weights = wt_s[t].astype(BF16)
            picked = dot(pick, weights)
            head = jnp.where(head_in, picked[:windows], 0.0)
            tail = jnp.where(tail_in, picked[windows:2 * windows], 0.0)
            count = jnp.sum(head + tail + picked[2 * windows:], axis=1, keepdims=True)
            scale = 1.0 / jnp.maximum(count, 1.0)
            rows_s[t] = jnp.concatenate([head, tail, wt_s[t]], axis=0).astype(BF16)
            window_s[2 + t] = jnp.broadcast_to(scale, (windows, 128))
            scale_r = jnp.sum(jnp.where(sub == lane, scale, 0.0), axis=0, keepdims=True)
            own = 1.0 - flags_ref[0, t:t + 1, :].astype(F32)
            own_c = jnp.sum(jnp.where(diagonal, own, 0.0), axis=1, keepdims=True)
            chosen = jnp.where(member, own_c, 0.0)
            member_s[t] = chosen.astype(BF16)
            alpha = jnp.sum(chosen * scale_r, axis=1, keepdims=True)
            alpha_s[t] = jnp.broadcast_to(alpha, (width, 128))
        pick_full = full.astype(BF16)
        window_s[4, :, :groups] = pick_full.astype(F32)

    size = y_ref.shape[3]
    delay = [delay_ref[s, pl.ds(time, 1), :] for s in range(2)]
    for s in range(2):
        cr, ci, fr, fi = phase_rows(delay[s], anchor, width)
        spread(coarse_s, s, cr, ci)
        fine_s[s, 0], fine_s[s, 1] = fr, fi

    def waves(block, carry):
        out = []
        for s in range(2):
            fr, fi = fine_s[s, 0], fine_s[s, 1]
            re, im = [], []
            for half in range(2):
                cr = coarse_s[block * 2 + half, 2 * s:2 * s + 1, :]
                ci = coarse_s[block * 2 + half, 2 * s + 1:2 * s + 2, :]
                re.append(cr * fr - ci * fi)
                im.append(cr * fi + ci * fr)
            out.append((jnp.concatenate(re, axis=0), jnp.concatenate(im, axis=0)))
        rows = pl.ds(pl.multiple_of(block * 16, 16), 16)
        (r0, i0), (r1, i1) = out
        for s in range(2):
            wave_s[s, 0, rows, :] = out[s][0]
            wave_s[s, 1, rows, :] = out[s][1]
        for slot, value in enumerate((r1 * r0 + i1 * i0, i1 * r0 - r1 * i0)):
            high, low = split_two(value)
            mix_s[slot, 0, rows, :] = high
            mix_s[slot, 1, rows, :] = low
        return carry

    lax.fori_loop(0, width // 16, waves, 0)

    rows = rows_s[time]
    sums = [dot(rows, mix_s[slot, 0]) + dot(rows, mix_s[slot, 1]) for slot in range(2)]
    gap = delay[1] - delay[0]
    per_group = np.float32(width / STEPS_PER_TURN)
    me_f = me.astype(F32)
    total_re, total_im = 0.0, 0.0
    for which in range(2):
        block = window_s[which][:, :1]
        pr, pi = sincos_turns(gap * ((block - me_f) * per_group))
        hr, hi = (part_sum[which * windows:(which + 1) * windows] for part_sum in sums)
        total_re = total_re + (pr * hr - pi * hi)
        total_im = total_im + (pr * hi + pi * hr)
    pr, pi = sincos_turns(gap * ((iota((groups, 1), 0) - me_f) * per_group))
    gr, gi = (part_sum[2 * windows:] for part_sum in sums)
    pick_full = window_s[4][:, :groups].astype(BF16)
    for slot, value in enumerate((pr * gr - pi * gi, pr * gi + pi * gr)):
        high, low = split_two(value)
        term = dot(pick_full, high) + dot(pick_full, low)
        if slot == 0:
            total_re = total_re + term
        else:
            total_im = total_im + term
    scale = window_s[2 + time][:, :1]
    chosen = member_s[time]
    for slot, value in enumerate((total_re, total_im)):
        high, low = split_two(value * (scale * scale))
        mexp_s[slot] = dot(chosen, high) + dot(chosen, low)

    for tile in range(size // 128):
        lanes = pl.ds(tile * 128, 128)

        def step(block, sums):
            rows = pl.ds(pl.multiple_of(block * 16, 16), 16)
            alpha = alpha_s[time, rows, :]
            mr, mi = mexp_s[0, rows, lanes], mexp_s[1, rows, lanes]
            r0, i0 = wave_s[0, 0, rows, lanes], wave_s[0, 1, rows, lanes]
            r1, i1 = wave_s[1, 0, rows, lanes], wave_s[1, 1, rows, lanes]
            factors = (
                (alpha * r0 - (mr * r1 + mi * i1), (mr * i1 - mi * r1) - alpha * i0),
                (alpha * r1 - (mr * r0 - mi * i0), (mr * i0 + mi * r0) - alpha * i1),
            )
            new = []
            for k in range(4):
                vr = vis_ref[0, 0, k, rows, lanes].astype(F32)
                vi = vis_ref[1, 0, k, rows, lanes].astype(F32)
                for s in range(2):
                    fr, fi = factors[s]
                    re = vr * fr - vi * fi
                    im = vr * fi + vi * fr
                    new.append(sums[len(new)] + (re[:8] + re[8:]))
                    new.append(sums[len(new)] + (im[:8] + im[8:]))
            return tuple(new)

        zero = jnp.zeros((8, 128), F32)
        sums = lax.fori_loop(0, width // 16, step, (zero,) * 16)
        for k in range(4):
            for s in range(2):
                for ri in range(2):
                    y_ref[ri, 0, s * 4 + k:s * 4 + k + 1, lanes] = jnp.sum(
                        sums[(k * 2 + s) * 2 + ri], axis=0, keepdims=True)


def solve_kernel(window_count, tracks_ref, hot_ref, first_ref, second_ref, *refs):
    parts, (gain_ref, model_ref, matrix_s, state_s) = refs[:-4], refs[-4:]
    total = [part[...] for part in parts]
    while len(total) > 1:
        total = [total[i] + total[i + 1] for i in range(0, len(total), 2)]
    total = total[0]
    re, im = total[:16], total[16:]
    wide = jnp.concatenate([re, im, -im, re] * 2, axis=0)
    matrix = 0.0
    for piece in split_three(wide):
        matrix = matrix + lax.dot_general(
            hot_ref[...], piece, (((1,), (1,)), ((), ())), preferred_element_type=F32)
    matrix_s[...] = matrix
    lane = lax.broadcasted_iota(jnp.int32, (ROWS, 128), 1)
    row = lax.broadcasted_iota(jnp.int32, (ROWS, 128), 0)
    quarter = lax.rem(lax.div(lane, 16), 4)
    inner = (quarter == 1) | (quarter == 2)
    for q in range(STATIONS):
        sign = jnp.where(inner & (row > q), -1.0, 1.0)
        matrix_s[q * ROWS:(q + 1) * ROWS, :] = matrix_s[q * ROWS:(q + 1) * ROWS, :] * sign

    def iterate(turn, state):
        state_s[...] = state
        pull = [jnp.zeros((ROWS, 128), F32) for _ in range(2)]
        for q in range(STATIONS):
            pull[q % 2] = pull[q % 2] + matrix_s[q * ROWS:(q + 1) * ROWS, :] * state_s[q:q + 1, :]
        pull = pull[0] + pull[1]
        pull = pull + pltpu.roll(pull, 32, 1)
        pull = jnp.where(inner, pltpu.roll(pull, 16, 1), pull)
        powers = state * state
        powers = powers + pltpu.roll(powers, 32, 1)
        denominator = window_count * (jnp.sum(powers, axis=0, keepdims=True) - powers) + DAMPING
        return 0.5 * (state + pull / denominator)

    state = jnp.where((quarter < 2) & (row < STATIONS), 1.0, 0.0)
    state = lax.fori_loop(0, GITERS, iterate, state)
    turned = jnp.transpose(jnp.concatenate([state, jnp.zeros((128 - ROWS, 128), F32)], axis=0))
    index = lax.broadcasted_iota(jnp.int32, (16, 128), 0)
    visible = jnp.zeros((16, 128), F32)
    for t in range(2):
        for s in range(2):
            here = lax.div(index, 4) == t * 2 + s
            visible = jnp.where(here, tracks_ref[s, t].astype(F32), visible)
    gains = [turned[:16] * visible, turned[32:48] * visible]
    for ri in range(2):
        for t in range(2):
            for s in range(2):
                at = t * 8 + s * 4
                gain_ref[ri, s, t] = gains[ri][at:at + 4, :STATIONS]
    both = jnp.concatenate(gains, axis=0)[:, :STATIONS]
    stacked = jnp.concatenate([piece.astype(F32) for piece in split_three(both)], axis=0).astype(BF16)
    ends = []
    for table in (first_ref, second_ref):
        wide = dot(stacked, table[...])
        ends.append((wide[:32] + wide[32:64]) + wide[64:])
    left, right = ends
    lr, li, rr, ri_ = left[:16], left[16:], right[:16], right[16:]
    model = (lr * rr + li * ri_, li * rr - lr * ri_)
    for ri in range(2):
        for t in range(2):
            model_ref[ri, t] = model[ri][t * 8:(t + 1) * 8]


def clean_kernel(width, me_ref, delay_ref, model_ref, vis_ref, out_ref, coarse_s):
    time = pl.program_id(0)
    anchor = me_ref[0].astype(F32) * float(width)
    size = out_ref.shape[4]
    fine = []
    for s in range(2):
        cr, ci, fr, fi = phase_rows(delay_ref[s, pl.ds(time, 1), :], anchor, width)
        spread(coarse_s, s, cr, ci)
        fine.append((fr, fi))
    for tile in range(size // 128):
        cut = slice(tile * 128, tile * 128 + 128)
        lanes = pl.ds(tile * 128, 128)
        near = [(fine[s][0][:, cut], fine[s][1][:, cut]) for s in range(2)]
        model = [[[jnp.broadcast_to(model_ref[ri, 0, s * 4 + k:s * 4 + k + 1, lanes], (8, 128))
                   for ri in range(2)] for k in range(4)] for s in range(2)]

        def step(block, carry):
            rows = pl.ds(pl.multiple_of(block * 16, 16), 16)
            wave = [[], []]
            for half in range(2):
                for s in range(2):
                    fr, fi = near[s]
                    cr = coarse_s[block * 2 + half, 2 * s:2 * s + 1, lanes]
                    ci = coarse_s[block * 2 + half, 2 * s + 1:2 * s + 2, lanes]
                    wave[s].append((cr * fr - ci * fi, cr * fi + ci * fr))
            for k in range(4):
                vr = vis_ref[0, 0, k, rows, lanes].astype(F32)
                vi = vis_ref[1, 0, k, rows, lanes].astype(F32)
                re, im = [], []
                for half in range(2):
                    total_re, total_im = 0.0, 0.0
                    for s in range(2):
                        mr, mi = model[s][k]
                        wr, wi = wave[s][half]
                        total_re = total_re + (mr * wr - mi * wi)
                        total_im = total_im + (mr * wi + mi * wr)
                    re.append(vr[half * 8:half * 8 + 8] - total_re)
                    im.append(vi[half * 8:half * 8 + 8] - total_im)
                out_ref[0, 0, k, rows, lanes] = jnp.concatenate(re, axis=0).astype(BF16)
                out_ref[1, 0, k, rows, lanes] = jnp.concatenate(im, axis=0).astype(BF16)
            return carry

        lax.fori_loop(0, width // 16, step, 0)


def partners(value, axis, stride, radix):
    count = lax.axis_size(axis)
    return [lax.ppermute(value, axis, [(i, i ^ (stride * d)) for i in range(count)]) for d in range(1, radix)]


def radices(count):
    stages, stride = [], 1
    while stride < count:
        radix = 4 if count // stride >= 4 else 2
        stages.append((stride, radix))
        stride *= radix
    return stages


def tables():
    first, second = np.triu_indices(STATIONS, 1)
    pairs = len(first)
    hot = np.zeros((STATIONS, ROWS, pairs), np.float32)
    hot[second, first, np.arange(pairs)] = 1.0
    hot[first, second, np.arange(pairs)] = 1.0
    eye = np.eye(STATIONS, dtype=np.float32)
    as_bf16 = lambda value: jnp.asarray(value, BF16)
    return as_bf16(hot.reshape(STATIONS * ROWS, pairs)), as_bf16(eye[:, first]), as_bf16(eye[:, second])


def smem():
    return pl.BlockSpec(memory_space=pltpu.SMEM)


def local(visibilities, delays, flags, windows, tracks):
    width = visibilities.shape[4]
    pairs = visibilities.shape[3]
    count = lax.axis_size("sub")
    window_count = windows.shape[0]
    turned = jnp.transpose(visibilities, (0, 1, 2, 4, 3))
    me = lax.axis_index("sub").astype(jnp.int32).reshape(1)
    gathered = flags[None]
    for stride, radix in radices(count):
        gathered = jnp.concatenate([gathered] + partners(gathered, "sub", stride, radix), axis=0)
    parts = pl.cdiv(pairs, LANES)
    delay_spec = pl.BlockSpec((2, 2, LANES), lambda t, b: (0, 0, b))
    vis_spec = pl.BlockSpec((2, 1, 4, width, LANES), lambda t, b: (0, t, 0, 0, b))
    rows = 2 * window_count + count
    vmem = lambda *shape: pltpu.VMEM(shape, F32)
    y = pl.pallas_call(
        lambda *refs: sums_kernel(width, *refs),
        grid=(2, parts),
        in_specs=[
            smem(),
            pl.BlockSpec((1, window_count), lambda t, b: (0, 0)),
            pl.BlockSpec((count, 2, width), lambda t, b: (0, 0, 0)),
            delay_spec,
            vis_spec,
        ],
        out_specs=pl.BlockSpec((2, 1, 8, LANES), lambda t, b: (0, t, 0, b)),
        out_shape=jax.ShapeDtypeStruct((2, 2, 8, pairs), F32),
        scratch_shapes=[
            pltpu.VMEM((2, rows, width), BF16),
            pltpu.VMEM((2, width, window_count), BF16),
            vmem(2, width, 128),
            vmem(5, window_count, 128),
            vmem(width // 8, 4, LANES),
            vmem(2, 2, 8, LANES),
            vmem(2, 2, width, LANES),
            pltpu.VMEM((2, 2, width, LANES), BF16),
            vmem(2, width, LANES),
            vmem(2, count, width),
        ],
        compiler_params=pltpu.CompilerParams(vmem_limit_bytes=40 * 2 ** 20),
        name="window_sums",
    )(me, windows.reshape(1, window_count), gathered, delays, turned)
    y = y.reshape(32, pairs)
    stages = radices(count)
    pieces = [y]
    for stride, radix in stages:
        if len(pieces) > 1:
            while len(pieces) > 1:
                pieces = [pieces[i] + pieces[i + 1] for i in range(0, len(pieces), 2)]
        pieces = pieces + partners(pieces[0], "sub", stride, radix)
    hot, first, second = tables()
    gains, model = pl.pallas_call(
        lambda *refs: solve_kernel(float(window_count), *refs),
        in_specs=[smem()] + [pl.BlockSpec(memory_space=pltpu.VMEM)] * (3 + len(pieces)),
        out_specs=[pl.BlockSpec(memory_space=pltpu.VMEM)] * 2,
        out_shape=[
            jax.ShapeDtypeStruct((2, 2, 2, 4, STATIONS), F32),
            jax.ShapeDtypeStruct((2, 2, 8, pairs), F32),
        ],
        scratch_shapes=[vmem(STATIONS * ROWS, 128), vmem(ROWS, 128)],
        compiler_params=pltpu.CompilerParams(vmem_limit_bytes=40 * 2 ** 20),
        name="gain_solve",
    )(tracks, hot, first, second, *pieces)
    cleaned = pl.pallas_call(
        lambda *refs: clean_kernel(width, *refs),
        grid=(2, parts),
        in_specs=[
            smem(),
            delay_spec,
            pl.BlockSpec((2, 1, 8, LANES), lambda t, b: (0, t, 0, b)),
            vis_spec,
        ],
        out_specs=vis_spec,
        out_shape=jax.ShapeDtypeStruct(turned.shape, BF16),
        scratch_shapes=[vmem(width // 8, 4, LANES)],
        compiler_params=pltpu.CompilerParams(vmem_limit_bytes=40 * 2 ** 20),
        name="clean",
    )(me, delays, model, turned)
    return jnp.transpose(cleaned, (0, 1, 2, 4, 3)), gains


def solution(mesh):
    return jax.shard_map(
        local,
        mesh=mesh,
        in_specs=(
            P(None, "obs", None, None, "sub"),
            P(None, "obs", None),
            P("obs", "sub"),
            P(),
            P(None, "obs"),
        ),
        out_specs=(P(None, "obs", None, None, "sub"), P(None, None, "obs", None, None)),
        check_vma=False,
    )
```

profile of v0, /device:TPU:0, one launch (start us, length us, event | category | flops | bytes accessed | tf_op | source)
XLA Modules:
  0.0 61.9 jit_solution(4366626941692939417)
XLA Ops:
  0.6 0.0 copy-start.3
  0.6 0.0 copy-start.6
  0.7 0.0 copy-start.7
  0.7 2.5 %collective-permute-start.2 = (s32[1,2,192]{2,1,0:T(2,128)}, s32[1,2,192]{2,1,0:T(2,128)S(1)}, u32[]{:S(2)}, u32[]{:S(2)}) collective-permute-start(s32[1,2,192]{2,1,0:T(2,128)} %bitcast.15), channel_id=1, source_target_pairs={{0,3},{1,2},{2,1},{3,0},{4,7},{5,6},{6,5},{7,4},{8,11},{9,10},{10,... | collective-permute-start | bytes 4616 | tf_op jit(solution)/shard_map/ppermute | solution.py:327
  3.1 0.6 %collective-permute-start.1 = (s32[1,2,192]{2,1,0:T(2,128)}, s32[1,2,192]{2,1,0:T(2,128)S(1)}, u32[]{:S(2)}, u32[]{:S(2)}) collective-permute-start(s32[1,2,192]{2,1,0:T(2,128)} %bitcast.16), channel_id=1, source_target_pairs={{0,2},{1,3},{2,0},{3,1},{4,6},{5,7},{6,4},{7,5},{8,10},{9,11},{10,... | collective-permute-start | bytes 4616 | tf_op jit(solution)/shard_map/ppermute | solution.py:327
  3.8 0.0 collective-permute-start
  3.8 0.7 %constant_dynamic-update-slice_fusion.6 = s32[16,2,192]{2,1,0:T(2,128)S(1)} fusion(s32[2,192]{1,0:T(2,128)} %param.10), kind=kLoop, calls=%fused_computation.7 | loop fusion | bytes 3584
  4.5 0.1 collective-permute-done.2
  4.7 2.3 %collective-permute-done.1 = s32[1,2,192]{2,1,0:T(2,128)S(1)} collective-permute-done((s32[1,2,192]{2,1,0:T(2,128)}, s32[1,2,192]{2,1,0:T(2,128)S(1)}, u32[]{:S(2)}, u32[]{:S(2)}) %collective-permute-start.1) | collective-permute-done | bytes 1568 | tf_op jit(solution)/shard_map/ppermute | solution.py:327
  6.9 0.0 collective-permute-done
  6.9 0.7 %pad_add_fusion = s32[4,2,192]{2,1,0:T(2,128)S(1)} fusion(s32[1,2,192]{2,1,0:T(2,128)S(1)} %collective-permute-done.2, s32[1,2,192]{2,1,0:T(2,128)S(1)} %collective-permute-done.1, s32[1,2,192]{2,1,0:T(2,128)S(1)} %collective-permute-done, s32[1,2,192]{2,1,0:T(2,128)} %bitcast.18), kind=kLoop, calls=%fused_computation.8 | loop fusion | flops 4608 | bytes 12288 | tf_op jit(solution)/shard_map/concatenate | solution.py:363
  7.6 3.6 %collective-permute-start.5 = (s32[4,2,192]{2,1,0:T(2,128)S(1)}, s32[4,2,192]{2,1,0:T(2,128)S(1)}, u32[]{:S(2)}, u32[]{:S(2)}) collective-permute-start(s32[4,2,192]{2,1,0:T(2,128)S(1)} %pad_add_fusion), channel_id=1, source_target_pairs={{0,12},{1,13},{2,14},{3,15},{4,8},{5,9},{6,10},{7,11},{8,4},{9,5},... | collective-permute-start | bytes 18440 | tf_op jit(solution)/shard_map/ppermute | solution.py:327
  11.2 0.0 collective-permute-start.4
  11.2 0.8 %collective-permute-start.3 = (s32[4,2,192]{2,1,0:T(2,128)S(1)}, s32[4,2,192]{2,1,0:T(2,128)S(1)}, u32[]{:S(2)}, u32[]{:S(2)}) collective-permute-start(s32[4,2,192]{2,1,0:T(2,128)S(1)} %pad_add_fusion), channel_id=1, source_target_pairs={{0,4},{1,5},{2,6},{3,7},{4,0},{5,1},{6,2},{7,3},{8,12},{9,13},{10,... | collective-permute-start | bytes 18440 | tf_op jit(solution)/shard_map/ppermute | solution.py:327
  12.0 2.8 %collective-permute-done.3 = s32[4,2,192]{2,1,0:T(2,128)S(1)} collective-permute-done((s32[4,2,192]{2,1,0:T(2,128)S(1)}, s32[4,2,192]{2,1,0:T(2,128)S(1)}, u32[]{:S(2)}, u32[]{:S(2)}) %collective-permute-start.3) | collective-permute-done | bytes 6176 | tf_op jit(solution)/shard_map/ppermute | solution.py:327
  14.9 0.9 %collective-permute-done.4 = s32[4,2,192]{2,1,0:T(2,128)S(1)} collective-permute-done((s32[4,2,192]{2,1,0:T(2,128)S(1)}, s32[4,2,192]{2,1,0:T(2,128)S(1)}, u32[]{:S(2)}, u32[]{:S(2)}) %collective-permute-start.4) | collective-permute-done | bytes 6176 | tf_op jit(solution)/shard_map/ppermute | solution.py:327
  15.8 0.0 collective-permute-done.5
  15.8 0.0 copy-start
  15.8 2.3 %copy-done = bf16[2,2,4,703,192]{3,4,2,1,0:T(8,128)(2,1)S(1)} copy-done((bf16[2,2,4,703,192]{3,4,2,1,0:T(8,128)(2,1)S(1)}, bf16[2,2,4,703,192]{3,4,2,1,0:T(8,128)(2,1)}, u32[]{:S(2)}) %copy-start) | copy-done | bytes 4319256
  18.1 0.0 copy-start.5
  18.1 0.7 %copy-done.5 = f32[2,2,703]{2,1,0:T(2,128)S(1)} copy-done((f32[2,2,703]{2,1,0:T(2,128)S(1)}, f32[2,2,703]{2,1,0:T(2,128)}, u32[]{:S(2)}) %copy-start.5) | copy-done | bytes 11272
  18.8 0.0 copy-start.8
  18.8 0.7 %copy-done.8 = s32[32]{0:T(128)S(1)} copy-done((s32[32]{0:T(128)S(1)}, s32[32]{0:T(128)}, u32[]{:S(2)}) %copy-start.8) | copy-done | bytes 152
  19.5 0.0 copy-start.4
  19.5 0.0 copy-start.1
  19.5 11.1 %window_sums.1 = f32[2,2,8,703]{3,2,1,0:T(8,128)S(1)} custom-call(s32[1]{0:T(128)} %bitcast.refs_0_, s32[1,32]{1,0:T(1,128)S(1)} %bitcast.13, s32[16,2,192]{2,1,0:T(2,128)S(1)} %constant_dynamic-update-slice_fusion.refs_2_, f32[2,2,703]{2,1,0:T(2,128)S(1)} %copy-done.5, bf16[2,2,4,192,703]{4,3,2,1,0:T(8,128)(2,1)S(1)} %bitcast.8), custom_call_target="tpu_custom_call" | custom-call | tf_op jit(solution)/shard_map/window_sums/pallas_call | solution.py:369
  30.6 0.7 %collective-permute-start.7 = (f32[32,703]{1,0:T(8,128)S(1)}, f32[32,703]{1,0:T(8,128)S(1)}, u32[]{:S(2)}, u32[]{:S(2)}) collective-permute-start(f32[32,703]{1,0:T(8,128)S(1)} %bitcast.10), channel_id=1, source_target_pairs={{0,2},{1,3},{2,0},{3,1},{4,6},{5,7},{6,4},{7,5},{8,10},{9,11},{10,... | collective-permute-start | bytes 269960 | tf_op jit(solution)/shard_map/ppermute | solution.py:327
  31.3 0.0 collective-permute-start.8
  31.3 1.5 %collective-permute-start.6 = (f32[32,703]{1,0:T(8,128)S(1)}, f32[32,703]{1,0:T(8,128)S(1)}, u32[]{:S(2)}, u32[]{:S(2)}) collective-permute-start(f32[32,703]{1,0:T(8,128)S(1)} %bitcast.12), channel_id=1, source_target_pairs={{0,1},{1,0},{2,3},{3,2},{4,5},{5,4},{6,7},{7,6},{8,9},{9,8},{10,11... | collective-permute-start | bytes 269960 | tf_op jit(solution)/shard_map/ppermute | solution.py:327
  32.8 3.5 %collective-permute-done.7 = f32[32,703]{1,0:T(8,128)S(1)} collective-permute-done((f32[32,703]{1,0:T(8,128)S(1)}, f32[32,703]{1,0:T(8,128)S(1)}, u32[]{:S(2)}, u32[]{:S(2)}) %collective-permute-start.7) | collective-permute-done | bytes 90016 | tf_op jit(solution)/shard_map/ppermute | solution.py:327
  36.3 0.1 collective-permute-done.8
  36.4 0.0 collective-permute-done.6
  36.5 1.5 %collective-permute-start.11 = (f32[32,703]{1,0:T(8,128)S(1)}, f32[32,703]{1,0:T(8,128)S(1)}, u32[]{:S(2)}, u32[]{:S(2)}) collective-permute-start(f32[32,703]{1,0:T(8,128)S(1)} %add_add_fusion.refs_4_), channel_id=1, source_target_pairs={{0,12},{1,13},{2,14},{3,15},{4,8},{5,9},{6,10},{7,11},{8,4},{9,5},... | collective-permute-start | bytes 269960 | tf_op jit(solution)/shard_map/ppermute | solution.py:327
  38.0 0.6 %collective-permute-start.10 = (f32[32,703]{1,0:T(8,128)S(1)}, f32[32,703]{1,0:T(8,128)S(1)}, u32[]{:S(2)}, u32[]{:S(2)}) collective-permute-start(f32[32,703]{1,0:T(8,128)S(1)} %add_add_fusion.refs_4_), channel_id=1, source_target_pairs={{0,8},{1,9},{2,10},{3,11},{4,12},{5,13},{6,14},{7,15},{8,0},{9,1},... | collective-permute-start | bytes 269960 | tf_op jit(solution)/shard_map/ppermute | solution.py:327
  38.6 2.3 %collective-permute-start.9 = (f32[32,703]{1,0:T(8,128)S(1)}, f32[32,703]{1,0:T(8,128)S(1)}, u32[]{:S(2)}, u32[]{:S(2)}) collective-permute-start(f32[32,703]{1,0:T(8,128)S(1)} %add_add_fusion.refs_4_), channel_id=1, source_target_pairs={{0,4},{1,5},{2,6},{3,7},{4,0},{5,1},{6,2},{7,3},{8,12},{9,13},{10,... | collective-permute-start | bytes 269960 | tf_op jit(solution)/shard_map/ppermute | solution.py:327
  40.9 3.2 %collective-permute-done.11.refs_7_ = f32[32,703]{1,0:T(8,128)S(1)} collective-permute-done((f32[32,703]{1,0:T(8,128)S(1)}, f32[32,703]{1,0:T(8,128)S(1)}, u32[]{:S(2)}, u32[]{:S(2)}) %collective-permute-start.11) | collective-permute-done | bytes 90016 | tf_op jit(solution)/shard_map/ppermute | solution.py:327
  44.1 4.3 %collective-permute-done.10.refs_6_ = f32[32,703]{1,0:T(8,128)S(1)} collective-permute-done((f32[32,703]{1,0:T(8,128)S(1)}, f32[32,703]{1,0:T(8,128)S(1)}, u32[]{:S(2)}, u32[]{:S(2)}) %collective-permute-start.10) | collective-permute-done | bytes 90016 | tf_op jit(solution)/shard_map/ppermute | solution.py:327
  48.4 0.0 collective-permute-done.9.refs_5_
  48.4 0.0 copy-done.3
  48.4 0.0 copy-done.7
  48.4 0.0 copy-done.4
  48.4 0.0 copy-start.2
  48.4 1.6 %copy-done.2 = bf16[1520,703]{1,0:T(8,128)(2,1)S(1)} copy-done((bf16[1520,703]{1,0:T(8,128)(2,1)S(1)}, bf16[1520,703]{1,0:T(8,128)(2,1)}, u32[]{:S(2)}) %copy-start.2) | copy-done | bytes 2137144
  50.1 5.0 %gain_solve.1 = (f32[2,2,2,4,38]{4,3,2,1,0:T(4,128)}, f32[2,2,8,703]{3,2,1,0:T(8,128)S(1)}) custom-call(s32[2,2]{1,0:T(2,128)S(1)} %copy-done.7, bf16[1520,703]{1,0:T(8,128)(2,1)S(1)} %copy-done.2, bf16[38,703]{1,0:T(8,128)(2,1)S(1)} %copy-done.4, bf16[38,703]{1,0:T(8,128)(2,1)S(1)} %copy-done.3, f32[32,703]{1,0:T(8,128)S(1)} %add_add_fusion.refs_4_, ...), custom_call_target="tpu_custom_call" | custom-call | tf_op jit(solution)/shard_map/gain_solve/pallas_call | solution.py:405
  55.1 0.0 copy-done.6
  55.1 0.0 copy-done.1
  55.1 6.8 %clean.1 = bf16[2,2,4,192,703]{4,3,2,1,0:T(8,128)(2,1)} custom-call(s32[1]{0:T(128)} %bitcast.refs_0_, f32[2,2,703]{2,1,0:T(2,128)S(1)} %copy-done.6, f32[2,2,8,703]{3,2,1,0:T(8,128)S(1)} %get-tuple-element.4.refs_2_, bf16[2,2,4,192,703]{4,3,2,1,0:T(8,128)(2,1)S(1)} %bitcast.9), custom_call_target="tpu_custom_call" | custom-call | tf_op jit(solution)/shard_map/clean/pallas_call | solution.py:417
  (7 shorter events, 0.1 us)
Async XLA Ops:
  0.6 47.8 %copy-start.3 = (bf16[38,703]{1,0:T(8,128)(2,1)S(1)}, bf16[38,703]{1,0:T(8,128)(2,1)}, u32[]{:S(2)}) copy-start(bf16[38,703]{1,0:T(8,128)(2,1)} %constant.12.clone.refs_3_) | copy-start | bytes 160288
  0.6 54.4 %copy-start.6 = (f32[2,2,703]{2,1,0:T(2,128)S(1)}, f32[2,2,703]{2,1,0:T(2,128)}, u32[]{:S(2)}) copy-start(f32[2,2,703]{2,1,0:T(2,128)} %refs_1_.2) | copy-start | bytes 33748
  0.7 47.8 %copy-start.7 = (s32[2,2]{1,0:T(2,128)S(1)}, s32[2,2]{1,0:T(2,128)}, u32[]{:S(2)}) copy-start(s32[2,2]{1,0:T(2,128)} %refs_0_.1) | copy-start | bytes 52
  0.7 4.0 %collective-permute-start.2 = (s32[1,2,192]{2,1,0:T(2,128)}, s32[1,2,192]{2,1,0:T(2,128)S(1)}, u32[]{:S(2)}, u32[]{:S(2)}) collective-permute-start(s32[1,2,192]{2,1,0:T(2,128)} %bitcast.15), channel_id=1, source_target_pairs={{0,3},{1,2},{2,1},{3,0},{4,7},{5,6},{6,5},{7,4},{8,11},{9,10},{10,... | collective-permute-start | bytes 4616 | tf_op jit(solution)/shard_map/ppermute | solution.py:327
  3.1 3.8 %collective-permute-start.1 = (s32[1,2,192]{2,1,0:T(2,128)}, s32[1,2,192]{2,1,0:T(2,128)S(1)}, u32[]{:S(2)}, u32[]{:S(2)}) collective-permute-start(s32[1,2,192]{2,1,0:T(2,128)} %bitcast.16), channel_id=1, source_target_pairs={{0,2},{1,3},{2,0},{3,1},{4,6},{5,7},{6,4},{7,5},{8,10},{9,11},{10,... | collective-permute-start | bytes 4616 | tf_op jit(solution)/shard_map/ppermute | solution.py:327
  3.8 3.2 %collective-permute-start = (s32[1,2,192]{2,1,0:T(2,128)}, s32[1,2,192]{2,1,0:T(2,128)S(1)}, u32[]{:S(2)}, u32[]{:S(2)}) collective-permute-start(s32[1,2,192]{2,1,0:T(2,128)} %bitcast.17), channel_id=1, source_target_pairs={{0,1},{1,0},{2,3},{3,2},{4,5},{5,4},{6,7},{7,6},{8,9},{9,8},{10,11... | collective-permute-start | bytes 4616 | tf_op jit(solution)/shard_map/ppermute | solution.py:327
  7.6 8.2 %collective-permute-start.5 = (s32[4,2,192]{2,1,0:T(2,128)S(1)}, s32[4,2,192]{2,1,0:T(2,128)S(1)}, u32[]{:S(2)}, u32[]{:S(2)}) collective-permute-start(s32[4,2,192]{2,1,0:T(2,128)S(1)} %pad_add_fusion), channel_id=1, source_target_pairs={{0,12},{1,13},{2,14},{3,15},{4,8},{5,9},{6,10},{7,11},{8,4},{9,5},... | collective-permute-start | bytes 18440 | tf_op jit(solution)/shard_map/ppermute | solution.py:327
  11.2 4.5 %collective-permute-start.4 = (s32[4,2,192]{2,1,0:T(2,128)S(1)}, s32[4,2,192]{2,1,0:T(2,128)S(1)}, u32[]{:S(2)}, u32[]{:S(2)}) collective-permute-start(s32[4,2,192]{2,1,0:T(2,128)S(1)} %pad_add_fusion), channel_id=1, source_target_pairs={{0,8},{1,9},{2,10},{3,11},{4,12},{5,13},{6,14},{7,15},{8,0},{9,1},... | collective-permute-start | bytes 18440 | tf_op jit(solution)/shard_map/ppermute | solution.py:327
  11.2 3.7 %collective-permute-start.3 = (s32[4,2,192]{2,1,0:T(2,128)S(1)}, s32[4,2,192]{2,1,0:T(2,128)S(1)}, u32[]{:S(2)}, u32[]{:S(2)}) collective-permute-start(s32[4,2,192]{2,1,0:T(2,128)S(1)} %pad_add_fusion), channel_id=1, source_target_pairs={{0,4},{1,5},{2,6},{3,7},{4,0},{5,1},{6,2},{7,3},{8,12},{9,13},{10,... | collective-permute-start | bytes 18440 | tf_op jit(solution)/shard_map/ppermute | solution.py:327
  15.8 2.3 %copy-start = (bf16[2,2,4,703,192]{3,4,2,1,0:T(8,128)(2,1)S(1)}, bf16[2,2,4,703,192]{3,4,2,1,0:T(8,128)(2,1)}, u32[]{:S(2)}) copy-start(bf16[2,2,4,703,192]{3,4,2,1,0:T(8,128)(2,1)} %param.8) | copy-start | bytes 12957700
  18.1 0.7 %copy-start.5 = (f32[2,2,703]{2,1,0:T(2,128)S(1)}, f32[2,2,703]{2,1,0:T(2,128)}, u32[]{:S(2)}) copy-start(f32[2,2,703]{2,1,0:T(2,128)} %refs_1_.2) | copy-start | bytes 33748
  18.8 0.7 %copy-start.8 = (s32[32]{0:T(128)S(1)}, s32[32]{0:T(128)}, u32[]{:S(2)}) copy-start(s32[32]{0:T(128)} %param.11) | copy-start | bytes 388
  19.5 28.9 %copy-start.4 = (bf16[38,703]{1,0:T(8,128)(2,1)S(1)}, bf16[38,703]{1,0:T(8,128)(2,1)}, u32[]{:S(2)}) copy-start(bf16[38,703]{1,0:T(8,128)(2,1)} %constant.11.clone.refs_2_) | copy-start | bytes 160288
  19.5 35.6 %copy-start.1 = (bf16[2,2,4,703,192]{3,4,2,1,0:T(8,128)(2,1)S(1)}, bf16[2,2,4,703,192]{3,4,2,1,0:T(8,128)(2,1)}, u32[]{:S(2)}) copy-start(bf16[2,2,4,703,192]{3,4,2,1,0:T(8,128)(2,1)} %param.8) | copy-start | bytes 12957700
  30.6 5.7 %collective-permute-start.7 = (f32[32,703]{1,0:T(8,128)S(1)}, f32[32,703]{1,0:T(8,128)S(1)}, u32[]{:S(2)}, u32[]{:S(2)}) collective-permute-start(f32[32,703]{1,0:T(8,128)S(1)} %bitcast.10), channel_id=1, source_target_pairs={{0,2},{1,3},{2,0},{3,1},{4,6},{5,7},{6,4},{7,5},{8,10},{9,11},{10,... | collective-permute-start | bytes 269960 | tf_op jit(solution)/shard_map/ppermute | solution.py:327
  31.3 5.1 %collective-permute-start.8 = (f32[32,703]{1,0:T(8,128)S(1)}, f32[32,703]{1,0:T(8,128)S(1)}, u32[]{:S(2)}, u32[]{:S(2)}) collective-permute-start(f32[32,703]{1,0:T(8,128)S(1)} %bitcast.11), channel_id=1, source_target_pairs={{0,3},{1,2},{2,1},{3,0},{4,7},{5,6},{6,5},{7,4},{8,11},{9,10},{10,... | collective-permute-start | bytes 269960 | tf_op jit(solution)/shard_map/ppermute | solution.py:327
  31.3 5.1 %collective-permute-start.6 = (f32[32,703]{1,0:T(8,128)S(1)}, f32[32,703]{1,0:T(8,128)S(1)}, u32[]{:S(2)}, u32[]{:S(2)}) collective-permute-start(f32[32,703]{1,0:T(8,128)S(1)} %bitcast.12), channel_id=1, source_target_pairs={{0,1},{1,0},{2,3},{3,2},{4,5},{5,4},{6,7},{7,6},{8,9},{9,8},{10,11... | collective-permute-start | bytes 269960 | tf_op jit(solution)/shard_map/ppermute | solution.py:327
  36.5 7.7 %collective-permute-start.11 = (f32[32,703]{1,0:T(8,128)S(1)}, f32[32,703]{1,0:T(8,128)S(1)}, u32[]{:S(2)}, u32[]{:S(2)}) collective-permute-start(f32[32,703]{1,0:T(8,128)S(1)} %add_add_fusion.refs_4_), channel_id=1, source_target_pairs={{0,12},{1,13},{2,14},{3,15},{4,8},{5,9},{6,10},{7,11},{8,4},{9,5},... | collective-permute-start | bytes 269960 | tf_op jit(solution)/shard_map/ppermute | solution.py:327
  38.0 10.4 %collective-permute-start.10 = (f32[32,703]{1,0:T(8,128)S(1)}, f32[32,703]{1,0:T(8,128)S(1)}, u32[]{:S(2)}, u32[]{:S(2)}) collective-permute-start(f32[32,703]{1,0:T(8,128)S(1)} %add_add_fusion.refs_4_), channel_id=1, source_target_pairs={{0,8},{1,9},{2,10},{3,11},{4,12},{5,13},{6,14},{7,15},{8,0},{9,1},... | collective-permute-start | bytes 269960 | tf_op jit(solution)/shard_map/ppermute | solution.py:327
  38.6 9.8 %collective-permute-start.9 = (f32[32,703]{1,0:T(8,128)S(1)}, f32[32,703]{1,0:T(8,128)S(1)}, u32[]{:S(2)}, u32[]{:S(2)}) collective-permute-start(f32[32,703]{1,0:T(8,128)S(1)} %add_add_fusion.refs_4_), channel_id=1, source_target_pairs={{0,4},{1,5},{2,6},{3,7},{4,0},{5,1},{6,2},{7,3},{8,12},{9,13},{10,... | collective-permute-start | bytes 269960 | tf_op jit(solution)/shard_map/ppermute | solution.py:327
  48.4 1.7 %copy-start.2 = (bf16[1520,703]{1,0:T(8,128)(2,1)S(1)}, bf16[1520,703]{1,0:T(8,128)(2,1)}, u32[]{:S(2)}) copy-start(bf16[1520,703]{1,0:T(8,128)(2,1)} %constant.10.clone.refs_1_) | copy-start | bytes 6411364
where the time goes:
time: 62.2 us; the launch traced here: 61.9 us
  Pallas kernels  22.9 us (37%)
  waiting for transfers between devices  17.2 us (28%)
  starting transfers between devices  14.2 us (23%)
  local copies, waits for them, and re-layouts  6.13 us (10%)
  other arithmetic  0.71 us (1%)
  between operations  0.71 us (1%)
    ppermute x12, waiting for transfers between devices, partners(): lax.ppermute(value, axis, [(i, i ^ stride * d) for i in range(count)])  17.2 us
    ppermute x12, starting transfers between devices, partners(): lax.ppermute(value, axis, [(i, i ^ stride * d) for i in range(count)])  14.2 us
    pallas_call x1, Pallas kernels, local(): pl.pallas_call(lambda *refs: sums_kernel(width, *refs), grid=(2, parts),...  11.1 us
    pallas_call x1, Pallas kernels, local(): pl.pallas_call(lambda *refs: clean_kernel(width, *refs), grid=(2, parts),...  6.79 us
    unnamed x24, local copies, waits for them, and re-layouts  6.13 us
    pallas_call x1, Pallas kernels, local(): pl.pallas_call(lambda *refs: solve_kernel(float(window_count), *refs), in...  4.98 us
  transfers between devices with their start and end apart: 12, of which 8 were waited for; matrix products, arithmetic and copies ran while one was open for 1% of the time, Pallas kernels for 0%

commit v1 on v0

--- a/solution.py
+++ b/solution.py
@@ -12,6 +12,7 @@
 STEPS_PER_TURN = 64.0
 ROWS = 40
 LANES = 384
+SYSTEMS = 16
 
 F32 = jnp.float32
 BF16 = jnp.bfloat16
@@ -102,7 +103,7 @@
         window_s[1] = jnp.broadcast_to(last_g, (windows, 128))
         for t in range(2):
             for g in range(groups):
-                wt_s[t, g:g + 1, :] = 1.0 - flags_ref[lax.bitwise_xor(me, g), t:t + 1, :].astype(F32)
+                wt_s[t, g:g + 1, :] = 1.0 - flags_ref[g, t:t + 1, :].astype(F32)
             weights = wt_s[t].astype(BF16)
             picked = dot(pick, weights)
             head = jnp.where(head_in, picked[:windows], 0.0)
@@ -112,7 +113,7 @@
             rows_s[t] = jnp.concatenate([head, tail, wt_s[t]], axis=0).astype(BF16)
             window_s[2 + t] = jnp.broadcast_to(scale, (windows, 128))
             scale_r = jnp.sum(jnp.where(sub == lane, scale, 0.0), axis=0, keepdims=True)
-            own = 1.0 - flags_ref[0, t:t + 1, :].astype(F32)
+            own = 1.0 - flags_ref[me, t:t + 1, :].astype(F32)
             own_c = jnp.sum(jnp.where(diagonal, own, 0.0), axis=1, keepdims=True)
             chosen = jnp.where(member, own_c, 0.0)
             member_s[t] = chosen.astype(BF16)
@@ -121,7 +122,7 @@
         pick_full = full.astype(BF16)
         window_s[4, :, :groups] = pick_full.astype(F32)
 
-    size = y_ref.shape[3]
+    size = y_ref.shape[2]
     delay = [delay_ref[s, pl.ds(time, 1), :] for s in range(2)]
     for s in range(2):
         cr, ci, fr, fi = phase_rows(delay[s], anchor, width)
@@ -210,77 +211,78 @@
         for k in range(4):
             for s in range(2):
                 for ri in range(2):
-                    y_ref[ri, 0, s * 4 + k:s * 4 + k + 1, lanes] = jnp.sum(
+                    y_ref[s * 4 + k, ri:ri + 1, lanes] = jnp.sum(
                         sums[(k * 2 + s) * 2 + ri], axis=0, keepdims=True)
 
 
-def solve_kernel(window_count, tracks_ref, hot_ref, first_ref, second_ref, *refs):
-    parts, (gain_ref, model_ref, matrix_s, state_s) = refs[:-4], refs[-4:]
-    total = [part[...] for part in parts]
-    while len(total) > 1:
-        total = [total[i] + total[i + 1] for i in range(0, len(total), 2)]
-    total = total[0]
-    re, im = total[:16], total[16:]
-    wide = jnp.concatenate([re, im, -im, re] * 2, axis=0)
-    matrix = 0.0
-    for piece in split_three(wide):
-        matrix = matrix + lax.dot_general(
-            hot_ref[...], piece, (((1,), (1,)), ((), ())), preferred_element_type=F32)
-    matrix_s[...] = matrix
-    lane = lax.broadcasted_iota(jnp.int32, (ROWS, 128), 1)
-    row = lax.broadcasted_iota(jnp.int32, (ROWS, 128), 0)
-    quarter = lax.rem(lax.div(lane, 16), 4)
-    inner = (quarter == 1) | (quarter == 2)
-    for q in range(STATIONS):
-        sign = jnp.where(inner & (row > q), -1.0, 1.0)
-        matrix_s[q * ROWS:(q + 1) * ROWS, :] = matrix_s[q * ROWS:(q + 1) * ROWS, :] * sign
-
-    def iterate(turn, state):
-        state_s[...] = state
-        pull = [jnp.zeros((ROWS, 128), F32) for _ in range(2)]
-        for q in range(STATIONS):
-            pull[q % 2] = pull[q % 2] + matrix_s[q * ROWS:(q + 1) * ROWS, :] * state_s[q:q + 1, :]
-        pull = pull[0] + pull[1]
-        pull = pull + pltpu.roll(pull, 32, 1)
-        pull = jnp.where(inner, pltpu.roll(pull, 16, 1), pull)
-        powers = state * state
-        powers = powers + pltpu.roll(powers, 32, 1)
-        denominator = window_count * (jnp.sum(powers, axis=0, keepdims=True) - powers) + DAMPING
-        return 0.5 * (state + pull / denominator)
-
-    state = jnp.where((quarter < 2) & (row < STATIONS), 1.0, 0.0)
-    state = lax.fori_loop(0, GITERS, iterate, state)
-    turned = jnp.transpose(jnp.concatenate([state, jnp.zeros((128 - ROWS, 128), F32)], axis=0))
-    index = lax.broadcasted_iota(jnp.int32, (16, 128), 0)
-    visible = jnp.zeros((16, 128), F32)
-    for t in range(2):
-        for s in range(2):
-            here = lax.div(index, 4) == t * 2 + s
-            visible = jnp.where(here, tracks_ref[s, t].astype(F32), visible)
-    gains = [turned[:16] * visible, turned[32:48] * visible]
-    for ri in range(2):
+def solve_kernel(window_count, me_ref, tracks_ref, first_ref, second_ref, part_ref, gain_ref):
+    system = lax.rem(me_ref[0], SYSTEMS)
+    total = part_ref[0]
+    for source in range(1, part_ref.shape[0]):
+        total = total + part_ref[source]
+    rows = []
+    hot = first_ref[...]
+    other = second_ref[...]
+    for table in (hot, other):
+        for ri in range(2):
+            rows += [table * piece for piece in split_three(total[ri:ri + 1])]
+    rows = [row.astype(BF16) for row in rows]
+    nt = lambda left, right: lax.dot_general(
+        left, right, (((1,), (1,)), ((), ())), preferred_element_type=F32)
+    upper = nt(jnp.concatenate(rows[:6], axis=0), other)
+    lower = nt(jnp.concatenate(rows[6:], axis=0), hot)
+    cut = lambda value, i: value[i * ROWS:(i + 1) * ROWS]
+    join = lambda value, i: (cut(value, 3 * i) + cut(value, 3 * i + 1)) + cut(value, 3 * i + 2)
+    re = join(upper, 0) + join(lower, 0)
+    im = join(upper, 1) - join(lower, 1)
+    live_r = iota((1, ROWS), 1) < float(STATIONS)
+    live_c = iota((ROWS, 1), 0) < float(STATIONS)
+    row_re, row_im = jnp.where(live_r, 1.0, 0.0), jnp.zeros((1, ROWS), F32)
+    col_re, col_im = jnp.where(live_c, 1.0, 0.0), jnp.zeros((ROWS, 1), F32)
+    for turn in range(GITERS):
+        pull_cr = jnp.sum(re * row_re - im * row_im, axis=1, keepdims=True)
+        pull_ci = jnp.sum(re * row_im + im * row_re, axis=1, keepdims=True)
+        pull_rr = jnp.sum(re * col_re + im * col_im, axis=0, keepdims=True)
+        pull_ri = jnp.sum(re * col_im - im * col_re, axis=0, keepdims=True)
+        power_r = row_re * row_re + row_im * row_im
+        power_c = col_re * col_re + col_im * col_im
+        total = jnp.sum(power_c, axis=0, keepdims=True)
+        inverse_r = 1.0 / (window_count * (total - power_r) + DAMPING)
+        inverse_c = 1.0 / (window_count * (total - power_c) + DAMPING)
+        row_re, row_im = 0.5 * (row_re + pull_rr * inverse_r), 0.5 * (row_im + pull_ri * inverse_r)
+        col_re, col_im = 0.5 * (col_re + pull_cr * inverse_c), 0.5 * (col_im + pull_ci * inverse_c)
+    visible = tracks_ref[lax.rem(lax.div(system, 4), 2), lax.div(system, 8)].astype(F32)
+    gains = jnp.concatenate([row_re, row_im], axis=0)[:, :STATIONS] * visible
+    for target in range(gain_ref.shape[0]):
+        gain_ref[target] = gains
+
+
+def clean_kernel(width, me_ref, delay_ref, first_ref, second_ref, gain_ref, vis_ref, out_ref, gain_out_ref,
+                 coarse_s, split_s):
+    time, part = pl.program_id(0), pl.program_id(1)
+    anchor = me_ref[0].astype(F32) * float(width)
+    size = out_ref.shape[4]
+
+    @pl.when((time == 0) & (part == 0))
+    def prepare():
         for t in range(2):
             for s in range(2):
-                at = t * 8 + s * 4
-                gain_ref[ri, s, t] = gains[ri][at:at + 4, :STATIONS]
-    both = jnp.concatenate(gains, axis=0)[:, :STATIONS]
-    stacked = jnp.concatenate([piece.astype(F32) for piece in split_three(both)], axis=0).astype(BF16)
+                for k in range(4):
+                    pair = gain_ref[t * 8 + s * 4 + k]
+                    for ri in range(2):
+                        gain_out_ref[ri, s, t, k:k + 1, :] = pair[ri:ri + 1]
+        for t in range(2):
+            both = jnp.concatenate(
+                [jnp.concatenate([gain_out_ref[ri, s, t] for s in range(2)], axis=0) for ri in range(2)], axis=0)
+            split_s[t] = jnp.concatenate(split_three(both), axis=0)
+
     ends = []
     for table in (first_ref, second_ref):
-        wide = dot(stacked, table[...])
-        ends.append((wide[:32] + wide[32:64]) + wide[64:])
+        wide = dot(split_s[time], table[...])
+        ends.append((wide[:16] + wide[16:32]) + wide[32:])
     left, right = ends
-    lr, li, rr, ri_ = left[:16], left[16:], right[:16], right[16:]
-    model = (lr * rr + li * ri_, li * rr - lr * ri_)
-    for ri in range(2):
-        for t in range(2):
-            model_ref[ri, t] = model[ri][t * 8:(t + 1) * 8]
-
-
-def clean_kernel(width, me_ref, delay_ref, model_ref, vis_ref, out_ref, coarse_s):
-    time = pl.program_id(0)
-    anchor = me_ref[0].astype(F32) * float(width)
-    size = out_ref.shape[4]
+    model_re = left[:8] * right[:8] + left[8:] * right[8:]
+    model_im = left[8:] * right[:8] - left[:8] * right[8:]
     fine = []
     for s in range(2):
         cr, ci, fr, fi = phase_rows(delay_ref[s, pl.ds(time, 1), :], anchor, width)
@@ -290,8 +292,8 @@
         cut = slice(tile * 128, tile * 128 + 128)
         lanes = pl.ds(tile * 128, 128)
         near = [(fine[s][0][:, cut], fine[s][1][:, cut]) for s in range(2)]
-        model = [[[jnp.broadcast_to(model_ref[ri, 0, s * 4 + k:s * 4 + k + 1, lanes], (8, 128))
-                   for ri in range(2)] for k in range(4)] for s in range(2)]
+        model = [[[jnp.broadcast_to(value[s * 4 + k:s * 4 + k + 1, cut], (8, 128))
+                   for value in (model_re, model_im)] for k in range(4)] for s in range(2)]
 
         def step(block, carry):
             rows = pl.ds(pl.multiple_of(block * 16, 16), 16)
@@ -322,29 +324,14 @@
         lax.fori_loop(0, width // 16, step, 0)
 
 
-def partners(value, axis, stride, radix):
-    count = lax.axis_size(axis)
-    return [lax.ppermute(value, axis, [(i, i ^ (stride * d)) for i in range(count)]) for d in range(1, radix)]
-
-
-def radices(count):
-    stages, stride = [], 1
-    while stride < count:
-        radix = 4 if count // stride >= 4 else 2
-        stages.append((stride, radix))
-        stride *= radix
-    return stages
-
-
 def tables():
     first, second = np.triu_indices(STATIONS, 1)
-    pairs = len(first)
-    hot = np.zeros((STATIONS, ROWS, pairs), np.float32)
-    hot[second, first, np.arange(pairs)] = 1.0
-    hot[first, second, np.arange(pairs)] = 1.0
-    eye = np.eye(STATIONS, dtype=np.float32)
-    as_bf16 = lambda value: jnp.asarray(value, BF16)
-    return as_bf16(hot.reshape(STATIONS * ROWS, pairs)), as_bf16(eye[:, first]), as_bf16(eye[:, second])
+    eye = np.eye(ROWS, dtype=np.float32)
+    return jnp.asarray(eye[:, first], BF16), jnp.asarray(eye[:, second], BF16)
+
+
+def exchange(value):
+    return lax.all_to_all(value, "sub", 0, 0)
 
 
 def smem():
@@ -358,9 +345,7 @@
     window_count = windows.shape[0]
     turned = jnp.transpose(visibilities, (0, 1, 2, 4, 3))
     me = lax.axis_index("sub").astype(jnp.int32).reshape(1)
-    gathered = flags[None]
-    for stride, radix in radices(count):
-        gathered = jnp.concatenate([gathered] + partners(gathered, "sub", stride, radix), axis=0)
+    gathered = exchange(jnp.broadcast_to(flags[None], (count,) + flags.shape))
     parts = pl.cdiv(pairs, LANES)
     delay_spec = pl.BlockSpec((2, 2, LANES), lambda t, b: (0, 0, b))
     vis_spec = pl.BlockSpec((2, 1, 4, width, LANES), lambda t, b: (0, t, 0, 0, b))
@@ -376,8 +361,8 @@
             delay_spec,
             vis_spec,
         ],
-        out_specs=pl.BlockSpec((2, 1, 8, LANES), lambda t, b: (0, t, 0, b)),
-        out_shape=jax.ShapeDtypeStruct((2, 2, 8, pairs), F32),
+        out_specs=pl.BlockSpec((8, 2, LANES), lambda t, b: (t, 0, b)),
+        out_shape=jax.ShapeDtypeStruct((SYSTEMS, 2, pairs), F32),
         scratch_shapes=[
             pltpu.VMEM((2, rows, width), BF16),
             pltpu.VMEM((2, width, window_count), BF16),
@@ -390,45 +375,43 @@
             vmem(2, width, LANES),
             vmem(2, count, width),
         ],
-        compiler_params=pltpu.CompilerParams(vmem_limit_bytes=40 * 2 ** 20),
+        compiler_params=pltpu.CompilerParams(vmem_limit_bytes=60 * 2 ** 20),
         name="window_sums",
     )(me, windows.reshape(1, window_count), gathered, delays, turned)
-    y = y.reshape(32, pairs)
-    stages = radices(count)
-    pieces = [y]
-    for stride, radix in stages:
-        if len(pieces) > 1:
-            while len(pieces) > 1:
-                pieces = [pieces[i] + pieces[i + 1] for i in range(0, len(pieces), 2)]
-        pieces = pieces + partners(pieces[0], "sub", stride, radix)
-    hot, first, second = tables()
-    gains, model = pl.pallas_call(
+    if count > SYSTEMS:
+        y = jnp.tile(y, (count // SYSTEMS, 1, 1))
+    y = exchange(y)
+    first, second = tables()
+    gains = pl.pallas_call(
         lambda *refs: solve_kernel(float(window_count), *refs),
-        in_specs=[smem()] + [pl.BlockSpec(memory_space=pltpu.VMEM)] * (3 + len(pieces)),
-        out_specs=[pl.BlockSpec(memory_space=pltpu.VMEM)] * 2,
-        out_shape=[
-            jax.ShapeDtypeStruct((2, 2, 2, 4, STATIONS), F32),
-            jax.ShapeDtypeStruct((2, 2, 8, pairs), F32),
-        ],
-        scratch_shapes=[vmem(STATIONS * ROWS, 128), vmem(ROWS, 128)],
+        in_specs=[smem(), smem()] + [pl.BlockSpec(memory_space=pltpu.VMEM)] * 3,
+        out_specs=pl.BlockSpec(memory_space=pltpu.VMEM),
+        out_shape=jax.ShapeDtypeStruct((count, 2, STATIONS), F32),
         compiler_params=pltpu.CompilerParams(vmem_limit_bytes=40 * 2 ** 20),
         name="gain_solve",
-    )(tracks, hot, first, second, *pieces)
-    cleaned = pl.pallas_call(
+    )(me, tracks, first, second, y)
+    gains = exchange(gains)
+    table_spec = pl.BlockSpec((STATIONS, LANES), lambda t, b: (0, b))
+    cleaned, gains = pl.pallas_call(
         lambda *refs: clean_kernel(width, *refs),
         grid=(2, parts),
         in_specs=[
             smem(),
             delay_spec,
-            pl.BlockSpec((2, 1, 8, LANES), lambda t, b: (0, t, 0, b)),
+            table_spec,
+            table_spec,
+            pl.BlockSpec((count, 2, STATIONS), lambda t, b: (0, 0, 0)),
             vis_spec,
         ],
-        out_specs=vis_spec,
-        out_shape=jax.ShapeDtypeStruct(turned.shape, BF16),
-        scratch_shapes=[vmem(width // 8, 4, LANES)],
-        compiler_params=pltpu.CompilerParams(vmem_limit_bytes=40 * 2 ** 20),
+        out_specs=[vis_spec, pl.BlockSpec((2, 2, 2, 4, STATIONS), lambda t, b: (0, 0, 0, 0, 0))],
+        out_shape=[
+            jax.ShapeDtypeStruct(turned.shape, BF16),
+            jax.ShapeDtypeStruct((2, 2, 2, 4, STATIONS), F32),
+        ],
+        scratch_shapes=[vmem(width // 8, 4, LANES), pltpu.VMEM((2, 48, STATIONS), BF16)],
+        compiler_params=pltpu.CompilerParams(vmem_limit_bytes=60 * 2 ** 20),
         name="clean",
-    )(me, delays, model, turned)
+    )(me, delays, first[:STATIONS], second[:STATIONS], gains, turned)
     return jnp.transpose(cleaned, (0, 1, 2, 4, 3)), gains
 
 

time: 62.2 us -> 60 us (0.965)
  blocking collectives: 0 us -> 20.6 us
  waiting for transfers between devices: 17.2 us -> 6.63 us
  starting transfers between devices: 14.2 us -> 7.39 us
  local copies, waits for them, and re-layouts: 6.13 us -> 1.97 us
  other arithmetic: 0.71 us -> 0 us
    all_to_all x0 -> x2, blocking collectives: none -> 20.6 us  [exchange(): return lax.all_to_all(value, 'sub', 0, 0)]
    ppermute x12 -> x0, waiting for transfers between devices: 17.2 us -> none  [partners(): lax.ppermute(value, axis, [(i, i ^ stride * d) for i in range(count)])]
    ppermute x12 -> x0, starting transfers between devices: 14.2 us -> none  [partners(): lax.ppermute(value, axis, [(i, i ^ stride * d) for i in range(count)])]
    all_to_all x0 -> x1, starting transfers between devices: none -> 7.39 us  [exchange(): return lax.all_to_all(value, 'sub', 0, 0)]
    all_to_all x0 -> x1, waiting for transfers between devices: none -> 6.63 us  [exchange(): return lax.all_to_all(value, 'sub', 0, 0)]
    unnamed x24 -> x8, local copies, waits for them, and re-layouts: 6.13 us -> 0.63 us
    pallas_call x1, Pallas kernels: 4.98 us -> 1.37 us  [local(): pl.pallas_call(lambda *refs: solve_kernel(float(window_count), *refs), in...]
    pallas_call x1, Pallas kernels: 6.79 us -> 8.35 us  [local(): pl.pallas_call(lambda *refs: clean_kernel(width, *refs), grid=(2, parts),...]
  transfers between devices with their start and end apart: 12 -> 1, of which waited for: 8 -> 1; matrix products, arithmetic and copies ran while one was open for 1% -> 0% of each run, Pallas kernels for 0% -> 0%
where the time goes in v1:
time: 60 us; the launch traced here: 59.6 us
  Pallas kernels  22.3 us (37%)
  blocking collectives  20.6 us (34%)
  starting transfers between devices  7.39 us (12%)
  waiting for transfers between devices  6.63 us (11%)
  local copies, waits for them, and re-layouts  1.97 us (3%)
  between operations  0.68 us (1%)
    all_to_all x2, blocking collectives, exchange(): return lax.all_to_all(value, 'sub', 0, 0)  20.6 us
    pallas_call x1, Pallas kernels, local(): pl.pallas_call(lambda *refs: sums_kernel(width, *refs), grid=(2, parts),...  12.6 us
    pallas_call x1, Pallas kernels, local(): pl.pallas_call(lambda *refs: clean_kernel(width, *refs), grid=(2, parts),...  8.35 us
    all_to_all x1, starting transfers between devices, exchange(): return lax.all_to_all(value, 'sub', 0, 0)  7.39 us
    all_to_all x1, waiting for transfers between devices, exchange(): return lax.all_to_all(value, 'sub', 0, 0)  6.63 us
    pallas_call x1, Pallas kernels, local(): pl.pallas_call(lambda *refs: solve_kernel(float(window_count), *refs), in...  1.37 us
    broadcast_in_dim x1, local copies, waits for them, and re-layouts, local(): gathered = exchange(jnp.broadcast_to(flags[None], (count,) + flags.shape))  1.35 us
  transfers between devices with their start and end apart: 1, of which 1 were waited for; matrix products, arithmetic and copies ran while one was open for 0% of the time, Pallas kernels for 0%

profile of v1, /device:TPU:0, one launch (start us, length us, event | category | flops | bytes accessed | tf_op | source)
XLA Modules:
  0.0 59.6 jit_solution(9661124783242756604)
XLA Ops:
  0.6 0.0 copy-start
  0.6 0.0 copy-start.1
  0.7 0.0 copy-start.2
  0.7 1.3 %broadcast_in_dim.2 = s32[16,2,192]{2,1,0:T(2,128)} broadcast(s32[2,192]{1,0:T(2,128)} %param.9), dimensions={1,2} | broadcast | bytes 26112 | tf_op jit(solution)/shard_map/broadcast_in_dim | solution.py:348
  2.0 7.4 %all-to-all-start = ((s32[16,2,192]{2,1,0:T(2,128)}), s32[16,2,192]{2,1,0:T(2,128)S(1)}, u32[]{:S(2)}, u32[]{:S(2)}) async-start(s32[16,2,192]{2,1,0:T(2,128)} %broadcast_in_dim.2), calls=%async_computation | async-start | bytes 65536 | tf_op jit(solution)/shard_map/all_to_all | solution.py:334
  9.4 6.6 %all-to-all-done.refs_2_ = s32[16,2,192]{2,1,0:T(2,128)S(1)} async-done(((s32[16,2,192]{2,1,0:T(2,128)}), s32[16,2,192]{2,1,0:T(2,128)S(1)}, u32[]{:S(2)}, u32[]{:S(2)}) %all-to-all-start) | async-done | bytes 24608 | tf_op jit(solution)/shard_map/all_to_all | solution.py:334
  16.0 0.0 copy-start.3
  16.0 0.6 %copy-done.3 = s32[16,2,192]{2,1,0:T(2,128)} copy-done((s32[16,2,192]{2,1,0:T(2,128)}, s32[16,2,192]{2,1,0:T(2,128)S(1)}, u32[]{:S(2)}) %copy-start.3) | copy-done | bytes 24600
  16.6 12.6 %window_sums.1 = f32[16,2,703]{2,1,0:T(2,128)} custom-call(s32[1]{0:T(128)} %bitcast.refs_0_, s32[1,32]{1,0:T(1,128)} %bitcast.6, s32[16,2,192]{2,1,0:T(2,128)} %copy-done.3, f32[2,2,703]{2,1,0:T(2,128)} %refs_1_.3, bf16[2,2,4,192,703]{4,3,2,1,0:T(8,128)(2,1)} %bitcast.4), custom_call_target="tpu_custom_call" | custom-call | tf_op jit(solution)/shard_map/window_sums/pallas_call | solution.py:354
  29.2 10.9 %all_to_all.15.refs_4_ = f32[16,2,703]{2,1,0:T(2,128)S(1)} all-to-all(f32[16,2,703]{2,1,0:T(2,128)} %window_sums.1), channel_id=1, replica_groups=mesh['obs'=2,'sub'=16] {'sub'}, dimensions={0} | all-to-all | bytes 179968 | tf_op jit(solution)/shard_map/all_to_all | solution.py:334
  40.1 0.0 copy-done
  40.1 0.0 copy-done.1
  40.1 0.0 copy-done.2
  40.1 1.4 %gain_solve.1 = f32[16,2,38]{2,1,0:T(2,128)S(1)} custom-call(s32[1]{0:T(128)} %bitcast.refs_0_, s32[2,2]{1,0:T(2,128)S(1)} %copy-done.2, bf16[40,703]{1,0:T(8,128)(2,1)S(1)} %copy-done.1, bf16[40,703]{1,0:T(8,128)(2,1)S(1)} %copy-done, f32[16,2,703]{2,1,0:T(2,128)S(1)} %all_to_all.15.refs_4_), custom_call_target="tpu_custom_call" | custom-call | tf_op jit(solution)/shard_map/gain_solve/pallas_call | solution.py:385
  41.5 9.8 %all_to_all.16.refs_4_ = f32[16,2,38]{2,1,0:T(2,128)} all-to-all(f32[16,2,38]{2,1,0:T(2,128)S(1)} %gain_solve.1), channel_id=1, replica_groups=mesh['obs'=2,'sub'=16] {'sub'}, dimensions={0} | all-to-all | bytes 9728 | tf_op jit(solution)/shard_map/all_to_all | solution.py:334
  51.2 8.4 %clean.1 = (bf16[2,2,4,192,703]{4,3,2,1,0:T(8,128)(2,1)}, f32[2,2,2,4,38]{4,3,2,1,0:T(4,128)}) custom-call(s32[1]{0:T(128)} %bitcast.refs_0_, f32[2,2,703]{2,1,0:T(2,128)} %refs_1_.3, bf16[38,703]{1,0:T(8,128)(2,1)} %constant.10.refs_2_, bf16[38,703]{1,0:T(8,128)(2,1)} %constant.11.refs_3_, f32[16,2,38]{2,1,0:T(2,128)} %all_to_all.16.refs_4_, ...), custom_call_target="tpu_custom_call" | custom-call | tf_op jit(solution)/shard_map/clean/pallas_call | solution.py:395
Async XLA Ops:
  0.6 39.5 %copy-start = (bf16[40,703]{1,0:T(8,128)(2,1)S(1)}, bf16[40,703]{1,0:T(8,128)(2,1)}, u32[]{:S(2)}) copy-start(bf16[40,703]{1,0:T(8,128)(2,1)} %constant.9.clone.refs_3_) | copy-start | bytes 168724
  0.6 39.4 %copy-start.1 = (bf16[40,703]{1,0:T(8,128)(2,1)S(1)}, bf16[40,703]{1,0:T(8,128)(2,1)}, u32[]{:S(2)}) copy-start(bf16[40,703]{1,0:T(8,128)(2,1)} %constant.8.clone.refs_2_) | copy-start | bytes 168724
  0.7 39.4 %copy-start.2 = (s32[2,2]{1,0:T(2,128)S(1)}, s32[2,2]{1,0:T(2,128)}, u32[]{:S(2)}) copy-start(s32[2,2]{1,0:T(2,128)} %refs_1_.2) | copy-start | bytes 52
  2.0 14.0 %all-to-all-start = ((s32[16,2,192]{2,1,0:T(2,128)}), s32[16,2,192]{2,1,0:T(2,128)S(1)}, u32[]{:S(2)}, u32[]{:S(2)}) async-start(s32[16,2,192]{2,1,0:T(2,128)} %broadcast_in_dim.2), calls=%async_computation | async-start | bytes 65536 | tf_op jit(solution)/shard_map/all_to_all | solution.py:334
  16.0 0.6 %copy-start.3 = (s32[16,2,192]{2,1,0:T(2,128)}, s32[16,2,192]{2,1,0:T(2,128)S(1)}, u32[]{:S(2)}) copy-start(s32[16,2,192]{2,1,0:T(2,128)S(1)} %all-to-all-done.refs_2_) | copy-start | bytes 73732

commit v2 on v1

--- a/solution.py
+++ b/solution.py
@@ -12,7 +12,6 @@
 STEPS_PER_TURN = 64.0
 ROWS = 40
 LANES = 384
-SYSTEMS = 16
 
 F32 = jnp.float32
 BF16 = jnp.bfloat16
@@ -67,11 +66,14 @@
         rows_ref[row, 2 * source + 1:2 * source + 2, :] = imag[row:row + 1]
 
 
-def sums_kernel(width, me_ref, win_ref, flags_ref, delay_ref, vis_ref, y_ref,
-                rows_s, member_s, alpha_s, window_s, coarse_s, fine_s, wave_s, mix_s, mexp_s, wt_s):
-    time, part = pl.program_id(0), pl.program_id(1)
+def sums_kernel(width, stages, me_ref, win_ref, *refs):
+    flag_refs, refs = refs[:stages], refs[stages:]
+    (delay_ref, vis_ref, keep_ref, send_ref,
+     rows_s, member_s, alpha_s, window_s, coarse_s, fine_s, wave_s, mix_s, mexp_s, wt_s) = refs
+    part, time = pl.program_id(0), pl.program_id(1)
     me = me_ref[0]
-    groups = flags_ref.shape[0]
+    near = flag_refs[0].shape[0]
+    groups = near * stages
     windows = win_ref.shape[1]
     anchor = me.astype(F32) * float(width)
 
@@ -102,18 +104,19 @@
         window_s[0] = jnp.broadcast_to(first_g, (windows, 128))
         window_s[1] = jnp.broadcast_to(last_g, (windows, 128))
         for t in range(2):
-            for g in range(groups):
-                wt_s[t, g:g + 1, :] = 1.0 - flags_ref[g, t:t + 1, :].astype(F32)
-            weights = wt_s[t].astype(BF16)
+            for slot in range(groups):
+                row = flag_refs[slot // near][slot % near, t:t + 1, :].astype(F32)
+                wt_s[lax.bitwise_xor(me, slot), t:t + 1, :] = 1.0 - row
+            weights = wt_s[:, t, :].astype(BF16)
             picked = dot(pick, weights)
             head = jnp.where(head_in, picked[:windows], 0.0)
             tail = jnp.where(tail_in, picked[windows:2 * windows], 0.0)
             count = jnp.sum(head + tail + picked[2 * windows:], axis=1, keepdims=True)
             scale = 1.0 / jnp.maximum(count, 1.0)
-            rows_s[t] = jnp.concatenate([head, tail, wt_s[t]], axis=0).astype(BF16)
+            rows_s[t] = jnp.concatenate([head, tail, wt_s[:, t, :]], axis=0).astype(BF16)
             window_s[2 + t] = jnp.broadcast_to(scale, (windows, 128))
             scale_r = jnp.sum(jnp.where(sub == lane, scale, 0.0), axis=0, keepdims=True)
-            own = 1.0 - flags_ref[me, t:t + 1, :].astype(F32)
+            own = 1.0 - flag_refs[0][0, t:t + 1, :].astype(F32)
             own_c = jnp.sum(jnp.where(diagonal, own, 0.0), axis=1, keepdims=True)
             chosen = jnp.where(member, own_c, 0.0)
             member_s[t] = chosen.astype(BF16)
@@ -122,7 +125,7 @@
         pick_full = full.astype(BF16)
         window_s[4, :, :groups] = pick_full.astype(F32)
 
-    size = y_ref.shape[2]
+    size = keep_ref.shape[2]
     delay = [delay_ref[s, pl.ds(time, 1), :] for s in range(2)]
     for s in range(2):
         cr, ci, fr, fi = phase_rows(delay[s], anchor, width)
@@ -151,7 +154,7 @@
             mix_s[slot, 1, rows, :] = low
         return carry
 
-    lax.fori_loop(0, width // 16, waves, 0)
+    lax.fori_loop(0, width // 16, waves, 0, unroll=4)
 
     rows = rows_s[time]
     sums = [dot(rows, mix_s[slot, 0]) + dot(rows, mix_s[slot, 1]) for slot in range(2)]
@@ -207,70 +210,86 @@
             return tuple(new)
 
         zero = jnp.zeros((8, 128), F32)
-        sums = lax.fori_loop(0, width // 16, step, (zero,) * 16)
-        for k in range(4):
-            for s in range(2):
-                for ri in range(2):
-                    y_ref[s * 4 + k, ri:ri + 1, lanes] = jnp.sum(
-                        sums[(k * 2 + s) * 2 + ri], axis=0, keepdims=True)
-
-
-def solve_kernel(window_count, me_ref, tracks_ref, first_ref, second_ref, part_ref, gain_ref):
-    system = lax.rem(me_ref[0], SYSTEMS)
-    total = part_ref[0]
-    for source in range(1, part_ref.shape[0]):
-        total = total + part_ref[source]
-    rows = []
+        sums = lax.fori_loop(0, width // 16, step, (zero,) * 16, unroll=4)
+        for out_ref, chosen_half in ((keep_ref, 0), (send_ref, 1)):
+            @pl.when(lax.bitwise_xor(time, lax.bitwise_and(me, 1)) == chosen_half)
+            def write():
+                for k in range(4):
+                    for s in range(2):
+                        place = lax.bitwise_xor(s, lax.bitwise_and(lax.div(me, 2), 1)) * 4 + k
+                        for ri in range(2):
+                            out_ref[place, ri:ri + 1, lanes] = jnp.sum(
+                                sums[(k * 2 + s) * 2 + ri], axis=0, keepdims=True)
+
+
+def solve_kernel(window_count, me_ref, tracks_ref, first_ref, second_ref, *refs):
+    parts, gain_ref = refs[:-1], refs[-1]
+    me = me_ref[0]
+    systems = gain_ref.shape[0]
+    total = parts[0][...]
+    for part in parts[1:]:
+        total = total + part[...]
     hot = first_ref[...]
     other = second_ref[...]
-    for table in (hot, other):
-        for ri in range(2):
-            rows += [table * piece for piece in split_three(total[ri:ri + 1])]
-    rows = [row.astype(BF16) for row in rows]
     nt = lambda left, right: lax.dot_general(
         left, right, (((1,), (1,)), ((), ())), preferred_element_type=F32)
-    upper = nt(jnp.concatenate(rows[:6], axis=0), other)
-    lower = nt(jnp.concatenate(rows[6:], axis=0), hot)
+    upper, lower = [], []
+    for system in range(systems):
+        for ri in range(2):
+            for piece in split_two(total[system, ri:ri + 1]):
+                upper.append(hot * piece)
+                lower.append(other * piece)
+    upper = nt(jnp.concatenate(upper, axis=0), other)
+    lower = nt(jnp.concatenate(lower, axis=0), hot)
     cut = lambda value, i: value[i * ROWS:(i + 1) * ROWS]
-    join = lambda value, i: (cut(value, 3 * i) + cut(value, 3 * i + 1)) + cut(value, 3 * i + 2)
-    re = join(upper, 0) + join(lower, 0)
-    im = join(upper, 1) - join(lower, 1)
-    live_r = iota((1, ROWS), 1) < float(STATIONS)
-    live_c = iota((ROWS, 1), 0) < float(STATIONS)
-    row_re, row_im = jnp.where(live_r, 1.0, 0.0), jnp.zeros((1, ROWS), F32)
-    col_re, col_im = jnp.where(live_c, 1.0, 0.0), jnp.zeros((ROWS, 1), F32)
+    join = lambda value, i: cut(value, 2 * i) + cut(value, 2 * i + 1)
+    live_r = jnp.where(iota((1, ROWS), 1) < float(STATIONS), 1.0, 0.0)
+    live_c = jnp.where(iota((ROWS, 1), 0) < float(STATIONS), 1.0, 0.0)
+    matrices = [(join(upper, 2 * i) + join(lower, 2 * i), join(upper, 2 * i + 1) - join(lower, 2 * i + 1))
+                for i in range(systems)]
+    states = [(live_r, 0.0 * live_r, live_c, 0.0 * live_c)] * systems
     for turn in range(GITERS):
-        pull_cr = jnp.sum(re * row_re - im * row_im, axis=1, keepdims=True)
-        pull_ci = jnp.sum(re * row_im + im * row_re, axis=1, keepdims=True)
-        pull_rr = jnp.sum(re * col_re + im * col_im, axis=0, keepdims=True)
-        pull_ri = jnp.sum(re * col_im - im * col_re, axis=0, keepdims=True)
-        power_r = row_re * row_re + row_im * row_im
-        power_c = col_re * col_re + col_im * col_im
-        total = jnp.sum(power_c, axis=0, keepdims=True)
-        inverse_r = 1.0 / (window_count * (total - power_r) + DAMPING)
-        inverse_c = 1.0 / (window_count * (total - power_c) + DAMPING)
-        row_re, row_im = 0.5 * (row_re + pull_rr * inverse_r), 0.5 * (row_im + pull_ri * inverse_r)
-        col_re, col_im = 0.5 * (col_re + pull_cr * inverse_c), 0.5 * (col_im + pull_ci * inverse_c)
-    visible = tracks_ref[lax.rem(lax.div(system, 4), 2), lax.div(system, 8)].astype(F32)
-    gains = jnp.concatenate([row_re, row_im], axis=0)[:, :STATIONS] * visible
-    for target in range(gain_ref.shape[0]):
-        gain_ref[target] = gains
-
-
-def clean_kernel(width, me_ref, delay_ref, first_ref, second_ref, gain_ref, vis_ref, out_ref, gain_out_ref,
-                 coarse_s, split_s):
-    time, part = pl.program_id(0), pl.program_id(1)
-    anchor = me_ref[0].astype(F32) * float(width)
+        for system in range(systems):
+            re, im = matrices[system]
+            row_re, row_im, col_re, col_im = states[system]
+            pull_cr = jnp.sum(re * row_re - im * row_im, axis=1, keepdims=True)
+            pull_ci = jnp.sum(re * row_im + im * row_re, axis=1, keepdims=True)
+            pull_rr = jnp.sum(re * col_re + im * col_im, axis=0, keepdims=True)
+            pull_ri = jnp.sum(re * col_im - im * col_re, axis=0, keepdims=True)
+            power_r = row_re * row_re + row_im * row_im
+            power_c = col_re * col_re + col_im * col_im
+            total = jnp.sum(power_c, axis=0, keepdims=True)
+            inverse_r = 0.5 / (window_count * (total - power_r) + DAMPING)
+            inverse_c = 0.5 / (window_count * (total - power_c) + DAMPING)
+            states[system] = (0.5 * row_re + pull_rr * inverse_r, 0.5 * row_im + pull_ri * inverse_r,
+                              0.5 * col_re + pull_cr * inverse_c, 0.5 * col_im + pull_ci * inverse_c)
+    visible = tracks_ref[lax.bitwise_and(lax.div(me, 2), 1), lax.bitwise_and(me, 1)].astype(F32)
+    for system in range(systems):
+        row_re, row_im = states[system][:2]
+        gain_ref[system] = jnp.concatenate([row_re, row_im], axis=0)[:, :STATIONS] * visible
+
+
+def clean_kernel(width, me_ref, delay_ref, first_ref, second_ref, *refs):
+    gain_refs, refs = refs[:4], refs[4:]
+    vis_ref, out_ref, gain_out_ref, coarse_s, split_s = refs
+    part, time = pl.program_id(0), pl.program_id(1)
+    me = me_ref[0]
+    anchor = me.astype(F32) * float(width)
     size = out_ref.shape[4]
 
     @pl.when((time == 0) & (part == 0))
     def prepare():
+        mine = lax.bitwise_and(me, 3)
+        held = [ref[...] for ref in gain_refs]
         for t in range(2):
             for s in range(2):
+                owner = t + 2 * s
+                group = held[0]
+                for d in range(1, 4):
+                    group = jnp.where(lax.bitwise_xor(mine, owner) == d, held[d], group)
                 for k in range(4):
-                    pair = gain_ref[t * 8 + s * 4 + k]
                     for ri in range(2):
-                        gain_out_ref[ri, s, t, k:k + 1, :] = pair[ri:ri + 1]
+                        gain_out_ref[ri, s, t, k:k + 1, :] = group[k, ri:ri + 1]
         for t in range(2):
             both = jnp.concatenate(
                 [jnp.concatenate([gain_out_ref[ri, s, t] for s in range(2)], axis=0) for ri in range(2)], axis=0)
@@ -321,7 +340,7 @@
                 out_ref[1, 0, k, rows, lanes] = jnp.concatenate(im, axis=0).astype(BF16)
             return carry
 
-        lax.fori_loop(0, width // 16, step, 0)
+        lax.fori_loop(0, width // 16, step, 0, unroll=4)
 
 
 def tables():
@@ -330,8 +349,9 @@
     return jnp.asarray(eye[:, first], BF16), jnp.asarray(eye[:, second], BF16)
 
 
-def exchange(value):
-    return lax.all_to_all(value, "sub", 0, 0)
+def partner(value, bits):
+    count = lax.axis_size("sub")
+    return lax.ppermute(value, "sub", [(i, i ^ bits) for i in range(count)])
 
 
 def smem():
@@ -345,24 +365,29 @@
     window_count = windows.shape[0]
     turned = jnp.transpose(visibilities, (0, 1, 2, 4, 3))
     me = lax.axis_index("sub").astype(jnp.int32).reshape(1)
-    gathered = exchange(jnp.broadcast_to(flags[None], (count,) + flags.shape))
+    gathered = [flags[None]]
+    stride = 1
+    while stride < count:
+        gathered = [jnp.concatenate(gathered, axis=0)] if len(gathered) > 1 else gathered
+        gathered += [partner(gathered[0], stride * d) for d in range(1, min(4, count // stride))]
+        stride *= 4
     parts = pl.cdiv(pairs, LANES)
-    delay_spec = pl.BlockSpec((2, 2, LANES), lambda t, b: (0, 0, b))
-    vis_spec = pl.BlockSpec((2, 1, 4, width, LANES), lambda t, b: (0, t, 0, 0, b))
+    delay_spec = pl.BlockSpec((2, 2, LANES), lambda b, t: (0, 0, b))
+    vis_spec = pl.BlockSpec((2, 1, 4, width, LANES), lambda b, t: (0, t, 0, 0, b))
     rows = 2 * window_count + count
     vmem = lambda *shape: pltpu.VMEM(shape, F32)
-    y = pl.pallas_call(
-        lambda *refs: sums_kernel(width, *refs),
-        grid=(2, parts),
+    keep, send = pl.pallas_call(
+        lambda *refs: sums_kernel(width, len(gathered), *refs),
+        grid=(parts, 2),
         in_specs=[
             smem(),
-            pl.BlockSpec((1, window_count), lambda t, b: (0, 0)),
-            pl.BlockSpec((count, 2, width), lambda t, b: (0, 0, 0)),
+            pl.BlockSpec((1, window_count), lambda b, t: (0, 0)),
+        ] + [pl.BlockSpec(piece.shape, lambda b, t: (0, 0, 0)) for piece in gathered] + [
             delay_spec,
             vis_spec,
         ],
-        out_specs=pl.BlockSpec((8, 2, LANES), lambda t, b: (t, 0, b)),
-        out_shape=jax.ShapeDtypeStruct((SYSTEMS, 2, pairs), F32),
+        out_specs=[pl.BlockSpec((8, 2, LANES), lambda b, t: (0, 0, b))] * 2,
+        out_shape=[jax.ShapeDtypeStruct((8, 2, pairs), F32)] * 2,
         scratch_shapes=[
             pltpu.VMEM((2, rows, width), BF16),
             pltpu.VMEM((2, width, window_count), BF16),
@@ -373,37 +398,43 @@
             vmem(2, 2, width, LANES),
             pltpu.VMEM((2, 2, width, LANES), BF16),
             vmem(2, width, LANES),
-            vmem(2, count, width),
+            vmem(count, 2, width),
         ],
         compiler_params=pltpu.CompilerParams(vmem_limit_bytes=60 * 2 ** 20),
         name="window_sums",
-    )(me, windows.reshape(1, window_count), gathered, delays, turned)
-    if count > SYSTEMS:
-        y = jnp.tile(y, (count // SYSTEMS, 1, 1))
-    y = exchange(y)
+    )(me, windows.reshape(1, window_count), *gathered, delays, turned)
+    got = partner(send, 1)
+    send = keep[4:] + got[4:]
+    keep = keep[:4] + got[:4]
+    pieces = [keep, partner(send, 2)]
+    stride = 4
+    while stride < count:
+        keep = pieces[0] + pieces[1]
+        pieces = [keep, partner(keep, stride)]
+        stride *= 2
     first, second = tables()
     gains = pl.pallas_call(
         lambda *refs: solve_kernel(float(window_count), *refs),
-        in_specs=[smem(), smem()] + [pl.BlockSpec(memory_space=pltpu.VMEM)] * 3,
+        in_specs=[smem(), smem()] + [pl.BlockSpec(memory_space=pltpu.VMEM)] * (2 + len(pieces)),
         out_specs=pl.BlockSpec(memory_space=pltpu.VMEM),
-        out_shape=jax.ShapeDtypeStruct((count, 2, STATIONS), F32),
+        out_shape=jax.ShapeDtypeStruct((4, 2, STATIONS), F32),
         compiler_params=pltpu.CompilerParams(vmem_limit_bytes=40 * 2 ** 20),
         name="gain_solve",
-    )(me, tracks, first, second, y)
-    gains = exchange(gains)
-    table_spec = pl.BlockSpec((STATIONS, LANES), lambda t, b: (0, b))
+    )(me, tracks, first, second, *pieces)
+    gains = [gains] + [partner(gains, d) for d in range(1, 4)]
+    table_spec = pl.BlockSpec((STATIONS, LANES), lambda b, t: (0, b))
     cleaned, gains = pl.pallas_call(
         lambda *refs: clean_kernel(width, *refs),
-        grid=(2, parts),
+        grid=(parts, 2),
         in_specs=[
             smem(),
             delay_spec,
             table_spec,
             table_spec,
-            pl.BlockSpec((count, 2, STATIONS), lambda t, b: (0, 0, 0)),
+        ] + [pl.BlockSpec((4, 2, STATIONS), lambda b, t: (0, 0, 0))] * 4 + [
             vis_spec,
         ],
-        out_specs=[vis_spec, pl.BlockSpec((2, 2, 2, 4, STATIONS), lambda t, b: (0, 0, 0, 0, 0))],
+        out_specs=[vis_spec, pl.BlockSpec((2, 2, 2, 4, STATIONS), lambda b, t: (0, 0, 0, 0, 0))],
         out_shape=[
             jax.ShapeDtypeStruct(turned.shape, BF16),
             jax.ShapeDtypeStruct((2, 2, 2, 4, STATIONS), F32),
@@ -411,7 +442,7 @@
         scratch_shapes=[vmem(width // 8, 4, LANES), pltpu.VMEM((2, 48, STATIONS), BF16)],
         compiler_params=pltpu.CompilerParams(vmem_limit_bytes=60 * 2 ** 20),
         name="clean",
-    )(me, delays, first[:STATIONS], second[:STATIONS], gains, turned)
+    )(me, delays, first[:STATIONS], second[:STATIONS], *gains, turned)
     return jnp.transpose(cleaned, (0, 1, 2, 4, 3)), gains
 
 

time: 60 us -> 58.8 us (0.980)
  blocking collectives: 20.6 us -> 0 us
  waiting for transfers between devices: 6.63 us -> 19.6 us
  starting transfers between devices: 7.39 us -> 12.6 us
  other arithmetic: 0 us -> 2.21 us
  Pallas kernels: 22.3 us -> 21.5 us
    all_to_all x2 -> x0, blocking collectives: 20.6 us -> none  [exchange(): return lax.all_to_all(value, 'sub', 0, 0)]
    ppermute x0 -> x13, waiting for transfers between devices: none -> 19.6 us  [partner(): return lax.ppermute(value, 'sub', [(i, i ^ bits) for i in range(count)])]
    ppermute x0 -> x13, starting transfers between devices: none -> 12.6 us  [partner(): return lax.ppermute(value, 'sub', [(i, i ^ bits) for i in range(count)])]
    all_to_all x1 -> x0, starting transfers between devices: 7.39 us -> none  [exchange(): return lax.all_to_all(value, 'sub', 0, 0)]
    all_to_all x1 -> x0, waiting for transfers between devices: 6.63 us -> none  [exchange(): return lax.all_to_all(value, 'sub', 0, 0)]
    add x0 -> x3, other arithmetic: none -> 1.52 us  [the longest x2 0.77 us: local(): keep = pieces[0] + pieces[1]]
    broadcast_in_dim x1 -> x0, local copies, waits for them, and re-layouts: 1.35 us -> none  [local(): gathered = exchange(jnp.broadcast_to(flags[None], (count,) + flags.shape))]
    pallas_call x2, Pallas kernels: 20.9 us -> 19.6 us  [the longest x1 11.5 us: local(): pl.pallas_call(lambda *refs: sums_kernel(width, len(gathered), *refs), gr...]
  transfers between devices with their start and end apart: 1 -> 13, of which waited for: 1 -> 10; matrix products, arithmetic and copies ran while one was open for 0% -> 0% of each run, Pallas kernels for 0% -> 0%
where the time goes in v2:
time: 58.8 us; the launch traced here: 58.4 us
  Pallas kernels  21.5 us (37%)
  waiting for transfers between devices  19.6 us (33%)
  starting transfers between devices  12.6 us (21%)
  other arithmetic  2.21 us (4%)
  local copies, waits for them, and re-layouts  1.77 us (3%)
  between operations  0.74 us (1%)
    ppermute x13, waiting for transfers between devices, partner(): return lax.ppermute(value, 'sub', [(i, i ^ bits) for i in range(count)])  19.6 us
    ppermute x13, starting transfers between devices, partner(): return lax.ppermute(value, 'sub', [(i, i ^ bits) for i in range(count)])  12.6 us
    pallas_call x1, Pallas kernels, local(): pl.pallas_call(lambda *refs: sums_kernel(width, len(gathered), *refs), gr...  11.5 us
    pallas_call x1, Pallas kernels, local(): pl.pallas_call(lambda *refs: clean_kernel(width, *refs), grid=(parts, 2),...  8.12 us
    pallas_call x1, Pallas kernels, local(): pl.pallas_call(lambda *refs: solve_kernel(float(window_count), *refs), in...  1.9 us
    unnamed x22, local copies, waits for them, and re-layouts  1.77 us
  transfers between devices with their start and end apart: 13, of which 10 were waited for; matrix products, arithmetic and copies ran while one was open for 0% of the time, Pallas kernels for 0%

profile of v2, /device:TPU:0, one launch (start us, length us, event | category | flops | bytes accessed | tf_op | source)
XLA Modules:
  0.0 58.4 jit_solution(7107615187025136963)
XLA Ops:
  0.6 0.0 copy-start
  0.6 0.0 copy-start.1
  0.7 0.0 copy-start.3
  0.7 2.5 %collective-permute-start.2 = (s32[1,2,192]{2,1,0:T(2,128)}, s32[1,2,192]{2,1,0:T(2,128)S(1)}, u32[]{:S(2)}, u32[]{:S(2)}) collective-permute-start(s32[1,2,192]{2,1,0:T(2,128)} %bitcast.7), channel_id=1, source_target_pairs={{0,3},{1,2},{2,1},{3,0},{4,7},{5,6},{6,5},{7,4},{8,11},{9,10},{10,... | collective-permute-start | bytes 4616 | tf_op jit(solution)/shard_map/ppermute | solution.py:354
  3.1 0.6 %collective-permute-start.1 = (s32[1,2,192]{2,1,0:T(2,128)}, s32[1,2,192]{2,1,0:T(2,128)S(1)}, u32[]{:S(2)}, u32[]{:S(2)}) collective-permute-start(s32[1,2,192]{2,1,0:T(2,128)} %bitcast.8), channel_id=1, source_target_pairs={{0,2},{1,3},{2,0},{3,1},{4,6},{5,7},{6,4},{7,5},{8,10},{9,11},{10,... | collective-permute-start | bytes 4616 | tf_op jit(solution)/shard_map/ppermute | solution.py:354
  3.8 0.0 collective-permute-start
  3.8 0.8 %collective-permute-done.2 = s32[1,2,192]{2,1,0:T(2,128)S(1)} collective-permute-done((s32[1,2,192]{2,1,0:T(2,128)}, s32[1,2,192]{2,1,0:T(2,128)S(1)}, u32[]{:S(2)}, u32[]{:S(2)}) %collective-permute-start.2) | collective-permute-done | bytes 1568 | tf_op jit(solution)/shard_map/ppermute | solution.py:354
  4.7 2.3 %collective-permute-done.1 = s32[1,2,192]{2,1,0:T(2,128)S(1)} collective-permute-done((s32[1,2,192]{2,1,0:T(2,128)}, s32[1,2,192]{2,1,0:T(2,128)S(1)}, u32[]{:S(2)}, u32[]{:S(2)}) %collective-permute-start.1) | collective-permute-done | bytes 1568 | tf_op jit(solution)/shard_map/ppermute | solution.py:354
  6.9 0.0 collective-permute-done
  6.9 0.7 %pad_add_fusion.refs_2_ = s32[4,2,192]{2,1,0:T(2,128)S(1)} fusion(s32[1,2,192]{2,1,0:T(2,128)S(1)} %collective-permute-done.2, s32[1,2,192]{2,1,0:T(2,128)S(1)} %collective-permute-done.1, s32[1,2,192]{2,1,0:T(2,128)S(1)} %collective-permute-done, s32[1,2,192]{2,1,0:T(2,128)} %bitcast.10), kind=kLoop, calls=%fused_computation.3 | loop fusion | flops 4608 | bytes 12288 | tf_op jit(solution)/shard_map/concatenate | solution.py:371
  7.6 0.0 copy-start.4
  7.6 3.6 %collective-permute-start.5 = (s32[4,2,192]{2,1,0:T(2,128)S(1)}, s32[4,2,192]{2,1,0:T(2,128)S(1)}, u32[]{:S(2)}, u32[]{:S(2)}) collective-permute-start(s32[4,2,192]{2,1,0:T(2,128)S(1)} %pad_add_fusion.refs_2_), channel_id=1, source_target_pairs={{0,12},{1,13},{2,14},{3,15},{4,8},{5,9},{6,10},{7,11},{8,4},{9,5},... | collective-permute-start | bytes 18440 | tf_op jit(solution)/shard_map/ppermute | solution.py:354
  11.2 0.0 collective-permute-start.4
  11.2 0.8 %collective-permute-start.3 = (s32[4,2,192]{2,1,0:T(2,128)S(1)}, s32[4,2,192]{2,1,0:T(2,128)S(1)}, u32[]{:S(2)}, u32[]{:S(2)}) collective-permute-start(s32[4,2,192]{2,1,0:T(2,128)S(1)} %pad_add_fusion.refs_2_), channel_id=1, source_target_pairs={{0,4},{1,5},{2,6},{3,7},{4,0},{5,1},{6,2},{7,3},{8,12},{9,13},{10,... | collective-permute-start | bytes 18440 | tf_op jit(solution)/shard_map/ppermute | solution.py:354
  12.0 1.2 %collective-permute-done.5.refs_5_ = s32[4,2,192]{2,1,0:T(2,128)S(1)} collective-permute-done((s32[4,2,192]{2,1,0:T(2,128)S(1)}, s32[4,2,192]{2,1,0:T(2,128)S(1)}, u32[]{:S(2)}, u32[]{:S(2)}) %collective-permute-start.5) | collective-permute-done | bytes 6176 | tf_op jit(solution)/shard_map/ppermute | solution.py:354
  13.2 2.6 %collective-permute-done.4.refs_4_ = s32[4,2,192]{2,1,0:T(2,128)S(1)} collective-permute-done((s32[4,2,192]{2,1,0:T(2,128)S(1)}, s32[4,2,192]{2,1,0:T(2,128)S(1)}, u32[]{:S(2)}, u32[]{:S(2)}) %collective-permute-start.4) | collective-permute-done | bytes 6176 | tf_op jit(solution)/shard_map/ppermute | solution.py:354
  15.8 0.0 collective-permute-done.3.refs_3_
  15.8 0.0 copy-done.4
  15.8 0.0 copy-done.5
  15.8 0.6 copy-done.6
  16.4 0.0 copy-done.7
  16.4 11.5 %window_sums.1 = (f32[8,2,703]{2,1,0:T(2,128)}, f32[8,2,703]{2,1,0:T(2,128)}) custom-call(s32[1]{0:T(128)} %bitcast.refs_0_, s32[1,32]{1,0:T(1,128)} %bitcast.11, s32[4,2,192]{2,1,0:T(2,128)} %copy-done.4, s32[4,2,192]{2,1,0:T(2,128)} %copy-done.7, s32[4,2,192]{2,1,0:T(2,128)} %copy-done.6, s32[4,2,192]{2,1,0:T(2,128)} %copy-done.5, f32[2,2,703]{2,1,0:T(2,128)} %refs_1_.3, ...), custom_call_target="tpu_custom_call" | custom-call | tf_op jit(solution)/shard_map/window_sums/pallas_call | solution.py:379
  27.8 0.0 collective-permute-start.6
  27.8 1.4 %collective-permute-done.6 = f32[8,2,703]{2,1,0:T(2,128)S(1)} collective-permute-done((f32[8,2,703]{2,1,0:T(2,128)}, f32[8,2,703]{2,1,0:T(2,128)S(1)}, u32[]{:S(2)}, u32[]{:S(2)}) %collective-permute-start.6) | collective-permute-done | bytes 45024 | tf_op jit(solution)/shard_map/ppermute | solution.py:354
  29.3 0.8 %slice_add_fusion = f32[4,2,703]{2,1,0:T(2,128)S(1)} fusion(f32[8,2,703]{2,1,0:T(2,128)S(1)} %collective-permute-done.6, f32[8,2,703]{2,1,0:T(2,128)} %get-tuple-element.6), kind=kLoop, calls=%fused_computation | loop fusion | flops 5624 | bytes 67488 | tf_op jit(solution)/shard_map/add | solution.py:407
  30.0 0.7 %collective-permute-start.7 = (f32[4,2,703]{2,1,0:T(2,128)S(1)}, f32[4,2,703]{2,1,0:T(2,128)S(1)}, u32[]{:S(2)}, u32[]{:S(2)}) collective-permute-start(f32[4,2,703]{2,1,0:T(2,128)S(1)} %slice_add_fusion), channel_id=1, source_target_pairs={{0,2},{1,3},{2,0},{3,1},{4,6},{5,7},{6,4},{7,5},{8,10},{9,11},{10,... | collective-permute-start | bytes 67496 | tf_op jit(solution)/shard_map/ppermute | solution.py:354
  30.7 3.2 %collective-permute-done.7 = f32[4,2,703]{2,1,0:T(2,128)S(1)} collective-permute-done((f32[4,2,703]{2,1,0:T(2,128)S(1)}, f32[4,2,703]{2,1,0:T(2,128)S(1)}, u32[]{:S(2)}, u32[]{:S(2)}) %collective-permute-start.7) | collective-permute-done | bytes 22528 | tf_op jit(solution)/shard_map/ppermute | solution.py:354
  33.9 0.8 %fusion = f32[4,2,703]{2,1,0:T(2,128)S(1)} fusion(f32[4,2,703]{2,1,0:T(2,128)S(1)} %collective-permute-done.7, f32[8,2,703]{2,1,0:T(2,128)S(1)} %collective-permute-done.6, f32[8,2,703]{2,1,0:T(2,128)} %get-tuple-element.6), kind=kLoop, calls=%fused_computation.2 | loop fusion | flops 11248 | bytes 89984 | tf_op jit(solution)/shard_map/add | solution.py:412
  34.7 0.1 collective-permute-start.8
  34.8 3.8 %collective-permute-done.8 = f32[4,2,703]{2,1,0:T(2,128)S(1)} collective-permute-done((f32[4,2,703]{2,1,0:T(2,128)S(1)}, f32[4,2,703]{2,1,0:T(2,128)S(1)}, u32[]{:S(2)}, u32[]{:S(2)}) %collective-permute-start.8) | collective-permute-done | bytes 22528 | tf_op jit(solution)/shard_map/ppermute | solution.py:354
  38.6 2.3 %collective-permute-start.9 = (f32[4,2,703]{2,1,0:T(2,128)S(1)}, f32[4,2,703]{2,1,0:T(2,128)S(1)}, u32[]{:S(2)}, u32[]{:S(2)}) collective-permute-start(f32[4,2,703]{2,1,0:T(2,128)S(1)} %add.15.refs_4_), channel_id=1, source_target_pairs={{0,8},{1,9},{2,10},{3,11},{4,12},{5,13},{6,14},{7,15},{8,0},{9,1},... | collective-permute-start | bytes 67496 | tf_op jit(solution)/shard_map/ppermute | solution.py:354
  40.9 2.5 %collective-permute-done.9.refs_5_ = f32[4,2,703]{2,1,0:T(2,128)S(1)} collective-permute-done((f32[4,2,703]{2,1,0:T(2,128)S(1)}, f32[4,2,703]{2,1,0:T(2,128)S(1)}, u32[]{:S(2)}, u32[]{:S(2)}) %collective-permute-start.9) | collective-permute-done | bytes 22528 | tf_op jit(solution)/shard_map/ppermute | solution.py:354
  43.4 0.0 copy-done
  43.4 0.0 copy-done.1
  43.4 0.0 copy-done.3
  43.4 1.9 %gain_solve.1.refs_4_ = f32[4,2,38]{2,1,0:T(2,128)S(1)} custom-call(s32[1]{0:T(128)} %bitcast.refs_0_, s32[2,2]{1,0:T(2,128)S(1)} %copy-done.3, bf16[40,703]{1,0:T(8,128)(2,1)S(1)} %copy-done.1, bf16[40,703]{1,0:T(8,128)(2,1)S(1)} %copy-done, f32[4,2,703]{2,1,0:T(2,128)S(1)} %add.15.refs_4_, f32[4,2,703]{2,1,0:T(2,128)S(1)} %collective-permute-done.9.refs_5_), custom_call_target="tpu_custom_call" | custom-call | tf_op jit(solution)/shard_map/gain_solve/pallas_call | solution.py:416
  45.3 0.0 copy-start.2
  45.3 0.1 collective-permute-start.12
  45.4 0.7 %collective-permute-start.11 = (f32[4,2,38]{2,1,0:T(2,128)S(1)}, f32[4,2,38]{2,1,0:T(2,128)S(1)}, u32[]{:S(2)}, u32[]{:S(2)}) collective-permute-start(f32[4,2,38]{2,1,0:T(2,128)S(1)} %gain_solve.1.refs_4_), channel_id=1, source_target_pairs={{0,2},{1,3},{2,0},{3,1},{4,6},{5,7},{6,4},{7,5},{8,10},{9,11},{10,... | collective-permute-start | bytes 3656 | tf_op jit(solution)/shard_map/ppermute | solution.py:354
  46.1 1.1 %collective-permute-start.10 = (f32[4,2,38]{2,1,0:T(2,128)S(1)}, f32[4,2,38]{2,1,0:T(2,128)S(1)}, u32[]{:S(2)}, u32[]{:S(2)}) collective-permute-start(f32[4,2,38]{2,1,0:T(2,128)S(1)} %gain_solve.1.refs_4_), channel_id=1, source_target_pairs={{0,1},{1,0},{2,3},{3,2},{4,5},{5,4},{6,7},{7,6},{8,9},{9,8},{10,11... | collective-permute-start | bytes 3656 | tf_op jit(solution)/shard_map/ppermute | solution.py:354
  47.2 1.2 %collective-permute-done.12.refs_7_ = f32[4,2,38]{2,1,0:T(2,128)S(1)} collective-permute-done((f32[4,2,38]{2,1,0:T(2,128)S(1)}, f32[4,2,38]{2,1,0:T(2,128)S(1)}, u32[]{:S(2)}, u32[]{:S(2)}) %collective-permute-start.12) | collective-permute-done | bytes 1248 | tf_op jit(solution)/shard_map/ppermute | solution.py:354
  48.4 0.7 %collective-permute-done.11.refs_6_ = f32[4,2,38]{2,1,0:T(2,128)S(1)} collective-permute-done((f32[4,2,38]{2,1,0:T(2,128)S(1)}, f32[4,2,38]{2,1,0:T(2,128)S(1)}, u32[]{:S(2)}, u32[]{:S(2)}) %collective-permute-start.11) | collective-permute-done | bytes 1248 | tf_op jit(solution)/shard_map/ppermute | solution.py:354
  49.1 0.0 collective-permute-done.10.refs_5_
  49.1 0.0 copy-done.2
  49.1 0.0 copy-done.8
  49.1 0.6 copy-done.9
  49.6 0.6 %copy-done.10 = f32[4,2,38]{2,1,0:T(2,128)} copy-done((f32[4,2,38]{2,1,0:T(2,128)}, f32[4,2,38]{2,1,0:T(2,128)S(1)}, u32[]{:S(2)}) %copy-start.10) | copy-done | bytes 1240
  50.2 8.1 %clean.1 = (bf16[2,2,4,192,703]{4,3,2,1,0:T(8,128)(2,1)}, f32[2,2,2,4,38]{4,3,2,1,0:T(4,128)}) custom-call(s32[1]{0:T(128)} %bitcast.refs_0_, f32[2,2,703]{2,1,0:T(2,128)} %refs_1_.3, bf16[38,703]{1,0:T(8,128)(2,1)} %constant.10.refs_2_, bf16[38,703]{1,0:T(8,128)(2,1)} %constant.11.refs_3_, f32[4,2,38]{2,1,0:T(2,128)} %copy-done.2, f32[4,2,38]{2,1,0:T(2,128)} %copy-done.10, ...), custom_call_target="tpu_custom_call" | custom-call | tf_op jit(solution)/shard_map/clean/pallas_call | solution.py:426
  (7 shorter events, 0.0 us)
Async XLA Ops:
  0.6 42.8 %copy-start = (bf16[40,703]{1,0:T(8,128)(2,1)S(1)}, bf16[40,703]{1,0:T(8,128)(2,1)}, u32[]{:S(2)}) copy-start(bf16[40,703]{1,0:T(8,128)(2,1)} %constant.9.clone.refs_3_) | copy-start | bytes 168724
  0.6 42.7 %copy-start.1 = (bf16[40,703]{1,0:T(8,128)(2,1)S(1)}, bf16[40,703]{1,0:T(8,128)(2,1)}, u32[]{:S(2)}) copy-start(bf16[40,703]{1,0:T(8,128)(2,1)} %constant.8.clone.refs_2_) | copy-start | bytes 168724
  0.7 42.7 %copy-start.3 = (s32[2,2]{1,0:T(2,128)S(1)}, s32[2,2]{1,0:T(2,128)}, u32[]{:S(2)}) copy-start(s32[2,2]{1,0:T(2,128)} %refs_1_.2) | copy-start | bytes 52
  0.7 4.0 %collective-permute-start.2 = (s32[1,2,192]{2,1,0:T(2,128)}, s32[1,2,192]{2,1,0:T(2,128)S(1)}, u32[]{:S(2)}, u32[]{:S(2)}) collective-permute-start(s32[1,2,192]{2,1,0:T(2,128)} %bitcast.7), channel_id=1, source_target_pairs={{0,3},{1,2},{2,1},{3,0},{4,7},{5,6},{6,5},{7,4},{8,11},{9,10},{10,... | collective-permute-start | bytes 4616 | tf_op jit(solution)/shard_map/ppermute | solution.py:354
  3.1 3.8 %collective-permute-start.1 = (s32[1,2,192]{2,1,0:T(2,128)}, s32[1,2,192]{2,1,0:T(2,128)S(1)}, u32[]{:S(2)}, u32[]{:S(2)}) collective-permute-start(s32[1,2,192]{2,1,0:T(2,128)} %bitcast.8), channel_id=1, source_target_pairs={{0,2},{1,3},{2,0},{3,1},{4,6},{5,7},{6,4},{7,5},{8,10},{9,11},{10,... | collective-permute-start | bytes 4616 | tf_op jit(solution)/shard_map/ppermute | solution.py:354
  3.8 3.2 %collective-permute-start = (s32[1,2,192]{2,1,0:T(2,128)}, s32[1,2,192]{2,1,0:T(2,128)S(1)}, u32[]{:S(2)}, u32[]{:S(2)}) collective-permute-start(s32[1,2,192]{2,1,0:T(2,128)} %bitcast.9), channel_id=1, source_target_pairs={{0,1},{1,0},{2,3},{3,2},{4,5},{5,4},{6,7},{7,6},{8,9},{9,8},{10,11... | collective-permute-start | bytes 4616 | tf_op jit(solution)/shard_map/ppermute | solution.py:354
  7.6 8.2 %copy-start.4 = (s32[4,2,192]{2,1,0:T(2,128)}, s32[4,2,192]{2,1,0:T(2,128)S(1)}, u32[]{:S(2)}) copy-start(s32[4,2,192]{2,1,0:T(2,128)S(1)} %pad_add_fusion.refs_2_) | copy-start | bytes 18436
  7.6 5.6 %collective-permute-start.5 = (s32[4,2,192]{2,1,0:T(2,128)S(1)}, s32[4,2,192]{2,1,0:T(2,128)S(1)}, u32[]{:S(2)}, u32[]{:S(2)}) collective-permute-start(s32[4,2,192]{2,1,0:T(2,128)S(1)} %pad_add_fusion.refs_2_), channel_id=1, source_target_pairs={{0,12},{1,13},{2,14},{3,15},{4,8},{5,9},{6,10},{7,11},{8,4},{9,5},... | collective-permute-start | bytes 18440 | tf_op jit(solution)/shard_map/ppermute | solution.py:354
  11.2 4.5 %collective-permute-start.4 = (s32[4,2,192]{2,1,0:T(2,128)S(1)}, s32[4,2,192]{2,1,0:T(2,128)S(1)}, u32[]{:S(2)}, u32[]{:S(2)}) collective-permute-start(s32[4,2,192]{2,1,0:T(2,128)S(1)} %pad_add_fusion.refs_2_), channel_id=1, source_target_pairs={{0,8},{1,9},{2,10},{3,11},{4,12},{5,13},{6,14},{7,15},{8,0},{9,1},... | collective-permute-start | bytes 18440 | tf_op jit(solution)/shard_map/ppermute | solution.py:354
  11.2 4.6 %collective-permute-start.3 = (s32[4,2,192]{2,1,0:T(2,128)S(1)}, s32[4,2,192]{2,1,0:T(2,128)S(1)}, u32[]{:S(2)}, u32[]{:S(2)}) collective-permute-start(s32[4,2,192]{2,1,0:T(2,128)S(1)} %pad_add_fusion.refs_2_), channel_id=1, source_target_pairs={{0,4},{1,5},{2,6},{3,7},{4,0},{5,1},{6,2},{7,3},{8,12},{9,13},{10,... | collective-permute-start | bytes 18440 | tf_op jit(solution)/shard_map/ppermute | solution.py:354
  13.2 2.6 %copy-start.5 = (s32[4,2,192]{2,1,0:T(2,128)}, s32[4,2,192]{2,1,0:T(2,128)S(1)}, u32[]{:S(2)}) copy-start(s32[4,2,192]{2,1,0:T(2,128)S(1)} %collective-permute-done.5.refs_5_) | copy-start | bytes 18436
  15.8 0.6 %copy-start.6 = (s32[4,2,192]{2,1,0:T(2,128)}, s32[4,2,192]{2,1,0:T(2,128)S(1)}, u32[]{:S(2)}) copy-start(s32[4,2,192]{2,1,0:T(2,128)S(1)} %collective-permute-done.4.refs_4_) | copy-start | bytes 18436
  15.8 0.6 %copy-start.7 = (s32[4,2,192]{2,1,0:T(2,128)}, s32[4,2,192]{2,1,0:T(2,128)S(1)}, u32[]{:S(2)}) copy-start(s32[4,2,192]{2,1,0:T(2,128)S(1)} %collective-permute-done.3.refs_3_) | copy-start | bytes 18436
  27.8 1.4 %collective-permute-start.6 = (f32[8,2,703]{2,1,0:T(2,128)}, f32[8,2,703]{2,1,0:T(2,128)S(1)}, u32[]{:S(2)}, u32[]{:S(2)}) collective-permute-start(f32[8,2,703]{2,1,0:T(2,128)} %get-tuple-element.7), channel_id=1, source_target_pairs={{0,1},{1,0},{2,3},{3,2},{4,5},{5,4},{6,7},{7,6},{8,9},{9,8},{10,11... | collective-permute-start | bytes 134984 | tf_op jit(solution)/shard_map/ppermute | solution.py:354
  30.0 3.9 %collective-permute-start.7 = (f32[4,2,703]{2,1,0:T(2,128)S(1)}, f32[4,2,703]{2,1,0:T(2,128)S(1)}, u32[]{:S(2)}, u32[]{:S(2)}) collective-permute-start(f32[4,2,703]{2,1,0:T(2,128)S(1)} %slice_add_fusion), channel_id=1, source_target_pairs={{0,2},{1,3},{2,0},{3,1},{4,6},{5,7},{6,4},{7,5},{8,10},{9,11},{10,... | collective-permute-start | bytes 67496 | tf_op jit(solution)/shard_map/ppermute | solution.py:354
  34.7 3.9 %collective-permute-start.8 = (f32[4,2,703]{2,1,0:T(2,128)S(1)}, f32[4,2,703]{2,1,0:T(2,128)S(1)}, u32[]{:S(2)}, u32[]{:S(2)}) collective-permute-start(f32[4,2,703]{2,1,0:T(2,128)S(1)} %fusion), channel_id=1, source_target_pairs={{0,4},{1,5},{2,6},{3,7},{4,0},{5,1},{6,2},{7,3},{8,12},{9,13},{10,... | collective-permute-start | bytes 67496 | tf_op jit(solution)/shard_map/ppermute | solution.py:354
  38.6 4.8 %collective-permute-start.9 = (f32[4,2,703]{2,1,0:T(2,128)S(1)}, f32[4,2,703]{2,1,0:T(2,128)S(1)}, u32[]{:S(2)}, u32[]{:S(2)}) collective-permute-start(f32[4,2,703]{2,1,0:T(2,128)S(1)} %add.15.refs_4_), channel_id=1, source_target_pairs={{0,8},{1,9},{2,10},{3,11},{4,12},{5,13},{6,14},{7,15},{8,0},{9,1},... | collective-permute-start | bytes 67496 | tf_op jit(solution)/shard_map/ppermute | solution.py:354
  45.3 3.8 %copy-start.2 = (f32[4,2,38]{2,1,0:T(2,128)}, f32[4,2,38]{2,1,0:T(2,128)S(1)}, u32[]{:S(2)}) copy-start(f32[4,2,38]{2,1,0:T(2,128)S(1)} %gain_solve.1.refs_4_) | copy-start | bytes 3652
  45.3 3.1 %collective-permute-start.12 = (f32[4,2,38]{2,1,0:T(2,128)S(1)}, f32[4,2,38]{2,1,0:T(2,128)S(1)}, u32[]{:S(2)}, u32[]{:S(2)}) collective-permute-start(f32[4,2,38]{2,1,0:T(2,128)S(1)} %gain_solve.1.refs_4_), channel_id=1, source_target_pairs={{0,3},{1,2},{2,1},{3,0},{4,7},{5,6},{6,5},{7,4},{8,11},{9,10},{10,... | collective-permute-start | bytes 3656 | tf_op jit(solution)/shard_map/ppermute | solution.py:354
  45.4 3.7 %collective-permute-start.11 = (f32[4,2,38]{2,1,0:T(2,128)S(1)}, f32[4,2,38]{2,1,0:T(2,128)S(1)}, u32[]{:S(2)}, u32[]{:S(2)}) collective-permute-start(f32[4,2,38]{2,1,0:T(2,128)S(1)} %gain_solve.1.refs_4_), channel_id=1, source_target_pairs={{0,2},{1,3},{2,0},{3,1},{4,6},{5,7},{6,4},{7,5},{8,10},{9,11},{10,... | collective-permute-start | bytes 3656 | tf_op jit(solution)/shard_map/ppermute | solution.py:354
  46.1 3.0 %collective-permute-start.10 = (f32[4,2,38]{2,1,0:T(2,128)S(1)}, f32[4,2,38]{2,1,0:T(2,128)S(1)}, u32[]{:S(2)}, u32[]{:S(2)}) collective-permute-start(f32[4,2,38]{2,1,0:T(2,128)S(1)} %gain_solve.1.refs_4_), channel_id=1, source_target_pairs={{0,1},{1,0},{2,3},{3,2},{4,5},{5,4},{6,7},{7,6},{8,9},{9,8},{10,11... | collective-permute-start | bytes 3656 | tf_op jit(solution)/shard_map/ppermute | solution.py:354
  48.4 0.7 %copy-start.8 = (f32[4,2,38]{2,1,0:T(2,128)}, f32[4,2,38]{2,1,0:T(2,128)S(1)}, u32[]{:S(2)}) copy-start(f32[4,2,38]{2,1,0:T(2,128)S(1)} %collective-permute-done.12.refs_7_) | copy-start | bytes 3652
  49.1 0.6 copy-start.9
  49.6 0.6 %copy-start.10 = (f32[4,2,38]{2,1,0:T(2,128)}, f32[4,2,38]{2,1,0:T(2,128)S(1)}, u32[]{:S(2)}) copy-start(f32[4,2,38]{2,1,0:T(2,128)S(1)} %collective-permute-done.10.refs_5_) | copy-start | bytes 3652

commit v3 on v2

v3 whole, which is shorter than its diff:
```python
import jax
import jax.numpy as jnp
import numpy as np
from jax import lax
from jax.experimental import pallas as pl
from jax.experimental.pallas import tpu as pltpu
from jax.sharding import PartitionSpec as P

STATIONS = 38
GITERS = 8
DAMPING = 1.0
STEPS_PER_TURN = 64
GAINS_AT = 768
ROWS = 40

F32 = jnp.float32
BF16 = jnp.bfloat16


def iota(shape, dim):
    return lax.broadcasted_iota(jnp.int32, shape, dim).astype(F32)


def sincos_turns(turns):
    half = (turns - jnp.floor(turns + 0.5)) * np.float32(np.pi)
    sq = half * half
    sin = np.float32(-1.0 / 39916800)
    for term in (1.0 / 362880, -1.0 / 5040, 1.0 / 120, -1.0 / 6, 1.0):
        sin = sin * sq + np.float32(term)
    sin = sin * half
    cos = np.float32(1.0 / 479001600)
    for term in (-1.0 / 3628800, 1.0 / 40320, -1.0 / 720, 1.0 / 24, -0.5, 1.0):
        cos = cos * sq + np.float32(term)
    return 1.0 - 2.0 * (sin * sin), 2.0 * (sin * cos)


def split_two(value):
    high = value.astype(BF16)
    low = (value - high.astype(F32)).astype(BF16)
    return high, low


def split_three(value):
    high = value.astype(BF16)
    rest = value - high.astype(F32)
    mid = rest.astype(BF16)
    low = (rest - mid.astype(F32)).astype(BF16)
    return high, mid, low


def dot(left, right):
    return jnp.dot(left, right, preferred_element_type=F32)


def times(left, right):
    (lr, li), (rr, ri) = left, right
    return lr * rr - li * ri, lr * ri + li * rr


def phase_rows(delays, anchor, width):
    place = iota((8, 1), 0)
    second = place >= 4.0
    turns = jnp.where(second, delays[1], delays[0])
    at = anchor + float(STEPS_PER_TURN) * jnp.where(second, place - 4.0, place)
    base = sincos_turns(turns * (at * np.float32(1.0 / STEPS_PER_TURN)))
    fine, coarse = [], []
    for s in range(2):
        low = sincos_turns(delays[s] * (place * np.float32(1.0 / STEPS_PER_TURN)))
        high = low
        for doubling in range(3):
            high = times(high, high)
        rows = [times(tuple(part[4 * s + a:4 * s + a + 1] for part in base), high)
                for a in range(width // STEPS_PER_TURN)]
        fine.append(low)
        coarse.append(rows)
    return fine, coarse


def sums_kernel(width, stages, me_ref, win_ref, *refs):
    flag_refs, refs = refs[:stages], refs[stages:]
    delay_ref, vis_ref, out_refs, coarse_ref, fine_ref = refs[0], refs[1], refs[2:6], refs[6], refs[7]
    rows_s, member_s, pick_s, alpha_s, scale_s, wave_s, mix_s, mexp_s, wt_s = refs[8:]
    time = pl.program_id(0)
    me = me_ref[0]
    near = flag_refs[0].shape[0]
    groups = near * stages
    windows = win_ref.shape[1]
    anchor = me.astype(F32) * float(width)
    size = wave_s.shape[3]

    @pl.when(time == 0)
    def prepare():
        win_row = win_ref[...].astype(F32)
        sub, lane = iota((windows, windows), 0), iota((windows, windows), 1)
        end_c = jnp.sum(jnp.where(lane <= sub, win_row, 0.0), axis=1, keepdims=True)
        start_c = jnp.sum(jnp.where(lane < sub, win_row, 0.0), axis=1, keepdims=True)
        win_c = end_c - start_c
        end_r = jnp.sum(jnp.where(sub <= lane, win_c, 0.0), axis=0, keepdims=True)
        start_r = jnp.sum(jnp.where(sub < lane, win_c, 0.0), axis=0, keepdims=True)
        group = iota((windows, groups), 1)
        low = group * float(width)
        first_hot = jnp.where((low <= start_c) & (start_c < low + float(width)), 1.0, 0.0)
        last_hot = jnp.where((low < end_c) & (end_c <= low + float(width)), 1.0, 0.0)
        first_g = jnp.sum(first_hot * group, axis=1, keepdims=True)
        last_g = jnp.sum(last_hot * group, axis=1, keepdims=True)
        full = jnp.where((group > first_g) & (group < last_g), 1.0, 0.0)
        pick = jnp.concatenate([first_hot, last_hot, full], axis=0).astype(BF16)
        pick_s[...] = pick
        place = iota((windows, width), 1)
        head_at = first_g * float(width) + place
        head_in = (head_at >= start_c) & (head_at < end_c)
        tail_in = (last_g > first_g) & (last_g * float(width) + place < end_c)
        channel = anchor + iota((width, windows), 0)
        member = (channel >= start_r) & (channel < end_r)
        diagonal = iota((width, width), 0) == iota((width, width), 1)
        for t in range(2):
            for slot in range(groups):
                row = flag_refs[slot // near][slot % near, t:t + 1, :].astype(F32)
                wt_s[lax.bitwise_xor(me, slot), t:t + 1, :] = 1.0 - row
        for t in range(2):
            weights = wt_s[:, t, :]
            picked = dot(pick, weights.astype(BF16))
            head = jnp.where(head_in, picked[:windows], 0.0)
            tail = jnp.where(tail_in, picked[windows:2 * windows], 0.0)
            count = jnp.sum(head + tail + picked[2 * windows:], axis=1, keepdims=True)
            scale = 1.0 / jnp.maximum(count, 1.0)
            rows_s[t] = jnp.concatenate([head, tail, weights], axis=0).astype(BF16)
            scale_s[t] = jnp.broadcast_to(scale, (windows, 128))
            scale_r = jnp.sum(jnp.where(sub == lane, scale, 0.0), axis=0, keepdims=True)
            own = 1.0 - flag_refs[0][0, t:t + 1, :].astype(F32)
            own_c = jnp.sum(jnp.where(diagonal, own, 0.0), axis=1, keepdims=True)
            chosen = jnp.where(member, own_c, 0.0)
            member_s[t] = chosen.astype(BF16)
            alpha = jnp.sum(chosen * scale_r, axis=1, keepdims=True)
            alpha_s[t] = jnp.broadcast_to(alpha, (width, 128))

    def waves(tile, carry):
        lanes = pl.ds(pl.multiple_of(tile * 128, 128), 128)
        delays = [jnp.where(time == 0, delay_ref[s, 0:1, lanes], delay_ref[s, 1:2, lanes]) for s in range(2)]
        fine, coarse = phase_rows(delays, anchor, width)
        for s in range(2):
            for ri in range(2):
                fine_ref[0, 2 * s + ri, :, lanes] = fine[s][ri]
                for a, rows in enumerate(coarse[s]):
                    coarse_ref[0, 2 * s + ri, 8 * a:8 * a + 8, lanes] = rows[ri]
        for block in range(width // 16):
            found = []
            for s in range(2):
                halves = []
                for half in range(2):
                    a, b = divmod(2 * block + half, 8)
                    halves.append(times(tuple(part[b:b + 1] for part in coarse[s][a]), fine[s]))
                found.append([jnp.concatenate([h[ri] for h in halves], axis=0) for ri in range(2)])
            rows = slice(block * 16, block * 16 + 16)
            (r0, i0), (r1, i1) = found
            for s in range(2):
                for ri in range(2):
                    wave_s[s, ri, rows, lanes] = found[s][ri]
            for slot, value in enumerate((r1 * r0 + i1 * i0, i1 * r0 - r1 * i0)):
                high, low = split_two(value)
                mix_s[slot, 0, rows, lanes] = high
                mix_s[slot, 1, rows, lanes] = low
        return carry

    lax.fori_loop(0, size // 128, waves, 0)

    pick = pick_s[...]
    gap = delay_ref[1, pl.ds(time, 1), :] - delay_ref[0, pl.ds(time, 1), :]
    apart = iota((groups, 1), 0) - me.astype(F32)
    phase = sincos_turns(gap * (apart * np.float32(width / STEPS_PER_TURN)))
    picked = []
    for value in phase:
        high, low = split_two(value)
        ends = pick[:2 * windows]
        picked.append(dot(ends, high) + dot(ends, low))
    rows = rows_s[time]
    sums = [dot(rows, mix_s[slot, 0]) + dot(rows, mix_s[slot, 1]) for slot in range(2)]
    total = [0.0, 0.0]
    for which in range(2):
        cut = slice(which * windows, (which + 1) * windows)
        terms = times(tuple(value[cut] for value in picked), tuple(value[cut] for value in sums))
        total = [old + new for old, new in zip(total, terms)]
    terms = times(phase, tuple(value[2 * windows:] for value in sums))
    scale = scale_s[time][:, :1]
    chosen = member_s[time]
    for slot in range(2):
        high, low = split_two(terms[slot])
        value = total[slot] + (dot(pick[2 * windows:], high) + dot(pick[2 * windows:], low))
        high, low = split_two(value * (scale * scale))
        mexp_s[slot] = dot(chosen, high) + dot(chosen, low)

    def main(tile, carry):
        lanes = pl.ds(pl.multiple_of(tile * 128, 128), 128)

        def step(block, sums):
            rows = pl.ds(pl.multiple_of(block * 16, 16), 16)
            alpha = alpha_s[time, rows, :]
            mr, mi = mexp_s[0, rows, lanes], mexp_s[1, rows, lanes]
            r0, i0 = wave_s[0, 0, rows, lanes], wave_s[0, 1, rows, lanes]
            r1, i1 = wave_s[1, 0, rows, lanes], wave_s[1, 1, rows, lanes]
            factors = []
            for fr, fi in (
                (alpha * r0 - (mr * r1 + mi * i1), (mr * i1 - mi * r1) - alpha * i0),
                (alpha * r1 - (mr * r0 - mi * i0), (mr * i0 + mi * r0) - alpha * i1),
            ):
                factors.append((fr, fi - fr, fr + fi))
            new = []
            for k in range(4):
                vr = vis_ref[0, 0, k, rows, lanes].astype(F32)
                vi = vis_ref[1, 0, k, rows, lanes].astype(F32)
                vs = vr + vi
                for s in range(2):
                    for v, f in zip((vs, vr, vi), factors[s]):
                        product = v * f
                        new.append(sums[len(new)] + (product[:8] + product[8:]))
            return tuple(new)

        zero = jnp.zeros((8, 128), F32)
        sums = lax.fori_loop(0, width // 16, step, (zero,) * 24, unroll=4)
        for s in range(2):
            owner = lax.bitwise_xor(lax.bitwise_and(me, 3), time + 2 * s)
            found = []
            for k in range(4):
                one, two, three = sums[(k * 2 + s) * 3:(k * 2 + s) * 3 + 3]
                found.append([jnp.sum(value, axis=0, keepdims=True) for value in (one - three, one + two)])
            for d in range(4):
                @pl.when(owner == d)
                def write():
                    for k in range(4):
                        for ri in range(2):
                            out_refs[d][k, ri:ri + 1, lanes] = found[k][ri]
        return carry

    lax.fori_loop(0, size // 128, main, 0)


def solve_kernel(window_count, me_ref, tracks_ref, first_ref, second_ref, *refs):
    parts, gain_ref = refs[:-1], refs[-1]
    me = me_ref[0]
    systems = gain_ref.shape[0]
    total = [part[...] for part in parts]
    while len(total) > 1:
        total = [total[i] + total[i + 1] for i in range(0, len(total), 2)]
    total = total[0]
    hot = first_ref[...]
    other = second_ref[...]
    nt = lambda left, right: lax.dot_general(
        left, right, (((1,), (1,)), ((), ())), preferred_element_type=F32)
    upper, lower = [], []
    for system in range(systems):
        for ri in range(2):
            for piece in split_two(total[system, ri:ri + 1]):
                upper.append(hot * piece)
                lower.append(other * piece)
    upper = nt(jnp.concatenate(upper, axis=0), other)
    lower = nt(jnp.concatenate(lower, axis=0), hot)
    cut = lambda value, i: value[i * ROWS:(i + 1) * ROWS]
    join = lambda value, i: cut(value, 2 * i) + cut(value, 2 * i + 1)
    live_r = jnp.where(iota((1, ROWS), 1) < float(STATIONS), 1.0, 0.0)
    live_c = jnp.where(iota((ROWS, 1), 0) < float(STATIONS), 1.0, 0.0)
    matrices = [(join(upper, 2 * i) + join(lower, 2 * i), join(upper, 2 * i + 1) - join(lower, 2 * i + 1))
                for i in range(systems)]
    states = [(live_r, 0.0 * live_r, live_c, 0.0 * live_c)] * systems
    for turn in range(GITERS):
        for system in range(systems):
            re, im = matrices[system]
            row_re, row_im, col_re, col_im = states[system]
            pull_cr = jnp.sum(re * row_re - im * row_im, axis=1, keepdims=True)
            pull_ci = jnp.sum(re * row_im + im * row_re, axis=1, keepdims=True)
            pull_rr = jnp.sum(re * col_re + im * col_im, axis=0, keepdims=True)
            pull_ri = jnp.sum(re * col_im - im * col_re, axis=0, keepdims=True)
            power_r = row_re * row_re + row_im * row_im
            power_c = col_re * col_re + col_im * col_im
            total = jnp.sum(power_c, axis=0, keepdims=True)
            inverse_r = 0.5 / (window_count * (total - power_r) + DAMPING)
            inverse_c = 0.5 / (window_count * (total - power_c) + DAMPING)
            states[system] = (0.5 * row_re + pull_rr * inverse_r, 0.5 * row_im + pull_ri * inverse_r,
                              0.5 * col_re + pull_cr * inverse_c, 0.5 * col_im + pull_ci * inverse_c)
    visible = tracks_ref[lax.bitwise_and(lax.div(me, 2), 1), lax.bitwise_and(me, 1)].astype(F32)
    gains = [state[ri] * visible for state in states for ri in range(2)]
    gains = jnp.concatenate(gains, axis=0)
    stacked = jnp.concatenate([piece.astype(F32) for piece in split_three(gains)], axis=0).astype(BF16)
    ends = []
    for table in (hot, other):
        wide = dot(stacked, table)
        ends.append((wide[:8] + wide[8:16]) + wide[16:])
    pairs = hot.shape[1]
    for system in range(systems):
        (lr, li), (rr, ri_) = [[end[2 * system + ri:2 * system + ri + 1] for ri in range(2)] for end in ends]
        gain_ref[system, 0:1, :pairs] = lr * rr + li * ri_
        gain_ref[system, 1:2, :pairs] = li * rr - lr * ri_
        gain_ref[system, :, GAINS_AT:] = gains[2 * system:2 * system + 2, :STATIONS]


def clean_kernel(width, me_ref, coarse_ref, fine_ref, *refs):
    piece_refs, (vis_ref, out_ref, gain_out_ref, model_s) = refs[:4], refs[4:]
    time = pl.program_id(0)
    pairs = out_ref.shape[4]
    size = model_s.shape[2]

    @pl.when(time == 0)
    def prepare():
        mine = lax.bitwise_and(me_ref[0], 3)
        for d, piece in enumerate(piece_refs):
            owner = lax.bitwise_xor(mine, d)
            t, s = lax.bitwise_and(owner, 1), lax.div(owner, 2)
            for k in range(4):
                for ri in range(2):
                    gain_out_ref[ri, s, t, k:k + 1, :] = piece[k, ri:ri + 1, GAINS_AT:]
                re, im = piece[k, 0:1, :GAINS_AT], piece[k, 1:2, :GAINS_AT]
                for slot, value in enumerate((re, im - re, re + im)):
                    model_s[owner, 3 * k + slot:3 * k + slot + 1, :] = value

    def main(tile, carry):
        lanes = pl.ds(pl.multiple_of(tile * 128, 128), 128)
        fine = [[fine_ref[0, 2 * s + ri, :, lanes] for ri in range(2)] for s in range(2)]
        for a in range(width // STEPS_PER_TURN):
            coarse = [[coarse_ref[0, 2 * s + ri, 8 * a:8 * a + 8, lanes] for ri in range(2)] for s in range(2)]
            for b in range(0, 8, 2):
                block = (8 * a + b) // 2
                rows = slice(block * 16, block * 16 + 16)
                waves = []
                for s in range(2):
                    halves = [times(tuple(part[b + half:b + half + 1] for part in coarse[s]), fine[s])
                              for half in range(2)]
                    re, im = (jnp.concatenate([h[ri] for h in halves], axis=0) for ri in range(2))
                    waves.append((re + im, re, im))
                for k in range(4):
                    sums = []
                    for slot in range(3):
                        one, two = (waves[s][slot] * model_s[time + 2 * s, 3 * k + slot:3 * k + slot + 1, lanes]
                                    for s in range(2))
                        sums.append(one + two)
                    vr = vis_ref[0, 0, k, rows, lanes].astype(F32)
                    vi = vis_ref[1, 0, k, rows, lanes].astype(F32)
                    out_ref[0, 0, k, rows, lanes] = (vr - (sums[0] - sums[2])).astype(BF16)
                    out_ref[1, 0, k, rows, lanes] = (vi - (sums[0] + sums[1])).astype(BF16)
        return carry

    lax.fori_loop(0, size // 128, main, 0)


def tables():
    first, second = np.triu_indices(STATIONS, 1)
    eye = np.eye(ROWS, dtype=np.float32)
    return jnp.asarray(eye[:, first], BF16), jnp.asarray(eye[:, second], BF16)


def partner(value, bits):
    count = lax.axis_size("sub")
    return lax.ppermute(value, "sub", [(i, i ^ bits) for i in range(count)])


def smem():
    return pl.BlockSpec(memory_space=pltpu.SMEM)


def local(visibilities, delays, flags, windows, tracks):
    width = visibilities.shape[4]
    pairs = visibilities.shape[3]
    count = lax.axis_size("sub")
    window_count = windows.shape[0]
    turned = jnp.transpose(visibilities, (0, 1, 2, 4, 3))
    me = lax.axis_index("sub").astype(jnp.int32).reshape(1)
    gathered = [flags[None]]
    stride = 1
    while stride < count:
        gathered = [jnp.concatenate(gathered, axis=0)] if len(gathered) > 1 else gathered
        gathered += [partner(gathered[0], stride * d) for d in range(1, min(4, count // stride))]
        stride *= 4
    lanes = 128 * pl.cdiv(pairs, 128)
    whole = lambda *shape: pl.BlockSpec(shape, lambda t: (0,) * len(shape))
    phases = lambda rows: pl.BlockSpec((1, 4, rows, lanes), lambda t: (t, 0, 0, 0))
    vis_spec = pl.BlockSpec((2, 1, 4, width, lanes), lambda t: (0, t, 0, 0, 0))
    rows = 2 * window_count + count
    vmem = lambda *shape: pltpu.VMEM(shape, F32)
    params = pltpu.CompilerParams(vmem_limit_bytes=57 * 2 ** 20)
    *quarters, coarse, fine = pl.pallas_call(
        lambda *refs: sums_kernel(width, len(gathered), *refs),
        grid=(2,),
        in_specs=[smem(), whole(1, window_count)] + [whole(*piece.shape) for piece in gathered] + [
            whole(2, 2, lanes), vis_spec],
        out_specs=[whole(4, 2, lanes)] * 4 + [phases(width // 8), phases(8)],
        out_shape=[jax.ShapeDtypeStruct((4, 2, pairs), F32)] * 4 + [
            jax.ShapeDtypeStruct((2, 4, rows, pairs), F32) for rows in (width // 8, 8)],
        scratch_shapes=[
            pltpu.VMEM((2, rows, width), BF16),
            pltpu.VMEM((2, width, window_count), BF16),
            pltpu.VMEM((3 * window_count, count), BF16),
            vmem(2, width, 128),
            vmem(2, window_count, 128),
            vmem(2, 2, width, lanes),
            pltpu.VMEM((2, 2, width, lanes), BF16),
            vmem(2, width, lanes),
            vmem(count, 2, width),
        ],
        compiler_params=params,
        name="window_sums",
    )(me, windows.reshape(1, window_count), *gathered, delays, turned)
    pieces = [quarters[0]] + [partner(quarters[d], d) for d in range(1, 4)]
    stride = 4
    while stride < count:
        while len(pieces) > 1:
            pieces = [pieces[i] + pieces[i + 1] for i in range(0, len(pieces), 2)]
        pieces += [partner(pieces[0], stride * d) for d in range(1, min(4, count // stride))]
        stride *= 4
    first, second = tables()
    model = pl.pallas_call(
        lambda *refs: solve_kernel(float(window_count), *refs),
        in_specs=[smem(), smem()] + [pl.BlockSpec(memory_space=pltpu.VMEM)] * (2 + len(pieces)),
        out_specs=pl.BlockSpec(memory_space=pltpu.VMEM),
        out_shape=jax.ShapeDtypeStruct((4, 2, GAINS_AT + STATIONS), F32),
        compiler_params=params,
        name="gain_solve",
    )(me, tracks, first, second, *pieces)
    model = [model] + [partner(model, d) for d in range(1, 4)]
    cleaned, gains = pl.pallas_call(
        lambda *refs: clean_kernel(width, *refs),
        grid=(2,),
        in_specs=[smem(), phases(width // 8), phases(8)] + [whole(4, 2, GAINS_AT + STATIONS)] * 4 + [vis_spec],
        out_specs=[vis_spec, whole(2, 2, 2, 4, STATIONS)],
        out_shape=[
            jax.ShapeDtypeStruct(turned.shape, BF16),
            jax.ShapeDtypeStruct((2, 2, 2, 4, STATIONS), F32),
        ],
        scratch_shapes=[vmem(4, 16, lanes)],
        compiler_params=params,
        name="clean",
    )(me, coarse, fine, *model, turned)
    return jnp.transpose(cleaned, (0, 1, 2, 4, 3)), gains


def solution(mesh):
    return jax.shard_map(
        local,
        mesh=mesh,
        in_specs=(
            P(None, "obs", None, None, "sub"),
            P(None, "obs", None),
            P("obs", "sub"),
            P(),
            P(None, "obs"),
        ),
        out_specs=(P(None, "obs", None, None, "sub"), P(None, None, "obs", None, None)),
        check_vma=False,
    )
```

time: 58.8 us -> 54.9 us (0.934)
  waiting for transfers between devices: 19.6 us -> 13.8 us
  starting transfers between devices: 12.6 us -> 15.7 us
  other arithmetic: 2.21 us -> 1.44 us
  Pallas kernels: 21.5 us -> 20.8 us
    ppermute x13 -> x15, waiting for transfers between devices: 19.6 us -> 13.8 us  [partner(): return lax.ppermute(value, 'sub', [(i, i ^ bits) for i in range(count)])]
    ppermute x13 -> x15, starting transfers between devices: 12.6 us -> 15.7 us  [partner(): return lax.ppermute(value, 'sub', [(i, i ^ bits) for i in range(count)])]
    pallas_call x1, Pallas kernels: 8.12 us -> 6.55 us  [local(): pl.pallas_call(lambda *refs: clean_kernel(width, *refs), grid=(2,), in_sp...]
    pallas_call x1, Pallas kernels: 1.9 us -> 3.01 us  [local(): pl.pallas_call(lambda *refs: solve_kernel(float(window_count), *refs), in...]
    add x3 -> x1, other arithmetic: 1.52 us -> 0.75 us  [local(): pieces = [pieces[i] + pieces[i + 1] for i in range(0, len(pieces), 2)]]
  transfers between devices with their start and end apart: 13 -> 15, of which waited for: 10 -> 11; matrix products, arithmetic and copies ran while one was open for 0% -> 0% of each run, Pallas kernels for 0% -> 0%
where the time goes in v3:
time: 54.9 us; the launch traced here: 54.6 us
  Pallas kernels  20.8 us (38%)
  starting transfers between devices  15.7 us (29%)
  waiting for transfers between devices  13.8 us (25%)
  local copies, waits for them, and re-layouts  2.16 us (4%)
  other arithmetic  1.44 us (3%)
  between operations  0.68 us (1%)
    ppermute x15, starting transfers between devices, partner(): return lax.ppermute(value, 'sub', [(i, i ^ bits) for i in range(count)])  15.7 us
    ppermute x15, waiting for transfers between devices, partner(): return lax.ppermute(value, 'sub', [(i, i ^ bits) for i in range(count)])  13.8 us
    pallas_call x1, Pallas kernels, local(): pl.pallas_call(lambda *refs: sums_kernel(width, len(gathered), *refs), gr...  11.3 us
    pallas_call x1, Pallas kernels, local(): pl.pallas_call(lambda *refs: clean_kernel(width, *refs), grid=(2,), in_sp...  6.55 us
    pallas_call x1, Pallas kernels, local(): pl.pallas_call(lambda *refs: solve_kernel(float(window_count), *refs), in...  3.01 us
    unnamed x22, local copies, waits for them, and re-layouts  2.16 us
  transfers between devices with their start and end apart: 15, of which 11 were waited for; matrix products, arithmetic and copies ran while one was open for 0% of the time, Pallas kernels for 0%

profile of v3, /device:TPU:0, one launch (start us, length us, event | category | flops | bytes accessed | tf_op | source)
XLA Modules:
  0.0 54.6 jit_solution(12688428577190740265)
XLA Ops:
  0.6 2.5 %collective-permute-start.2 = (s32[1,2,192]{2,1,0:T(2,128)}, s32[1,2,192]{2,1,0:T(2,128)S(1)}, u32[]{:S(2)}, u32[]{:S(2)}) collective-permute-start(s32[1,2,192]{2,1,0:T(2,128)} %bitcast.20), channel_id=1, source_target_pairs={{0,3},{1,2},{2,1},{3,0},{4,7},{5,6},{6,5},{7,4},{8,11},{9,10},{10,... | collective-permute-start | bytes 4616 | tf_op jit(solution)/shard_map/ppermute | solution.py:351
  3.1 0.6 %collective-permute-start.1 = (s32[1,2,192]{2,1,0:T(2,128)}, s32[1,2,192]{2,1,0:T(2,128)S(1)}, u32[]{:S(2)}, u32[]{:S(2)}) collective-permute-start(s32[1,2,192]{2,1,0:T(2,128)} %bitcast.21), channel_id=1, source_target_pairs={{0,2},{1,3},{2,0},{3,1},{4,6},{5,7},{6,4},{7,5},{8,10},{9,11},{10,... | collective-permute-start | bytes 4616 | tf_op jit(solution)/shard_map/ppermute | solution.py:351
  3.7 0.0 collective-permute-start
  3.8 0.8 %collective-permute-done.2 = s32[1,2,192]{2,1,0:T(2,128)S(1)} collective-permute-done((s32[1,2,192]{2,1,0:T(2,128)}, s32[1,2,192]{2,1,0:T(2,128)S(1)}, u32[]{:S(2)}, u32[]{:S(2)}) %collective-permute-start.2) | collective-permute-done | bytes 1568 | tf_op jit(solution)/shard_map/ppermute | solution.py:351
  4.6 2.3 %collective-permute-done.1 = s32[1,2,192]{2,1,0:T(2,128)S(1)} collective-permute-done((s32[1,2,192]{2,1,0:T(2,128)}, s32[1,2,192]{2,1,0:T(2,128)S(1)}, u32[]{:S(2)}, u32[]{:S(2)}) %collective-permute-start.1) | collective-permute-done | bytes 1568 | tf_op jit(solution)/shard_map/ppermute | solution.py:351
  6.9 0.0 collective-permute-done
  6.9 0.7 %pad_add_fusion.refs_2_ = s32[4,2,192]{2,1,0:T(2,128)S(1)} fusion(s32[1,2,192]{2,1,0:T(2,128)S(1)} %collective-permute-done.2, s32[1,2,192]{2,1,0:T(2,128)S(1)} %collective-permute-done.1, s32[1,2,192]{2,1,0:T(2,128)S(1)} %collective-permute-done, s32[1,2,192]{2,1,0:T(2,128)} %bitcast.23), kind=kLoop, calls=%fused_computation.1 | loop fusion | flops 4608 | bytes 12288 | tf_op jit(solution)/shard_map/concatenate | solution.py:368
  7.6 0.0 copy-start.1
  7.6 3.6 %collective-permute-start.5 = (s32[4,2,192]{2,1,0:T(2,128)S(1)}, s32[4,2,192]{2,1,0:T(2,128)S(1)}, u32[]{:S(2)}, u32[]{:S(2)}) collective-permute-start(s32[4,2,192]{2,1,0:T(2,128)S(1)} %pad_add_fusion.refs_2_), channel_id=1, source_target_pairs={{0,12},{1,13},{2,14},{3,15},{4,8},{5,9},{6,10},{7,11},{8,4},{9,5},... | collective-permute-start | bytes 18440 | tf_op jit(solution)/shard_map/ppermute | solution.py:351
  11.2 0.0 collective-permute-start.4
  11.2 0.8 %collective-permute-start.3 = (s32[4,2,192]{2,1,0:T(2,128)S(1)}, s32[4,2,192]{2,1,0:T(2,128)S(1)}, u32[]{:S(2)}, u32[]{:S(2)}) collective-permute-start(s32[4,2,192]{2,1,0:T(2,128)S(1)} %pad_add_fusion.refs_2_), channel_id=1, source_target_pairs={{0,4},{1,5},{2,6},{3,7},{4,0},{5,1},{6,2},{7,3},{8,12},{9,13},{10,... | collective-permute-start | bytes 18440 | tf_op jit(solution)/shard_map/ppermute | solution.py:351
  12.0 1.2 %collective-permute-done.5.refs_5_ = s32[4,2,192]{2,1,0:T(2,128)S(1)} collective-permute-done((s32[4,2,192]{2,1,0:T(2,128)S(1)}, s32[4,2,192]{2,1,0:T(2,128)S(1)}, u32[]{:S(2)}, u32[]{:S(2)}) %collective-permute-start.5) | collective-permute-done | bytes 6176 | tf_op jit(solution)/shard_map/ppermute | solution.py:351
  13.2 0.0 copy-start.8
  13.2 2.6 %collective-permute-done.4.refs_4_ = s32[4,2,192]{2,1,0:T(2,128)S(1)} collective-permute-done((s32[4,2,192]{2,1,0:T(2,128)S(1)}, s32[4,2,192]{2,1,0:T(2,128)S(1)}, u32[]{:S(2)}, u32[]{:S(2)}) %collective-permute-start.4) | collective-permute-done | bytes 6176 | tf_op jit(solution)/shard_map/ppermute | solution.py:351
  15.7 0.0 collective-permute-done.3.refs_3_
  15.8 0.0 copy-done.1
  15.8 0.0 copy-done.8
  15.8 0.6 %copy-done.9 = s32[4,2,192]{2,1,0:T(2,128)} copy-done((s32[4,2,192]{2,1,0:T(2,128)}, s32[4,2,192]{2,1,0:T(2,128)S(1)}, u32[]{:S(2)}) %copy-start.9) | copy-done | bytes 6168
  16.3 0.0 copy-done.10
  16.3 11.3 %window_sums.1 = (f32[4,2,703]{2,1,0:T(2,128)}, f32[4,2,703]{2,1,0:T(2,128)}, f32[4,2,703]{2,1,0:T(2,128)}, f32[4,2,703]{2,1,0:T(2,128)}, f32[2,4,24,703]{3,2,1,0:T(8,128)}, /*index=5*/f32[2,4,8,703]{3,2,1,0:T(8,128)}) custom-call(s32[1]{0:T(128)} %bitcast.refs_0_, s32[1,32]{1,0:T(1,128)} %bitcast.24, s32[4,2,192]{2,1,0:T(2,128)} %copy-done.1, ...), custom_call_target="tpu_custom_call" | custom-call | tf_op jit(solution)/shard_map/window_sums/pallas_call | solution.py:378
  27.6 0.0 collective-permute-start.6
  27.6 0.7 %collective-permute-start.7 = (f32[4,2,703]{2,1,0:T(2,128)}, f32[4,2,703]{2,1,0:T(2,128)S(1)}, u32[]{:S(2)}, u32[]{:S(2)}) collective-permute-start(f32[4,2,703]{2,1,0:T(2,128)} %get-tuple-element.14), channel_id=1, source_target_pairs={{0,2},{1,3},{2,0},{3,1},{4,6},{5,7},{6,4},{7,5},{8,10},{9,11},{10,... | collective-permute-start | bytes 67496 | tf_op jit(solution)/shard_map/ppermute | solution.py:351
  28.3 1.2 %collective-permute-start.8 = (f32[4,2,703]{2,1,0:T(2,128)}, f32[4,2,703]{2,1,0:T(2,128)S(1)}, u32[]{:S(2)}, u32[]{:S(2)}) collective-permute-start(f32[4,2,703]{2,1,0:T(2,128)} %get-tuple-element.15), channel_id=1, source_target_pairs={{0,3},{1,2},{2,1},{3,0},{4,7},{5,6},{6,5},{7,4},{8,11},{9,10},{10,... | collective-permute-start | bytes 67496 | tf_op jit(solution)/shard_map/ppermute | solution.py:351
  29.5 0.0 collective-permute-done.6
  29.5 2.4 %collective-permute-done.7 = f32[4,2,703]{2,1,0:T(2,128)S(1)} collective-permute-done((f32[4,2,703]{2,1,0:T(2,128)}, f32[4,2,703]{2,1,0:T(2,128)S(1)}, u32[]{:S(2)}, u32[]{:S(2)}) %collective-permute-start.7) | collective-permute-done | bytes 22528 | tf_op jit(solution)/shard_map/ppermute | solution.py:351
  31.9 0.1 collective-permute-done.8
  32.1 0.7 %add_add_fusion = f32[1,8,703]{2,1,0:T(8,128)S(1)} fusion(f32[1,8,703]{2,1,0:T(8,128)S(1)} %bitcast.18, f32[1,8,703]{2,1,0:T(8,128)S(1)} %bitcast.19, f32[1,8,703]{2,1,0:T(8,128)} %bitcast.16, f32[1,8,703]{2,1,0:T(8,128)S(1)} %bitcast.17), kind=kLoop, calls=%fused_computation | loop fusion | flops 16872 | bytes 112480 | tf_op jit(solution)/shard_map/add | solution.py:404
  32.8 1.5 %collective-permute-start.11 = (f32[4,2,703]{2,1,0:T(2,128)S(1)}, f32[4,2,703]{2,1,0:T(2,128)S(1)}, u32[]{:S(2)}, u32[]{:S(2)}) collective-permute-start(f32[4,2,703]{2,1,0:T(2,128)S(1)} %bitcast.12), channel_id=1, source_target_pairs={{0,12},{1,13},{2,14},{3,15},{4,8},{5,9},{6,10},{7,11},{8,4},{9,5},... | collective-permute-start | bytes 67496 | tf_op jit(solution)/shard_map/ppermute | solution.py:351
  34.3 0.6 %collective-permute-start.10 = (f32[4,2,703]{2,1,0:T(2,128)S(1)}, f32[4,2,703]{2,1,0:T(2,128)S(1)}, u32[]{:S(2)}, u32[]{:S(2)}) collective-permute-start(f32[4,2,703]{2,1,0:T(2,128)S(1)} %bitcast.13), channel_id=1, source_target_pairs={{0,8},{1,9},{2,10},{3,11},{4,12},{5,13},{6,14},{7,15},{8,0},{9,1},... | collective-permute-start | bytes 67496 | tf_op jit(solution)/shard_map/ppermute | solution.py:351
  35.0 2.3 %collective-permute-start.9 = (f32[4,2,703]{2,1,0:T(2,128)S(1)}, f32[4,2,703]{2,1,0:T(2,128)S(1)}, u32[]{:S(2)}, u32[]{:S(2)}) collective-permute-start(f32[4,2,703]{2,1,0:T(2,128)S(1)} %bitcast.14), channel_id=1, source_target_pairs={{0,4},{1,5},{2,6},{3,7},{4,0},{5,1},{6,2},{7,3},{8,12},{9,13},{10,... | collective-permute-start | bytes 67496 | tf_op jit(solution)/shard_map/ppermute | solution.py:351
  37.3 1.5 %collective-permute-done.11.refs_7_ = f32[4,2,703]{2,1,0:T(2,128)S(1)} collective-permute-done((f32[4,2,703]{2,1,0:T(2,128)S(1)}, f32[4,2,703]{2,1,0:T(2,128)S(1)}, u32[]{:S(2)}, u32[]{:S(2)}) %collective-permute-start.11) | collective-permute-done | bytes 22528 | tf_op jit(solution)/shard_map/ppermute | solution.py:351
  38.7 0.3 collective-permute-done.10.refs_6_
  39.1 0.2 collective-permute-done.9.refs_5_
  39.3 0.0 copy-done
  39.3 0.0 copy-done.5
  39.3 0.3 copy-done.6
  39.7 0.6 %copy-done.7 = f32[4,2,703]{2,1,0:T(2,128)} copy-done((f32[4,2,703]{2,1,0:T(2,128)}, f32[4,2,703]{2,1,0:T(2,128)S(1)}, u32[]{:S(2)}) %copy-start.7) | copy-done | bytes 22520
  40.3 3.0 %gain_solve.1.refs_3_ = f32[4,2,806]{2,1,0:T(2,128)} custom-call(s32[1]{0:T(128)} %bitcast.refs_0_, s32[2,2]{1,0:T(2,128)} %refs_1_.1, bf16[40,703]{1,0:T(8,128)(2,1)} %constant.8.clone.refs_2_, bf16[40,703]{1,0:T(8,128)(2,1)} %constant.9.clone.refs_3_, f32[4,2,703]{2,1,0:T(2,128)} %bitcast.15, f32[4,2,703]{2,1,0:T(2,128)} %copy-done.7, ...), custom_call_target="tpu_custom_call" | custom-call | tf_op jit(solution)/shard_map/gain_solve/pallas_call | solution.py:408
  43.3 0.0 collective-permute-start.14
  43.3 1.2 %collective-permute-start.13 = (f32[4,2,806]{2,1,0:T(2,128)}, f32[4,2,806]{2,1,0:T(2,128)S(1)}, u32[]{:S(2)}, u32[]{:S(2)}) collective-permute-start(f32[4,2,806]{2,1,0:T(2,128)} %gain_solve.1.refs_3_), channel_id=1, source_target_pairs={{0,2},{1,3},{2,0},{3,1},{4,6},{5,7},{6,4},{7,5},{8,10},{9,11},{10,... | collective-permute-start | bytes 77384 | tf_op jit(solution)/shard_map/ppermute | solution.py:351
  44.4 0.7 %collective-permute-start.12 = (f32[4,2,806]{2,1,0:T(2,128)}, f32[4,2,806]{2,1,0:T(2,128)S(1)}, u32[]{:S(2)}, u32[]{:S(2)}) collective-permute-start(f32[4,2,806]{2,1,0:T(2,128)} %gain_solve.1.refs_3_), channel_id=1, source_target_pairs={{0,1},{1,0},{2,3},{3,2},{4,5},{5,4},{6,7},{7,6},{8,9},{9,8},{10,11... | collective-permute-start | bytes 77384 | tf_op jit(solution)/shard_map/ppermute | solution.py:351
  45.2 1.6 %collective-permute-done.14.refs_6_ = f32[4,2,806]{2,1,0:T(2,128)S(1)} collective-permute-done((f32[4,2,806]{2,1,0:T(2,128)}, f32[4,2,806]{2,1,0:T(2,128)S(1)}, u32[]{:S(2)}, u32[]{:S(2)}) %collective-permute-start.14) | collective-permute-done | bytes 25824 | tf_op jit(solution)/shard_map/ppermute | solution.py:351
  46.8 0.7 %collective-permute-done.13.refs_5_ = f32[4,2,806]{2,1,0:T(2,128)S(1)} collective-permute-done((f32[4,2,806]{2,1,0:T(2,128)}, f32[4,2,806]{2,1,0:T(2,128)S(1)}, u32[]{:S(2)}, u32[]{:S(2)}) %collective-permute-start.13) | collective-permute-done | bytes 25824 | tf_op jit(solution)/shard_map/ppermute | solution.py:351
  47.5 0.0 collective-permute-done.12.refs_4_
  47.5 0.0 copy-done.2
  47.5 0.6 %copy-done.3 = f32[4,2,806]{2,1,0:T(2,128)} copy-done((f32[4,2,806]{2,1,0:T(2,128)}, f32[4,2,806]{2,1,0:T(2,128)S(1)}, u32[]{:S(2)}) %copy-start.3) | copy-done | bytes 25816
  48.1 0.0 copy-done.4
  48.1 6.6 %clean.1 = (bf16[2,2,4,192,703]{4,3,2,1,0:T(8,128)(2,1)}, f32[2,2,2,4,38]{4,3,2,1,0:T(4,128)}) custom-call(s32[1]{0:T(128)} %bitcast.refs_0_, f32[2,4,24,703]{3,2,1,0:T(8,128)} %get-tuple-element.10.refs_1_, f32[2,4,8,703]{3,2,1,0:T(8,128)} %get-tuple-element.11.refs_2_, f32[4,2,806]{2,1,0:T(2,128)} %gain_solve.1.refs_3_, f32[4,2,806]{2,1,0:T(2,128)} %copy-done.4, ...), custom_call_target="tpu_custom_call" | custom-call | tf_op jit(solution)/shard_map/clean/pallas_call | solution.py:417
  (9 shorter events, 0.0 us)
Async XLA Ops:
  0.6 4.0 %collective-permute-start.2 = (s32[1,2,192]{2,1,0:T(2,128)}, s32[1,2,192]{2,1,0:T(2,128)S(1)}, u32[]{:S(2)}, u32[]{:S(2)}) collective-permute-start(s32[1,2,192]{2,1,0:T(2,128)} %bitcast.20), channel_id=1, source_target_pairs={{0,3},{1,2},{2,1},{3,0},{4,7},{5,6},{6,5},{7,4},{8,11},{9,10},{10,... | collective-permute-start | bytes 4616 | tf_op jit(solution)/shard_map/ppermute | solution.py:351
  3.1 3.8 %collective-permute-start.1 = (s32[1,2,192]{2,1,0:T(2,128)}, s32[1,2,192]{2,1,0:T(2,128)S(1)}, u32[]{:S(2)}, u32[]{:S(2)}) collective-permute-start(s32[1,2,192]{2,1,0:T(2,128)} %bitcast.21), channel_id=1, source_target_pairs={{0,2},{1,3},{2,0},{3,1},{4,6},{5,7},{6,4},{7,5},{8,10},{9,11},{10,... | collective-permute-start | bytes 4616 | tf_op jit(solution)/shard_map/ppermute | solution.py:351
  3.7 3.2 %collective-permute-start = (s32[1,2,192]{2,1,0:T(2,128)}, s32[1,2,192]{2,1,0:T(2,128)S(1)}, u32[]{:S(2)}, u32[]{:S(2)}) collective-permute-start(s32[1,2,192]{2,1,0:T(2,128)} %bitcast.22), channel_id=1, source_target_pairs={{0,1},{1,0},{2,3},{3,2},{4,5},{5,4},{6,7},{7,6},{8,9},{9,8},{10,11... | collective-permute-start | bytes 4616 | tf_op jit(solution)/shard_map/ppermute | solution.py:351
  7.6 8.2 %copy-start.1 = (s32[4,2,192]{2,1,0:T(2,128)}, s32[4,2,192]{2,1,0:T(2,128)S(1)}, u32[]{:S(2)}) copy-start(s32[4,2,192]{2,1,0:T(2,128)S(1)} %pad_add_fusion.refs_2_) | copy-start | bytes 18436
  7.6 5.6 %collective-permute-start.5 = (s32[4,2,192]{2,1,0:T(2,128)S(1)}, s32[4,2,192]{2,1,0:T(2,128)S(1)}, u32[]{:S(2)}, u32[]{:S(2)}) collective-permute-start(s32[4,2,192]{2,1,0:T(2,128)S(1)} %pad_add_fusion.refs_2_), channel_id=1, source_target_pairs={{0,12},{1,13},{2,14},{3,15},{4,8},{5,9},{6,10},{7,11},{8,4},{9,5},... | collective-permute-start | bytes 18440 | tf_op jit(solution)/shard_map/ppermute | solution.py:351
  11.2 4.5 %collective-permute-start.4 = (s32[4,2,192]{2,1,0:T(2,128)S(1)}, s32[4,2,192]{2,1,0:T(2,128)S(1)}, u32[]{:S(2)}, u32[]{:S(2)}) collective-permute-start(s32[4,2,192]{2,1,0:T(2,128)S(1)} %pad_add_fusion.refs_2_), channel_id=1, source_target_pairs={{0,8},{1,9},{2,10},{3,11},{4,12},{5,13},{6,14},{7,15},{8,0},{9,1},... | collective-permute-start | bytes 18440 | tf_op jit(solution)/shard_map/ppermute | solution.py:351
  11.2 4.6 %collective-permute-start.3 = (s32[4,2,192]{2,1,0:T(2,128)S(1)}, s32[4,2,192]{2,1,0:T(2,128)S(1)}, u32[]{:S(2)}, u32[]{:S(2)}) collective-permute-start(s32[4,2,192]{2,1,0:T(2,128)S(1)} %pad_add_fusion.refs_2_), channel_id=1, source_target_pairs={{0,4},{1,5},{2,6},{3,7},{4,0},{5,1},{6,2},{7,3},{8,12},{9,13},{10,... | collective-permute-start | bytes 18440 | tf_op jit(solution)/shard_map/ppermute | solution.py:351
  13.2 2.6 %copy-start.8 = (s32[4,2,192]{2,1,0:T(2,128)}, s32[4,2,192]{2,1,0:T(2,128)S(1)}, u32[]{:S(2)}) copy-start(s32[4,2,192]{2,1,0:T(2,128)S(1)} %collective-permute-done.5.refs_5_) | copy-start | bytes 18436
  15.7 0.6 %copy-start.9 = (s32[4,2,192]{2,1,0:T(2,128)}, s32[4,2,192]{2,1,0:T(2,128)S(1)}, u32[]{:S(2)}) copy-start(s32[4,2,192]{2,1,0:T(2,128)S(1)} %collective-permute-done.4.refs_4_) | copy-start | bytes 18436
  15.7 0.6 %copy-start.10 = (s32[4,2,192]{2,1,0:T(2,128)}, s32[4,2,192]{2,1,0:T(2,128)S(1)}, u32[]{:S(2)}) copy-start(s32[4,2,192]{2,1,0:T(2,128)S(1)} %collective-permute-done.3.refs_3_) | copy-start | bytes 18436
  27.6 1.9 %collective-permute-start.6 = (f32[4,2,703]{2,1,0:T(2,128)}, f32[4,2,703]{2,1,0:T(2,128)S(1)}, u32[]{:S(2)}, u32[]{:S(2)}) collective-permute-start(f32[4,2,703]{2,1,0:T(2,128)} %get-tuple-element.13), channel_id=1, source_target_pairs={{0,1},{1,0},{2,3},{3,2},{4,5},{5,4},{6,7},{7,6},{8,9},{9,8},{10,11... | collective-permute-start | bytes 67496 | tf_op jit(solution)/shard_map/ppermute | solution.py:351
  27.6 4.3 %collective-permute-start.7 = (f32[4,2,703]{2,1,0:T(2,128)}, f32[4,2,703]{2,1,0:T(2,128)S(1)}, u32[]{:S(2)}, u32[]{:S(2)}) collective-permute-start(f32[4,2,703]{2,1,0:T(2,128)} %get-tuple-element.14), channel_id=1, source_target_pairs={{0,2},{1,3},{2,0},{3,1},{4,6},{5,7},{6,4},{7,5},{8,10},{9,11},{10,... | collective-permute-start | bytes 67496 | tf_op jit(solution)/shard_map/ppermute | solution.py:351
  28.3 3.7 %collective-permute-start.8 = (f32[4,2,703]{2,1,0:T(2,128)}, f32[4,2,703]{2,1,0:T(2,128)S(1)}, u32[]{:S(2)}, u32[]{:S(2)}) collective-permute-start(f32[4,2,703]{2,1,0:T(2,128)} %get-tuple-element.15), channel_id=1, source_target_pairs={{0,3},{1,2},{2,1},{3,0},{4,7},{5,6},{6,5},{7,4},{8,11},{9,10},{10,... | collective-permute-start | bytes 67496 | tf_op jit(solution)/shard_map/ppermute | solution.py:351
  32.8 6.5 %copy-start = (f32[1,8,703]{2,1,0:T(8,128)}, f32[1,8,703]{2,1,0:T(8,128)S(1)}, u32[]{:S(2)}) copy-start(f32[1,8,703]{2,1,0:T(8,128)S(1)} %add_add_fusion) | copy-start | bytes 67492
  32.8 5.9 %collective-permute-start.11 = (f32[4,2,703]{2,1,0:T(2,128)S(1)}, f32[4,2,703]{2,1,0:T(2,128)S(1)}, u32[]{:S(2)}, u32[]{:S(2)}) collective-permute-start(f32[4,2,703]{2,1,0:T(2,128)S(1)} %bitcast.12), channel_id=1, source_target_pairs={{0,12},{1,13},{2,14},{3,15},{4,8},{5,9},{6,10},{7,11},{8,4},{9,5},... | collective-permute-start | bytes 67496 | tf_op jit(solution)/shard_map/ppermute | solution.py:351
  34.3 4.7 %collective-permute-start.10 = (f32[4,2,703]{2,1,0:T(2,128)S(1)}, f32[4,2,703]{2,1,0:T(2,128)S(1)}, u32[]{:S(2)}, u32[]{:S(2)}) collective-permute-start(f32[4,2,703]{2,1,0:T(2,128)S(1)} %bitcast.13), channel_id=1, source_target_pairs={{0,8},{1,9},{2,10},{3,11},{4,12},{5,13},{6,14},{7,15},{8,0},{9,1},... | collective-permute-start | bytes 67496 | tf_op jit(solution)/shard_map/ppermute | solution.py:351
  35.0 4.3 %collective-permute-start.9 = (f32[4,2,703]{2,1,0:T(2,128)S(1)}, f32[4,2,703]{2,1,0:T(2,128)S(1)}, u32[]{:S(2)}, u32[]{:S(2)}) collective-permute-start(f32[4,2,703]{2,1,0:T(2,128)S(1)} %bitcast.14), channel_id=1, source_target_pairs={{0,4},{1,5},{2,6},{3,7},{4,0},{5,1},{6,2},{7,3},{8,12},{9,13},{10,... | collective-permute-start | bytes 67496 | tf_op jit(solution)/shard_map/ppermute | solution.py:351
  38.7 0.6 %copy-start.5 = (f32[4,2,703]{2,1,0:T(2,128)}, f32[4,2,703]{2,1,0:T(2,128)S(1)}, u32[]{:S(2)}) copy-start(f32[4,2,703]{2,1,0:T(2,128)S(1)} %collective-permute-done.11.refs_7_) | copy-start | bytes 67492
  39.1 0.6 %copy-start.6 = (f32[4,2,703]{2,1,0:T(2,128)}, f32[4,2,703]{2,1,0:T(2,128)S(1)}, u32[]{:S(2)}) copy-start(f32[4,2,703]{2,1,0:T(2,128)S(1)} %collective-permute-done.10.refs_6_) | copy-start | bytes 67492
  39.7 0.6 %copy-start.7 = (f32[4,2,703]{2,1,0:T(2,128)}, f32[4,2,703]{2,1,0:T(2,128)S(1)}, u32[]{:S(2)}) copy-start(f32[4,2,703]{2,1,0:T(2,128)S(1)} %collective-permute-done.9.refs_5_) | copy-start | bytes 67492
  43.3 3.5 %collective-permute-start.14 = (f32[4,2,806]{2,1,0:T(2,128)}, f32[4,2,806]{2,1,0:T(2,128)S(1)}, u32[]{:S(2)}, u32[]{:S(2)}) collective-permute-start(f32[4,2,806]{2,1,0:T(2,128)} %gain_solve.1.refs_3_), channel_id=1, source_target_pairs={{0,3},{1,2},{2,1},{3,0},{4,7},{5,6},{6,5},{7,4},{8,11},{9,10},{10,... | collective-permute-start | bytes 77384 | tf_op jit(solution)/shard_map/ppermute | solution.py:351
  43.3 4.2 %collective-permute-start.13 = (f32[4,2,806]{2,1,0:T(2,128)}, f32[4,2,806]{2,1,0:T(2,128)S(1)}, u32[]{:S(2)}, u32[]{:S(2)}) collective-permute-start(f32[4,2,806]{2,1,0:T(2,128)} %gain_solve.1.refs_3_), channel_id=1, source_target_pairs={{0,2},{1,3},{2,0},{3,1},{4,6},{5,7},{6,4},{7,5},{8,10},{9,11},{10,... | collective-permute-start | bytes 77384 | tf_op jit(solution)/shard_map/ppermute | solution.py:351
  44.4 3.0 %collective-permute-start.12 = (f32[4,2,806]{2,1,0:T(2,128)}, f32[4,2,806]{2,1,0:T(2,128)S(1)}, u32[]{:S(2)}, u32[]{:S(2)}) collective-permute-start(f32[4,2,806]{2,1,0:T(2,128)} %gain_solve.1.refs_3_), channel_id=1, source_target_pairs={{0,1},{1,0},{2,3},{3,2},{4,5},{5,4},{6,7},{7,6},{8,9},{9,8},{10,11... | collective-permute-start | bytes 77384 | tf_op jit(solution)/shard_map/ppermute | solution.py:351
  46.8 0.7 %copy-start.2 = (f32[4,2,806]{2,1,0:T(2,128)}, f32[4,2,806]{2,1,0:T(2,128)S(1)}, u32[]{:S(2)}) copy-start(f32[4,2,806]{2,1,0:T(2,128)S(1)} %collective-permute-done.14.refs_6_) | copy-start | bytes 77380
  47.5 0.6 %copy-start.3 = (f32[4,2,806]{2,1,0:T(2,128)}, f32[4,2,806]{2,1,0:T(2,128)S(1)}, u32[]{:S(2)}) copy-start(f32[4,2,806]{2,1,0:T(2,128)S(1)} %collective-permute-done.13.refs_5_) | copy-start | bytes 77380
  47.5 0.6 %copy-start.4 = (f32[4,2,806]{2,1,0:T(2,128)}, f32[4,2,806]{2,1,0:T(2,128)S(1)}, u32[]{:S(2)}) copy-start(f32[4,2,806]{2,1,0:T(2,128)S(1)} %collective-permute-done.12.refs_4_) | copy-start | bytes 77380

commit v4 on v3

v4 whole, which is shorter than its diff:
```python
import jax
import jax.numpy as jnp
import numpy as np
from jax import lax
from jax.experimental import pallas as pl
from jax.experimental.pallas import tpu as pltpu
from jax.sharding import PartitionSpec as P

STATIONS = 38
GITERS = 8
DAMPING = 1.0
STEPS_PER_TURN = 64
GAINS_AT = 768
CHUNK = 48
ROWS = 40

F32 = jnp.float32
BF16 = jnp.bfloat16


def iota(shape, dim):
    return lax.broadcasted_iota(jnp.int32, shape, dim).astype(F32)


def sincos_turns(turns):
    half = (turns - jnp.floor(turns + 0.5)) * np.float32(np.pi)
    sq = half * half
    sin = np.float32(-1.0 / 39916800)
    for term in (1.0 / 362880, -1.0 / 5040, 1.0 / 120, -1.0 / 6, 1.0):
        sin = sin * sq + np.float32(term)
    sin = sin * half
    cos = np.float32(1.0 / 479001600)
    for term in (-1.0 / 3628800, 1.0 / 40320, -1.0 / 720, 1.0 / 24, -0.5, 1.0):
        cos = cos * sq + np.float32(term)
    return 1.0 - 2.0 * (sin * sin), 2.0 * (sin * cos)


def split_two(value):
    high = value.astype(BF16)
    low = (value - high.astype(F32)).astype(BF16)
    return high, low


def split_three(value):
    high = value.astype(BF16)
    rest = value - high.astype(F32)
    mid = rest.astype(BF16)
    low = (rest - mid.astype(F32)).astype(BF16)
    return high, mid, low


def dot(left, right):
    return jnp.dot(left, right, preferred_element_type=F32)


def times(left, right):
    (lr, li), (rr, ri) = left, right
    return lr * rr - li * ri, lr * ri + li * rr


def phase_rows(delays, anchor, width):
    place = iota((8, 1), 0)
    second = place >= 4.0
    turns = jnp.where(second, delays[1], delays[0])
    at = anchor + float(STEPS_PER_TURN) * jnp.where(second, place - 4.0, place)
    base = sincos_turns(turns * (at * np.float32(1.0 / STEPS_PER_TURN)))
    fine, coarse = [], []
    for s in range(2):
        low = sincos_turns(delays[s] * (place * np.float32(1.0 / STEPS_PER_TURN)))
        high = low
        for doubling in range(3):
            high = times(high, high)
        rows = [times(tuple(part[4 * s + a:4 * s + a + 1] for part in base), high)
                for a in range(width // STEPS_PER_TURN)]
        fine.append(low)
        coarse.append(rows)
    return fine, coarse


def tiles(pairs, body):
    full = pairs // 128

    def step(tile, carry):
        body(pl.ds(pl.multiple_of(tile * 128, 128), 128), 128)
        return carry

    lax.fori_loop(0, full, step, 0)
    if pairs % 128:
        body(pl.ds(full * 128, pairs % 128), pairs % 128)


def phase_kernel(width, me_ref, delay_ref, vis_hbm, vis_ref, wave_ref, mix_ref, sems):
    anchor = me_ref[0].astype(F32) * float(width)
    pairs = delay_ref.shape[2]
    copies = [pltpu.make_async_copy(vis_hbm.at[:, t], vis_ref.at[:, t], sems.at[t]) for t in range(2)]
    for copy in copies:
        copy.start()
    for t in range(2):
        def waves(lanes, count):
            delays = [delay_ref[s, t:t + 1, lanes] for s in range(2)]
            fine, coarse = phase_rows(delays, anchor, width)
            for block in range(width // 16):
                found = []
                for s in range(2):
                    halves = []
                    for half in range(2):
                        a, b = divmod(2 * block + half, 8)
                        halves.append(times(tuple(part[b:b + 1] for part in coarse[s][a]), fine[s]))
                    found.append([jnp.concatenate([h[ri] for h in halves], axis=0) for ri in range(2)])
                rows = slice(block * 16, block * 16 + 16)
                (r0, i0), (r1, i1) = found
                for s in range(2):
                    for ri in range(2):
                        wave_ref[t, s, ri, rows, lanes] = found[s][ri]
                for slot, value in enumerate((r1 * r0 + i1 * i0, i1 * r0 - r1 * i0)):
                    high, low = split_two(value)
                    mix_ref[t, slot, 0, rows, lanes] = high
                    mix_ref[t, slot, 1, rows, lanes] = low

        tiles(pairs, waves)
    for copy in copies:
        copy.wait()


def sums_kernel(width, stages, me_ref, win_ref, *refs):
    flag_refs, refs = refs[:stages], refs[stages:]
    delay_ref, vis_ref, wave_ref, mix_ref = refs[:4]
    out_refs, (alpha_s, mexp_s, wt_s) = refs[4:8], refs[8:]
    me = me_ref[0]
    near = flag_refs[0].shape[0]
    groups = near * stages
    windows = win_ref.shape[1]
    pairs = delay_ref.shape[2]
    anchor = me.astype(F32) * float(width)
    final = anchor + float(width - 1)

    win_row = win_ref[...].astype(F32)
    sub, lane = iota((windows, windows), 0), iota((windows, windows), 1)
    end_c = jnp.sum(jnp.where(lane <= sub, win_row, 0.0), axis=1, keepdims=True)
    start_c = jnp.sum(jnp.where(lane < sub, win_row, 0.0), axis=1, keepdims=True)
    win_c = end_c - start_c
    end_r = jnp.sum(jnp.where(sub <= lane, win_c, 0.0), axis=0, keepdims=True)
    start_r = jnp.sum(jnp.where(sub < lane, win_c, 0.0), axis=0, keepdims=True)
    first_c = jnp.where((start_c <= anchor) & (anchor < end_c), 1.0, 0.0)
    last_c = jnp.where((start_c <= final) & (final < end_c), 1.0, 0.0)
    from_first = jnp.sum(first_c * start_c, axis=0, keepdims=True)
    to_last = jnp.sum(last_c * end_c, axis=0, keepdims=True)
    here = anchor + iota((windows, width), 1)
    member_wc = (here >= start_c) & (here < end_c)
    there = iota((width, windows), 0) + anchor
    member_cw = (there >= start_r) & (there < end_r)
    apart = iota((groups, 1), 0) - me.astype(F32)
    channel = iota((groups, width), 0) * float(width) + iota((groups, width), 1)
    remote = ((channel < anchor) & (channel >= from_first)) | ((channel > final) & (channel < to_last))
    diagonal = iota((width, width), 0) == iota((width, width), 1)

    def both_sides(value):
        return (jnp.sum(jnp.where(apart < 0.0, value, 0.0), axis=0, keepdims=True),
                jnp.sum(jnp.where(apart > 0.0, value, 0.0), axis=0, keepdims=True))

    for t in range(2):
        for slot in range(groups):
            row = flag_refs[slot // near][slot % near, t:t + 1, :].astype(F32)
            wt_s[t, pl.ds(lax.bitwise_xor(me, slot), 1), :] = 1.0 - row
        own = 1.0 - flag_refs[0][0, t:t + 1, :].astype(F32)
        inside = jnp.where(member_wc, own, 0.0)
        outside = jnp.where(remote, wt_s[t], 0.0)
        before, after = both_sides(jnp.sum(outside, axis=1, keepdims=True))
        count = jnp.sum(inside, axis=1, keepdims=True) + first_c * before + last_c * after
        scale = 1.0 / jnp.maximum(count, 1.0)
        rows = jnp.concatenate([inside, outside], axis=0).astype(BF16)
        scale_r = jnp.sum(jnp.where(sub == lane, scale, 0.0), axis=0, keepdims=True)
        own_c = jnp.sum(jnp.where(diagonal, own, 0.0), axis=1, keepdims=True)
        chosen = jnp.where(member_cw, own_c, 0.0)
        alpha_s[t] = jnp.broadcast_to(jnp.sum(chosen * scale_r, axis=1, keepdims=True), (width, 128))
        chosen = chosen.astype(BF16)
        sums = [dot(rows, mix_ref[t, slot, 0]) + dot(rows, mix_ref[t, slot, 1]) for slot in range(2)]
        gap = delay_ref[1, t:t + 1, :] - delay_ref[0, t:t + 1, :]
        phase = sincos_turns(gap * (apart * np.float32(width / STEPS_PER_TURN)))
        away = times(phase, tuple(value[windows:] for value in sums))
        for slot in range(2):
            before, after = both_sides(away[slot])
            total = sums[slot][:windows] + first_c * before + last_c * after
            high, low = split_two(total * (scale * scale))
            mexp_s[t, slot] = dot(chosen, high) + dot(chosen, low)

    for t in range(2):
        def main(lanes, count):
            def step(block, sums):
                rows = pl.ds(pl.multiple_of(block * 16, 16), 16)
                alpha = alpha_s[t, rows, :count]
                mr, mi = mexp_s[t, 0, rows, lanes], mexp_s[t, 1, rows, lanes]
                r0, i0 = wave_ref[t, 0, 0, rows, lanes], wave_ref[t, 0, 1, rows, lanes]
                r1, i1 = wave_ref[t, 1, 0, rows, lanes], wave_ref[t, 1, 1, rows, lanes]
                factors = []
                for fr, fi in (
                    (alpha * r0 - (mr * r1 + mi * i1), (mr * i1 - mi * r1) - alpha * i0),
                    (alpha * r1 - (mr * r0 - mi * i0), (mr * i0 + mi * r0) - alpha * i1),
                ):
                    factors.append((fr, fi - fr, fr + fi))
                new = []
                for k in range(4):
                    vr = vis_ref[0, t, k, rows, lanes].astype(F32)
                    vi = vis_ref[1, t, k, rows, lanes].astype(F32)
                    vs = vr + vi
                    for s in range(2):
                        for v, f in zip((vs, vr, vi), factors[s]):
                            product = v * f
                            new.append(sums[len(new)] + (product[:8] + product[8:]))
                return tuple(new)

            zero = jnp.zeros((8, count), F32)
            sums = lax.fori_loop(0, width // 16, step, (zero,) * 24, unroll=4)
            for s in range(2):
                owner = lax.bitwise_xor(lax.bitwise_and(me, 3), t + 2 * s)
                found = []
                for k in range(4):
                    one, two, three = sums[(k * 2 + s) * 3:(k * 2 + s) * 3 + 3]
                    found.append([jnp.sum(value, axis=0, keepdims=True) for value in (one - three, one + two)])
                for d in range(4):
                    @pl.when(owner == d)
                    def write():
                        for k in range(4):
                            for ri in range(2):
                                out_refs[d][k, ri:ri + 1, lanes] = found[k][ri]

        tiles(pairs, main)


def station_hots(pairs):
    station, baseline = iota((ROWS, 1), 0), iota((1, pairs), 1)
    offset = station * (float(2 * STATIONS - 1) - station) * 0.5
    after = (station + 1.0) * (float(2 * STATIONS - 2) - station) * 0.5
    first = jnp.where((baseline >= offset) & (baseline < after), 1.0, 0.0)
    partner_of = baseline + 1.0 + jnp.sum(first * (station - offset), axis=0, keepdims=True)
    second = jnp.where(partner_of == station, 1.0, 0.0)
    return first.astype(BF16), second.astype(BF16)


def solve_kernel(window_count, me_ref, tracks_ref, *refs):
    parts, gain_ref = refs[:-1], refs[-1]
    me = me_ref[0]
    systems = gain_ref.shape[0]
    total = [part[...] for part in parts]
    while len(total) > 1:
        total = [total[i] + total[i + 1] for i in range(0, len(total), 2)]
    total = total[0]
    hot, other = station_hots(total.shape[2])
    nt = lambda left, right: lax.dot_general(
        left, right, (((1,), (1,)), ((), ())), preferred_element_type=F32)
    upper, lower = [], []
    for system in range(systems):
        for ri in range(2):
            for piece in split_two(total[system, ri:ri + 1]):
                upper.append(hot * piece)
                lower.append(other * piece)
    upper = nt(jnp.concatenate(upper, axis=0), other)
    lower = nt(jnp.concatenate(lower, axis=0), hot)
    cut = lambda value, i: value[i * ROWS:(i + 1) * ROWS]
    join = lambda value, i: cut(value, 2 * i) + cut(value, 2 * i + 1)
    live_r = jnp.where(iota((1, ROWS), 1) < float(STATIONS), 1.0, 0.0)
    live_c = jnp.where(iota((ROWS, 1), 0) < float(STATIONS), 1.0, 0.0)
    matrices = [(join(upper, 2 * i) + join(lower, 2 * i), join(upper, 2 * i + 1) - join(lower, 2 * i + 1))
                for i in range(systems)]
    states = [(live_r, 0.0 * live_r, live_c, 0.0 * live_c)] * systems
    for turn in range(GITERS):
        for system in range(systems):
            re, im = matrices[system]
            row_re, row_im, col_re, col_im = states[system]
            pull_cr = jnp.sum(re * row_re - im * row_im, axis=1, keepdims=True)
            pull_ci = jnp.sum(re * row_im + im * row_re, axis=1, keepdims=True)
            pull_rr = jnp.sum(re * col_re + im * col_im, axis=0, keepdims=True)
            pull_ri = jnp.sum(re * col_im - im * col_re, axis=0, keepdims=True)
            power_r = row_re * row_re + row_im * row_im
            power_c = col_re * col_re + col_im * col_im
            total = jnp.sum(power_c, axis=0, keepdims=True)
            inverse_r = 0.5 / (window_count * (total - power_r) + DAMPING)
            inverse_c = 0.5 / (window_count * (total - power_c) + DAMPING)
            states[system] = (0.5 * row_re + pull_rr * inverse_r, 0.5 * row_im + pull_ri * inverse_r,
                              0.5 * col_re + pull_cr * inverse_c, 0.5 * col_im + pull_ci * inverse_c)
    visible = tracks_ref[lax.bitwise_and(lax.div(me, 2), 1), lax.bitwise_and(me, 1)].astype(F32)
    gains = [state[ri] * visible for state in states for ri in range(2)]
    gains = jnp.concatenate(gains, axis=0)
    stacked = jnp.concatenate([piece.astype(F32) for piece in split_three(gains)], axis=0).astype(BF16)
    ends = []
    for table in (hot, other):
        wide = dot(stacked, table)
        ends.append((wide[:8] + wide[8:16]) + wide[16:])
    pairs = hot.shape[1]
    for system in range(systems):
        (lr, li), (rr, ri_) = [[end[2 * system + ri:2 * system + ri + 1] for ri in range(2)] for end in ends]
        gain_ref[system, 0:1, :pairs] = lr * rr + li * ri_
        gain_ref[system, 1:2, :pairs] = li * rr - lr * ri_
        gain_ref[system, :, GAINS_AT:] = gains[2 * system:2 * system + 2, :STATIONS]


def clean_kernel(width, me_ref, vis_ref, wave_ref, *refs):
    piece_refs, (out_hbm, gain_out_ref, out_s, model_s, sems) = refs[:4], refs[4:]
    pairs = wave_ref.shape[4]
    mine = lax.bitwise_and(me_ref[0], 3)
    for d, piece in enumerate(piece_refs):
        owner = lax.bitwise_xor(mine, d)
        t, s = lax.bitwise_and(owner, 1), lax.div(owner, 2)
        for k in range(4):
            for ri in range(2):
                gain_out_ref[ri, s, t, k:k + 1, :] = piece[k, ri:ri + 1, GAINS_AT:]
            re, im = piece[k, 0:1, :pairs], piece[k, 1:2, :pairs]
            for slot, value in enumerate((re, im - re, re + im)):
                model_s[owner, 3 * k + slot:3 * k + slot + 1, :] = value

    chunks = width // CHUNK

    def copy_out(index):
        t, rows = lax.div(index, chunks), pl.ds(pl.multiple_of(lax.rem(index, chunks) * CHUNK, CHUNK), CHUNK)
        return pltpu.make_async_copy(out_s.at[:, t, :, rows], out_hbm.at[:, t, :, rows], sems.at[index])

    def chunk(index, carry):
        t, base = lax.div(index, chunks), lax.rem(index, chunks) * CHUNK

        def main(lanes, count):
            for block in range(CHUNK // 16):
                rows = pl.ds(pl.multiple_of(base + block * 16, 16), 16)
                waves = []
                for s in range(2):
                    re, im = wave_ref[t, s, 0, rows, lanes], wave_ref[t, s, 1, rows, lanes]
                    waves.append((re + im, re, im))
                for k in range(4):
                    sums = []
                    for slot in range(3):
                        one, two = (waves[s][slot] * model_s[t + 2 * s, 3 * k + slot:3 * k + slot + 1, lanes]
                                    for s in range(2))
                        sums.append(one + two)
                    vr = vis_ref[0, t, k, rows, lanes].astype(F32)
                    vi = vis_ref[1, t, k, rows, lanes].astype(F32)
                    out_s[0, t, k, rows, lanes] = (vr - (sums[0] - sums[2])).astype(BF16)
                    out_s[1, t, k, rows, lanes] = (vi - (sums[0] + sums[1])).astype(BF16)

        tiles(pairs, main)
        copy_out(index).start()
        return carry

    lax.fori_loop(0, 2 * chunks, chunk, 0)
    for index in range(2 * chunks):
        copy_out(index).wait()


def partner(value, bits):
    count = lax.axis_size("sub")
    return lax.ppermute(value, "sub", [(i, i ^ bits) for i in range(count)])


def smem():
    return pl.BlockSpec(memory_space=pltpu.SMEM)


def local(visibilities, delays, flags, windows, tracks):
    width = visibilities.shape[4]
    pairs = visibilities.shape[3]
    count = lax.axis_size("sub")
    window_count = windows.shape[0]
    turned = jnp.transpose(visibilities, (0, 1, 2, 4, 3))
    me = lax.axis_index("sub").astype(jnp.int32).reshape(1)
    gathered = [flags[None]]
    stride = 1
    while stride < count:
        gathered = [jnp.concatenate(gathered, axis=0)] if len(gathered) > 1 else gathered
        gathered += [partner(gathered[0], stride * d) for d in range(1, min(4, count // stride))]
        stride *= 4
    vmem_ref = pl.BlockSpec(memory_space=pltpu.VMEM)
    hbm_ref = pl.BlockSpec(memory_space=pltpu.HBM)
    vmem = lambda *shape: pltpu.VMEM(shape, F32)
    params = pltpu.CompilerParams(vmem_limit_bytes=24 * 2 ** 20)
    held, waves, mixing = pl.pallas_call(
        lambda *refs: phase_kernel(width, *refs),
        in_specs=[smem(), vmem_ref, hbm_ref],
        out_specs=[vmem_ref] * 3,
        out_shape=[
            jax.ShapeDtypeStruct(turned.shape, BF16),
            jax.ShapeDtypeStruct((2, 2, 2, width, pairs), F32),
            jax.ShapeDtypeStruct((2, 2, 2, width, pairs), BF16),
        ],
        scratch_shapes=[pltpu.SemaphoreType.DMA((2,))],
        compiler_params=pltpu.CompilerParams(vmem_limit_bytes=40 * 2 ** 20),
        cost_estimate=pl.CostEstimate(flops=2 * 10 ** 7, bytes_accessed=12 * 2 ** 20, transcendentals=0),
        name="phases",
    )(me, delays, turned)
    quarters = pl.pallas_call(
        lambda *refs: sums_kernel(width, len(gathered), *refs),
        in_specs=[smem()] + [vmem_ref] * (len(gathered) + 5),
        out_specs=[vmem_ref] * 4,
        out_shape=[jax.ShapeDtypeStruct((4, 2, pairs), F32)] * 4,
        scratch_shapes=[vmem(2, width, 128), vmem(2, 2, width, pairs), vmem(2, count, width)],
        compiler_params=params,
        name="window_sums",
    )(me, windows.reshape(1, window_count), *gathered, delays, held, waves, mixing)
    pieces = [quarters[0]] + [partner(quarters[d], d) for d in range(1, 4)]
    stride = 4
    while stride < count:
        while len(pieces) > 1:
            pieces = [pieces[i] + pieces[i + 1] for i in range(0, len(pieces), 2)]
        pieces += [partner(pieces[0], stride * d) for d in range(1, min(4, count // stride))]
        stride *= 4
    model = pl.pallas_call(
        lambda *refs: solve_kernel(float(window_count), *refs),
        in_specs=[smem(), smem()] + [vmem_ref] * len(pieces),
        out_specs=vmem_ref,
        out_shape=jax.ShapeDtypeStruct((4, 2, GAINS_AT + STATIONS), F32),
        compiler_params=params,
        name="gain_solve",
    )(me, tracks, *pieces)
    model = [model] + [partner(model, d) for d in range(1, 4)]
    cleaned, gains = pl.pallas_call(
        lambda *refs: clean_kernel(width, *refs),
        in_specs=[smem()] + [vmem_ref] * 6,
        out_specs=[hbm_ref, vmem_ref],
        out_shape=[
            jax.ShapeDtypeStruct(turned.shape, BF16),
            jax.ShapeDtypeStruct((2, 2, 2, 4, STATIONS), F32),
        ],
        scratch_shapes=[
            pltpu.VMEM(turned.shape, BF16),
            vmem(4, 16, pairs),
            pltpu.SemaphoreType.DMA((2 * (width // CHUNK),)),
        ],
        compiler_params=params,
        name="clean",
    )(me, held, waves, *model)
    return jnp.transpose(cleaned, (0, 1, 2, 4, 3)), gains


def solution(mesh):
    return jax.shard_map(
        local,
        mesh=mesh,
        in_specs=(
            P(None, "obs", None, None, "sub"),
            P(None, "obs", None),
            P("obs", "sub"),
            P(),
            P(None, "obs"),
        ),
        out_specs=(P(None, "obs", None, None, "sub"), P(None, None, "obs", None, None)),
        check_vma=False,
    )
```

time: 54.9 us -> 44.9 us (0.82)
  Pallas kernels: 20.8 us -> 15 us
  waiting for transfers between devices: 13.8 us -> 11.7 us
  local copies, waits for them, and re-layouts: 2.16 us -> 0.71 us
  other arithmetic: 1.44 us -> 0.7 us
    pallas_call x2 -> x3, Pallas kernels: 17.8 us -> 13 us  [the longest x1 5.69 us: local(): pl.pallas_call(lambda *refs: sums_kernel(width, len(gathered), *refs), in...]
    ppermute x15, waiting for transfers between devices: 13.8 us -> 11.7 us  [partner(): return lax.ppermute(value, 'sub', [(i, i ^ bits) for i in range(count)])]
    unnamed x22 -> x6, local copies, waits for them, and re-layouts: 2.16 us -> 0.71 us
    pallas_call x1, Pallas kernels: 3.01 us -> 2.09 us  [local(): pl.pallas_call(lambda *refs: solve_kernel(float(window_count), *refs), in...]
    add x1, other arithmetic: 0.75 us -> 0.01 us  [local(): pieces = [pieces[i] + pieces[i + 1] for i in range(0, len(pieces), 2)]]
  transfers between devices with their start and end apart: 15 -> 15, of which waited for: 11 -> 9; matrix products, arithmetic and copies ran while one was open for 0% -> 0% of each run, Pallas kernels for 0% -> 5%
where the time goes in v4:
time: 44.9 us; the launch traced here: 44.7 us
  starting transfers between devices  15.8 us (35%)
  Pallas kernels  15 us (33%)
  waiting for transfers between devices  11.7 us (26%)
  local copies, waits for them, and re-layouts  0.71 us (2%)
  between operations  0.71 us (2%)
  other arithmetic  0.7 us (2%)
    ppermute x15, starting transfers between devices, partner(): return lax.ppermute(value, 'sub', [(i, i ^ bits) for i in range(count)])  15.8 us
    ppermute x15, waiting for transfers between devices, partner(): return lax.ppermute(value, 'sub', [(i, i ^ bits) for i in range(count)])  11.7 us
    pallas_call x1, Pallas kernels, local(): pl.pallas_call(lambda *refs: sums_kernel(width, len(gathered), *refs), in...  5.69 us
    pallas_call x1, Pallas kernels, local(): pl.pallas_call(lambda *refs: clean_kernel(width, *refs), in_specs=[smem()...  4.89 us
    pallas_call x1, Pallas kernels, local(): pl.pallas_call(lambda *refs: phase_kernel(width, *refs), in_specs=[smem()...  2.39 us
    pallas_call x1, Pallas kernels, local(): pl.pallas_call(lambda *refs: solve_kernel(float(window_count), *refs), in...  2.09 us
  transfers between devices with their start and end apart: 15, of which 9 were waited for; matrix products, arithmetic and copies ran while one was open for 0% of the time, Pallas kernels for 5%

profile of v4, /device:TPU:0, one launch (start us, length us, event | category | flops | bytes accessed | tf_op | source)
XLA Modules:
  0.0 44.7 jit_solution(7826109500522562655)
XLA Ops:
  0.6 0.0 copy-start.2
  0.6 2.5 %collective-permute-start.2 = (s32[1,2,192]{2,1,0:T(2,128)}, s32[1,2,192]{2,1,0:T(2,128)S(1)}, u32[]{:S(2)}, u32[]{:S(2)}) collective-permute-start(s32[1,2,192]{2,1,0:T(2,128)} %bitcast.20), channel_id=1, source_target_pairs={{0,3},{1,2},{2,1},{3,0},{4,7},{5,6},{6,5},{7,4},{8,11},{9,10},{10,... | collective-permute-start | bytes 4616 | tf_op jit(solution)/shard_map/ppermute | solution.py:349
  3.1 0.6 %collective-permute-start.1 = (s32[1,2,192]{2,1,0:T(2,128)}, s32[1,2,192]{2,1,0:T(2,128)S(1)}, u32[]{:S(2)}, u32[]{:S(2)}) collective-permute-start(s32[1,2,192]{2,1,0:T(2,128)} %bitcast.21), channel_id=1, source_target_pairs={{0,2},{1,3},{2,0},{3,1},{4,6},{5,7},{6,4},{7,5},{8,10},{9,11},{10,... | collective-permute-start | bytes 4616 | tf_op jit(solution)/shard_map/ppermute | solution.py:349
  3.8 0.0 collective-permute-start
  3.8 0.8 %collective-permute-done.2 = s32[1,2,192]{2,1,0:T(2,128)S(1)} collective-permute-done((s32[1,2,192]{2,1,0:T(2,128)}, s32[1,2,192]{2,1,0:T(2,128)S(1)}, u32[]{:S(2)}, u32[]{:S(2)}) %collective-permute-start.2) | collective-permute-done | bytes 1568 | tf_op jit(solution)/shard_map/ppermute | solution.py:349
  4.6 2.3 %collective-permute-done.1 = s32[1,2,192]{2,1,0:T(2,128)S(1)} collective-permute-done((s32[1,2,192]{2,1,0:T(2,128)}, s32[1,2,192]{2,1,0:T(2,128)S(1)}, u32[]{:S(2)}, u32[]{:S(2)}) %collective-permute-start.1) | collective-permute-done | bytes 1568 | tf_op jit(solution)/shard_map/ppermute | solution.py:349
  6.9 0.0 collective-permute-done
  6.9 0.7 %pad_add_fusion.refs_2_ = s32[4,2,192]{2,1,0:T(2,128)S(1)} fusion(s32[1,2,192]{2,1,0:T(2,128)S(1)} %collective-permute-done.2, s32[1,2,192]{2,1,0:T(2,128)S(1)} %collective-permute-done.1, s32[1,2,192]{2,1,0:T(2,128)S(1)} %collective-permute-done, s32[1,2,192]{2,1,0:T(2,128)} %bitcast.23), kind=kLoop, calls=%fused_computation.1 | loop fusion | flops 4608 | bytes 12288 | tf_op jit(solution)/shard_map/concatenate | solution.py:366
  7.6 3.6 %collective-permute-start.5 = (s32[4,2,192]{2,1,0:T(2,128)S(1)}, s32[4,2,192]{2,1,0:T(2,128)S(1)}, u32[]{:S(2)}, u32[]{:S(2)}) collective-permute-start(s32[4,2,192]{2,1,0:T(2,128)S(1)} %pad_add_fusion.refs_2_), channel_id=1, source_target_pairs={{0,12},{1,13},{2,14},{3,15},{4,8},{5,9},{6,10},{7,11},{8,4},{9,5},... | collective-permute-start | bytes 18440 | tf_op jit(solution)/shard_map/ppermute | solution.py:349
  11.2 0.0 collective-permute-start.4
  11.2 0.8 %collective-permute-start.3 = (s32[4,2,192]{2,1,0:T(2,128)S(1)}, s32[4,2,192]{2,1,0:T(2,128)S(1)}, u32[]{:S(2)}, u32[]{:S(2)}) collective-permute-start(s32[4,2,192]{2,1,0:T(2,128)S(1)} %pad_add_fusion.refs_2_), channel_id=1, source_target_pairs={{0,4},{1,5},{2,6},{3,7},{4,0},{5,1},{6,2},{7,3},{8,12},{9,13},{10,... | collective-permute-start | bytes 18440 | tf_op jit(solution)/shard_map/ppermute | solution.py:349
  12.0 0.0 copy-start
  12.0 0.7 %copy-done = f32[2,2,703]{2,1,0:T(2,128)S(1)} copy-done((f32[2,2,703]{2,1,0:T(2,128)S(1)}, f32[2,2,703]{2,1,0:T(2,128)}, u32[]{:S(2)}) %copy-start) | copy-done | bytes 11272
  12.7 2.4 %phases.1 = (bf16[2,2,4,192,703]{4,3,2,1,0:T(8,128)(2,1)S(1)}, f32[2,2,2,192,703]{4,3,2,1,0:T(8,128)S(1)}, bf16[2,2,2,192,703]{4,3,2,1,0:T(8,128)(2,1)S(1)}) custom-call(s32[1]{0:T(128)} %bitcast.refs_0_, f32[2,2,703]{2,1,0:T(2,128)S(1)} %copy-done, bf16[2,2,4,192,703]{4,3,2,1,0:T(8,128)(2,1)} %bitcast.16), custom_call_target="tpu_custom_call" | custom-call | flops 20000000 | bytes 12582912 | tf_op jit(solution)/shard_map/phases/pallas_call | solution.py:373
  15.1 0.0 collective-permute-done.5.refs_5_
  15.1 0.6 %collective-permute-done.4.refs_4_ = s32[4,2,192]{2,1,0:T(2,128)S(1)} collective-permute-done((s32[4,2,192]{2,1,0:T(2,128)S(1)}, s32[4,2,192]{2,1,0:T(2,128)S(1)}, u32[]{:S(2)}, u32[]{:S(2)}) %collective-permute-start.4) | collective-permute-done | bytes 6176 | tf_op jit(solution)/shard_map/ppermute | solution.py:349
  15.8 0.0 collective-permute-done.3.refs_3_
  15.8 0.0 copy-done.2
  15.8 0.0 copy-start.1
  15.8 5.7 %window_sums.1 = (f32[4,2,703]{2,1,0:T(2,128)S(1)}, f32[4,2,703]{2,1,0:T(2,128)S(1)}, f32[4,2,703]{2,1,0:T(2,128)S(1)}, f32[4,2,703]{2,1,0:T(2,128)S(1)}) custom-call(s32[1]{0:T(128)} %bitcast.refs_0_, s32[1,32]{1,0:T(1,128)S(1)} %bitcast.15, s32[4,2,192]{2,1,0:T(2,128)S(1)} %pad_add_fusion.refs_2_, s32[4,2,192]{2,1,0:T(2,128)S(1)} %collective-permute-done.3.refs_3_, ...), custom_call_target="tpu_custom_call" | custom-call | tf_op jit(solution)/shard_map/window_sums/pallas_call | solution.py:387
  21.5 0.1 collective-permute-start.6
  21.5 0.7 %collective-permute-start.7 = (f32[4,2,703]{2,1,0:T(2,128)S(1)}, f32[4,2,703]{2,1,0:T(2,128)S(1)}, u32[]{:S(2)}, u32[]{:S(2)}) collective-permute-start(f32[4,2,703]{2,1,0:T(2,128)S(1)} %get-tuple-element.16), channel_id=1, source_target_pairs={{0,2},{1,3},{2,0},{3,1},{4,6},{5,7},{6,4},{7,5},{8,10},{9,11},{10,... | collective-permute-start | bytes 67496 | tf_op jit(solution)/shard_map/ppermute | solution.py:349
  22.2 1.2 %collective-permute-start.8 = (f32[4,2,703]{2,1,0:T(2,128)S(1)}, f32[4,2,703]{2,1,0:T(2,128)S(1)}, u32[]{:S(2)}, u32[]{:S(2)}) collective-permute-start(f32[4,2,703]{2,1,0:T(2,128)S(1)} %get-tuple-element.17), channel_id=1, source_target_pairs={{0,3},{1,2},{2,1},{3,0},{4,7},{5,6},{6,5},{7,4},{8,11},{9,10},{10,... | collective-permute-start | bytes 67496 | tf_op jit(solution)/shard_map/ppermute | solution.py:349
  23.4 0.0 collective-permute-done.6
  23.4 2.2 %collective-permute-done.7 = f32[4,2,703]{2,1,0:T(2,128)S(1)} collective-permute-done((f32[4,2,703]{2,1,0:T(2,128)S(1)}, f32[4,2,703]{2,1,0:T(2,128)S(1)}, u32[]{:S(2)}, u32[]{:S(2)}) %collective-permute-start.7) | collective-permute-done | bytes 22528 | tf_op jit(solution)/shard_map/ppermute | solution.py:349
  25.6 0.1 collective-permute-done.8
  25.8 3.1 %collective-permute-start.11 = (f32[4,2,703]{2,1,0:T(2,128)S(1)}, f32[4,2,703]{2,1,0:T(2,128)S(1)}, u32[]{:S(2)}, u32[]{:S(2)}) collective-permute-start(f32[4,2,703]{2,1,0:T(2,128)S(1)} %bitcast.10), channel_id=1, source_target_pairs={{0,12},{1,13},{2,14},{3,15},{4,8},{5,9},{6,10},{7,11},{8,4},{9,5},... | collective-permute-start | bytes 67496 | tf_op jit(solution)/shard_map/ppermute | solution.py:349
  28.8 0.0 collective-permute-start.10
  28.8 1.4 %collective-permute-start.9 = (f32[4,2,703]{2,1,0:T(2,128)S(1)}, f32[4,2,703]{2,1,0:T(2,128)S(1)}, u32[]{:S(2)}, u32[]{:S(2)}) collective-permute-start(f32[4,2,703]{2,1,0:T(2,128)S(1)} %bitcast.12), channel_id=1, source_target_pairs={{0,4},{1,5},{2,6},{3,7},{4,0},{5,1},{6,2},{7,3},{8,12},{9,13},{10,... | collective-permute-start | bytes 67496 | tf_op jit(solution)/shard_map/ppermute | solution.py:349
  30.2 1.5 %collective-permute-done.11.refs_5_ = f32[4,2,703]{2,1,0:T(2,128)S(1)} collective-permute-done((f32[4,2,703]{2,1,0:T(2,128)S(1)}, f32[4,2,703]{2,1,0:T(2,128)S(1)}, u32[]{:S(2)}, u32[]{:S(2)}) %collective-permute-start.11) | collective-permute-done | bytes 22528 | tf_op jit(solution)/shard_map/ppermute | solution.py:349
  31.7 1.8 %collective-permute-done.10.refs_4_ = f32[4,2,703]{2,1,0:T(2,128)S(1)} collective-permute-done((f32[4,2,703]{2,1,0:T(2,128)S(1)}, f32[4,2,703]{2,1,0:T(2,128)S(1)}, u32[]{:S(2)}, u32[]{:S(2)}) %collective-permute-start.10) | collective-permute-done | bytes 22528 | tf_op jit(solution)/shard_map/ppermute | solution.py:349
  33.5 0.0 collective-permute-done.9.refs_3_
  33.6 0.0 copy-done.1
  33.6 2.1 %gain_solve.1.refs_3_ = f32[4,2,806]{2,1,0:T(2,128)S(1)} custom-call(s32[1]{0:T(128)} %bitcast.refs_0_, s32[2,2]{1,0:T(2,128)S(1)} %copy-done.1, f32[4,2,703]{2,1,0:T(2,128)S(1)} %bitcast.13, f32[4,2,703]{2,1,0:T(2,128)S(1)} %collective-permute-done.9.refs_3_, f32[4,2,703]{2,1,0:T(2,128)S(1)} %collective-permute-done.10.refs_4_, ...), custom_call_target="tpu_custom_call" | custom-call | tf_op jit(solution)/shard_map/gain_solve/pallas_call | solution.py:403
  35.6 0.1 collective-permute-start.14
  35.7 1.2 %collective-permute-start.13 = (f32[4,2,806]{2,1,0:T(2,128)S(1)}, f32[4,2,806]{2,1,0:T(2,128)S(1)}, u32[]{:S(2)}, u32[]{:S(2)}) collective-permute-start(f32[4,2,806]{2,1,0:T(2,128)S(1)} %gain_solve.1.refs_3_), channel_id=1, source_target_pairs={{0,2},{1,3},{2,0},{3,1},{4,6},{5,7},{6,4},{7,5},{8,10},{9,11},{10,... | collective-permute-start | bytes 77384 | tf_op jit(solution)/shard_map/ppermute | solution.py:349
  36.9 0.7 %collective-permute-start.12 = (f32[4,2,806]{2,1,0:T(2,128)S(1)}, f32[4,2,806]{2,1,0:T(2,128)S(1)}, u32[]{:S(2)}, u32[]{:S(2)}) collective-permute-start(f32[4,2,806]{2,1,0:T(2,128)S(1)} %gain_solve.1.refs_3_), channel_id=1, source_target_pairs={{0,1},{1,0},{2,3},{3,2},{4,5},{5,4},{6,7},{7,6},{8,9},{9,8},{10,11... | collective-permute-start | bytes 77384 | tf_op jit(solution)/shard_map/ppermute | solution.py:349
  37.6 1.4 %collective-permute-done.14.refs_6_ = f32[4,2,806]{2,1,0:T(2,128)S(1)} collective-permute-done((f32[4,2,806]{2,1,0:T(2,128)S(1)}, f32[4,2,806]{2,1,0:T(2,128)S(1)}, u32[]{:S(2)}, u32[]{:S(2)}) %collective-permute-start.14) | collective-permute-done | bytes 25824 | tf_op jit(solution)/shard_map/ppermute | solution.py:349
  39.0 0.8 %collective-permute-done.13.refs_5_ = f32[4,2,806]{2,1,0:T(2,128)S(1)} collective-permute-done((f32[4,2,806]{2,1,0:T(2,128)S(1)}, f32[4,2,806]{2,1,0:T(2,128)S(1)}, u32[]{:S(2)}, u32[]{:S(2)}) %collective-permute-start.13) | collective-permute-done | bytes 25824 | tf_op jit(solution)/shard_map/ppermute | solution.py:349
  39.8 0.0 collective-permute-done.12.refs_4_
  39.8 4.9 %clean.1 = (bf16[2,2,4,192,703]{4,3,2,1,0:T(8,128)(2,1)}, f32[2,2,2,4,38]{4,3,2,1,0:T(4,128)}) custom-call(s32[1]{0:T(128)} %bitcast.refs_0_, bf16[2,2,4,192,703]{4,3,2,1,0:T(8,128)(2,1)S(1)} %get-tuple-element.11.refs_7_.refs_1_, f32[2,2,2,192,703]{4,3,2,1,0:T(8,128)S(1)} %get-tuple-element.12.refs_8_.refs_2_, f32[4,2,806]{2,1,0:T(2,128)S(1)} %gain_solve.1.refs_3_, ...), custom_call_target="tpu_custom_call" | custom-call | tf_op jit(solution)/shard_map/clean/pallas_call | solution.py:412
  (1 shorter events, 0.0 us)
Async XLA Ops:
  0.6 15.1 %copy-start.2 = (s32[32]{0:T(128)S(1)}, s32[32]{0:T(128)}, u32[]{:S(2)}) copy-start(s32[32]{0:T(128)} %param.8) | copy-start | bytes 388
  0.6 4.0 %collective-permute-start.2 = (s32[1,2,192]{2,1,0:T(2,128)}, s32[1,2,192]{2,1,0:T(2,128)S(1)}, u32[]{:S(2)}, u32[]{:S(2)}) collective-permute-start(s32[1,2,192]{2,1,0:T(2,128)} %bitcast.20), channel_id=1, source_target_pairs={{0,3},{1,2},{2,1},{3,0},{4,7},{5,6},{6,5},{7,4},{8,11},{9,10},{10,... | collective-permute-start | bytes 4616 | tf_op jit(solution)/shard_map/ppermute | solution.py:349
  3.1 3.8 %collective-permute-start.1 = (s32[1,2,192]{2,1,0:T(2,128)}, s32[1,2,192]{2,1,0:T(2,128)S(1)}, u32[]{:S(2)}, u32[]{:S(2)}) collective-permute-start(s32[1,2,192]{2,1,0:T(2,128)} %bitcast.21), channel_id=1, source_target_pairs={{0,2},{1,3},{2,0},{3,1},{4,6},{5,7},{6,4},{7,5},{8,10},{9,11},{10,... | collective-permute-start | bytes 4616 | tf_op jit(solution)/shard_map/ppermute | solution.py:349
  3.8 3.2 %collective-permute-start = (s32[1,2,192]{2,1,0:T(2,128)}, s32[1,2,192]{2,1,0:T(2,128)S(1)}, u32[]{:S(2)}, u32[]{:S(2)}) collective-permute-start(s32[1,2,192]{2,1,0:T(2,128)} %bitcast.22), channel_id=1, source_target_pairs={{0,1},{1,0},{2,3},{3,2},{4,5},{5,4},{6,7},{7,6},{8,9},{9,8},{10,11... | collective-permute-start | bytes 4616 | tf_op jit(solution)/shard_map/ppermute | solution.py:349
  7.6 7.5 %collective-permute-start.5 = (s32[4,2,192]{2,1,0:T(2,128)S(1)}, s32[4,2,192]{2,1,0:T(2,128)S(1)}, u32[]{:S(2)}, u32[]{:S(2)}) collective-permute-start(s32[4,2,192]{2,1,0:T(2,128)S(1)} %pad_add_fusion.refs_2_), channel_id=1, source_target_pairs={{0,12},{1,13},{2,14},{3,15},{4,8},{5,9},{6,10},{7,11},{8,4},{9,5},... | collective-permute-start | bytes 18440 | tf_op jit(solution)/shard_map/ppermute | solution.py:349
  11.2 4.5 %collective-permute-start.4 = (s32[4,2,192]{2,1,0:T(2,128)S(1)}, s32[4,2,192]{2,1,0:T(2,128)S(1)}, u32[]{:S(2)}, u32[]{:S(2)}) collective-permute-start(s32[4,2,192]{2,1,0:T(2,128)S(1)} %pad_add_fusion.refs_2_), channel_id=1, source_target_pairs={{0,8},{1,9},{2,10},{3,11},{4,12},{5,13},{6,14},{7,15},{8,0},{9,1},... | collective-permute-start | bytes 18440 | tf_op jit(solution)/shard_map/ppermute | solution.py:349
  11.2 4.5 %collective-permute-start.3 = (s32[4,2,192]{2,1,0:T(2,128)S(1)}, s32[4,2,192]{2,1,0:T(2,128)S(1)}, u32[]{:S(2)}, u32[]{:S(2)}) collective-permute-start(s32[4,2,192]{2,1,0:T(2,128)S(1)} %pad_add_fusion.refs_2_), channel_id=1, source_target_pairs={{0,4},{1,5},{2,6},{3,7},{4,0},{5,1},{6,2},{7,3},{8,12},{9,13},{10,... | collective-permute-start | bytes 18440 | tf_op jit(solution)/shard_map/ppermute | solution.py:349
  12.0 0.7 %copy-start = (f32[2,2,703]{2,1,0:T(2,128)S(1)}, f32[2,2,703]{2,1,0:T(2,128)}, u32[]{:S(2)}) copy-start(f32[2,2,703]{2,1,0:T(2,128)} %refs_6_.1) | copy-start | bytes 33748
  15.8 17.8 %copy-start.1 = (s32[2,2]{1,0:T(2,128)S(1)}, s32[2,2]{1,0:T(2,128)}, u32[]{:S(2)}) copy-start(s32[2,2]{1,0:T(2,128)} %refs_1_.3) | copy-start | bytes 52
  21.5 1.9 %collective-permute-start.6 = (f32[4,2,703]{2,1,0:T(2,128)S(1)}, f32[4,2,703]{2,1,0:T(2,128)S(1)}, u32[]{:S(2)}, u32[]{:S(2)}) collective-permute-start(f32[4,2,703]{2,1,0:T(2,128)S(1)} %get-tuple-element.15), channel_id=1, source_target_pairs={{0,1},{1,0},{2,3},{3,2},{4,5},{5,4},{6,7},{7,6},{8,9},{9,8},{10,11... | collective-permute-start | bytes 67496 | tf_op jit(solution)/shard_map/ppermute | solution.py:349
  21.5 4.1 %collective-permute-start.7 = (f32[4,2,703]{2,1,0:T(2,128)S(1)}, f32[4,2,703]{2,1,0:T(2,128)S(1)}, u32[]{:S(2)}, u32[]{:S(2)}) collective-permute-start(f32[4,2,703]{2,1,0:T(2,128)S(1)} %get-tuple-element.16), channel_id=1, source_target_pairs={{0,2},{1,3},{2,0},{3,1},{4,6},{5,7},{6,4},{7,5},{8,10},{9,11},{10,... | collective-permute-start | bytes 67496 | tf_op jit(solution)/shard_map/ppermute | solution.py:349
  22.2 3.5 %collective-permute-start.8 = (f32[4,2,703]{2,1,0:T(2,128)S(1)}, f32[4,2,703]{2,1,0:T(2,128)S(1)}, u32[]{:S(2)}, u32[]{:S(2)}) collective-permute-start(f32[4,2,703]{2,1,0:T(2,128)S(1)} %get-tuple-element.17), channel_id=1, source_target_pairs={{0,3},{1,2},{2,1},{3,0},{4,7},{5,6},{6,5},{7,4},{8,11},{9,10},{10,... | collective-permute-start | bytes 67496 | tf_op jit(solution)/shard_map/ppermute | solution.py:349
  25.8 6.0 %collective-permute-start.11 = (f32[4,2,703]{2,1,0:T(2,128)S(1)}, f32[4,2,703]{2,1,0:T(2,128)S(1)}, u32[]{:S(2)}, u32[]{:S(2)}) collective-permute-start(f32[4,2,703]{2,1,0:T(2,128)S(1)} %bitcast.10), channel_id=1, source_target_pairs={{0,12},{1,13},{2,14},{3,15},{4,8},{5,9},{6,10},{7,11},{8,4},{9,5},... | collective-permute-start | bytes 67496 | tf_op jit(solution)/shard_map/ppermute | solution.py:349
  28.8 4.7 %collective-permute-start.10 = (f32[4,2,703]{2,1,0:T(2,128)S(1)}, f32[4,2,703]{2,1,0:T(2,128)S(1)}, u32[]{:S(2)}, u32[]{:S(2)}) collective-permute-start(f32[4,2,703]{2,1,0:T(2,128)S(1)} %bitcast.11), channel_id=1, source_target_pairs={{0,8},{1,9},{2,10},{3,11},{4,12},{5,13},{6,14},{7,15},{8,0},{9,1},... | collective-permute-start | bytes 67496 | tf_op jit(solution)/shard_map/ppermute | solution.py:349
  28.8 4.7 %collective-permute-start.9 = (f32[4,2,703]{2,1,0:T(2,128)S(1)}, f32[4,2,703]{2,1,0:T(2,128)S(1)}, u32[]{:S(2)}, u32[]{:S(2)}) collective-permute-start(f32[4,2,703]{2,1,0:T(2,128)S(1)} %bitcast.12), channel_id=1, source_target_pairs={{0,4},{1,5},{2,6},{3,7},{4,0},{5,1},{6,2},{7,3},{8,12},{9,13},{10,... | collective-permute-start | bytes 67496 | tf_op jit(solution)/shard_map/ppermute | solution.py:349
  35.6 3.4 %collective-permute-start.14 = (f32[4,2,806]{2,1,0:T(2,128)S(1)}, f32[4,2,806]{2,1,0:T(2,128)S(1)}, u32[]{:S(2)}, u32[]{:S(2)}) collective-permute-start(f32[4,2,806]{2,1,0:T(2,128)S(1)} %gain_solve.1.refs_3_), channel_id=1, source_target_pairs={{0,3},{1,2},{2,1},{3,0},{4,7},{5,6},{6,5},{7,4},{8,11},{9,10},{10,... | collective-permute-start | bytes 77384 | tf_op jit(solution)/shard_map/ppermute | solution.py:349
  35.7 4.1 %collective-permute-start.13 = (f32[4,2,806]{2,1,0:T(2,128)S(1)}, f32[4,2,806]{2,1,0:T(2,128)S(1)}, u32[]{:S(2)}, u32[]{:S(2)}) collective-permute-start(f32[4,2,806]{2,1,0:T(2,128)S(1)} %gain_solve.1.refs_3_), channel_id=1, source_target_pairs={{0,2},{1,3},{2,0},{3,1},{4,6},{5,7},{6,4},{7,5},{8,10},{9,11},{10,... | collective-permute-start | bytes 77384 | tf_op jit(solution)/shard_map/ppermute | solution.py:349
  36.9 2.9 %collective-permute-start.12 = (f32[4,2,806]{2,1,0:T(2,128)S(1)}, f32[4,2,806]{2,1,0:T(2,128)S(1)}, u32[]{:S(2)}, u32[]{:S(2)}) collective-permute-start(f32[4,2,806]{2,1,0:T(2,128)S(1)} %gain_solve.1.refs_3_), channel_id=1, source_target_pairs={{0,1},{1,0},{2,3},{3,2},{4,5},{5,4},{6,7},{7,6},{8,9},{9,8},{10,11... | collective-permute-start | bytes 77384 | tf_op jit(solution)/shard_map/ppermute | solution.py:349

commit v5 on v4

--- a/solution.py
+++ b/solution.py
@@ -12,6 +12,7 @@
 STEPS_PER_TURN = 64
 GAINS_AT = 768
 CHUNK = 48
+GRANTS = (50, 42)
 ROWS = 40
 
 F32 = jnp.float32
@@ -89,43 +90,46 @@
         body(pl.ds(full * 128, pairs % 128), pairs % 128)
 
 
-def phase_kernel(width, me_ref, delay_ref, vis_hbm, vis_ref, wave_ref, mix_ref, sems):
+def phase_kernel(width, t, me_ref, delay_ref, *refs):
+    if t == 0:
+        flag_ref, wave_ref, mix_ref, own_ref = refs
+        own_ref[...] = flag_ref[...]
+    else:
+        vis_hbm, wave_ref, mix_ref, vis_ref, sem = refs
+        copy = pltpu.make_async_copy(vis_hbm, vis_ref, sem)
+        copy.start()
     anchor = me_ref[0].astype(F32) * float(width)
     pairs = delay_ref.shape[2]
-    copies = [pltpu.make_async_copy(vis_hbm.at[:, t], vis_ref.at[:, t], sems.at[t]) for t in range(2)]
-    for copy in copies:
-        copy.start()
-    for t in range(2):
-        def waves(lanes, count):
-            delays = [delay_ref[s, t:t + 1, lanes] for s in range(2)]
-            fine, coarse = phase_rows(delays, anchor, width)
-            for block in range(width // 16):
-                found = []
-                for s in range(2):
-                    halves = []
-                    for half in range(2):
-                        a, b = divmod(2 * block + half, 8)
-                        halves.append(times(tuple(part[b:b + 1] for part in coarse[s][a]), fine[s]))
-                    found.append([jnp.concatenate([h[ri] for h in halves], axis=0) for ri in range(2)])
-                rows = slice(block * 16, block * 16 + 16)
-                (r0, i0), (r1, i1) = found
-                for s in range(2):
-                    for ri in range(2):
-                        wave_ref[t, s, ri, rows, lanes] = found[s][ri]
-                for slot, value in enumerate((r1 * r0 + i1 * i0, i1 * r0 - r1 * i0)):
-                    high, low = split_two(value)
-                    mix_ref[t, slot, 0, rows, lanes] = high
-                    mix_ref[t, slot, 1, rows, lanes] = low
-
-        tiles(pairs, waves)
-    for copy in copies:
+    def waves(lanes, count):
+        delays = [delay_ref[s, t:t + 1, lanes] for s in range(2)]
+        fine, coarse = phase_rows(delays, anchor, width)
+        for block in range(width // 16):
+            found = []
+            for s in range(2):
+                halves = []
+                for half in range(2):
+                    a, b = divmod(2 * block + half, 8)
+                    halves.append(times(tuple(part[b:b + 1] for part in coarse[s][a]), fine[s]))
+                found.append([jnp.concatenate([h[ri] for h in halves], axis=0) for ri in range(2)])
+            rows = slice(block * 16, block * 16 + 16)
+            (r0, i0), (r1, i1) = found
+            for s in range(2):
+                for ri in range(2):
+                    wave_ref[s, ri, rows, lanes] = found[s][ri]
+            for slot, value in enumerate((r1 * r0 + i1 * i0, i1 * r0 - r1 * i0)):
+                high, low = split_two(value)
+                mix_ref[slot, 0, rows, lanes] = high
+                mix_ref[slot, 1, rows, lanes] = low
+
+    tiles(pairs, waves)
+    if t == 1:
         copy.wait()
 
 
 def sums_kernel(width, stages, me_ref, win_ref, *refs):
     flag_refs, refs = refs[:stages], refs[stages:]
-    delay_ref, vis_ref, wave_ref, mix_ref = refs[:4]
-    out_refs, (alpha_s, mexp_s, wt_s) = refs[4:8], refs[8:]
+    delay_ref, vis_ref, wave_refs, mix_refs = refs[0], refs[1], refs[2:4], refs[4:6]
+    out_ref, alpha_s, mexp_s, wt_s = refs[6:]
     me = me_ref[0]
     near = flag_refs[0].shape[0]
     groups = near * stages
@@ -174,7 +178,7 @@
         chosen = jnp.where(member_cw, own_c, 0.0)
         alpha_s[t] = jnp.broadcast_to(jnp.sum(chosen * scale_r, axis=1, keepdims=True), (width, 128))
         chosen = chosen.astype(BF16)
-        sums = [dot(rows, mix_ref[t, slot, 0]) + dot(rows, mix_ref[t, slot, 1]) for slot in range(2)]
+        sums = [dot(rows, mix_refs[t][slot, 0]) + dot(rows, mix_refs[t][slot, 1]) for slot in range(2)]
         gap = delay_ref[1, t:t + 1, :] - delay_ref[0, t:t + 1, :]
         phase = sincos_turns(gap * (apart * np.float32(width / STEPS_PER_TURN)))
         away = times(phase, tuple(value[windows:] for value in sums))
@@ -190,8 +194,8 @@
                 rows = pl.ds(pl.multiple_of(block * 16, 16), 16)
                 alpha = alpha_s[t, rows, :count]
                 mr, mi = mexp_s[t, 0, rows, lanes], mexp_s[t, 1, rows, lanes]
-                r0, i0 = wave_ref[t, 0, 0, rows, lanes], wave_ref[t, 0, 1, rows, lanes]
-                r1, i1 = wave_ref[t, 1, 0, rows, lanes], wave_ref[t, 1, 1, rows, lanes]
+                r0, i0 = wave_refs[t][0, 0, rows, lanes], wave_refs[t][0, 1, rows, lanes]
+                r1, i1 = wave_refs[t][1, 0, rows, lanes], wave_refs[t][1, 1, rows, lanes]
                 factors = []
                 for fr, fi in (
                     (alpha * r0 - (mr * r1 + mi * i1), (mr * i1 - mi * r1) - alpha * i0),
@@ -212,17 +216,10 @@
             zero = jnp.zeros((8, count), F32)
             sums = lax.fori_loop(0, width // 16, step, (zero,) * 24, unroll=4)
             for s in range(2):
-                owner = lax.bitwise_xor(lax.bitwise_and(me, 3), t + 2 * s)
-                found = []
                 for k in range(4):
                     one, two, three = sums[(k * 2 + s) * 3:(k * 2 + s) * 3 + 3]
-                    found.append([jnp.sum(value, axis=0, keepdims=True) for value in (one - three, one + two)])
-                for d in range(4):
-                    @pl.when(owner == d)
-                    def write():
-                        for k in range(4):
-                            for ri in range(2):
-                                out_refs[d][k, ri:ri + 1, lanes] = found[k][ri]
+                    for ri, value in enumerate((one - three, one + two)):
+                        out_ref[t + 2 * s, k, ri:ri + 1, lanes] = jnp.sum(value, axis=0, keepdims=True)
 
         tiles(pairs, main)
 
@@ -240,7 +237,7 @@
 def solve_kernel(window_count, me_ref, tracks_ref, *refs):
     parts, gain_ref = refs[:-1], refs[-1]
     me = me_ref[0]
-    systems = gain_ref.shape[0]
+    systems = gain_ref.shape[1]
     total = [part[...] for part in parts]
     while len(total) > 1:
         total = [total[i] + total[i + 1] for i in range(0, len(total), 2)]
@@ -289,59 +286,59 @@
     pairs = hot.shape[1]
     for system in range(systems):
         (lr, li), (rr, ri_) = [[end[2 * system + ri:2 * system + ri + 1] for ri in range(2)] for end in ends]
-        gain_ref[system, 0:1, :pairs] = lr * rr + li * ri_
-        gain_ref[system, 1:2, :pairs] = li * rr - lr * ri_
-        gain_ref[system, :, GAINS_AT:] = gains[2 * system:2 * system + 2, :STATIONS]
-
-
-def clean_kernel(width, me_ref, vis_ref, wave_ref, *refs):
-    piece_refs, (out_hbm, gain_out_ref, out_s, model_s, sems) = refs[:4], refs[4:]
-    pairs = wave_ref.shape[4]
-    mine = lax.bitwise_and(me_ref[0], 3)
-    for d, piece in enumerate(piece_refs):
-        owner = lax.bitwise_xor(mine, d)
-        t, s = lax.bitwise_and(owner, 1), lax.div(owner, 2)
+        for copy in range(4):
+            gain_ref[copy, system, 0:1, :pairs] = lr * rr + li * ri_
+            gain_ref[copy, system, 1:2, :pairs] = li * rr - lr * ri_
+            gain_ref[copy, system, :, GAINS_AT:] = gains[2 * system:2 * system + 2, :STATIONS]
+
+
+def clean_kernel(width, *refs):
+    vis_ref, wave_refs = refs[0], refs[1:3]
+    piece_ref, out_hbm, gain_out_ref, out_s, model_s, sems = refs[3:]
+    pairs = wave_refs[0].shape[3]
+    for owner in range(4):
+        t, s = owner % 2, owner // 2
         for k in range(4):
             for ri in range(2):
-                gain_out_ref[ri, s, t, k:k + 1, :] = piece[k, ri:ri + 1, GAINS_AT:]
-            re, im = piece[k, 0:1, :pairs], piece[k, 1:2, :pairs]
+                gain_out_ref[ri, s, t, k:k + 1, :] = piece_ref[owner, k, ri:ri + 1, GAINS_AT:]
+            re, im = piece_ref[owner, k, 0:1, :pairs], piece_ref[owner, k, 1:2, :pairs]
             for slot, value in enumerate((re, im - re, re + im)):
                 model_s[owner, 3 * k + slot:3 * k + slot + 1, :] = value
 
     chunks = width // CHUNK
 
-    def copy_out(index):
-        t, rows = lax.div(index, chunks), pl.ds(pl.multiple_of(lax.rem(index, chunks) * CHUNK, CHUNK), CHUNK)
-        return pltpu.make_async_copy(out_s.at[:, t, :, rows], out_hbm.at[:, t, :, rows], sems.at[index])
-
-    def chunk(index, carry):
-        t, base = lax.div(index, chunks), lax.rem(index, chunks) * CHUNK
-
-        def main(lanes, count):
-            for block in range(CHUNK // 16):
-                rows = pl.ds(pl.multiple_of(base + block * 16, 16), 16)
-                waves = []
-                for s in range(2):
-                    re, im = wave_ref[t, s, 0, rows, lanes], wave_ref[t, s, 1, rows, lanes]
-                    waves.append((re + im, re, im))
-                for k in range(4):
-                    sums = []
-                    for slot in range(3):
-                        one, two = (waves[s][slot] * model_s[t + 2 * s, 3 * k + slot:3 * k + slot + 1, lanes]
-                                    for s in range(2))
-                        sums.append(one + two)
-                    vr = vis_ref[0, t, k, rows, lanes].astype(F32)
-                    vi = vis_ref[1, t, k, rows, lanes].astype(F32)
-                    out_s[0, t, k, rows, lanes] = (vr - (sums[0] - sums[2])).astype(BF16)
-                    out_s[1, t, k, rows, lanes] = (vi - (sums[0] + sums[1])).astype(BF16)
-
-        tiles(pairs, main)
-        copy_out(index).start()
-        return carry
-
-    lax.fori_loop(0, 2 * chunks, chunk, 0)
-    for index in range(2 * chunks):
-        copy_out(index).wait()
+    def copy_out(t, index):
+        rows = pl.ds(pl.multiple_of(index * CHUNK, CHUNK), CHUNK)
+        return pltpu.make_async_copy(out_s.at[:, t, :, rows], out_hbm.at[:, t, :, rows], sems.at[t, index])
+
+    for t in range(2):
+        def chunk(index, carry):
+            def main(lanes, count):
+                for block in range(CHUNK // 16):
+                    rows = pl.ds(pl.multiple_of(index * CHUNK + block * 16, 16), 16)
+                    waves = []
+                    for s in range(2):
+                        re, im = (wave_refs[t][s, ri, rows, lanes] for ri in range(2))
+                        waves.append((re + im, re, im))
+                    for k in range(4):
+                        sums = []
+                        for slot in range(3):
+                            one, two = (waves[s][slot] * model_s[t + 2 * s, 3 * k + slot:3 * k + slot + 1, lanes]
+                                        for s in range(2))
+                            sums.append(one + two)
+                        vr = vis_ref[0, t, k, rows, lanes].astype(F32)
+                        vi = vis_ref[1, t, k, rows, lanes].astype(F32)
+                        out_s[0, t, k, rows, lanes] = (vr - (sums[0] - sums[2])).astype(BF16)
+                        out_s[1, t, k, rows, lanes] = (vi - (sums[0] + sums[1])).astype(BF16)
+
+            tiles(pairs, main)
+            copy_out(t, index).start()
+            return carry
+
+        lax.fori_loop(0, chunks, chunk, 0)
+    for t in range(2):
+        for index in range(chunks):
+            copy_out(t, index).wait()
 
 
 def partner(value, bits):
@@ -360,40 +357,60 @@
     window_count = windows.shape[0]
     turned = jnp.transpose(visibilities, (0, 1, 2, 4, 3))
     me = lax.axis_index("sub").astype(jnp.int32).reshape(1)
-    gathered = [flags[None]]
-    stride = 1
-    while stride < count:
-        gathered = [jnp.concatenate(gathered, axis=0)] if len(gathered) > 1 else gathered
-        gathered += [partner(gathered[0], stride * d) for d in range(1, min(4, count // stride))]
-        stride *= 4
+    fours = [[base + d for d in range(4)] for base in range(0, count, 4)]
     vmem_ref = pl.BlockSpec(memory_space=pltpu.VMEM)
     hbm_ref = pl.BlockSpec(memory_space=pltpu.HBM)
     vmem = lambda *shape: pltpu.VMEM(shape, F32)
     params = pltpu.CompilerParams(vmem_limit_bytes=24 * 2 ** 20)
-    held, waves, mixing = pl.pallas_call(
-        lambda *refs: phase_kernel(width, *refs),
-        in_specs=[smem(), vmem_ref, hbm_ref],
-        out_specs=[vmem_ref] * 3,
-        out_shape=[
-            jax.ShapeDtypeStruct(turned.shape, BF16),
-            jax.ShapeDtypeStruct((2, 2, 2, width, pairs), F32),
-            jax.ShapeDtypeStruct((2, 2, 2, width, pairs), BF16),
-        ],
-        scratch_shapes=[pltpu.SemaphoreType.DMA((2,))],
-        compiler_params=pltpu.CompilerParams(vmem_limit_bytes=40 * 2 ** 20),
-        cost_estimate=pl.CostEstimate(flops=2 * 10 ** 7, bytes_accessed=12 * 2 ** 20, transcendentals=0),
-        name="phases",
-    )(me, delays, turned)
-    quarters = pl.pallas_call(
+    waves, mixing = [], []
+    own = flags[None]
+    gathered = [own]
+    stride = 1
+    for t, grant in enumerate(GRANTS):
+        if stride < count:
+            got = [partner(gathered[0], stride * d) for d in range(1, min(4, count // stride))]
+        made = pl.pallas_call(
+            lambda *refs: phase_kernel(width, t, *refs),
+            in_specs=[smem(), vmem_ref, hbm_ref if t else vmem_ref],
+            out_specs=[vmem_ref] * 3,
+            out_shape=[
+                jax.ShapeDtypeStruct((2, 2, width, pairs), F32),
+                jax.ShapeDtypeStruct((2, 2, width, pairs), BF16),
+                jax.ShapeDtypeStruct(turned.shape, BF16) if t else jax.ShapeDtypeStruct(own.shape, own.dtype),
+            ],
+            scratch_shapes=[pltpu.SemaphoreType.DMA] * t,
+            compiler_params=pltpu.CompilerParams(vmem_limit_bytes=grant * 2 ** 20),
+            cost_estimate=pl.CostEstimate(flops=10 ** 7, bytes_accessed=6 * 2 ** 20, transcendentals=0),
+            name="phases",
+        )(me, delays, turned if t else own)
+        waves.append(made[0])
+        mixing.append(made[1])
+        if t == 0:
+            own = made[2]
+        else:
+            held = made[2]
+        if stride < count:
+            gathered = [own if t == 0 else gathered[0]] + got
+            stride *= 4
+            if stride < count:
+                gathered = [jnp.concatenate(gathered, axis=0)]
+    while stride < count:
+        got = [partner(gathered[0], stride * d) for d in range(1, min(4, count // stride))]
+        gathered = gathered + got
+        stride *= 4
+        if stride < count:
+            gathered = [jnp.concatenate(gathered, axis=0)]
+    shares = pl.pallas_call(
         lambda *refs: sums_kernel(width, len(gathered), *refs),
-        in_specs=[smem()] + [vmem_ref] * (len(gathered) + 5),
-        out_specs=[vmem_ref] * 4,
-        out_shape=[jax.ShapeDtypeStruct((4, 2, pairs), F32)] * 4,
+        in_specs=[smem()] + [vmem_ref] * (len(gathered) + 7),
+        out_specs=vmem_ref,
+        out_shape=jax.ShapeDtypeStruct((4, 4, 2, pairs), F32),
         scratch_shapes=[vmem(2, width, 128), vmem(2, 2, width, pairs), vmem(2, count, width)],
         compiler_params=params,
         name="window_sums",
-    )(me, windows.reshape(1, window_count), *gathered, delays, held, waves, mixing)
-    pieces = [quarters[0]] + [partner(quarters[d], d) for d in range(1, 4)]
+    )(me, windows.reshape(1, window_count), *gathered, delays, held, *waves, *mixing)
+    shares = lax.all_to_all(shares, "sub", 0, 0, axis_index_groups=fours)
+    pieces = [shares[d] for d in range(4)]
     stride = 4
     while stride < count:
         while len(pieces) > 1:
@@ -404,14 +421,14 @@
         lambda *refs: solve_kernel(float(window_count), *refs),
         in_specs=[smem(), smem()] + [vmem_ref] * len(pieces),
         out_specs=vmem_ref,
-        out_shape=jax.ShapeDtypeStruct((4, 2, GAINS_AT + STATIONS), F32),
+        out_shape=jax.ShapeDtypeStruct((4, 4, 2, GAINS_AT + STATIONS), F32),
         compiler_params=params,
         name="gain_solve",
     )(me, tracks, *pieces)
-    model = [model] + [partner(model, d) for d in range(1, 4)]
+    model = lax.all_to_all(model, "sub", 0, 0, axis_index_groups=fours)
     cleaned, gains = pl.pallas_call(
         lambda *refs: clean_kernel(width, *refs),
-        in_specs=[smem()] + [vmem_ref] * 6,
+        in_specs=[vmem_ref] * 4,
         out_specs=[hbm_ref, vmem_ref],
         out_shape=[
             jax.ShapeDtypeStruct(turned.shape, BF16),
@@ -420,11 +437,11 @@
         scratch_shapes=[
             pltpu.VMEM(turned.shape, BF16),
             vmem(4, 16, pairs),
-            pltpu.SemaphoreType.DMA((2 * (width // CHUNK),)),
+            pltpu.SemaphoreType.DMA((2, width // CHUNK)),
         ],
         compiler_params=params,
         name="clean",
-    )(me, held, waves, *model)
+    )(held, *waves, model)
     return jnp.transpose(cleaned, (0, 1, 2, 4, 3)), gains
 
 

time: 44.9 us -> 48.2 us (1.073)
  blocking collectives: 0 us -> 13.5 us
  waiting for transfers between devices: 11.7 us -> 4.87 us
  starting transfers between devices: 15.8 us -> 12 us
  local copies, waits for them, and re-layouts: 0.71 us -> 1.42 us
  other arithmetic: 0.7 us -> 0.02 us
    all_to_all x0 -> x2, blocking collectives: none -> 13.5 us  [the longest x1 6.84 us: local(): model = lax.all_to_all(model, 'sub', 0, 0, axis_index_groups=fours)]
    ppermute x15 -> x9, waiting for transfers between devices: 11.7 us -> 4.87 us  [partner(): return lax.ppermute(value, 'sub', [(i, i ^ bits) for i in range(count)])]
    ppermute x15 -> x9, starting transfers between devices: 15.8 us -> 12 us  [partner(): return lax.ppermute(value, 'sub', [(i, i ^ bits) for i in range(count)])]
    pallas_call x2 -> x3, Pallas kernels: 7.28 us -> 7.99 us  [the longest x1 4.8 us: local(): pl.pallas_call(lambda *refs: clean_kernel(width, *refs), in_specs=[vmem_r...]
    unnamed x6 -> x11, local copies, waits for them, and re-layouts: 0.71 us -> 1.41 us
    concatenate x1 -> x0, other arithmetic: 0.69 us -> none  [local(): jnp.concatenate(gathered, axis=0)]
  transfers between devices with their start and end apart: 15 -> 9, of which waited for: 9 -> 4; matrix products, arithmetic and copies ran while one was open for 0% -> 0% of each run, Pallas kernels for 5% -> 7%
where the time goes in v5:
time: 48.2 us; the launch traced here: 47.9 us
  Pallas kernels  15.3 us (32%)
  blocking collectives  13.5 us (28%)
  starting transfers between devices  12 us (25%)
  waiting for transfers between devices  4.87 us (10%)
  local copies, waits for them, and re-layouts  1.42 us (3%)
  between operations  0.7 us (1%)
    ppermute x9, starting transfers between devices, partner(): return lax.ppermute(value, 'sub', [(i, i ^ bits) for i in range(count)])  12 us
    all_to_all x1, blocking collectives, local(): model = lax.all_to_all(model, 'sub', 0, 0, axis_index_groups=fours)  6.84 us
    all_to_all x1, blocking collectives, local(): shares = lax.all_to_all(shares, 'sub', 0, 0, axis_index_groups=fours)  6.67 us
    pallas_call x1, Pallas kernels, local(): pl.pallas_call(lambda *refs: sums_kernel(width, len(gathered), *refs), in...  5.25 us
    ppermute x9, waiting for transfers between devices, partner(): return lax.ppermute(value, 'sub', [(i, i ^ bits) for i in range(count)])  4.87 us
    pallas_call x1, Pallas kernels, local(): pl.pallas_call(lambda *refs: clean_kernel(width, *refs), in_specs=[vmem_r...  4.8 us
    pallas_call x2, Pallas kernels, local(): pl.pallas_call(lambda *refs: phase_kernel(width, t, *refs), in_specs=[sme...  3.2 us
    pallas_call x1, Pallas kernels, local(): pl.pallas_call(lambda *refs: solve_kernel(float(window_count), *refs), in...  2.09 us
  transfers between devices with their start and end apart: 9, of which 4 were waited for; matrix products, arithmetic and copies ran while one was open for 0% of the time, Pallas kernels for 7%

profile of v5, /device:TPU:0, one launch (start us, length us, event | category | flops | bytes accessed | tf_op | source)
XLA Modules:
  0.0 47.9 jit_solution(2607939990837703691)
XLA Ops:
  0.6 2.5 %collective-permute-start.2 = (s32[1,2,192]{2,1,0:T(2,128)}, s32[1,2,192]{2,1,0:T(2,128)S(1)}, u32[]{:S(2)}, u32[]{:S(2)}) collective-permute-start(s32[1,2,192]{2,1,0:T(2,128)} %bitcast.8), channel_id=1, source_target_pairs={{0,3},{1,2},{2,1},{3,0},{4,7},{5,6},{6,5},{7,4},{8,11},{9,10},{10,... | collective-permute-start | bytes 4616 | tf_op jit(solution)/shard_map/ppermute | solution.py:346
  3.1 0.6 %collective-permute-start.1 = (s32[1,2,192]{2,1,0:T(2,128)}, s32[1,2,192]{2,1,0:T(2,128)S(1)}, u32[]{:S(2)}, u32[]{:S(2)}) collective-permute-start(s32[1,2,192]{2,1,0:T(2,128)} %bitcast.9), channel_id=1, source_target_pairs={{0,2},{1,3},{2,0},{3,1},{4,6},{5,7},{6,4},{7,5},{8,10},{9,11},{10,... | collective-permute-start | bytes 4616 | tf_op jit(solution)/shard_map/ppermute | solution.py:346
  3.7 0.0 collective-permute-start
  3.8 0.0 copy-start
  3.8 0.7 %copy-done = f32[2,2,703]{2,1,0:T(2,128)S(1)} copy-done((f32[2,2,703]{2,1,0:T(2,128)S(1)}, f32[2,2,703]{2,1,0:T(2,128)}, u32[]{:S(2)}) %copy-start) | copy-done | bytes 11272
  4.5 0.0 copy-start.3
  4.5 0.7 %copy-done.3 = s32[2,192]{1,0:T(2,128)S(1)} copy-done((s32[2,192]{1,0:T(2,128)S(1)}, s32[2,192]{1,0:T(2,128)}, u32[]{:S(2)}) %copy-start.3) | copy-done | bytes 1560
  5.2 0.8 %phases.3 = (f32[2,2,192,703]{3,2,1,0:T(8,128)S(1)}, bf16[2,2,192,703]{3,2,1,0:T(8,128)(2,1)S(1)}, s32[1,2,192]{2,1,0:T(2,128)S(1)}) custom-call(s32[1]{0:T(128)} %bitcast.refs_0_, f32[2,2,703]{2,1,0:T(2,128)S(1)} %copy-done, s32[1,2,192]{2,1,0:T(2,128)S(1)} %bitcast.11), custom_call_target="tpu_custom_call" | custom-call | flops 10000000 | bytes 6291456 | tf_op jit(solution)/shard_map/phases/pallas_call | solution.py:372
  6.0 0.0 collective-permute-done
  6.0 0.9 %collective-permute-done.1 = s32[1,2,192]{2,1,0:T(2,128)S(1)} collective-permute-done((s32[1,2,192]{2,1,0:T(2,128)}, s32[1,2,192]{2,1,0:T(2,128)S(1)}, u32[]{:S(2)}, u32[]{:S(2)}) %collective-permute-start.1) | collective-permute-done | bytes 1568 | tf_op jit(solution)/shard_map/ppermute | solution.py:346
  6.9 0.0 collective-permute-done.2
  6.9 3.7 %collective-permute-start.5 = (s32[4,2,192]{2,1,0:T(2,128)S(1)}, s32[4,2,192]{2,1,0:T(2,128)S(1)}, u32[]{:S(2)}, u32[]{:S(2)}) collective-permute-start(s32[4,2,192]{2,1,0:T(2,128)S(1)} %constant_dynamic-update-slice_fusion.refs_2_), channel_id=1, source_target_pairs={{0,12},{1,13},{2,14},{3,15},{4,8},{5,9},{6,10},{7,11},{8,4},{9,5},... | collective-permute-start | bytes 18440 | tf_op jit(solution)/shard_map/ppermute | solution.py:346
  10.6 0.0 collective-permute-start.4
  10.6 0.8 %collective-permute-start.3 = (s32[4,2,192]{2,1,0:T(2,128)S(1)}, s32[4,2,192]{2,1,0:T(2,128)S(1)}, u32[]{:S(2)}, u32[]{:S(2)}) collective-permute-start(s32[4,2,192]{2,1,0:T(2,128)S(1)} %constant_dynamic-update-slice_fusion.refs_2_), channel_id=1, source_target_pairs={{0,4},{1,5},{2,6},{3,7},{4,0},{5,1},{6,2},{7,3},{8,12},{9,13},{10,... | collective-permute-start | bytes 18440 | tf_op jit(solution)/shard_map/ppermute | solution.py:346
  11.4 0.0 copy-start.2
  11.4 2.4 %phases.2 = (f32[2,2,192,703]{3,2,1,0:T(8,128)S(1)}, bf16[2,2,192,703]{3,2,1,0:T(8,128)(2,1)S(1)}, bf16[2,2,4,192,703]{4,3,2,1,0:T(8,128)(2,1)S(1)}) custom-call(s32[1]{0:T(128)} %bitcast.refs_0_, f32[2,2,703]{2,1,0:T(2,128)S(1)} %copy-done, bf16[2,2,4,192,703]{4,3,2,1,0:T(8,128)(2,1)} %bitcast.12), custom_call_target="tpu_custom_call" | custom-call | flops 10000000 | bytes 6291456 | tf_op jit(solution)/shard_map/phases/pallas_call | solution.py:372
  13.7 0.0 collective-permute-done.5.refs_5_
  13.7 1.4 %collective-permute-done.4.refs_4_ = s32[4,2,192]{2,1,0:T(2,128)S(1)} collective-permute-done((s32[4,2,192]{2,1,0:T(2,128)S(1)}, s32[4,2,192]{2,1,0:T(2,128)S(1)}, u32[]{:S(2)}, u32[]{:S(2)}) %collective-permute-start.4) | collective-permute-done | bytes 6176 | tf_op jit(solution)/shard_map/ppermute | solution.py:346
  15.1 0.0 collective-permute-done.3.refs_3_
  15.1 0.0 copy-done.2
  15.1 0.0 copy-start.1
  15.1 5.3 %window_sums.1 = f32[4,4,2,703]{3,2,1,0:T(2,128)S(1)} custom-call(s32[1]{0:T(128)} %bitcast.refs_0_, s32[1,32]{1,0:T(1,128)S(1)} %bitcast.7, s32[4,2,192]{2,1,0:T(2,128)S(1)} %constant_dynamic-update-slice_fusion.refs_2_, s32[4,2,192]{2,1,0:T(2,128)S(1)} %collective-permute-done.3.refs_3_, s32[4,2,192]{2,1,0:T(2,128)S(1)} %collective-permute-done.4.refs_4_, ...), custom_call_target="tpu_custom_call" | custom-call | tf_op jit(solution)/shard_map/window_sums/pallas_call | solution.py:403
  20.4 6.7 %all_to_all.10 = f32[4,4,2,703]{3,2,1,0:T(2,128)S(1)} all-to-all(f32[4,4,2,703]{3,2,1,0:T(2,128)S(1)} %window_sums.1), channel_id=1, replica_groups={{0,1,2,3},{4,5,6,7},{8,9,10,11},{12,13,14,15},{16,17,18,19},{20,21,22,2..., dimensions={0} | all-to-all | bytes 179968 | tf_op jit(solution)/shard_map/all_to_all | solution.py:412
  27.1 2.3 %collective-permute-start.8 = (f32[4,2,703]{2,1,0:T(2,128)S(1)}, f32[4,2,703]{2,1,0:T(2,128)S(1)}, u32[]{:S(2)}, u32[]{:S(2)}) collective-permute-start(f32[4,2,703]{2,1,0:T(2,128)S(1)} %fusion.1.refs_2_), channel_id=1, source_target_pairs={{0,12},{1,13},{2,14},{3,15},{4,8},{5,9},{6,10},{7,11},{8,4},{9,5},... | collective-permute-start | bytes 67496 | tf_op jit(solution)/shard_map/ppermute | solution.py:346
  29.4 0.0 collective-permute-start.7
  29.4 2.1 %collective-permute-start.6 = (f32[4,2,703]{2,1,0:T(2,128)S(1)}, f32[4,2,703]{2,1,0:T(2,128)S(1)}, u32[]{:S(2)}, u32[]{:S(2)}) collective-permute-start(f32[4,2,703]{2,1,0:T(2,128)S(1)} %fusion.1.refs_2_), channel_id=1, source_target_pairs={{0,4},{1,5},{2,6},{3,7},{4,0},{5,1},{6,2},{7,3},{8,12},{9,13},{10,... | collective-permute-start | bytes 67496 | tf_op jit(solution)/shard_map/ppermute | solution.py:346
  31.6 1.2 %collective-permute-done.8.refs_5_ = f32[4,2,703]{2,1,0:T(2,128)S(1)} collective-permute-done((f32[4,2,703]{2,1,0:T(2,128)S(1)}, f32[4,2,703]{2,1,0:T(2,128)S(1)}, u32[]{:S(2)}, u32[]{:S(2)}) %collective-permute-start.8) | collective-permute-done | bytes 22528 | tf_op jit(solution)/shard_map/ppermute | solution.py:346
  32.8 1.4 %collective-permute-done.7.refs_4_ = f32[4,2,703]{2,1,0:T(2,128)S(1)} collective-permute-done((f32[4,2,703]{2,1,0:T(2,128)S(1)}, f32[4,2,703]{2,1,0:T(2,128)S(1)}, u32[]{:S(2)}, u32[]{:S(2)}) %collective-permute-start.7) | collective-permute-done | bytes 22528 | tf_op jit(solution)/shard_map/ppermute | solution.py:346
  34.2 0.0 collective-permute-done.6.refs_3_
  34.2 0.0 copy-done.1
  34.2 2.1 %gain_solve.1 = f32[4,4,2,806]{3,2,1,0:T(2,128)S(1)} custom-call(s32[1]{0:T(128)} %bitcast.refs_0_, s32[2,2]{1,0:T(2,128)S(1)} %copy-done.1, f32[4,2,703]{2,1,0:T(2,128)S(1)} %fusion.1.refs_2_, f32[4,2,703]{2,1,0:T(2,128)S(1)} %collective-permute-done.6.refs_3_, f32[4,2,703]{2,1,0:T(2,128)S(1)} %collective-permute-done.7.refs_4_, ...), custom_call_target="tpu_custom_call" | custom-call | tf_op jit(solution)/shard_map/gain_solve/pallas_call | solution.py:420
  36.3 6.8 %all_to_all.11.refs_3_ = f32[4,4,2,806]{3,2,1,0:T(2,128)S(1)} all-to-all(f32[4,4,2,806]{3,2,1,0:T(2,128)S(1)} %gain_solve.1), channel_id=1, replica_groups={{0,1,2,3},{4,5,6,7},{8,9,10,11},{12,13,14,15},{16,17,18,19},{20,21,22,2..., dimensions={0} | all-to-all | bytes 206336 | tf_op jit(solution)/shard_map/all_to_all | solution.py:428
  43.1 4.8 %clean.1 = (bf16[2,2,4,192,703]{4,3,2,1,0:T(8,128)(2,1)}, f32[2,2,2,4,38]{4,3,2,1,0:T(4,128)}) custom-call(bf16[2,2,4,192,703]{4,3,2,1,0:T(8,128)(2,1)S(1)} %get-tuple-element.10.refs_7_.refs_0_, f32[2,2,192,703]{3,2,1,0:T(8,128)S(1)} %get-tuple-element.11.refs_8_.refs_1_, f32[2,2,192,703]{3,2,1,0:T(8,128)S(1)} %get-tuple-element.12.refs_9_.refs_2_, ...), custom_call_target="tpu_custom_call" | custom-call | tf_op jit(solution)/shard_map/clean/pallas_call | solution.py:429
  (5 shorter events, 0.1 us)
Async XLA Ops:
  0.6 6.3 %collective-permute-start.2 = (s32[1,2,192]{2,1,0:T(2,128)}, s32[1,2,192]{2,1,0:T(2,128)S(1)}, u32[]{:S(2)}, u32[]{:S(2)}) collective-permute-start(s32[1,2,192]{2,1,0:T(2,128)} %bitcast.8), channel_id=1, source_target_pairs={{0,3},{1,2},{2,1},{3,0},{4,7},{5,6},{6,5},{7,4},{8,11},{9,10},{10,... | collective-permute-start | bytes 4616 | tf_op jit(solution)/shard_map/ppermute | solution.py:346
  3.1 3.8 %collective-permute-start.1 = (s32[1,2,192]{2,1,0:T(2,128)}, s32[1,2,192]{2,1,0:T(2,128)S(1)}, u32[]{:S(2)}, u32[]{:S(2)}) collective-permute-start(s32[1,2,192]{2,1,0:T(2,128)} %bitcast.9), channel_id=1, source_target_pairs={{0,2},{1,3},{2,0},{3,1},{4,6},{5,7},{6,4},{7,5},{8,10},{9,11},{10,... | collective-permute-start | bytes 4616 | tf_op jit(solution)/shard_map/ppermute | solution.py:346
  3.7 2.3 %collective-permute-start = (s32[1,2,192]{2,1,0:T(2,128)}, s32[1,2,192]{2,1,0:T(2,128)S(1)}, u32[]{:S(2)}, u32[]{:S(2)}) collective-permute-start(s32[1,2,192]{2,1,0:T(2,128)} %bitcast.10), channel_id=1, source_target_pairs={{0,1},{1,0},{2,3},{3,2},{4,5},{5,4},{6,7},{7,6},{8,9},{9,8},{10,11... | collective-permute-start | bytes 4616 | tf_op jit(solution)/shard_map/ppermute | solution.py:346
  3.8 0.7 %copy-start = (f32[2,2,703]{2,1,0:T(2,128)S(1)}, f32[2,2,703]{2,1,0:T(2,128)}, u32[]{:S(2)}) copy-start(f32[2,2,703]{2,1,0:T(2,128)} %refs_6_.1) | copy-start | bytes 33748
  4.5 0.7 %copy-start.3 = (s32[2,192]{1,0:T(2,128)S(1)}, s32[2,192]{1,0:T(2,128)}, u32[]{:S(2)}) copy-start(s32[2,192]{1,0:T(2,128)} %param.7) | copy-start | bytes 4612
  6.9 6.8 %collective-permute-start.5 = (s32[4,2,192]{2,1,0:T(2,128)S(1)}, s32[4,2,192]{2,1,0:T(2,128)S(1)}, u32[]{:S(2)}, u32[]{:S(2)}) collective-permute-start(s32[4,2,192]{2,1,0:T(2,128)S(1)} %constant_dynamic-update-slice_fusion.refs_2_), channel_id=1, source_target_pairs={{0,12},{1,13},{2,14},{3,15},{4,8},{5,9},{6,10},{7,11},{8,4},{9,5},... | collective-permute-start | bytes 18440 | tf_op jit(solution)/shard_map/ppermute | solution.py:346
  10.6 4.5 %collective-permute-start.4 = (s32[4,2,192]{2,1,0:T(2,128)S(1)}, s32[4,2,192]{2,1,0:T(2,128)S(1)}, u32[]{:S(2)}, u32[]{:S(2)}) collective-permute-start(s32[4,2,192]{2,1,0:T(2,128)S(1)} %constant_dynamic-update-slice_fusion.refs_2_), channel_id=1, source_target_pairs={{0,8},{1,9},{2,10},{3,11},{4,12},{5,13},{6,14},{7,15},{8,0},{9,1},... | collective-permute-start | bytes 18440 | tf_op jit(solution)/shard_map/ppermute | solution.py:346
  10.6 4.5 %collective-permute-start.3 = (s32[4,2,192]{2,1,0:T(2,128)S(1)}, s32[4,2,192]{2,1,0:T(2,128)S(1)}, u32[]{:S(2)}, u32[]{:S(2)}) collective-permute-start(s32[4,2,192]{2,1,0:T(2,128)S(1)} %constant_dynamic-update-slice_fusion.refs_2_), channel_id=1, source_target_pairs={{0,4},{1,5},{2,6},{3,7},{4,0},{5,1},{6,2},{7,3},{8,12},{9,13},{10,... | collective-permute-start | bytes 18440 | tf_op jit(solution)/shard_map/ppermute | solution.py:346
  11.4 3.8 %copy-start.2 = (s32[32]{0:T(128)S(1)}, s32[32]{0:T(128)}, u32[]{:S(2)}) copy-start(s32[32]{0:T(128)} %param.8) | copy-start | bytes 388
  15.1 19.0 %copy-start.1 = (s32[2,2]{1,0:T(2,128)S(1)}, s32[2,2]{1,0:T(2,128)}, u32[]{:S(2)}) copy-start(s32[2,2]{1,0:T(2,128)} %refs_1_.5) | copy-start | bytes 52
  27.1 5.7 %collective-permute-start.8 = (f32[4,2,703]{2,1,0:T(2,128)S(1)}, f32[4,2,703]{2,1,0:T(2,128)S(1)}, u32[]{:S(2)}, u32[]{:S(2)}) collective-permute-start(f32[4,2,703]{2,1,0:T(2,128)S(1)} %fusion.1.refs_2_), channel_id=1, source_target_pairs={{0,12},{1,13},{2,14},{3,15},{4,8},{5,9},{6,10},{7,11},{8,4},{9,5},... | collective-permute-start | bytes 67496 | tf_op jit(solution)/shard_map/ppermute | solution.py:346
  29.4 4.8 %collective-permute-start.7 = (f32[4,2,703]{2,1,0:T(2,128)S(1)}, f32[4,2,703]{2,1,0:T(2,128)S(1)}, u32[]{:S(2)}, u32[]{:S(2)}) collective-permute-start(f32[4,2,703]{2,1,0:T(2,128)S(1)} %fusion.1.refs_2_), channel_id=1, source_target_pairs={{0,8},{1,9},{2,10},{3,11},{4,12},{5,13},{6,14},{7,15},{8,0},{9,1},... | collective-permute-start | bytes 67496 | tf_op jit(solution)/shard_map/ppermute | solution.py:346
  29.4 4.8 %collective-permute-start.6 = (f32[4,2,703]{2,1,0:T(2,128)S(1)}, f32[4,2,703]{2,1,0:T(2,128)S(1)}, u32[]{:S(2)}, u32[]{:S(2)}) collective-permute-start(f32[4,2,703]{2,1,0:T(2,128)S(1)} %fusion.1.refs_2_), channel_id=1, source_target_pairs={{0,4},{1,5},{2,6},{3,7},{4,0},{5,1},{6,2},{7,3},{8,12},{9,13},{10,... | collective-permute-start | bytes 67496 | tf_op jit(solution)/shard_map/ppermute | solution.py:346

commit v6 on v5

--- a/solution.py
+++ b/solution.py
@@ -12,7 +12,7 @@
 STEPS_PER_TURN = 64
 GAINS_AT = 768
 CHUNK = 48
-GRANTS = (50, 42)
+GRANTS = (45, 45)
 ROWS = 40
 
 F32 = jnp.float32
@@ -90,16 +90,22 @@
         body(pl.ds(full * 128, pairs % 128), pairs % 128)
 
 
-def phase_kernel(width, t, me_ref, delay_ref, *refs):
+def phase_kernel(width, t, reach, me_ref, *refs):
+    anchor = me_ref[0].astype(F32) * float(width)
+    vis_hbm, *refs, sem = refs
     if t == 0:
-        flag_ref, wave_ref, mix_ref, own_ref = refs
+        delay_ref, flag_ref, wave_ref, mix_ref, vis_ref, own_ref, hot_ref = refs
+    else:
+        delay_ref, win_ref, wave_ref, mix_ref, vis_ref, *mask_refs = refs
+    copy = pltpu.make_async_copy(vis_hbm.at[:, t], vis_ref, sem)
+    copy.start()
+    if t == 0:
         own_ref[...] = flag_ref[...]
+        hot_ref[0], hot_ref[1] = station_hots(delay_ref.shape[2])
     else:
-        vis_hbm, wave_ref, mix_ref, vis_ref, sem = refs
-        copy = pltpu.make_async_copy(vis_hbm, vis_ref, sem)
-        copy.start()
-    anchor = me_ref[0].astype(F32) * float(width)
+        window_masks(width, reach, me_ref[0], win_ref, *mask_refs)
     pairs = delay_ref.shape[2]
+
     def waves(lanes, count):
         delays = [delay_ref[s, t:t + 1, lanes] for s in range(2)]
         fine, coarse = phase_rows(delays, anchor, width)
@@ -122,22 +128,14 @@
                 mix_ref[slot, 1, rows, lanes] = low
 
     tiles(pairs, waves)
-    if t == 1:
-        copy.wait()
-
-
-def sums_kernel(width, stages, me_ref, win_ref, *refs):
-    flag_refs, refs = refs[:stages], refs[stages:]
-    delay_ref, vis_ref, wave_refs, mix_refs = refs[0], refs[1], refs[2:4], refs[4:6]
-    out_ref, alpha_s, mexp_s, wt_s = refs[6:]
-    me = me_ref[0]
-    near = flag_refs[0].shape[0]
-    groups = near * stages
+    copy.wait()
+
+
+def window_masks(width, reach, me, win_ref, inside_ref, chosen_ref, outside_ref, ends_ref):
+    anchor = me.astype(F32) * float(width)
+    lowest = (me - lax.rem(me, reach) - reach).astype(F32)
     windows = win_ref.shape[1]
-    pairs = delay_ref.shape[2]
-    anchor = me.astype(F32) * float(width)
     final = anchor + float(width - 1)
-
     win_row = win_ref[...].astype(F32)
     sub, lane = iota((windows, windows), 0), iota((windows, windows), 1)
     end_c = jnp.sum(jnp.where(lane <= sub, win_row, 0.0), axis=1, keepdims=True)
@@ -150,32 +148,51 @@
     from_first = jnp.sum(first_c * start_c, axis=0, keepdims=True)
     to_last = jnp.sum(last_c * end_c, axis=0, keepdims=True)
     here = anchor + iota((windows, width), 1)
-    member_wc = (here >= start_c) & (here < end_c)
-    there = iota((width, windows), 0) + anchor
-    member_cw = (there >= start_r) & (there < end_r)
-    apart = iota((groups, 1), 0) - me.astype(F32)
-    channel = iota((groups, width), 0) * float(width) + iota((groups, width), 1)
+    inside_ref[...] = jnp.where((here >= start_c) & (here < end_c), 1.0, 0.0)
+    there = anchor + iota((width, windows), 0)
+    chosen_ref[...] = jnp.where((there >= start_r) & (there < end_r), 1.0, 0.0)
+    shape = outside_ref.shape
+    channel = (lowest + iota(shape, 0)) * float(width) + iota(shape, 1)
     remote = ((channel < anchor) & (channel >= from_first)) | ((channel > final) & (channel < to_last))
+    outside_ref[...] = jnp.where(remote, 1.0, 0.0)
+    ends_ref[0] = jnp.broadcast_to(first_c, ends_ref.shape[1:])
+    ends_ref[1] = jnp.broadcast_to(last_c, ends_ref.shape[1:])
+
+
+def sums_kernel(width, reach, me_ref, *refs):
+    flag_refs, refs = refs[:3], refs[3:]
+    inside_ref, chosen_ref, outside_ref, ends_ref, delay_ref = refs[:5]
+    vis_refs, wave_refs, mix_refs, refs = refs[5:7], refs[7:9], refs[9:11], refs[11:]
+    out_refs, (alpha_s, mexp_s, wt_s) = refs[:4], refs[4:]
+    me = me_ref[0]
+    place = lax.rem(me, reach)
+    windows = inside_ref.shape[0]
+    pairs = delay_ref.shape[2]
+    sub, lane = iota((windows, windows), 0), iota((windows, windows), 1)
+    first_c, last_c = ends_ref[0][:, :1], ends_ref[1][:, :1]
+    apart = iota((outside_ref.shape[0], 1), 0) - (place + reach).astype(F32)
     diagonal = iota((width, width), 0) == iota((width, width), 1)
+    wt_s[...] = jnp.zeros_like(wt_s)
 
     def both_sides(value):
         return (jnp.sum(jnp.where(apart < 0.0, value, 0.0), axis=0, keepdims=True),
                 jnp.sum(jnp.where(apart > 0.0, value, 0.0), axis=0, keepdims=True))
 
     for t in range(2):
-        for slot in range(groups):
-            row = flag_refs[slot // near][slot % near, t:t + 1, :].astype(F32)
-            wt_s[t, pl.ds(lax.bitwise_xor(me, slot), 1), :] = 1.0 - row
+        for group, side in enumerate((1, 0, 2)):
+            for slot in range(reach):
+                row = flag_refs[group][slot, t:t + 1, :].astype(F32)
+                wt_s[t, pl.ds(side * reach + lax.bitwise_xor(place, slot), 1), :] = 1.0 - row
         own = 1.0 - flag_refs[0][0, t:t + 1, :].astype(F32)
-        inside = jnp.where(member_wc, own, 0.0)
-        outside = jnp.where(remote, wt_s[t], 0.0)
+        inside = inside_ref[...] * own
+        outside = outside_ref[...] * wt_s[t]
         before, after = both_sides(jnp.sum(outside, axis=1, keepdims=True))
         count = jnp.sum(inside, axis=1, keepdims=True) + first_c * before + last_c * after
         scale = 1.0 / jnp.maximum(count, 1.0)
         rows = jnp.concatenate([inside, outside], axis=0).astype(BF16)
         scale_r = jnp.sum(jnp.where(sub == lane, scale, 0.0), axis=0, keepdims=True)
         own_c = jnp.sum(jnp.where(diagonal, own, 0.0), axis=1, keepdims=True)
-        chosen = jnp.where(member_cw, own_c, 0.0)
+        chosen = chosen_ref[...] * own_c
         alpha_s[t] = jnp.broadcast_to(jnp.sum(chosen * scale_r, axis=1, keepdims=True), (width, 128))
         chosen = chosen.astype(BF16)
         sums = [dot(rows, mix_refs[t][slot, 0]) + dot(rows, mix_refs[t][slot, 1]) for slot in range(2)]
@@ -204,8 +221,8 @@
                     factors.append((fr, fi - fr, fr + fi))
                 new = []
                 for k in range(4):
-                    vr = vis_ref[0, t, k, rows, lanes].astype(F32)
-                    vi = vis_ref[1, t, k, rows, lanes].astype(F32)
+                    vr = vis_refs[t][0, k, rows, lanes].astype(F32)
+                    vi = vis_refs[t][1, k, rows, lanes].astype(F32)
                     vs = vr + vi
                     for s in range(2):
                         for v, f in zip((vs, vr, vi), factors[s]):
@@ -216,10 +233,17 @@
             zero = jnp.zeros((8, count), F32)
             sums = lax.fori_loop(0, width // 16, step, (zero,) * 24, unroll=4)
             for s in range(2):
+                owner = lax.bitwise_xor(lax.bitwise_and(me, 3), t + 2 * s)
+                found = []
                 for k in range(4):
                     one, two, three = sums[(k * 2 + s) * 3:(k * 2 + s) * 3 + 3]
-                    for ri, value in enumerate((one - three, one + two)):
-                        out_ref[t + 2 * s, k, ri:ri + 1, lanes] = jnp.sum(value, axis=0, keepdims=True)
+                    found.append([jnp.sum(value, axis=0, keepdims=True) for value in (one - three, one + two)])
+                for d in range(4):
+                    @pl.when(owner == d)
+                    def write():
+                        for k in range(4):
+                            for ri in range(2):
+                                out_refs[d][k, ri:ri + 1, lanes] = found[k][ri]
 
         tiles(pairs, main)
 
@@ -234,15 +258,15 @@
     return first.astype(BF16), second.astype(BF16)
 
 
-def solve_kernel(window_count, me_ref, tracks_ref, *refs):
+def solve_kernel(window_count, me_ref, tracks_ref, hot_ref, *refs):
     parts, gain_ref = refs[:-1], refs[-1]
     me = me_ref[0]
-    systems = gain_ref.shape[1]
+    systems = gain_ref.shape[0]
     total = [part[...] for part in parts]
     while len(total) > 1:
         total = [total[i] + total[i + 1] for i in range(0, len(total), 2)]
     total = total[0]
-    hot, other = station_hots(total.shape[2])
+    hot, other = hot_ref[0], hot_ref[1]
     nt = lambda left, right: lax.dot_general(
         left, right, (((1,), (1,)), ((), ())), preferred_element_type=F32)
     upper, lower = [], []
@@ -286,31 +310,31 @@
     pairs = hot.shape[1]
     for system in range(systems):
         (lr, li), (rr, ri_) = [[end[2 * system + ri:2 * system + ri + 1] for ri in range(2)] for end in ends]
-        for copy in range(4):
-            gain_ref[copy, system, 0:1, :pairs] = lr * rr + li * ri_
-            gain_ref[copy, system, 1:2, :pairs] = li * rr - lr * ri_
-            gain_ref[copy, system, :, GAINS_AT:] = gains[2 * system:2 * system + 2, :STATIONS]
-
-
-def clean_kernel(width, *refs):
-    vis_ref, wave_refs = refs[0], refs[1:3]
-    piece_ref, out_hbm, gain_out_ref, out_s, model_s, sems = refs[3:]
+        gain_ref[system, 0:1, :pairs] = lr * rr + li * ri_
+        gain_ref[system, 1:2, :pairs] = li * rr - lr * ri_
+        gain_ref[system, :, GAINS_AT:] = gains[2 * system:2 * system + 2, :STATIONS]
+
+
+def clean_kernel(width, me_ref, *refs):
+    vis_refs, wave_refs, piece_refs = refs[:2], refs[2:4], refs[4:8]
+    out_hbm, gain_out_ref, out_s, model_s, sems = refs[8:]
     pairs = wave_refs[0].shape[3]
-    for owner in range(4):
-        t, s = owner % 2, owner // 2
+    mine = lax.bitwise_and(me_ref[0], 3)
+    for d, piece in enumerate(piece_refs):
+        owner = lax.bitwise_xor(mine, d)
+        t, s = lax.bitwise_and(owner, 1), lax.div(owner, 2)
         for k in range(4):
             for ri in range(2):
-                gain_out_ref[ri, s, t, k:k + 1, :] = piece_ref[owner, k, ri:ri + 1, GAINS_AT:]
-            re, im = piece_ref[owner, k, 0:1, :pairs], piece_ref[owner, k, 1:2, :pairs]
+                gain_out_ref[ri, s, t, k:k + 1, :] = piece[k, ri:ri + 1, GAINS_AT:]
+            re, im = piece[k, 0:1, :pairs], piece[k, 1:2, :pairs]
             for slot, value in enumerate((re, im - re, re + im)):
                 model_s[owner, 3 * k + slot:3 * k + slot + 1, :] = value
-
-    chunks = width // CHUNK
 
     def copy_out(t, index):
         rows = pl.ds(pl.multiple_of(index * CHUNK, CHUNK), CHUNK)
         return pltpu.make_async_copy(out_s.at[:, t, :, rows], out_hbm.at[:, t, :, rows], sems.at[t, index])
 
+    chunks = width // CHUNK
     for t in range(2):
         def chunk(index, carry):
             def main(lanes, count):
@@ -326,8 +350,8 @@
                             one, two = (waves[s][slot] * model_s[t + 2 * s, 3 * k + slot:3 * k + slot + 1, lanes]
                                         for s in range(2))
                             sums.append(one + two)
-                        vr = vis_ref[0, t, k, rows, lanes].astype(F32)
-                        vi = vis_ref[1, t, k, rows, lanes].astype(F32)
+                        vr = vis_refs[t][0, k, rows, lanes].astype(F32)
+                        vi = vis_refs[t][1, k, rows, lanes].astype(F32)
                         out_s[0, t, k, rows, lanes] = (vr - (sums[0] - sums[2])).astype(BF16)
                         out_s[1, t, k, rows, lanes] = (vi - (sums[0] + sums[1])).astype(BF16)
 
@@ -344,6 +368,12 @@
 def partner(value, bits):
     count = lax.axis_size("sub")
     return lax.ppermute(value, "sub", [(i, i ^ bits) for i in range(count)])
+
+
+def from_both_sides(value, shift):
+    count = lax.axis_size("sub")
+    return [lax.ppermute(value, "sub", [(i, i + move) for i in range(count) if 0 <= i + move < count])
+            for move in (shift, -shift)]
 
 
 def smem():
@@ -357,60 +387,61 @@
     window_count = windows.shape[0]
     turned = jnp.transpose(visibilities, (0, 1, 2, 4, 3))
     me = lax.axis_index("sub").astype(jnp.int32).reshape(1)
-    fours = [[base + d for d in range(4)] for base in range(0, count, 4)]
     vmem_ref = pl.BlockSpec(memory_space=pltpu.VMEM)
     hbm_ref = pl.BlockSpec(memory_space=pltpu.HBM)
     vmem = lambda *shape: pltpu.VMEM(shape, F32)
     params = pltpu.CompilerParams(vmem_limit_bytes=24 * 2 ** 20)
-    waves, mixing = [], []
-    own = flags[None]
-    gathered = [own]
-    stride = 1
-    for t, grant in enumerate(GRANTS):
-        if stride < count:
-            got = [partner(gathered[0], stride * d) for d in range(1, min(4, count // stride))]
-        made = pl.pallas_call(
-            lambda *refs: phase_kernel(width, t, *refs),
-            in_specs=[smem(), vmem_ref, hbm_ref if t else vmem_ref],
-            out_specs=[vmem_ref] * 3,
-            out_shape=[
-                jax.ShapeDtypeStruct((2, 2, width, pairs), F32),
-                jax.ShapeDtypeStruct((2, 2, width, pairs), BF16),
-                jax.ShapeDtypeStruct(turned.shape, BF16) if t else jax.ShapeDtypeStruct(own.shape, own.dtype),
-            ],
-            scratch_shapes=[pltpu.SemaphoreType.DMA] * t,
-            compiler_params=pltpu.CompilerParams(vmem_limit_bytes=grant * 2 ** 20),
+    flags = flags[None]
+
+    reach = count // 4
+    remote_rows = 16 * pl.cdiv(3 * reach, 16)
+
+    made = []
+    beside = [partner(flags, d) for d in range(1, 4)]
+    for t in range(2):
+        shape = lambda *dims: jax.ShapeDtypeStruct(dims, F32)
+        out_shape = [
+            shape(2, 2, width, pairs),
+            jax.ShapeDtypeStruct((2, 2, width, pairs), BF16),
+            jax.ShapeDtypeStruct((2, 4, width, pairs), BF16),
+        ]
+        if t == 0:
+            operands = (me, turned, delays, flags)
+            out_shape += [jax.ShapeDtypeStruct(flags.shape, flags.dtype),
+                          jax.ShapeDtypeStruct((2, ROWS, pairs), BF16)]
+        else:
+            operands = (me, turned, delays, windows.reshape(1, window_count))
+            out_shape += [shape(window_count, width), shape(width, window_count),
+                          shape(remote_rows, width), shape(2, window_count, 128)]
+        made.append(pl.pallas_call(
+            lambda *refs: phase_kernel(width, t, reach, *refs),
+            in_specs=[smem(), hbm_ref] + [vmem_ref] * (len(operands) - 2),
+            out_specs=[vmem_ref] * len(out_shape),
+            out_shape=out_shape,
+            scratch_shapes=[pltpu.SemaphoreType.DMA],
+            compiler_params=pltpu.CompilerParams(vmem_limit_bytes=GRANTS[t] * 2 ** 20),
             cost_estimate=pl.CostEstimate(flops=10 ** 7, bytes_accessed=6 * 2 ** 20, transcendentals=0),
             name="phases",
-        )(me, delays, turned if t else own)
-        waves.append(made[0])
-        mixing.append(made[1])
+        )(*operands))
         if t == 0:
-            own = made[2]
-        else:
-            held = made[2]
-        if stride < count:
-            gathered = [own if t == 0 else gathered[0]] + got
-            stride *= 4
-            if stride < count:
-                gathered = [jnp.concatenate(gathered, axis=0)]
-    while stride < count:
-        got = [partner(gathered[0], stride * d) for d in range(1, min(4, count // stride))]
-        gathered = gathered + got
-        stride *= 4
-        if stride < count:
-            gathered = [jnp.concatenate(gathered, axis=0)]
-    shares = pl.pallas_call(
-        lambda *refs: sums_kernel(width, len(gathered), *refs),
-        in_specs=[smem()] + [vmem_ref] * (len(gathered) + 7),
-        out_specs=vmem_ref,
-        out_shape=jax.ShapeDtypeStruct((4, 4, 2, pairs), F32),
-        scratch_shapes=[vmem(2, width, 128), vmem(2, 2, width, pairs), vmem(2, count, width)],
+            gathered = jnp.concatenate([made[0][3]] + beside, axis=0)
+            while gathered.shape[0] < reach:
+                stride = gathered.shape[0]
+                gathered = jnp.concatenate([gathered] + [partner(gathered, stride * d) for d in range(1, 4)], axis=0)
+            gathered = [gathered] + from_both_sides(gathered, reach)
+    waves, mixing, held = ([part[i] for part in made] for i in range(3))
+    masks = made[1][3:]
+    hots = made[0][4]
+    quarters = pl.pallas_call(
+        lambda *refs: sums_kernel(width, reach, *refs),
+        in_specs=[smem()] + [vmem_ref] * 14,
+        out_specs=[vmem_ref] * 4,
+        out_shape=[jax.ShapeDtypeStruct((4, 2, pairs), F32)] * 4,
+        scratch_shapes=[vmem(2, width, 128), vmem(2, 2, width, pairs), vmem(2, remote_rows, width)],
         compiler_params=params,
         name="window_sums",
-    )(me, windows.reshape(1, window_count), *gathered, delays, held, *waves, *mixing)
-    shares = lax.all_to_all(shares, "sub", 0, 0, axis_index_groups=fours)
-    pieces = [shares[d] for d in range(4)]
+    )(me, *gathered, *masks, delays, *held, *waves, *mixing)
+    pieces = [quarters[0]] + [partner(quarters[d], d) for d in range(1, 4)]
     stride = 4
     while stride < count:
         while len(pieces) > 1:
@@ -419,16 +450,16 @@
         stride *= 4
     model = pl.pallas_call(
         lambda *refs: solve_kernel(float(window_count), *refs),
-        in_specs=[smem(), smem()] + [vmem_ref] * len(pieces),
+        in_specs=[smem(), smem()] + [vmem_ref] * (1 + len(pieces)),
         out_specs=vmem_ref,
-        out_shape=jax.ShapeDtypeStruct((4, 4, 2, GAINS_AT + STATIONS), F32),
+        out_shape=jax.ShapeDtypeStruct((4, 2, GAINS_AT + STATIONS), F32),
         compiler_params=params,
         name="gain_solve",
-    )(me, tracks, *pieces)
-    model = lax.all_to_all(model, "sub", 0, 0, axis_index_groups=fours)
+    )(me, tracks, hots, *pieces)
+    model = [model] + [partner(model, d) for d in range(1, 4)]
     cleaned, gains = pl.pallas_call(
         lambda *refs: clean_kernel(width, *refs),
-        in_specs=[vmem_ref] * 4,
+        in_specs=[smem()] + [vmem_ref] * 8,
         out_specs=[hbm_ref, vmem_ref],
         out_shape=[
             jax.ShapeDtypeStruct(turned.shape, BF16),
@@ -441,7 +472,7 @@
         ],
         compiler_params=params,
         name="clean",
-    )(held, *waves, model)
+    )(me, *held, *waves, *model)
     return jnp.transpose(cleaned, (0, 1, 2, 4, 3)), gains
 
 

time: 48.2 us -> 45.4 us (0.942)
  blocking collectives: 13.5 us -> 0 us
  starting transfers between devices: 12 us -> 17.5 us
  waiting for transfers between devices: 4.87 us -> 9.51 us
  Pallas kernels: 15.3 us -> 15.9 us
    all_to_all x2 -> x0, blocking collectives: 13.5 us -> none  [the longest x1 6.84 us: local(): model = lax.all_to_all(model, 'sub', 0, 0, axis_index_groups=fours)]
    ppermute x0 -> x2, starting transfers between devices: none -> 5.84 us  [from_both_sides(): lax.ppermute(value, 'sub', [(i, i + move) for i in range(count) if 0 <= i...]
    ppermute x9 -> x12, waiting for transfers between devices: 4.87 us -> 9.51 us  [partner(): return lax.ppermute(value, 'sub', [(i, i ^ bits) for i in range(count)])]
    pallas_call x4, Pallas kernels: 13.2 us -> 13.8 us  [the longest x1 5.64 us: local(): pl.pallas_call(lambda *refs: sums_kernel(width, reach, *refs), in_specs=[...]
    ppermute x9 -> x12, starting transfers between devices: 12 us -> 11.6 us  [partner(): return lax.ppermute(value, 'sub', [(i, i ^ bits) for i in range(count)])]
  transfers between devices with their start and end apart: 9 -> 14, of which waited for: 4 -> 6; matrix products, arithmetic and copies ran while one was open for 0% -> 0% of each run, Pallas kernels for 7% -> 7%
where the time goes in v6:
time: 45.4 us; the launch traced here: 45.1 us
  starting transfers between devices  17.5 us (39%)
  Pallas kernels  15.9 us (35%)
  waiting for transfers between devices  9.51 us (21%)
  local copies, waits for them, and re-layouts  1.43 us (3%)
  between operations  0.78 us (2%)
    ppermute x12, starting transfers between devices, partner(): return lax.ppermute(value, 'sub', [(i, i ^ bits) for i in range(count)])  11.6 us
    ppermute x12, waiting for transfers between devices, partner(): return lax.ppermute(value, 'sub', [(i, i ^ bits) for i in range(count)])  9.51 us
    ppermute x2, starting transfers between devices, from_both_sides(): lax.ppermute(value, 'sub', [(i, i + move) for i in range(count) if 0 <= i...  5.84 us
    pallas_call x1, Pallas kernels, local(): pl.pallas_call(lambda *refs: sums_kernel(width, reach, *refs), in_specs=[...  5.64 us
    pallas_call x1, Pallas kernels, local(): pl.pallas_call(lambda *refs: clean_kernel(width, *refs), in_specs=[smem()...  4.82 us
    pallas_call x2, Pallas kernels, local(): pl.pallas_call(lambda *refs: phase_kernel(width, t, reach, *refs), in_spe...  3.37 us
    pallas_call x1, Pallas kernels, local(): pl.pallas_call(lambda *refs: solve_kernel(float(window_count), *refs), in...  2.07 us
    unnamed x11, local copies, waits for them, and re-layouts  1.42 us
  transfers between devices with their start and end apart: 14, of which 6 were waited for; matrix products, arithmetic and copies ran while one was open for 0% of the time, Pallas kernels for 7%

profile of v6, /device:TPU:0, one launch (start us, length us, event | category | flops | bytes accessed | tf_op | source)
XLA Modules:
  0.0 45.1 jit_solution(5716279292552225563)
XLA Ops:
  0.6 2.5 %collective-permute-start.2 = (s32[1,2,192]{2,1,0:T(2,128)}, s32[1,2,192]{2,1,0:T(2,128)S(1)}, u32[]{:S(2)}, u32[]{:S(2)}) collective-permute-start(s32[1,2,192]{2,1,0:T(2,128)} %bitcast.15), channel_id=1, source_target_pairs={{0,3},{1,2},{2,1},{3,0},{4,7},{5,6},{6,5},{7,4},{8,11},{9,10},{10,... | collective-permute-start | bytes 4616 | tf_op jit(solution)/shard_map/ppermute | solution.py:370
  3.1 0.6 %collective-permute-start.1 = (s32[1,2,192]{2,1,0:T(2,128)}, s32[1,2,192]{2,1,0:T(2,128)S(1)}, u32[]{:S(2)}, u32[]{:S(2)}) collective-permute-start(s32[1,2,192]{2,1,0:T(2,128)} %bitcast.16), channel_id=1, source_target_pairs={{0,2},{1,3},{2,0},{3,1},{4,6},{5,7},{6,4},{7,5},{8,10},{9,11},{10,... | collective-permute-start | bytes 4616 | tf_op jit(solution)/shard_map/ppermute | solution.py:370
  3.7 0.0 collective-permute-start
  3.8 0.0 copy-start
  3.8 0.7 %copy-done = f32[2,2,703]{2,1,0:T(2,128)S(1)} copy-done((f32[2,2,703]{2,1,0:T(2,128)S(1)}, f32[2,2,703]{2,1,0:T(2,128)}, u32[]{:S(2)}) %copy-start) | copy-done | bytes 11272
  4.5 0.0 copy-start.1
  4.5 0.7 %copy-done.1 = s32[2,192]{1,0:T(2,128)S(1)} copy-done((s32[2,192]{1,0:T(2,128)S(1)}, s32[2,192]{1,0:T(2,128)}, u32[]{:S(2)}) %copy-start.1) | copy-done | bytes 1560
  5.2 0.0 copy-start.3
  5.2 1.7 %phases.2 = (f32[2,2,192,703]{3,2,1,0:T(8,128)S(1)}, bf16[2,2,192,703]{3,2,1,0:T(8,128)(2,1)S(1)}, bf16[2,4,192,703]{3,2,1,0:T(8,128)(2,1)S(1)}, s32[1,2,192]{2,1,0:T(2,128)S(1)}, bf16[2,40,703]{2,1,0:T(8,128)(2,1)S(1)}) custom-call(s32[1]{0:T(128)} %bitcast.refs_0_, bf16[2,2,4,192,703]{4,3,2,1,0:T(8,128)(2,1)} %bitcast.20, f32[2,2,703]{2,1,0:T(2,128)S(1)} %copy-done, ...), custom_call_target="tpu_custom_call" | custom-call | flops 10000000 | bytes 6291456 | tf_op jit(solution)/shard_map/phases/pallas_call | solution.py:416
  6.9 0.0 collective-permute-done
  6.9 0.0 collective-permute-done.1
  6.9 0.0 collective-permute-done.2
  6.9 1.3 %collective-permute-start.4 = (s32[4,2,192]{2,1,0:T(2,128)S(1)}, s32[4,2,192]{2,1,0:T(2,128)S(1)}, u32[]{:S(2)}, u32[]{:S(2)}) collective-permute-start(s32[4,2,192]{2,1,0:T(2,128)S(1)} %constant_dynamic-update-slice_fusion.refs_1_), channel_id=1, source_target_pairs={{4,0},{5,1},{6,2},{7,3},{8,4},{9,5},{10,6},{11,7},{12,8},{13,9},{1... | collective-permute-start | bytes 18440 | tf_op jit(solution)/shard_map/ppermute | solution.py:375
  8.2 4.5 %collective-permute-start.3 = (s32[4,2,192]{2,1,0:T(2,128)S(1)}, s32[4,2,192]{2,1,0:T(2,128)S(1)}, u32[]{:S(2)}, u32[]{:S(2)}) collective-permute-start(s32[4,2,192]{2,1,0:T(2,128)S(1)} %constant_dynamic-update-slice_fusion.refs_1_), channel_id=1, source_target_pairs={{0,4},{1,5},{2,6},{3,7},{4,8},{5,9},{6,10},{7,11},{8,12},{9,13},{1... | collective-permute-start | bytes 18440 | tf_op jit(solution)/shard_map/ppermute | solution.py:375
  12.8 0.0 copy-done.3
  12.8 1.7 %phases.3 = (f32[2,2,192,703]{3,2,1,0:T(8,128)S(1)}, bf16[2,2,192,703]{3,2,1,0:T(8,128)(2,1)S(1)}, bf16[2,4,192,703]{3,2,1,0:T(8,128)(2,1)S(1)}, f32[32,192]{1,0...) custom-call(s32[1]{0:T(128)} %bitcast.refs_0_, ...), custom_call_target="tpu_custom_call" | custom-call | flops 10000000 | bytes 6291456 | tf_op jit(solution)/shard_map/phases/pallas_call | solution.py:416
  14.5 0.0 collective-permute-done.4.refs_3_
  14.5 0.0 collective-permute-done.3.refs_2_
  14.5 0.0 copy-start.2
  14.5 5.6 %window_sums.1 = (f32[4,2,703]{2,1,0:T(2,128)S(1)}, f32[4,2,703]{2,1,0:T(2,128)S(1)}, f32[4,2,703]{2,1,0:T(2,128)S(1)}, f32[4,2,703]{2,1,0:T(2,128)S(1)}) custom-call(s32[1]{0:T(128)} %bitcast.refs_0_, s32[4,2,192]{2,1,0:T(2,128)S(1)} %constant_dynamic-update-slice_fusion.refs_1_, s32[4,2,192]{2,1,0:T(2,128)S(1)} %collective-permute-done.3.refs_2_, ...), custom_call_target="tpu_custom_call" | custom-call | tf_op jit(solution)/shard_map/window_sums/pallas_call | solution.py:435
  20.2 0.1 collective-permute-start.5
  20.3 1.8 %collective-permute-start.6 = (f32[4,2,703]{2,1,0:T(2,128)S(1)}, f32[4,2,703]{2,1,0:T(2,128)S(1)}, u32[]{:S(2)}, u32[]{:S(2)}) collective-permute-start(f32[4,2,703]{2,1,0:T(2,128)S(1)} %get-tuple-element.34), channel_id=1, source_target_pairs={{0,2},{1,3},{2,0},{3,1},{4,6},{5,7},{6,4},{7,5},{8,10},{9,11},{10,... | collective-permute-start | bytes 67496 | tf_op jit(solution)/shard_map/ppermute | solution.py:370
  22.1 0.1 collective-permute-start.7
  22.1 0.0 collective-permute-done.5
  22.1 2.0 %collective-permute-done.6 = f32[4,2,703]{2,1,0:T(2,128)S(1)} collective-permute-done((f32[4,2,703]{2,1,0:T(2,128)S(1)}, f32[4,2,703]{2,1,0:T(2,128)S(1)}, u32[]{:S(2)}, u32[]{:S(2)}) %collective-permute-start.6) | collective-permute-done | bytes 22528 | tf_op jit(solution)/shard_map/ppermute | solution.py:370
  24.1 1.2 %collective-permute-done.7 = f32[4,2,703]{2,1,0:T(2,128)S(1)} collective-permute-done((f32[4,2,703]{2,1,0:T(2,128)S(1)}, f32[4,2,703]{2,1,0:T(2,128)S(1)}, u32[]{:S(2)}, u32[]{:S(2)}) %collective-permute-start.7) | collective-permute-done | bytes 22528 | tf_op jit(solution)/shard_map/ppermute | solution.py:370
  25.3 4.0 %collective-permute-start.10 = (f32[4,2,703]{2,1,0:T(2,128)S(1)}, f32[4,2,703]{2,1,0:T(2,128)S(1)}, u32[]{:S(2)}, u32[]{:S(2)}) collective-permute-start(f32[4,2,703]{2,1,0:T(2,128)S(1)} %bitcast.10), channel_id=1, source_target_pairs={{0,12},{1,13},{2,14},{3,15},{4,8},{5,9},{6,10},{7,11},{8,4},{9,5},... | collective-permute-start | bytes 67496 | tf_op jit(solution)/shard_map/ppermute | solution.py:370
  29.3 0.0 collective-permute-start.9
  29.3 0.6 %collective-permute-start.8 = (f32[4,2,703]{2,1,0:T(2,128)S(1)}, f32[4,2,703]{2,1,0:T(2,128)S(1)}, u32[]{:S(2)}, u32[]{:S(2)}) collective-permute-start(f32[4,2,703]{2,1,0:T(2,128)S(1)} %bitcast.12), channel_id=1, source_target_pairs={{0,4},{1,5},{2,6},{3,7},{4,0},{5,1},{6,2},{7,3},{8,12},{9,13},{10,... | collective-permute-start | bytes 67496 | tf_op jit(solution)/shard_map/ppermute | solution.py:370
  30.0 1.2 %collective-permute-done.10.refs_6_ = f32[4,2,703]{2,1,0:T(2,128)S(1)} collective-permute-done((f32[4,2,703]{2,1,0:T(2,128)S(1)}, f32[4,2,703]{2,1,0:T(2,128)S(1)}, u32[]{:S(2)}, u32[]{:S(2)}) %collective-permute-start.10) | collective-permute-done | bytes 22528 | tf_op jit(solution)/shard_map/ppermute | solution.py:370
  31.1 2.9 %collective-permute-done.9.refs_5_ = f32[4,2,703]{2,1,0:T(2,128)S(1)} collective-permute-done((f32[4,2,703]{2,1,0:T(2,128)S(1)}, f32[4,2,703]{2,1,0:T(2,128)S(1)}, u32[]{:S(2)}, u32[]{:S(2)}) %collective-permute-start.9) | collective-permute-done | bytes 22528 | tf_op jit(solution)/shard_map/ppermute | solution.py:370
  34.0 0.0 collective-permute-done.8.refs_4_
  34.0 0.0 copy-done.2
  34.0 2.1 %gain_solve.1.refs_5_ = f32[4,2,806]{2,1,0:T(2,128)S(1)} custom-call(s32[1]{0:T(128)} %bitcast.refs_0_, s32[2,2]{1,0:T(2,128)S(1)} %copy-done.2, bf16[2,40,703]{2,1,0:T(8,128)(2,1)S(1)} %get-tuple-element.24.refs_2_, f32[4,2,703]{2,1,0:T(2,128)S(1)} %bitcast.13, f32[4,2,703]{2,1,0:T(2,128)S(1)} %collective-permute-done.8.refs_4_, ...), custom_call_target="tpu_custom_call" | custom-call | tf_op jit(solution)/shard_map/gain_solve/pallas_call | solution.py:451
  36.1 0.1 collective-permute-start.13
  36.2 0.8 %collective-permute-start.12 = (f32[4,2,806]{2,1,0:T(2,128)S(1)}, f32[4,2,806]{2,1,0:T(2,128)S(1)}, u32[]{:S(2)}, u32[]{:S(2)}) collective-permute-start(f32[4,2,806]{2,1,0:T(2,128)S(1)} %gain_solve.1.refs_5_), channel_id=1, source_target_pairs={{0,2},{1,3},{2,0},{3,1},{4,6},{5,7},{6,4},{7,5},{8,10},{9,11},{10,... | collective-permute-start | bytes 77384 | tf_op jit(solution)/shard_map/ppermute | solution.py:370
  37.0 1.0 %collective-permute-start.11 = (f32[4,2,806]{2,1,0:T(2,128)S(1)}, f32[4,2,806]{2,1,0:T(2,128)S(1)}, u32[]{:S(2)}, u32[]{:S(2)}) collective-permute-start(f32[4,2,806]{2,1,0:T(2,128)S(1)} %gain_solve.1.refs_5_), channel_id=1, source_target_pairs={{0,1},{1,0},{2,3},{3,2},{4,5},{5,4},{6,7},{7,6},{8,9},{9,8},{10,11... | collective-permute-start | bytes 77384 | tf_op jit(solution)/shard_map/ppermute | solution.py:370
  38.1 1.4 %collective-permute-done.13.refs_8_ = f32[4,2,806]{2,1,0:T(2,128)S(1)} collective-permute-done((f32[4,2,806]{2,1,0:T(2,128)S(1)}, f32[4,2,806]{2,1,0:T(2,128)S(1)}, u32[]{:S(2)}, u32[]{:S(2)}) %collective-permute-start.13) | collective-permute-done | bytes 25824 | tf_op jit(solution)/shard_map/ppermute | solution.py:370
  39.5 0.8 %collective-permute-done.12.refs_7_ = f32[4,2,806]{2,1,0:T(2,128)S(1)} collective-permute-done((f32[4,2,806]{2,1,0:T(2,128)S(1)}, f32[4,2,806]{2,1,0:T(2,128)S(1)}, u32[]{:S(2)}, u32[]{:S(2)}) %collective-permute-start.12) | collective-permute-done | bytes 25824 | tf_op jit(solution)/shard_map/ppermute | solution.py:370
  40.3 0.0 collective-permute-done.11.refs_6_
  40.3 4.8 %clean.1 = (bf16[2,2,4,192,703]{4,3,2,1,0:T(8,128)(2,1)}, f32[2,2,2,4,38]{4,3,2,1,0:T(4,128)}) custom-call(s32[1]{0:T(128)} %bitcast.refs_0_, bf16[2,4,192,703]{3,2,1,0:T(8,128)(2,1)S(1)} %get-tuple-element.20.refs_9_.refs_1_, bf16[2,4,192,703]{3,2,1,0:T(8,128)(2,1)S(1)} %get-tuple-element.21.refs_10_.refs_2_, ...), custom_call_target="tpu_custom_call" | custom-call | tf_op jit(solution)/shard_map/clean/pallas_call | solution.py:460
  (5 shorter events, 0.0 us)
Async XLA Ops:
  0.6 6.3 %collective-permute-start.2 = (s32[1,2,192]{2,1,0:T(2,128)}, s32[1,2,192]{2,1,0:T(2,128)S(1)}, u32[]{:S(2)}, u32[]{:S(2)}) collective-permute-start(s32[1,2,192]{2,1,0:T(2,128)} %bitcast.15), channel_id=1, source_target_pairs={{0,3},{1,2},{2,1},{3,0},{4,7},{5,6},{6,5},{7,4},{8,11},{9,10},{10,... | collective-permute-start | bytes 4616 | tf_op jit(solution)/shard_map/ppermute | solution.py:370
  3.1 3.8 %collective-permute-start.1 = (s32[1,2,192]{2,1,0:T(2,128)}, s32[1,2,192]{2,1,0:T(2,128)S(1)}, u32[]{:S(2)}, u32[]{:S(2)}) collective-permute-start(s32[1,2,192]{2,1,0:T(2,128)} %bitcast.16), channel_id=1, source_target_pairs={{0,2},{1,3},{2,0},{3,1},{4,6},{5,7},{6,4},{7,5},{8,10},{9,11},{10,... | collective-permute-start | bytes 4616 | tf_op jit(solution)/shard_map/ppermute | solution.py:370
  3.7 3.1 %collective-permute-start = (s32[1,2,192]{2,1,0:T(2,128)}, s32[1,2,192]{2,1,0:T(2,128)S(1)}, u32[]{:S(2)}, u32[]{:S(2)}) collective-permute-start(s32[1,2,192]{2,1,0:T(2,128)} %bitcast.17), channel_id=1, source_target_pairs={{0,1},{1,0},{2,3},{3,2},{4,5},{5,4},{6,7},{7,6},{8,9},{9,8},{10,11... | collective-permute-start | bytes 4616 | tf_op jit(solution)/shard_map/ppermute | solution.py:370
  3.8 0.7 %copy-start = (f32[2,2,703]{2,1,0:T(2,128)S(1)}, f32[2,2,703]{2,1,0:T(2,128)}, u32[]{:S(2)}) copy-start(f32[2,2,703]{2,1,0:T(2,128)} %refs_8_.1) | copy-start | bytes 33748
  4.5 0.7 %copy-start.1 = (s32[2,192]{1,0:T(2,128)S(1)}, s32[2,192]{1,0:T(2,128)}, u32[]{:S(2)}) copy-start(s32[2,192]{1,0:T(2,128)} %param.7) | copy-start | bytes 4612
  5.2 7.6 %copy-start.3 = (s32[32]{0:T(128)S(1)}, s32[32]{0:T(128)}, u32[]{:S(2)}) copy-start(s32[32]{0:T(128)} %param.8) | copy-start | bytes 388
  6.9 7.6 %collective-permute-start.4 = (s32[4,2,192]{2,1,0:T(2,128)S(1)}, s32[4,2,192]{2,1,0:T(2,128)S(1)}, u32[]{:S(2)}, u32[]{:S(2)}) collective-permute-start(s32[4,2,192]{2,1,0:T(2,128)S(1)} %constant_dynamic-update-slice_fusion.refs_1_), channel_id=1, source_target_pairs={{4,0},{5,1},{6,2},{7,3},{8,4},{9,5},{10,6},{11,7},{12,8},{13,9},{1... | collective-permute-start | bytes 18440 | tf_op jit(solution)/shard_map/ppermute | solution.py:375
  8.2 6.3 %collective-permute-start.3 = (s32[4,2,192]{2,1,0:T(2,128)S(1)}, s32[4,2,192]{2,1,0:T(2,128)S(1)}, u32[]{:S(2)}, u32[]{:S(2)}) collective-permute-start(s32[4,2,192]{2,1,0:T(2,128)S(1)} %constant_dynamic-update-slice_fusion.refs_1_), channel_id=1, source_target_pairs={{0,4},{1,5},{2,6},{3,7},{4,8},{5,9},{6,10},{7,11},{8,12},{9,13},{1... | collective-permute-start | bytes 18440 | tf_op jit(solution)/shard_map/ppermute | solution.py:375
  14.5 19.5 %copy-start.2 = (s32[2,2]{1,0:T(2,128)S(1)}, s32[2,2]{1,0:T(2,128)}, u32[]{:S(2)}) copy-start(s32[2,2]{1,0:T(2,128)} %refs_1_.1) | copy-start | bytes 52
  20.2 2.0 %collective-permute-start.5 = (f32[4,2,703]{2,1,0:T(2,128)S(1)}, f32[4,2,703]{2,1,0:T(2,128)S(1)}, u32[]{:S(2)}, u32[]{:S(2)}) collective-permute-start(f32[4,2,703]{2,1,0:T(2,128)S(1)} %get-tuple-element.33), channel_id=1, source_target_pairs={{0,1},{1,0},{2,3},{3,2},{4,5},{5,4},{6,7},{7,6},{8,9},{9,8},{10,11... | collective-permute-start | bytes 67496 | tf_op jit(solution)/shard_map/ppermute | solution.py:370
  20.3 3.9 %collective-permute-start.6 = (f32[4,2,703]{2,1,0:T(2,128)S(1)}, f32[4,2,703]{2,1,0:T(2,128)S(1)}, u32[]{:S(2)}, u32[]{:S(2)}) collective-permute-start(f32[4,2,703]{2,1,0:T(2,128)S(1)} %get-tuple-element.34), channel_id=1, source_target_pairs={{0,2},{1,3},{2,0},{3,1},{4,6},{5,7},{6,4},{7,5},{8,10},{9,11},{10,... | collective-permute-start | bytes 67496 | tf_op jit(solution)/shard_map/ppermute | solution.py:370
  22.1 3.3 %collective-permute-start.7 = (f32[4,2,703]{2,1,0:T(2,128)S(1)}, f32[4,2,703]{2,1,0:T(2,128)S(1)}, u32[]{:S(2)}, u32[]{:S(2)}) collective-permute-start(f32[4,2,703]{2,1,0:T(2,128)S(1)} %get-tuple-element.35), channel_id=1, source_target_pairs={{0,3},{1,2},{2,1},{3,0},{4,7},{5,6},{6,5},{7,4},{8,11},{9,10},{10,... | collective-permute-start | bytes 67496 | tf_op jit(solution)/shard_map/ppermute | solution.py:370
  25.3 5.8 %collective-permute-start.10 = (f32[4,2,703]{2,1,0:T(2,128)S(1)}, f32[4,2,703]{2,1,0:T(2,128)S(1)}, u32[]{:S(2)}, u32[]{:S(2)}) collective-permute-start(f32[4,2,703]{2,1,0:T(2,128)S(1)} %bitcast.10), channel_id=1, source_target_pairs={{0,12},{1,13},{2,14},{3,15},{4,8},{5,9},{6,10},{7,11},{8,4},{9,5},... | collective-permute-start | bytes 67496 | tf_op jit(solution)/shard_map/ppermute | solution.py:370
  29.3 4.7 %collective-permute-start.9 = (f32[4,2,703]{2,1,0:T(2,128)S(1)}, f32[4,2,703]{2,1,0:T(2,128)S(1)}, u32[]{:S(2)}, u32[]{:S(2)}) collective-permute-start(f32[4,2,703]{2,1,0:T(2,128)S(1)} %bitcast.11), channel_id=1, source_target_pairs={{0,8},{1,9},{2,10},{3,11},{4,12},{5,13},{6,14},{7,15},{8,0},{9,1},... | collective-permute-start | bytes 67496 | tf_op jit(solution)/shard_map/ppermute | solution.py:370
  29.3 4.7 %collective-permute-start.8 = (f32[4,2,703]{2,1,0:T(2,128)S(1)}, f32[4,2,703]{2,1,0:T(2,128)S(1)}, u32[]{:S(2)}, u32[]{:S(2)}) collective-permute-start(f32[4,2,703]{2,1,0:T(2,128)S(1)} %bitcast.12), channel_id=1, source_target_pairs={{0,4},{1,5},{2,6},{3,7},{4,0},{5,1},{6,2},{7,3},{8,12},{9,13},{10,... | collective-permute-start | bytes 67496 | tf_op jit(solution)/shard_map/ppermute | solution.py:370
  36.1 3.4 %collective-permute-start.13 = (f32[4,2,806]{2,1,0:T(2,128)S(1)}, f32[4,2,806]{2,1,0:T(2,128)S(1)}, u32[]{:S(2)}, u32[]{:S(2)}) collective-permute-start(f32[4,2,806]{2,1,0:T(2,128)S(1)} %gain_solve.1.refs_5_), channel_id=1, source_target_pairs={{0,3},{1,2},{2,1},{3,0},{4,7},{5,6},{6,5},{7,4},{8,11},{9,10},{10,... | collective-permute-start | bytes 77384 | tf_op jit(solution)/shard_map/ppermute | solution.py:370
  36.2 4.1 %collective-permute-start.12 = (f32[4,2,806]{2,1,0:T(2,128)S(1)}, f32[4,2,806]{2,1,0:T(2,128)S(1)}, u32[]{:S(2)}, u32[]{:S(2)}) collective-permute-start(f32[4,2,806]{2,1,0:T(2,128)S(1)} %gain_solve.1.refs_5_), channel_id=1, source_target_pairs={{0,2},{1,3},{2,0},{3,1},{4,6},{5,7},{6,4},{7,5},{8,10},{9,11},{10,... | collective-permute-start | bytes 77384 | tf_op jit(solution)/shard_map/ppermute | solution.py:370
  37.0 3.2 %collective-permute-start.11 = (f32[4,2,806]{2,1,0:T(2,128)S(1)}, f32[4,2,806]{2,1,0:T(2,128)S(1)}, u32[]{:S(2)}, u32[]{:S(2)}) collective-permute-start(f32[4,2,806]{2,1,0:T(2,128)S(1)} %gain_solve.1.refs_5_), channel_id=1, source_target_pairs={{0,1},{1,0},{2,3},{3,2},{4,5},{5,4},{6,7},{7,6},{8,9},{9,8},{10,11... | collective-permute-start | bytes 77384 | tf_op jit(solution)/shard_map/ppermute | solution.py:370

commit v7 on v6

--- a/solution.py
+++ b/solution.py
@@ -12,7 +12,7 @@
 STEPS_PER_TURN = 64
 GAINS_AT = 768
 CHUNK = 48
-GRANTS = (45, 45)
+GRANT = 40
 ROWS = 40
 
 F32 = jnp.float32
@@ -92,13 +92,10 @@
 
 def phase_kernel(width, t, reach, me_ref, *refs):
     anchor = me_ref[0].astype(F32) * float(width)
-    vis_hbm, *refs, sem = refs
     if t == 0:
-        delay_ref, flag_ref, wave_ref, mix_ref, vis_ref, own_ref, hot_ref = refs
+        delay_ref, flag_ref, wave_ref, mix_ref, own_ref, hot_ref = refs
     else:
-        delay_ref, win_ref, wave_ref, mix_ref, vis_ref, *mask_refs = refs
-    copy = pltpu.make_async_copy(vis_hbm.at[:, t], vis_ref, sem)
-    copy.start()
+        delay_ref, win_ref, wave_ref, mix_ref, *mask_refs = refs
     if t == 0:
         own_ref[...] = flag_ref[...]
         hot_ref[0], hot_ref[1] = station_hots(delay_ref.shape[2])
@@ -128,7 +125,6 @@
                 mix_ref[slot, 1, rows, lanes] = low
 
     tiles(pairs, waves)
-    copy.wait()
 
 
 def window_masks(width, reach, me, win_ref, inside_ref, chosen_ref, outside_ref, ends_ref):
@@ -162,8 +158,11 @@
 def sums_kernel(width, reach, me_ref, *refs):
     flag_refs, refs = refs[:3], refs[3:]
     inside_ref, chosen_ref, outside_ref, ends_ref, delay_ref = refs[:5]
-    vis_refs, wave_refs, mix_refs, refs = refs[5:7], refs[7:9], refs[9:11], refs[11:]
-    out_refs, (alpha_s, mexp_s, wt_s) = refs[:4], refs[4:]
+    vis_hbm, wave_refs, mix_refs, refs = refs[5], refs[6:8], refs[8:10], refs[10:]
+    out_refs, (vis_ref, alpha_s, mexp_s, wt_s, sems) = refs[:4], refs[4:]
+    copies = [pltpu.make_async_copy(vis_hbm.at[:, t], vis_ref.at[:, t], sems.at[t]) for t in range(2)]
+    for copy in copies:
+        copy.start()
     me = me_ref[0]
     place = lax.rem(me, reach)
     windows = inside_ref.shape[0]
@@ -179,7 +178,8 @@
                 jnp.sum(jnp.where(apart > 0.0, value, 0.0), axis=0, keepdims=True))
 
     for t in range(2):
-        for group, side in enumerate((1, 0, 2)):
+        odd = lax.rem(lax.div(me, reach), 2)
+        for group, side in enumerate((1, 2 - 2 * odd, 2 * odd)):
             for slot in range(reach):
                 row = flag_refs[group][slot, t:t + 1, :].astype(F32)
                 wt_s[t, pl.ds(side * reach + lax.bitwise_xor(place, slot), 1), :] = 1.0 - row
@@ -221,8 +221,8 @@
                     factors.append((fr, fi - fr, fr + fi))
                 new = []
                 for k in range(4):
-                    vr = vis_refs[t][0, k, rows, lanes].astype(F32)
-                    vi = vis_refs[t][1, k, rows, lanes].astype(F32)
+                    vr = vis_ref[0, t, k, rows, lanes].astype(F32)
+                    vi = vis_ref[1, t, k, rows, lanes].astype(F32)
                     vs = vr + vi
                     for s in range(2):
                         for v, f in zip((vs, vr, vi), factors[s]):
@@ -245,6 +245,7 @@
                             for ri in range(2):
                                 out_refs[d][k, ri:ri + 1, lanes] = found[k][ri]
 
+        copies[t].wait()
         tiles(pairs, main)
 
 
@@ -316,8 +317,8 @@
 
 
 def clean_kernel(width, me_ref, *refs):
-    vis_refs, wave_refs, piece_refs = refs[:2], refs[2:4], refs[4:8]
-    out_hbm, gain_out_ref, out_s, model_s, sems = refs[8:]
+    vis_ref, wave_refs, piece_refs = refs[0], refs[1:3], refs[3:7]
+    out_hbm, gain_out_ref, out_s, model_s, sems = refs[7:]
     pairs = wave_refs[0].shape[3]
     mine = lax.bitwise_and(me_ref[0], 3)
     for d, piece in enumerate(piece_refs):
@@ -350,8 +351,8 @@
                             one, two = (waves[s][slot] * model_s[t + 2 * s, 3 * k + slot:3 * k + slot + 1, lanes]
                                         for s in range(2))
                             sums.append(one + two)
-                        vr = vis_refs[t][0, k, rows, lanes].astype(F32)
-                        vi = vis_refs[t][1, k, rows, lanes].astype(F32)
+                        vr = vis_ref[0, t, k, rows, lanes].astype(F32)
+                        vi = vis_ref[1, t, k, rows, lanes].astype(F32)
                         out_s[0, t, k, rows, lanes] = (vr - (sums[0] - sums[2])).astype(BF16)
                         out_s[1, t, k, rows, lanes] = (vi - (sums[0] + sums[1])).astype(BF16)
 
@@ -370,10 +371,14 @@
     return lax.ppermute(value, "sub", [(i, i ^ bits) for i in range(count)])
 
 
-def from_both_sides(value, shift):
+def from_both_sides(value, reach):
     count = lax.axis_size("sub")
-    return [lax.ppermute(value, "sub", [(i, i + move) for i in range(count) if 0 <= i + move < count])
-            for move in (shift, -shift)]
+    pairings = [[], []]
+    for i in range(count):
+        for pairing, other in enumerate(((i // reach) ^ 1, ((i // reach + 1) ^ 1) - 1)):
+            if 0 <= other < count // reach:
+                pairings[pairing].append((i, other * reach + i % reach))
+    return [lax.ppermute(value, "sub", pairing) for pairing in pairings]
 
 
 def smem():
@@ -403,44 +408,43 @@
         out_shape = [
             shape(2, 2, width, pairs),
             jax.ShapeDtypeStruct((2, 2, width, pairs), BF16),
-            jax.ShapeDtypeStruct((2, 4, width, pairs), BF16),
         ]
         if t == 0:
-            operands = (me, turned, delays, flags)
+            operands = (me, delays, flags)
             out_shape += [jax.ShapeDtypeStruct(flags.shape, flags.dtype),
                           jax.ShapeDtypeStruct((2, ROWS, pairs), BF16)]
         else:
-            operands = (me, turned, delays, windows.reshape(1, window_count))
+            operands = (me, delays, windows.reshape(1, window_count))
             out_shape += [shape(window_count, width), shape(width, window_count),
                           shape(remote_rows, width), shape(2, window_count, 128)]
         made.append(pl.pallas_call(
             lambda *refs: phase_kernel(width, t, reach, *refs),
-            in_specs=[smem(), hbm_ref] + [vmem_ref] * (len(operands) - 2),
+            in_specs=[smem()] + [vmem_ref] * (len(operands) - 1),
             out_specs=[vmem_ref] * len(out_shape),
             out_shape=out_shape,
-            scratch_shapes=[pltpu.SemaphoreType.DMA],
-            compiler_params=pltpu.CompilerParams(vmem_limit_bytes=GRANTS[t] * 2 ** 20),
+            compiler_params=params,
             cost_estimate=pl.CostEstimate(flops=10 ** 7, bytes_accessed=6 * 2 ** 20, transcendentals=0),
             name="phases",
         )(*operands))
         if t == 0:
-            gathered = jnp.concatenate([made[0][3]] + beside, axis=0)
+            gathered = jnp.concatenate([made[0][2]] + beside, axis=0)
             while gathered.shape[0] < reach:
                 stride = gathered.shape[0]
                 gathered = jnp.concatenate([gathered] + [partner(gathered, stride * d) for d in range(1, 4)], axis=0)
             gathered = [gathered] + from_both_sides(gathered, reach)
-    waves, mixing, held = ([part[i] for part in made] for i in range(3))
-    masks = made[1][3:]
-    hots = made[0][4]
-    quarters = pl.pallas_call(
+    waves, mixing = ([part[i] for part in made] for i in range(2))
+    masks = made[1][2:]
+    hots = made[0][3]
+    *quarters, held = pl.pallas_call(
         lambda *refs: sums_kernel(width, reach, *refs),
-        in_specs=[smem()] + [vmem_ref] * 14,
-        out_specs=[vmem_ref] * 4,
-        out_shape=[jax.ShapeDtypeStruct((4, 2, pairs), F32)] * 4,
-        scratch_shapes=[vmem(2, width, 128), vmem(2, 2, width, pairs), vmem(2, remote_rows, width)],
-        compiler_params=params,
+        in_specs=[smem()] + [vmem_ref] * 8 + [hbm_ref] + [vmem_ref] * 4,
+        out_specs=[vmem_ref] * 5,
+        out_shape=[jax.ShapeDtypeStruct((4, 2, pairs), F32)] * 4 + [jax.ShapeDtypeStruct(turned.shape, BF16)],
+        scratch_shapes=[vmem(2, width, 128), vmem(2, 2, width, pairs), vmem(2, remote_rows, width),
+                        pltpu.SemaphoreType.DMA((2,))],
+        compiler_params=pltpu.CompilerParams(vmem_limit_bytes=GRANT * 2 ** 20),
         name="window_sums",
-    )(me, *gathered, *masks, delays, *held, *waves, *mixing)
+    )(me, *gathered, *masks, delays, turned, *waves, *mixing)
     pieces = [quarters[0]] + [partner(quarters[d], d) for d in range(1, 4)]
     stride = 4
     while stride < count:
@@ -459,7 +463,7 @@
     model = [model] + [partner(model, d) for d in range(1, 4)]
     cleaned, gains = pl.pallas_call(
         lambda *refs: clean_kernel(width, *refs),
-        in_specs=[smem()] + [vmem_ref] * 8,
+        in_specs=[smem()] + [vmem_ref] * 7,
         out_specs=[hbm_ref, vmem_ref],
         out_shape=[
             jax.ShapeDtypeStruct(turned.shape, BF16),
@@ -472,7 +476,7 @@
         ],
         compiler_params=params,
         name="clean",
-    )(me, *held, *waves, *model)
+    )(me, held, *waves, *model)
     return jnp.transpose(cleaned, (0, 1, 2, 4, 3)), gains
 
 

time: 45.4 us -> 44 us (0.969)
  local copies, waits for them, and re-layouts: 1.43 us -> 2.77 us
  waiting for transfers between devices: 9.51 us -> 8.43 us
  starting transfers between devices: 17.5 us -> 16.6 us
  Pallas kernels: 15.9 us -> 15.1 us
    pallas_call x2, Pallas kernels: 3.37 us -> 1.84 us  [local(): pl.pallas_call(lambda *refs: phase_kernel(width, t, reach, *refs), in_spe...]
    unnamed x11 -> x13, local copies, waits for them, and re-layouts: 1.42 us -> 2.77 us
    ppermute x12, waiting for transfers between devices: 9.51 us -> 8.42 us  [partner(): return lax.ppermute(value, 'sub', [(i, i ^ bits) for i in range(count)])]
    pallas_call x1, Pallas kernels: 5.64 us -> 6.41 us  [local(): pl.pallas_call(lambda *refs: sums_kernel(width, reach, *refs), in_specs=[...]
    ppermute x2, starting transfers between devices: 5.84 us -> 5.12 us  [from_both_sides(): return [lax.ppermute(value, 'sub', pairing) for pairing in pairings]]
  transfers between devices with their start and end apart: 14 -> 14, of which waited for: 6 -> 8; matrix products, arithmetic and copies ran while one was open for 0% -> 0% of each run, Pallas kernels for 7% -> 4%
where the time goes in v7:
time: 44 us; the launch traced here: 43.6 us
  starting transfers between devices  16.6 us (38%)
  Pallas kernels  15.1 us (34%)
  waiting for transfers between devices  8.43 us (19%)
  local copies, waits for them, and re-layouts  2.77 us (6%)
  between operations  0.73 us (2%)
    ppermute x12, starting transfers between devices, partner(): return lax.ppermute(value, 'sub', [(i, i ^ bits) for i in range(count)])  11.5 us
    ppermute x12, waiting for transfers between devices, partner(): return lax.ppermute(value, 'sub', [(i, i ^ bits) for i in range(count)])  8.42 us
    pallas_call x1, Pallas kernels, local(): pl.pallas_call(lambda *refs: sums_kernel(width, reach, *refs), in_specs=[...  6.41 us
    ppermute x2, starting transfers between devices, from_both_sides(): return [lax.ppermute(value, 'sub', pairing) for pairing in pairings]  5.12 us
    pallas_call x1, Pallas kernels, local(): pl.pallas_call(lambda *refs: clean_kernel(width, *refs), in_specs=[smem()...  4.8 us
    unnamed x13, local copies, waits for them, and re-layouts  2.77 us
    pallas_call x1, Pallas kernels, local(): pl.pallas_call(lambda *refs: solve_kernel(float(window_count), *refs), in...  2.07 us
    pallas_call x2, Pallas kernels, local(): pl.pallas_call(lambda *refs: phase_kernel(width, t, reach, *refs), in_spe...  1.84 us
  transfers between devices with their start and end apart: 14, of which 8 were waited for; matrix products, arithmetic and copies ran while one was open for 0% of the time, Pallas kernels for 4%

profile of v7, /device:TPU:0, one launch (start us, length us, event | category | flops | bytes accessed | tf_op | source)
XLA Modules:
  0.0 43.6 jit_solution(1927805384539638675)
XLA Ops:
  0.6 2.5 %collective-permute-start.2 = (s32[1,2,192]{2,1,0:T(2,128)}, s32[1,2,192]{2,1,0:T(2,128)S(1)}, u32[]{:S(2)}, u32[]{:S(2)}) collective-permute-start(s32[1,2,192]{2,1,0:T(2,128)} %bitcast.15), channel_id=1, source_target_pairs={{0,3},{1,2},{2,1},{3,0},{4,7},{5,6},{6,5},{7,4},{8,11},{9,10},{10,... | collective-permute-start | bytes 4616 | tf_op jit(solution)/shard_map/ppermute | solution.py:371
  3.1 0.6 %collective-permute-start.1 = (s32[1,2,192]{2,1,0:T(2,128)}, s32[1,2,192]{2,1,0:T(2,128)S(1)}, u32[]{:S(2)}, u32[]{:S(2)}) collective-permute-start(s32[1,2,192]{2,1,0:T(2,128)} %bitcast.16), channel_id=1, source_target_pairs={{0,2},{1,3},{2,0},{3,1},{4,6},{5,7},{6,4},{7,5},{8,10},{9,11},{10,... | collective-permute-start | bytes 4616 | tf_op jit(solution)/shard_map/ppermute | solution.py:371
  3.7 0.0 collective-permute-start
  3.8 0.0 copy-start
  3.8 0.7 %copy-done = f32[2,2,703]{2,1,0:T(2,128)S(1)} copy-done((f32[2,2,703]{2,1,0:T(2,128)S(1)}, f32[2,2,703]{2,1,0:T(2,128)}, u32[]{:S(2)}) %copy-start) | copy-done | bytes 11272
  4.5 0.0 copy-start.3
  4.5 0.7 %copy-done.3 = s32[2,192]{1,0:T(2,128)S(1)} copy-done((s32[2,192]{1,0:T(2,128)S(1)}, s32[2,192]{1,0:T(2,128)}, u32[]{:S(2)}) %copy-start.3) | copy-done | bytes 1560
  5.2 0.9 %phases.2 = (f32[2,2,192,703]{3,2,1,0:T(8,128)S(1)}, bf16[2,2,192,703]{3,2,1,0:T(8,128)(2,1)S(1)}, s32[1,2,192]{2,1,0:T(2,128)S(1)}, bf16[2,40,703]{2,1,0:T(8,128)(2,1)S(1)}) custom-call(s32[1]{0:T(128)} %bitcast.refs_0_, f32[2,2,703]{2,1,0:T(2,128)S(1)} %copy-done, s32[1,2,192]{2,1,0:T(2,128)S(1)} %bitcast.18), custom_call_target="tpu_custom_call" | custom-call | flops 10000000 | bytes 6291456 | tf_op jit(solution)/shard_map/phases/pallas_call | solution.py:420
  6.1 0.0 collective-permute-done
  6.1 0.8 %collective-permute-done.1 = s32[1,2,192]{2,1,0:T(2,128)S(1)} collective-permute-done((s32[1,2,192]{2,1,0:T(2,128)}, s32[1,2,192]{2,1,0:T(2,128)S(1)}, u32[]{:S(2)}, u32[]{:S(2)}) %collective-permute-start.1) | collective-permute-done | bytes 1568 | tf_op jit(solution)/shard_map/ppermute | solution.py:371
  6.9 0.0 collective-permute-done.2
  6.9 0.7 %collective-permute-start.4 = (s32[4,2,192]{2,1,0:T(2,128)S(1)}, s32[4,2,192]{2,1,0:T(2,128)S(1)}, u32[]{:S(2)}, u32[]{:S(2)}) collective-permute-start(s32[4,2,192]{2,1,0:T(2,128)S(1)} %constant_dynamic-update-slice_fusion.refs_1_), channel_id=1, source_target_pairs={{4,8},{5,9},{6,10},{7,11},{8,4},{9,5},{10,6},{11,7},{20,24},{21,25... | collective-permute-start | bytes 18440 | tf_op jit(solution)/shard_map/ppermute | solution.py:381
  7.6 4.5 %collective-permute-start.3 = (s32[4,2,192]{2,1,0:T(2,128)S(1)}, s32[4,2,192]{2,1,0:T(2,128)S(1)}, u32[]{:S(2)}, u32[]{:S(2)}) collective-permute-start(s32[4,2,192]{2,1,0:T(2,128)S(1)} %constant_dynamic-update-slice_fusion.refs_1_), channel_id=1, source_target_pairs={{0,4},{1,5},{2,6},{3,7},{4,0},{5,1},{6,2},{7,3},{8,12},{9,13},{10,... | collective-permute-start | bytes 18440 | tf_op jit(solution)/shard_map/ppermute | solution.py:381
  12.0 0.0 copy-start.4
  12.0 0.7 %copy-done.4 = s32[32]{0:T(128)S(1)} copy-done((s32[32]{0:T(128)S(1)}, s32[32]{0:T(128)}, u32[]{:S(2)}) %copy-start.4) | copy-done | bytes 152
  12.7 1.0 %phases.3 = (f32[2,2,192,703]{3,2,1,0:T(8,128)S(1)}, bf16[2,2,192,703]{3,2,1,0:T(8,128)(2,1)S(1)}, f32[32,192]{1,0:T(8,128)S(1)}, f32[192,32]{1,0:T(8,128)S(1)},...) custom-call(s32[1]{0:T(128)} %bitcast.refs_0_, f32[2,2,703]{2,1,0:T(2,128)S(1)} %copy-done, s32[1,32]{1,0:T(1,128)S(1)} %bitcast.19), custom_call_target="tpu_custom_call" | custom-call | flops 10000000 | bytes 6291456 | tf_op jit(solution)/shard_map/phases/pallas_call | solution.py:420
  13.7 0.0 collective-permute-done.4.refs_3_
  13.7 0.0 collective-permute-done.3.refs_2_
  13.7 0.0 copy-start.1
  13.7 0.7 %copy-done.1 = f32[2,2,703]{2,1,0:T(2,128)S(1)} copy-done((f32[2,2,703]{2,1,0:T(2,128)S(1)}, f32[2,2,703]{2,1,0:T(2,128)}, u32[]{:S(2)}) %copy-start.1) | copy-done | bytes 11272
  14.4 0.0 copy-start.2
  14.4 6.4 %window_sums.1 = (f32[4,2,703]{2,1,0:T(2,128)S(1)}, f32[4,2,703]{2,1,0:T(2,128)S(1)}, f32[4,2,703]{2,1,0:T(2,128)S(1)}, f32[4,2,703]{2,1,0:T(2,128)S(1)}, bf16[2,2,4,192,703]{4,3,2,1,0:T(8,128)(2,1)S(1)}) custom-call(s32[1]{0:T(128)} %bitcast.refs_0_, s32[4,2,192]{2,1,0:T(2,128)S(1)} %constant_dynamic-update-slice_fusion.refs_1_, ...), custom_call_target="tpu_custom_call" | custom-call | tf_op jit(solution)/shard_map/window_sums/pallas_call | solution.py:438
  20.8 0.1 collective-permute-start.5
  20.9 1.0 %collective-permute-start.6 = (f32[4,2,703]{2,1,0:T(2,128)S(1)}, f32[4,2,703]{2,1,0:T(2,128)S(1)}, u32[]{:S(2)}, u32[]{:S(2)}) collective-permute-start(f32[4,2,703]{2,1,0:T(2,128)S(1)} %get-tuple-element.32), channel_id=1, source_target_pairs={{0,2},{1,3},{2,0},{3,1},{4,6},{5,7},{6,4},{7,5},{8,10},{9,11},{10,... | collective-permute-start | bytes 67496 | tf_op jit(solution)/shard_map/ppermute | solution.py:371
  21.9 0.8 %collective-permute-start.7 = (f32[4,2,703]{2,1,0:T(2,128)S(1)}, f32[4,2,703]{2,1,0:T(2,128)S(1)}, u32[]{:S(2)}, u32[]{:S(2)}) collective-permute-start(f32[4,2,703]{2,1,0:T(2,128)S(1)} %get-tuple-element.33), channel_id=1, source_target_pairs={{0,3},{1,2},{2,1},{3,0},{4,7},{5,6},{6,5},{7,4},{8,11},{9,10},{10,... | collective-permute-start | bytes 67496 | tf_op jit(solution)/shard_map/ppermute | solution.py:371
  22.7 0.0 collective-permute-done.5
  22.8 2.0 %collective-permute-done.6 = f32[4,2,703]{2,1,0:T(2,128)S(1)} collective-permute-done((f32[4,2,703]{2,1,0:T(2,128)S(1)}, f32[4,2,703]{2,1,0:T(2,128)S(1)}, u32[]{:S(2)}, u32[]{:S(2)}) %collective-permute-start.6) | collective-permute-done | bytes 22528 | tf_op jit(solution)/shard_map/ppermute | solution.py:371
  24.8 0.4 collective-permute-done.7
  25.2 1.4 %collective-permute-start.10 = (f32[4,2,703]{2,1,0:T(2,128)S(1)}, f32[4,2,703]{2,1,0:T(2,128)S(1)}, u32[]{:S(2)}, u32[]{:S(2)}) collective-permute-start(f32[4,2,703]{2,1,0:T(2,128)S(1)} %bitcast.10), channel_id=1, source_target_pairs={{0,12},{1,13},{2,14},{3,15},{4,8},{5,9},{6,10},{7,11},{8,4},{9,5},... | collective-permute-start | bytes 67496 | tf_op jit(solution)/shard_map/ppermute | solution.py:371
  26.6 2.1 %collective-permute-start.9 = (f32[4,2,703]{2,1,0:T(2,128)S(1)}, f32[4,2,703]{2,1,0:T(2,128)S(1)}, u32[]{:S(2)}, u32[]{:S(2)}) collective-permute-start(f32[4,2,703]{2,1,0:T(2,128)S(1)} %bitcast.11), channel_id=1, source_target_pairs={{0,8},{1,9},{2,10},{3,11},{4,12},{5,13},{6,14},{7,15},{8,0},{9,1},... | collective-permute-start | bytes 67496 | tf_op jit(solution)/shard_map/ppermute | solution.py:371
  28.7 0.9 %collective-permute-start.8 = (f32[4,2,703]{2,1,0:T(2,128)S(1)}, f32[4,2,703]{2,1,0:T(2,128)S(1)}, u32[]{:S(2)}, u32[]{:S(2)}) collective-permute-start(f32[4,2,703]{2,1,0:T(2,128)S(1)} %bitcast.12), channel_id=1, source_target_pairs={{0,4},{1,5},{2,6},{3,7},{4,0},{5,1},{6,2},{7,3},{8,12},{9,13},{10,... | collective-permute-start | bytes 67496 | tf_op jit(solution)/shard_map/ppermute | solution.py:371
  29.6 1.6 %collective-permute-done.10.refs_6_ = f32[4,2,703]{2,1,0:T(2,128)S(1)} collective-permute-done((f32[4,2,703]{2,1,0:T(2,128)S(1)}, f32[4,2,703]{2,1,0:T(2,128)S(1)}, u32[]{:S(2)}, u32[]{:S(2)}) %collective-permute-start.10) | collective-permute-done | bytes 22528 | tf_op jit(solution)/shard_map/ppermute | solution.py:371
  31.2 0.3 collective-permute-done.9.refs_5_
  31.5 1.1 %collective-permute-done.8.refs_4_ = f32[4,2,703]{2,1,0:T(2,128)S(1)} collective-permute-done((f32[4,2,703]{2,1,0:T(2,128)S(1)}, f32[4,2,703]{2,1,0:T(2,128)S(1)}, u32[]{:S(2)}, u32[]{:S(2)}) %collective-permute-start.8) | collective-permute-done | bytes 22528 | tf_op jit(solution)/shard_map/ppermute | solution.py:371
  32.6 0.0 copy-done.2
  32.6 2.1 %gain_solve.1.refs_4_ = f32[4,2,806]{2,1,0:T(2,128)S(1)} custom-call(s32[1]{0:T(128)} %bitcast.refs_0_, s32[2,2]{1,0:T(2,128)S(1)} %copy-done.2, bf16[2,40,703]{2,1,0:T(8,128)(2,1)S(1)} %get-tuple-element.29.refs_2_, f32[4,2,703]{2,1,0:T(2,128)S(1)} %bitcast.13, f32[4,2,703]{2,1,0:T(2,128)S(1)} %collective-permute-done.8.refs_4_, ...), custom_call_target="tpu_custom_call" | custom-call | tf_op jit(solution)/shard_map/gain_solve/pallas_call | solution.py:455
  34.6 0.1 collective-permute-start.13
  34.7 1.1 %collective-permute-start.12 = (f32[4,2,806]{2,1,0:T(2,128)S(1)}, f32[4,2,806]{2,1,0:T(2,128)S(1)}, u32[]{:S(2)}, u32[]{:S(2)}) collective-permute-start(f32[4,2,806]{2,1,0:T(2,128)S(1)} %gain_solve.1.refs_4_), channel_id=1, source_target_pairs={{0,2},{1,3},{2,0},{3,1},{4,6},{5,7},{6,4},{7,5},{8,10},{9,11},{10,... | collective-permute-start | bytes 77384 | tf_op jit(solution)/shard_map/ppermute | solution.py:371
  35.8 0.7 %collective-permute-start.11 = (f32[4,2,806]{2,1,0:T(2,128)S(1)}, f32[4,2,806]{2,1,0:T(2,128)S(1)}, u32[]{:S(2)}, u32[]{:S(2)}) collective-permute-start(f32[4,2,806]{2,1,0:T(2,128)S(1)} %gain_solve.1.refs_4_), channel_id=1, source_target_pairs={{0,1},{1,0},{2,3},{3,2},{4,5},{5,4},{6,7},{7,6},{8,9},{9,8},{10,11... | collective-permute-start | bytes 77384 | tf_op jit(solution)/shard_map/ppermute | solution.py:371
  36.6 1.4 %collective-permute-done.13.refs_7_ = f32[4,2,806]{2,1,0:T(2,128)S(1)} collective-permute-done((f32[4,2,806]{2,1,0:T(2,128)S(1)}, f32[4,2,806]{2,1,0:T(2,128)S(1)}, u32[]{:S(2)}, u32[]{:S(2)}) %collective-permute-start.13) | collective-permute-done | bytes 25824 | tf_op jit(solution)/shard_map/ppermute | solution.py:371
  38.0 0.8 %collective-permute-done.12.refs_6_ = f32[4,2,806]{2,1,0:T(2,128)S(1)} collective-permute-done((f32[4,2,806]{2,1,0:T(2,128)S(1)}, f32[4,2,806]{2,1,0:T(2,128)S(1)}, u32[]{:S(2)}, u32[]{:S(2)}) %collective-permute-start.12) | collective-permute-done | bytes 25824 | tf_op jit(solution)/shard_map/ppermute | solution.py:371
  38.8 0.0 collective-permute-done.11.refs_5_
  38.8 4.8 %clean.1 = (bf16[2,2,4,192,703]{4,3,2,1,0:T(8,128)(2,1)}, f32[2,2,2,4,38]{4,3,2,1,0:T(4,128)}) custom-call(s32[1]{0:T(128)} %bitcast.refs_0_, bf16[2,2,4,192,703]{4,3,2,1,0:T(8,128)(2,1)S(1)} %get-tuple-element.28.refs_1_, f32[2,2,192,703]{3,2,1,0:T(8,128)S(1)} %get-tuple-element.24.refs_10_.refs_2_, ...), custom_call_target="tpu_custom_call" | custom-call | tf_op jit(solution)/shard_map/clean/pallas_call | solution.py:464
  (5 shorter events, 0.0 us)
Async XLA Ops:
  0.6 6.3 %collective-permute-start.2 = (s32[1,2,192]{2,1,0:T(2,128)}, s32[1,2,192]{2,1,0:T(2,128)S(1)}, u32[]{:S(2)}, u32[]{:S(2)}) collective-permute-start(s32[1,2,192]{2,1,0:T(2,128)} %bitcast.15), channel_id=1, source_target_pairs={{0,3},{1,2},{2,1},{3,0},{4,7},{5,6},{6,5},{7,4},{8,11},{9,10},{10,... | collective-permute-start | bytes 4616 | tf_op jit(solution)/shard_map/ppermute | solution.py:371
  3.1 3.8 %collective-permute-start.1 = (s32[1,2,192]{2,1,0:T(2,128)}, s32[1,2,192]{2,1,0:T(2,128)S(1)}, u32[]{:S(2)}, u32[]{:S(2)}) collective-permute-start(s32[1,2,192]{2,1,0:T(2,128)} %bitcast.16), channel_id=1, source_target_pairs={{0,2},{1,3},{2,0},{3,1},{4,6},{5,7},{6,4},{7,5},{8,10},{9,11},{10,... | collective-permute-start | bytes 4616 | tf_op jit(solution)/shard_map/ppermute | solution.py:371
  3.7 2.3 %collective-permute-start = (s32[1,2,192]{2,1,0:T(2,128)}, s32[1,2,192]{2,1,0:T(2,128)S(1)}, u32[]{:S(2)}, u32[]{:S(2)}) collective-permute-start(s32[1,2,192]{2,1,0:T(2,128)} %bitcast.17), channel_id=1, source_target_pairs={{0,1},{1,0},{2,3},{3,2},{4,5},{5,4},{6,7},{7,6},{8,9},{9,8},{10,11... | collective-permute-start | bytes 4616 | tf_op jit(solution)/shard_map/ppermute | solution.py:371
  3.8 0.7 %copy-start = (f32[2,2,703]{2,1,0:T(2,128)S(1)}, f32[2,2,703]{2,1,0:T(2,128)}, u32[]{:S(2)}) copy-start(f32[2,2,703]{2,1,0:T(2,128)} %refs_8_.1) | copy-start | bytes 33748
  4.5 0.7 %copy-start.3 = (s32[2,192]{1,0:T(2,128)S(1)}, s32[2,192]{1,0:T(2,128)}, u32[]{:S(2)}) copy-start(s32[2,192]{1,0:T(2,128)} %param.7) | copy-start | bytes 4612
  6.9 6.7 %collective-permute-start.4 = (s32[4,2,192]{2,1,0:T(2,128)S(1)}, s32[4,2,192]{2,1,0:T(2,128)S(1)}, u32[]{:S(2)}, u32[]{:S(2)}) collective-permute-start(s32[4,2,192]{2,1,0:T(2,128)S(1)} %constant_dynamic-update-slice_fusion.refs_1_), channel_id=1, source_target_pairs={{4,8},{5,9},{6,10},{7,11},{8,4},{9,5},{10,6},{11,7},{20,24},{21,25... | collective-permute-start | bytes 18440 | tf_op jit(solution)/shard_map/ppermute | solution.py:381
  7.6 6.1 %collective-permute-start.3 = (s32[4,2,192]{2,1,0:T(2,128)S(1)}, s32[4,2,192]{2,1,0:T(2,128)S(1)}, u32[]{:S(2)}, u32[]{:S(2)}) collective-permute-start(s32[4,2,192]{2,1,0:T(2,128)S(1)} %constant_dynamic-update-slice_fusion.refs_1_), channel_id=1, source_target_pairs={{0,4},{1,5},{2,6},{3,7},{4,0},{5,1},{6,2},{7,3},{8,12},{9,13},{10,... | collective-permute-start | bytes 18440 | tf_op jit(solution)/shard_map/ppermute | solution.py:381
  12.0 0.7 %copy-start.4 = (s32[32]{0:T(128)S(1)}, s32[32]{0:T(128)}, u32[]{:S(2)}) copy-start(s32[32]{0:T(128)} %param.8) | copy-start | bytes 388
  13.7 0.7 %copy-start.1 = (f32[2,2,703]{2,1,0:T(2,128)S(1)}, f32[2,2,703]{2,1,0:T(2,128)}, u32[]{:S(2)}) copy-start(f32[2,2,703]{2,1,0:T(2,128)} %refs_8_.1) | copy-start | bytes 33748
  14.4 18.2 %copy-start.2 = (s32[2,2]{1,0:T(2,128)S(1)}, s32[2,2]{1,0:T(2,128)}, u32[]{:S(2)}) copy-start(s32[2,2]{1,0:T(2,128)} %refs_1_.5) | copy-start | bytes 52
  20.8 1.9 %collective-permute-start.5 = (f32[4,2,703]{2,1,0:T(2,128)S(1)}, f32[4,2,703]{2,1,0:T(2,128)S(1)}, u32[]{:S(2)}, u32[]{:S(2)}) collective-permute-start(f32[4,2,703]{2,1,0:T(2,128)S(1)} %get-tuple-element.31), channel_id=1, source_target_pairs={{0,1},{1,0},{2,3},{3,2},{4,5},{5,4},{6,7},{7,6},{8,9},{9,8},{10,11... | collective-permute-start | bytes 67496 | tf_op jit(solution)/shard_map/ppermute | solution.py:371
  20.9 3.9 %collective-permute-start.6 = (f32[4,2,703]{2,1,0:T(2,128)S(1)}, f32[4,2,703]{2,1,0:T(2,128)S(1)}, u32[]{:S(2)}, u32[]{:S(2)}) collective-permute-start(f32[4,2,703]{2,1,0:T(2,128)S(1)} %get-tuple-element.32), channel_id=1, source_target_pairs={{0,2},{1,3},{2,0},{3,1},{4,6},{5,7},{6,4},{7,5},{8,10},{9,11},{10,... | collective-permute-start | bytes 67496 | tf_op jit(solution)/shard_map/ppermute | solution.py:371
  21.9 3.3 %collective-permute-start.7 = (f32[4,2,703]{2,1,0:T(2,128)S(1)}, f32[4,2,703]{2,1,0:T(2,128)S(1)}, u32[]{:S(2)}, u32[]{:S(2)}) collective-permute-start(f32[4,2,703]{2,1,0:T(2,128)S(1)} %get-tuple-element.33), channel_id=1, source_target_pairs={{0,3},{1,2},{2,1},{3,0},{4,7},{5,6},{6,5},{7,4},{8,11},{9,10},{10,... | collective-permute-start | bytes 67496 | tf_op jit(solution)/shard_map/ppermute | solution.py:371
  25.2 6.0 %collective-permute-start.10 = (f32[4,2,703]{2,1,0:T(2,128)S(1)}, f32[4,2,703]{2,1,0:T(2,128)S(1)}, u32[]{:S(2)}, u32[]{:S(2)}) collective-permute-start(f32[4,2,703]{2,1,0:T(2,128)S(1)} %bitcast.10), channel_id=1, source_target_pairs={{0,12},{1,13},{2,14},{3,15},{4,8},{5,9},{6,10},{7,11},{8,4},{9,5},... | collective-permute-start | bytes 67496 | tf_op jit(solution)/shard_map/ppermute | solution.py:371
  26.6 4.9 %collective-permute-start.9 = (f32[4,2,703]{2,1,0:T(2,128)S(1)}, f32[4,2,703]{2,1,0:T(2,128)S(1)}, u32[]{:S(2)}, u32[]{:S(2)}) collective-permute-start(f32[4,2,703]{2,1,0:T(2,128)S(1)} %bitcast.11), channel_id=1, source_target_pairs={{0,8},{1,9},{2,10},{3,11},{4,12},{5,13},{6,14},{7,15},{8,0},{9,1},... | collective-permute-start | bytes 67496 | tf_op jit(solution)/shard_map/ppermute | solution.py:371
  28.7 3.8 %collective-permute-start.8 = (f32[4,2,703]{2,1,0:T(2,128)S(1)}, f32[4,2,703]{2,1,0:T(2,128)S(1)}, u32[]{:S(2)}, u32[]{:S(2)}) collective-permute-start(f32[4,2,703]{2,1,0:T(2,128)S(1)} %bitcast.12), channel_id=1, source_target_pairs={{0,4},{1,5},{2,6},{3,7},{4,0},{5,1},{6,2},{7,3},{8,12},{9,13},{10,... | collective-permute-start | bytes 67496 | tf_op jit(solution)/shard_map/ppermute | solution.py:371
  34.6 3.4 %collective-permute-start.13 = (f32[4,2,806]{2,1,0:T(2,128)S(1)}, f32[4,2,806]{2,1,0:T(2,128)S(1)}, u32[]{:S(2)}, u32[]{:S(2)}) collective-permute-start(f32[4,2,806]{2,1,0:T(2,128)S(1)} %gain_solve.1.refs_4_), channel_id=1, source_target_pairs={{0,3},{1,2},{2,1},{3,0},{4,7},{5,6},{6,5},{7,4},{8,11},{9,10},{10,... | collective-permute-start | bytes 77384 | tf_op jit(solution)/shard_map/ppermute | solution.py:371
  34.7 4.1 %collective-permute-start.12 = (f32[4,2,806]{2,1,0:T(2,128)S(1)}, f32[4,2,806]{2,1,0:T(2,128)S(1)}, u32[]{:S(2)}, u32[]{:S(2)}) collective-permute-start(f32[4,2,806]{2,1,0:T(2,128)S(1)} %gain_solve.1.refs_4_), channel_id=1, source_target_pairs={{0,2},{1,3},{2,0},{3,1},{4,6},{5,7},{6,4},{7,5},{8,10},{9,11},{10,... | collective-permute-start | bytes 77384 | tf_op jit(solution)/shard_map/ppermute | solution.py:371
  35.8 3.0 %collective-permute-start.11 = (f32[4,2,806]{2,1,0:T(2,128)S(1)}, f32[4,2,806]{2,1,0:T(2,128)S(1)}, u32[]{:S(2)}, u32[]{:S(2)}) collective-permute-start(f32[4,2,806]{2,1,0:T(2,128)S(1)} %gain_solve.1.refs_4_), channel_id=1, source_target_pairs={{0,1},{1,0},{2,3},{3,2},{4,5},{5,4},{6,7},{7,6},{8,9},{9,8},{10,11... | collective-permute-start | bytes 77384 | tf_op jit(solution)/shard_map/ppermute | solution.py:371

commit v8 on v7

--- a/solution.py
+++ b/solution.py
@@ -93,14 +93,18 @@
 def phase_kernel(width, t, reach, me_ref, *refs):
     anchor = me_ref[0].astype(F32) * float(width)
     if t == 0:
-        delay_ref, flag_ref, wave_ref, mix_ref, own_ref, hot_ref = refs
+        delay_ref, flag_ref, wave_ref, mix_ref, own_ref = refs
     else:
-        delay_ref, win_ref, wave_ref, mix_ref, *mask_refs = refs
+        delay_ref, win_ref, wave_ref, mix_ref, apart_ref, *mask_refs = refs
     if t == 0:
         own_ref[...] = flag_ref[...]
-        hot_ref[0], hot_ref[1] = station_hots(delay_ref.shape[2])
     else:
         window_masks(width, reach, me_ref[0], win_ref, *mask_refs)
+        apart = blocks_apart(me_ref[0], reach, apart_ref.shape[2])
+        for time in range(2):
+            gap = delay_ref[1, time:time + 1, :] - delay_ref[0, time:time + 1, :]
+            phase = sincos_turns(gap * (apart * np.float32(width / STEPS_PER_TURN)))
+            apart_ref[time, 0], apart_ref[time, 1] = phase
     pairs = delay_ref.shape[2]
 
     def waves(lanes, count):
@@ -127,10 +131,14 @@
     tiles(pairs, waves)
 
 
+def blocks_apart(me, reach, rows):
+    return iota((rows, 1), 0) - (lax.rem(me, reach) + reach).astype(F32)
+
+
 def window_masks(width, reach, me, win_ref, inside_ref, chosen_ref, outside_ref, ends_ref):
     anchor = me.astype(F32) * float(width)
     lowest = (me - lax.rem(me, reach) - reach).astype(F32)
-    windows = win_ref.shape[1]
+    windows = inside_ref.shape[0]
     final = anchor + float(width - 1)
     win_row = win_ref[...].astype(F32)
     sub, lane = iota((windows, windows), 0), iota((windows, windows), 1)
@@ -157,19 +165,18 @@
 
 def sums_kernel(width, reach, me_ref, *refs):
     flag_refs, refs = refs[:3], refs[3:]
-    inside_ref, chosen_ref, outside_ref, ends_ref, delay_ref = refs[:5]
+    apart_ref, inside_ref, chosen_ref, outside_ref, ends_ref = refs[:5]
     vis_hbm, wave_refs, mix_refs, refs = refs[5], refs[6:8], refs[8:10], refs[10:]
     out_refs, (vis_ref, alpha_s, mexp_s, wt_s, sems) = refs[:4], refs[4:]
     copies = [pltpu.make_async_copy(vis_hbm.at[:, t], vis_ref.at[:, t], sems.at[t]) for t in range(2)]
-    for copy in copies:
-        copy.start()
+    copies[0].start()
     me = me_ref[0]
     place = lax.rem(me, reach)
     windows = inside_ref.shape[0]
-    pairs = delay_ref.shape[2]
+    pairs = apart_ref.shape[3]
     sub, lane = iota((windows, windows), 0), iota((windows, windows), 1)
     first_c, last_c = ends_ref[0][:, :1], ends_ref[1][:, :1]
-    apart = iota((outside_ref.shape[0], 1), 0) - (place + reach).astype(F32)
+    apart = blocks_apart(me, reach, outside_ref.shape[0])
     diagonal = iota((width, width), 0) == iota((width, width), 1)
     wt_s[...] = jnp.zeros_like(wt_s)
 
@@ -178,8 +185,9 @@
                 jnp.sum(jnp.where(apart > 0.0, value, 0.0), axis=0, keepdims=True))
 
     for t in range(2):
-        odd = lax.rem(lax.div(me, reach), 2)
-        for group, side in enumerate((1, 2 - 2 * odd, 2 * odd)):
+        mine = lax.div(me, reach)
+        for group, other in enumerate((mine, lax.bitwise_xor(mine, 1), lax.bitwise_xor(mine, 3))):
+            side = jnp.where(jnp.abs(other - mine) > 1, 3, other - mine + 1)
             for slot in range(reach):
                 row = flag_refs[group][slot, t:t + 1, :].astype(F32)
                 wt_s[t, pl.ds(side * reach + lax.bitwise_xor(place, slot), 1), :] = 1.0 - row
@@ -196,9 +204,7 @@
         alpha_s[t] = jnp.broadcast_to(jnp.sum(chosen * scale_r, axis=1, keepdims=True), (width, 128))
         chosen = chosen.astype(BF16)
         sums = [dot(rows, mix_refs[t][slot, 0]) + dot(rows, mix_refs[t][slot, 1]) for slot in range(2)]
-        gap = delay_ref[1, t:t + 1, :] - delay_ref[0, t:t + 1, :]
-        phase = sincos_turns(gap * (apart * np.float32(width / STEPS_PER_TURN)))
-        away = times(phase, tuple(value[windows:] for value in sums))
+        away = times((apart_ref[t, 0], apart_ref[t, 1]), tuple(value[windows:] for value in sums))
         for slot in range(2):
             before, after = both_sides(away[slot])
             total = sums[slot][:windows] + first_c * before + last_c * after
@@ -246,6 +252,8 @@
                                 out_refs[d][k, ri:ri + 1, lanes] = found[k][ri]
 
         copies[t].wait()
+        if t == 0:
+            copies[1].start()
         tiles(pairs, main)
 
 
@@ -257,6 +265,10 @@
     partner_of = baseline + 1.0 + jnp.sum(first * (station - offset), axis=0, keepdims=True)
     second = jnp.where(partner_of == station, 1.0, 0.0)
     return first.astype(BF16), second.astype(BF16)
+
+
+def hots_kernel(hot_ref):
+    hot_ref[0], hot_ref[1] = station_hots(hot_ref.shape[2])
 
 
 def solve_kernel(window_count, me_ref, tracks_ref, hot_ref, *refs):
@@ -371,16 +383,6 @@
     return lax.ppermute(value, "sub", [(i, i ^ bits) for i in range(count)])
 
 
-def from_both_sides(value, reach):
-    count = lax.axis_size("sub")
-    pairings = [[], []]
-    for i in range(count):
-        for pairing, other in enumerate(((i // reach) ^ 1, ((i // reach + 1) ^ 1) - 1)):
-            if 0 <= other < count // reach:
-                pairings[pairing].append((i, other * reach + i % reach))
-    return [lax.ppermute(value, "sub", pairing) for pairing in pairings]
-
-
 def smem():
     return pl.BlockSpec(memory_space=pltpu.SMEM)
 
@@ -399,8 +401,16 @@
     flags = flags[None]
 
     reach = count // 4
-    remote_rows = 16 * pl.cdiv(3 * reach, 16)
-
+    remote_rows = 16 * pl.cdiv(4 * reach, 16)
+
+    hots = pl.pallas_call(
+        hots_kernel,
+        out_specs=vmem_ref,
+        out_shape=jax.ShapeDtypeStruct((2, ROWS, pairs), BF16),
+        compiler_params=params,
+        cost_estimate=pl.CostEstimate(flops=10 ** 7, bytes_accessed=6 * 2 ** 20, transcendentals=0),
+        name="station_hots",
+    )()
     made = []
     beside = [partner(flags, d) for d in range(1, 4)]
     for t in range(2):
@@ -411,11 +421,10 @@
         ]
         if t == 0:
             operands = (me, delays, flags)
-            out_shape += [jax.ShapeDtypeStruct(flags.shape, flags.dtype),
-                          jax.ShapeDtypeStruct((2, ROWS, pairs), BF16)]
+            out_shape += [jax.ShapeDtypeStruct(flags.shape, flags.dtype)]
         else:
             operands = (me, delays, windows.reshape(1, window_count))
-            out_shape += [shape(window_count, width), shape(width, window_count),
+            out_shape += [shape(2, 2, remote_rows, pairs), shape(window_count, width), shape(width, window_count),
                           shape(remote_rows, width), shape(2, window_count, 128)]
         made.append(pl.pallas_call(
             lambda *refs: phase_kernel(width, t, reach, *refs),
@@ -431,10 +440,9 @@
             while gathered.shape[0] < reach:
                 stride = gathered.shape[0]
                 gathered = jnp.concatenate([gathered] + [partner(gathered, stride * d) for d in range(1, 4)], axis=0)
-            gathered = [gathered] + from_both_sides(gathered, reach)
+            gathered = [gathered] + [partner(gathered, d * reach) for d in (1, 3)]
     waves, mixing = ([part[i] for part in made] for i in range(2))
     masks = made[1][2:]
-    hots = made[0][3]
     *quarters, held = pl.pallas_call(
         lambda *refs: sums_kernel(width, reach, *refs),
         in_specs=[smem()] + [vmem_ref] * 8 + [hbm_ref] + [vmem_ref] * 4,
@@ -444,7 +452,7 @@
                         pltpu.SemaphoreType.DMA((2,))],
         compiler_params=pltpu.CompilerParams(vmem_limit_bytes=GRANT * 2 ** 20),
         name="window_sums",
-    )(me, *gathered, *masks, delays, turned, *waves, *mixing)
+    )(me, *gathered, *masks, turned, *waves, *mixing)
     pieces = [quarters[0]] + [partner(quarters[d], d) for d in range(1, 4)]
     stride = 4
     while stride < count:

time: 44 us -> 42.5 us (0.966)
  starting transfers between devices: 16.6 us -> 15.1 us
  waiting for transfers between devices: 8.43 us -> 9.52 us
  local copies, waits for them, and re-layouts: 2.77 us -> 2.07 us
    ppermute x2 -> x0, starting transfers between devices: 5.12 us -> none  [from_both_sides(): return [lax.ppermute(value, 'sub', pairing) for pairing in pairings]]
    ppermute x12 -> x14, starting transfers between devices: 11.5 us -> 15.1 us  [partner(): return lax.ppermute(value, 'sub', [(i, i ^ bits) for i in range(count)])]
    ppermute x12 -> x14, waiting for transfers between devices: 8.42 us -> 9.52 us  [partner(): return lax.ppermute(value, 'sub', [(i, i ^ bits) for i in range(count)])]
    unnamed x13 -> x11, local copies, waits for them, and re-layouts: 2.77 us -> 2.07 us
  transfers between devices with their start and end apart: 14 -> 14, of which waited for: 8 -> 9; matrix products, arithmetic and copies ran while one was open for 0% -> 0% of each run, Pallas kernels for 4% -> 5%
where the time goes in v8:
time: 42.5 us; the launch traced here: 42.2 us
  starting transfers between devices  15.1 us (36%)
  Pallas kernels  14.8 us (35%)
  waiting for transfers between devices  9.52 us (22%)
  local copies, waits for them, and re-layouts  2.07 us (5%)
  between operations  0.71 us (2%)
    ppermute x14, starting transfers between devices, partner(): return lax.ppermute(value, 'sub', [(i, i ^ bits) for i in range(count)])  15.1 us
    ppermute x14, waiting for transfers between devices, partner(): return lax.ppermute(value, 'sub', [(i, i ^ bits) for i in range(count)])  9.52 us
    pallas_call x1, Pallas kernels, local(): pl.pallas_call(lambda *refs: sums_kernel(width, reach, *refs), in_specs=[...  5.98 us
    pallas_call x1, Pallas kernels, local(): pl.pallas_call(lambda *refs: clean_kernel(width, *refs), in_specs=[smem()...  4.82 us
    pallas_call x1, Pallas kernels, local(): pl.pallas_call(lambda *refs: solve_kernel(float(window_count), *refs), in...  2.07 us
    unnamed x11, local copies, waits for them, and re-layouts  2.07 us
    pallas_call x2, Pallas kernels, local(): pl.pallas_call(lambda *refs: phase_kernel(width, t, reach, *refs), in_spe...  1.85 us
  transfers between devices with their start and end apart: 14, of which 9 were waited for; matrix products, arithmetic and copies ran while one was open for 0% of the time, Pallas kernels for 5%

profile of v8, /device:TPU:0, one launch (start us, length us, event | category | flops | bytes accessed | tf_op | source)
XLA Modules:
  0.0 42.2 jit_solution(8161839341844258303)
XLA Ops:
  0.6 2.5 %collective-permute-start.2 = (s32[1,2,192]{2,1,0:T(2,128)}, s32[1,2,192]{2,1,0:T(2,128)S(1)}, u32[]{:S(2)}, u32[]{:S(2)}) collective-permute-start(s32[1,2,192]{2,1,0:T(2,128)} %bitcast.15), channel_id=1, source_target_pairs={{0,3},{1,2},{2,1},{3,0},{4,7},{5,6},{6,5},{7,4},{8,11},{9,10},{10,... | collective-permute-start | bytes 4616 | tf_op jit(solution)/shard_map/ppermute | solution.py:383
  3.1 0.6 %collective-permute-start.1 = (s32[1,2,192]{2,1,0:T(2,128)}, s32[1,2,192]{2,1,0:T(2,128)S(1)}, u32[]{:S(2)}, u32[]{:S(2)}) collective-permute-start(s32[1,2,192]{2,1,0:T(2,128)} %bitcast.16), channel_id=1, source_target_pairs={{0,2},{1,3},{2,0},{3,1},{4,6},{5,7},{6,4},{7,5},{8,10},{9,11},{10,... | collective-permute-start | bytes 4616 | tf_op jit(solution)/shard_map/ppermute | solution.py:383
  3.7 0.0 collective-permute-start
  3.8 0.0 copy-start.1
  3.8 0.7 %copy-done.1 = f32[2,2,703]{2,1,0:T(2,128)S(1)} copy-done((f32[2,2,703]{2,1,0:T(2,128)S(1)}, f32[2,2,703]{2,1,0:T(2,128)}, u32[]{:S(2)}) %copy-start.1) | copy-done | bytes 11272
  4.5 0.0 copy-start.2
  4.5 0.7 %copy-done.2 = s32[2,192]{1,0:T(2,128)S(1)} copy-done((s32[2,192]{1,0:T(2,128)S(1)}, s32[2,192]{1,0:T(2,128)}, u32[]{:S(2)}) %copy-start.2) | copy-done | bytes 1560
  5.2 0.8 %phases.2 = (f32[2,2,192,703]{3,2,1,0:T(8,128)S(1)}, bf16[2,2,192,703]{3,2,1,0:T(8,128)(2,1)S(1)}, s32[1,2,192]{2,1,0:T(2,128)S(1)}) custom-call(s32[1]{0:T(128)} %bitcast.refs_0_, f32[2,2,703]{2,1,0:T(2,128)S(1)} %copy-done.1, s32[1,2,192]{2,1,0:T(2,128)S(1)} %bitcast.18), custom_call_target="tpu_custom_call" | custom-call | flops 10000000 | bytes 6291456 | tf_op jit(solution)/shard_map/phases/pallas_call | solution.py:429
  6.0 0.0 collective-permute-done
  6.0 0.9 %collective-permute-done.1 = s32[1,2,192]{2,1,0:T(2,128)S(1)} collective-permute-done((s32[1,2,192]{2,1,0:T(2,128)}, s32[1,2,192]{2,1,0:T(2,128)S(1)}, u32[]{:S(2)}, u32[]{:S(2)}) %collective-permute-start.1) | collective-permute-done | bytes 1568 | tf_op jit(solution)/shard_map/ppermute | solution.py:383
  6.9 0.0 collective-permute-done.2
  6.9 3.7 %collective-permute-start.4 = (s32[4,2,192]{2,1,0:T(2,128)S(1)}, s32[4,2,192]{2,1,0:T(2,128)S(1)}, u32[]{:S(2)}, u32[]{:S(2)}) collective-permute-start(s32[4,2,192]{2,1,0:T(2,128)S(1)} %constant_dynamic-update-slice_fusion.refs_1_), channel_id=1, source_target_pairs={{0,12},{1,13},{2,14},{3,15},{4,8},{5,9},{6,10},{7,11},{8,4},{9,5},... | collective-permute-start | bytes 18440 | tf_op jit(solution)/shard_map/ppermute | solution.py:383
  10.6 0.0 collective-permute-start.3
  10.6 0.0 copy-start.3
  10.6 0.7 %copy-done.3 = s32[32]{0:T(128)S(1)} copy-done((s32[32]{0:T(128)S(1)}, s32[32]{0:T(128)}, u32[]{:S(2)}) %copy-start.3) | copy-done | bytes 152
  11.2 1.0 %phases.3 = (f32[2,2,192,703]{3,2,1,0:T(8,128)S(1)}, bf16[2,2,192,703]{3,2,1,0:T(8,128)(2,1)S(1)}, f32[2,2,16,703]{3,2,1,0:T(8,128)S(1)}, f32[32,192]{1,0:T(8,12...) custom-call(s32[1]{0:T(128)} %bitcast.refs_0_, f32[2,2,703]{2,1,0:T(2,128)S(1)} %copy-done.1, ...), custom_call_target="tpu_custom_call" | custom-call | flops 10000000 | bytes 6291456 | tf_op jit(solution)/shard_map/phases/pallas_call | solution.py:429
  12.3 0.2 collective-permute-done.4.refs_3_
  12.4 1.8 %collective-permute-done.3.refs_2_ = s32[4,2,192]{2,1,0:T(2,128)S(1)} collective-permute-done((s32[4,2,192]{2,1,0:T(2,128)S(1)}, s32[4,2,192]{2,1,0:T(2,128)S(1)}, u32[]{:S(2)}, u32[]{:S(2)}) %collective-permute-start.3) | collective-permute-done | bytes 6176 | tf_op jit(solution)/shard_map/ppermute | solution.py:383
  14.2 0.0 copy-start
  14.2 6.0 %window_sums.1 = (f32[4,2,703]{2,1,0:T(2,128)S(1)}, f32[4,2,703]{2,1,0:T(2,128)S(1)}, f32[4,2,703]{2,1,0:T(2,128)S(1)}, f32[4,2,703]{2,1,0:T(2,128)S(1)}, bf16[2,2,4,192,703]{4,3,2,1,0:T(8,128)(2,1)S(1)}) custom-call(s32[1]{0:T(128)} %bitcast.refs_0_, s32[4,2,192]{2,1,0:T(2,128)S(1)} %constant_dynamic-update-slice_fusion.refs_1_, ...), custom_call_target="tpu_custom_call" | custom-call | tf_op jit(solution)/shard_map/window_sums/pallas_call | solution.py:446
  20.2 0.1 collective-permute-start.5
  20.3 1.0 %collective-permute-start.6 = (f32[4,2,703]{2,1,0:T(2,128)S(1)}, f32[4,2,703]{2,1,0:T(2,128)S(1)}, u32[]{:S(2)}, u32[]{:S(2)}) collective-permute-start(f32[4,2,703]{2,1,0:T(2,128)S(1)} %get-tuple-element.32), channel_id=1, source_target_pairs={{0,2},{1,3},{2,0},{3,1},{4,6},{5,7},{6,4},{7,5},{8,10},{9,11},{10,... | collective-permute-start | bytes 67496 | tf_op jit(solution)/shard_map/ppermute | solution.py:383
  21.3 0.9 %collective-permute-start.7 = (f32[4,2,703]{2,1,0:T(2,128)S(1)}, f32[4,2,703]{2,1,0:T(2,128)S(1)}, u32[]{:S(2)}, u32[]{:S(2)}) collective-permute-start(f32[4,2,703]{2,1,0:T(2,128)S(1)} %get-tuple-element.33), channel_id=1, source_target_pairs={{0,3},{1,2},{2,1},{3,0},{4,7},{5,6},{6,5},{7,4},{8,11},{9,10},{10,... | collective-permute-start | bytes 67496 | tf_op jit(solution)/shard_map/ppermute | solution.py:383
  22.2 0.0 collective-permute-done.5
  22.2 2.0 %collective-permute-done.6 = f32[4,2,703]{2,1,0:T(2,128)S(1)} collective-permute-done((f32[4,2,703]{2,1,0:T(2,128)S(1)}, f32[4,2,703]{2,1,0:T(2,128)S(1)}, u32[]{:S(2)}, u32[]{:S(2)}) %collective-permute-start.6) | collective-permute-done | bytes 22528 | tf_op jit(solution)/shard_map/ppermute | solution.py:383
  24.2 0.4 collective-permute-done.7
  24.6 1.9 %collective-permute-start.10 = (f32[4,2,703]{2,1,0:T(2,128)S(1)}, f32[4,2,703]{2,1,0:T(2,128)S(1)}, u32[]{:S(2)}, u32[]{:S(2)}) collective-permute-start(f32[4,2,703]{2,1,0:T(2,128)S(1)} %bitcast.10), channel_id=1, source_target_pairs={{0,12},{1,13},{2,14},{3,15},{4,8},{5,9},{6,10},{7,11},{8,4},{9,5},... | collective-permute-start | bytes 67496 | tf_op jit(solution)/shard_map/ppermute | solution.py:383
  26.4 0.0 collective-permute-start.9
  26.4 2.6 %collective-permute-start.8 = (f32[4,2,703]{2,1,0:T(2,128)S(1)}, f32[4,2,703]{2,1,0:T(2,128)S(1)}, u32[]{:S(2)}, u32[]{:S(2)}) collective-permute-start(f32[4,2,703]{2,1,0:T(2,128)S(1)} %bitcast.12), channel_id=1, source_target_pairs={{0,4},{1,5},{2,6},{3,7},{4,0},{5,1},{6,2},{7,3},{8,12},{9,13},{10,... | collective-permute-start | bytes 67496 | tf_op jit(solution)/shard_map/ppermute | solution.py:383
  29.0 0.1 station_hots.1.refs_2_
  29.1 1.3 %collective-permute-done.10.refs_6_ = f32[4,2,703]{2,1,0:T(2,128)S(1)} collective-permute-done((f32[4,2,703]{2,1,0:T(2,128)S(1)}, f32[4,2,703]{2,1,0:T(2,128)S(1)}, u32[]{:S(2)}, u32[]{:S(2)}) %collective-permute-start.10) | collective-permute-done | bytes 22528 | tf_op jit(solution)/shard_map/ppermute | solution.py:383
  30.3 0.8 %collective-permute-done.9.refs_5_ = f32[4,2,703]{2,1,0:T(2,128)S(1)} collective-permute-done((f32[4,2,703]{2,1,0:T(2,128)S(1)}, f32[4,2,703]{2,1,0:T(2,128)S(1)}, u32[]{:S(2)}, u32[]{:S(2)}) %collective-permute-start.9) | collective-permute-done | bytes 22528 | tf_op jit(solution)/shard_map/ppermute | solution.py:383
  31.2 0.0 collective-permute-done.8.refs_4_
  31.2 0.0 copy-done
  31.2 2.1 %gain_solve.1.refs_4_ = f32[4,2,806]{2,1,0:T(2,128)S(1)} custom-call(s32[1]{0:T(128)} %bitcast.refs_0_, s32[2,2]{1,0:T(2,128)S(1)} %copy-done, bf16[2,40,703]{2,1,0:T(8,128)(2,1)S(1)} %station_hots.1.refs_2_, f32[4,2,703]{2,1,0:T(2,128)S(1)} %bitcast.13, f32[4,2,703]{2,1,0:T(2,128)S(1)} %collective-permute-done.8.refs_4_, ...), custom_call_target="tpu_custom_call" | custom-call | tf_op jit(solution)/shard_map/gain_solve/pallas_call | solution.py:463
  33.2 0.1 collective-permute-start.13
  33.3 1.2 %collective-permute-start.12 = (f32[4,2,806]{2,1,0:T(2,128)S(1)}, f32[4,2,806]{2,1,0:T(2,128)S(1)}, u32[]{:S(2)}, u32[]{:S(2)}) collective-permute-start(f32[4,2,806]{2,1,0:T(2,128)S(1)} %gain_solve.1.refs_4_), channel_id=1, source_target_pairs={{0,2},{1,3},{2,0},{3,1},{4,6},{5,7},{6,4},{7,5},{8,10},{9,11},{10,... | collective-permute-start | bytes 77384 | tf_op jit(solution)/shard_map/ppermute | solution.py:383
  34.5 0.7 %collective-permute-start.11 = (f32[4,2,806]{2,1,0:T(2,128)S(1)}, f32[4,2,806]{2,1,0:T(2,128)S(1)}, u32[]{:S(2)}, u32[]{:S(2)}) collective-permute-start(f32[4,2,806]{2,1,0:T(2,128)S(1)} %gain_solve.1.refs_4_), channel_id=1, source_target_pairs={{0,1},{1,0},{2,3},{3,2},{4,5},{5,4},{6,7},{7,6},{8,9},{9,8},{10,11... | collective-permute-start | bytes 77384 | tf_op jit(solution)/shard_map/ppermute | solution.py:383
  35.2 1.4 %collective-permute-done.13.refs_7_ = f32[4,2,806]{2,1,0:T(2,128)S(1)} collective-permute-done((f32[4,2,806]{2,1,0:T(2,128)S(1)}, f32[4,2,806]{2,1,0:T(2,128)S(1)}, u32[]{:S(2)}, u32[]{:S(2)}) %collective-permute-start.13) | collective-permute-done | bytes 25824 | tf_op jit(solution)/shard_map/ppermute | solution.py:383
  36.6 0.8 %collective-permute-done.12.refs_6_ = f32[4,2,806]{2,1,0:T(2,128)S(1)} collective-permute-done((f32[4,2,806]{2,1,0:T(2,128)S(1)}, f32[4,2,806]{2,1,0:T(2,128)S(1)}, u32[]{:S(2)}, u32[]{:S(2)}) %collective-permute-start.12) | collective-permute-done | bytes 25824 | tf_op jit(solution)/shard_map/ppermute | solution.py:383
  37.4 0.0 collective-permute-done.11.refs_5_
  37.4 4.8 %clean.1 = (bf16[2,2,4,192,703]{4,3,2,1,0:T(8,128)(2,1)}, f32[2,2,2,4,38]{4,3,2,1,0:T(4,128)}) custom-call(s32[1]{0:T(128)} %bitcast.refs_0_, bf16[2,2,4,192,703]{4,3,2,1,0:T(8,128)(2,1)S(1)} %get-tuple-element.29.refs_1_, f32[2,2,192,703]{3,2,1,0:T(8,128)S(1)} %get-tuple-element.25.refs_10_.refs_2_, ...), custom_call_target="tpu_custom_call" | custom-call | tf_op jit(solution)/shard_map/clean/pallas_call | solution.py:472
  (5 shorter events, 0.0 us)
Async XLA Ops:
  0.6 6.3 %collective-permute-start.2 = (s32[1,2,192]{2,1,0:T(2,128)}, s32[1,2,192]{2,1,0:T(2,128)S(1)}, u32[]{:S(2)}, u32[]{:S(2)}) collective-permute-start(s32[1,2,192]{2,1,0:T(2,128)} %bitcast.15), channel_id=1, source_target_pairs={{0,3},{1,2},{2,1},{3,0},{4,7},{5,6},{6,5},{7,4},{8,11},{9,10},{10,... | collective-permute-start | bytes 4616 | tf_op jit(solution)/shard_map/ppermute | solution.py:383
  3.1 3.8 %collective-permute-start.1 = (s32[1,2,192]{2,1,0:T(2,128)}, s32[1,2,192]{2,1,0:T(2,128)S(1)}, u32[]{:S(2)}, u32[]{:S(2)}) collective-permute-start(s32[1,2,192]{2,1,0:T(2,128)} %bitcast.16), channel_id=1, source_target_pairs={{0,2},{1,3},{2,0},{3,1},{4,6},{5,7},{6,4},{7,5},{8,10},{9,11},{10,... | collective-permute-start | bytes 4616 | tf_op jit(solution)/shard_map/ppermute | solution.py:383
  3.7 2.3 %collective-permute-start = (s32[1,2,192]{2,1,0:T(2,128)}, s32[1,2,192]{2,1,0:T(2,128)S(1)}, u32[]{:S(2)}, u32[]{:S(2)}) collective-permute-start(s32[1,2,192]{2,1,0:T(2,128)} %bitcast.17), channel_id=1, source_target_pairs={{0,1},{1,0},{2,3},{3,2},{4,5},{5,4},{6,7},{7,6},{8,9},{9,8},{10,11... | collective-permute-start | bytes 4616 | tf_op jit(solution)/shard_map/ppermute | solution.py:383
  3.8 0.7 %copy-start.1 = (f32[2,2,703]{2,1,0:T(2,128)S(1)}, f32[2,2,703]{2,1,0:T(2,128)}, u32[]{:S(2)}) copy-start(f32[2,2,703]{2,1,0:T(2,128)} %refs_1_.4) | copy-start | bytes 33748
  4.5 0.7 %copy-start.2 = (s32[2,192]{1,0:T(2,128)S(1)}, s32[2,192]{1,0:T(2,128)}, u32[]{:S(2)}) copy-start(s32[2,192]{1,0:T(2,128)} %param.7) | copy-start | bytes 4612
  6.9 5.5 %collective-permute-start.4 = (s32[4,2,192]{2,1,0:T(2,128)S(1)}, s32[4,2,192]{2,1,0:T(2,128)S(1)}, u32[]{:S(2)}, u32[]{:S(2)}) collective-permute-start(s32[4,2,192]{2,1,0:T(2,128)S(1)} %constant_dynamic-update-slice_fusion.refs_1_), channel_id=1, source_target_pairs={{0,12},{1,13},{2,14},{3,15},{4,8},{5,9},{6,10},{7,11},{8,4},{9,5},... | collective-permute-start | bytes 18440 | tf_op jit(solution)/shard_map/ppermute | solution.py:383
  10.6 3.7 %collective-permute-start.3 = (s32[4,2,192]{2,1,0:T(2,128)S(1)}, s32[4,2,192]{2,1,0:T(2,128)S(1)}, u32[]{:S(2)}, u32[]{:S(2)}) collective-permute-start(s32[4,2,192]{2,1,0:T(2,128)S(1)} %constant_dynamic-update-slice_fusion.refs_1_), channel_id=1, source_target_pairs={{0,4},{1,5},{2,6},{3,7},{4,0},{5,1},{6,2},{7,3},{8,12},{9,13},{10,... | collective-permute-start | bytes 18440 | tf_op jit(solution)/shard_map/ppermute | solution.py:383
  10.6 0.7 %copy-start.3 = (s32[32]{0:T(128)S(1)}, s32[32]{0:T(128)}, u32[]{:S(2)}) copy-start(s32[32]{0:T(128)} %param.8) | copy-start | bytes 388
  14.2 16.9 %copy-start = (s32[2,2]{1,0:T(2,128)S(1)}, s32[2,2]{1,0:T(2,128)}, u32[]{:S(2)}) copy-start(s32[2,2]{1,0:T(2,128)} %refs_1_.5) | copy-start | bytes 52
  20.2 1.9 %collective-permute-start.5 = (f32[4,2,703]{2,1,0:T(2,128)S(1)}, f32[4,2,703]{2,1,0:T(2,128)S(1)}, u32[]{:S(2)}, u32[]{:S(2)}) collective-permute-start(f32[4,2,703]{2,1,0:T(2,128)S(1)} %get-tuple-element.31), channel_id=1, source_target_pairs={{0,1},{1,0},{2,3},{3,2},{4,5},{5,4},{6,7},{7,6},{8,9},{9,8},{10,11... | collective-permute-start | bytes 67496 | tf_op jit(solution)/shard_map/ppermute | solution.py:383
  20.3 3.9 %collective-permute-start.6 = (f32[4,2,703]{2,1,0:T(2,128)S(1)}, f32[4,2,703]{2,1,0:T(2,128)S(1)}, u32[]{:S(2)}, u32[]{:S(2)}) collective-permute-start(f32[4,2,703]{2,1,0:T(2,128)S(1)} %get-tuple-element.32), channel_id=1, source_target_pairs={{0,2},{1,3},{2,0},{3,1},{4,6},{5,7},{6,4},{7,5},{8,10},{9,11},{10,... | collective-permute-start | bytes 67496 | tf_op jit(solution)/shard_map/ppermute | solution.py:383
  21.3 3.3 %collective-permute-start.7 = (f32[4,2,703]{2,1,0:T(2,128)S(1)}, f32[4,2,703]{2,1,0:T(2,128)S(1)}, u32[]{:S(2)}, u32[]{:S(2)}) collective-permute-start(f32[4,2,703]{2,1,0:T(2,128)S(1)} %get-tuple-element.33), channel_id=1, source_target_pairs={{0,3},{1,2},{2,1},{3,0},{4,7},{5,6},{6,5},{7,4},{8,11},{9,10},{10,... | collective-permute-start | bytes 67496 | tf_op jit(solution)/shard_map/ppermute | solution.py:383
  24.6 5.8 %collective-permute-start.10 = (f32[4,2,703]{2,1,0:T(2,128)S(1)}, f32[4,2,703]{2,1,0:T(2,128)S(1)}, u32[]{:S(2)}, u32[]{:S(2)}) collective-permute-start(f32[4,2,703]{2,1,0:T(2,128)S(1)} %bitcast.10), channel_id=1, source_target_pairs={{0,12},{1,13},{2,14},{3,15},{4,8},{5,9},{6,10},{7,11},{8,4},{9,5},... | collective-permute-start | bytes 67496 | tf_op jit(solution)/shard_map/ppermute | solution.py:383
  26.4 4.7 %collective-permute-start.9 = (f32[4,2,703]{2,1,0:T(2,128)S(1)}, f32[4,2,703]{2,1,0:T(2,128)S(1)}, u32[]{:S(2)}, u32[]{:S(2)}) collective-permute-start(f32[4,2,703]{2,1,0:T(2,128)S(1)} %bitcast.11), channel_id=1, source_target_pairs={{0,8},{1,9},{2,10},{3,11},{4,12},{5,13},{6,14},{7,15},{8,0},{9,1},... | collective-permute-start | bytes 67496 | tf_op jit(solution)/shard_map/ppermute | solution.py:383
  26.4 4.7 %collective-permute-start.8 = (f32[4,2,703]{2,1,0:T(2,128)S(1)}, f32[4,2,703]{2,1,0:T(2,128)S(1)}, u32[]{:S(2)}, u32[]{:S(2)}) collective-permute-start(f32[4,2,703]{2,1,0:T(2,128)S(1)} %bitcast.12), channel_id=1, source_target_pairs={{0,4},{1,5},{2,6},{3,7},{4,0},{5,1},{6,2},{7,3},{8,12},{9,13},{10,... | collective-permute-start | bytes 67496 | tf_op jit(solution)/shard_map/ppermute | solution.py:383
  33.2 3.4 %collective-permute-start.13 = (f32[4,2,806]{2,1,0:T(2,128)S(1)}, f32[4,2,806]{2,1,0:T(2,128)S(1)}, u32[]{:S(2)}, u32[]{:S(2)}) collective-permute-start(f32[4,2,806]{2,1,0:T(2,128)S(1)} %gain_solve.1.refs_4_), channel_id=1, source_target_pairs={{0,3},{1,2},{2,1},{3,0},{4,7},{5,6},{6,5},{7,4},{8,11},{9,10},{10,... | collective-permute-start | bytes 77384 | tf_op jit(solution)/shard_map/ppermute | solution.py:383
  33.3 4.1 %collective-permute-start.12 = (f32[4,2,806]{2,1,0:T(2,128)S(1)}, f32[4,2,806]{2,1,0:T(2,128)S(1)}, u32[]{:S(2)}, u32[]{:S(2)}) collective-permute-start(f32[4,2,806]{2,1,0:T(2,128)S(1)} %gain_solve.1.refs_4_), channel_id=1, source_target_pairs={{0,2},{1,3},{2,0},{3,1},{4,6},{5,7},{6,4},{7,5},{8,10},{9,11},{10,... | collective-permute-start | bytes 77384 | tf_op jit(solution)/shard_map/ppermute | solution.py:383
  34.5 2.9 %collective-permute-start.11 = (f32[4,2,806]{2,1,0:T(2,128)S(1)}, f32[4,2,806]{2,1,0:T(2,128)S(1)}, u32[]{:S(2)}, u32[]{:S(2)}) collective-permute-start(f32[4,2,806]{2,1,0:T(2,128)S(1)} %gain_solve.1.refs_4_), channel_id=1, source_target_pairs={{0,1},{1,0},{2,3},{3,2},{4,5},{5,4},{6,7},{7,6},{8,9},{9,8},{10,11... | collective-permute-start | bytes 77384 | tf_op jit(solution)/shard_map/ppermute | solution.py:383

commit v9 on v8

--- a/solution.py
+++ b/solution.py
@@ -11,7 +11,7 @@
 DAMPING = 1.0
 STEPS_PER_TURN = 64
 GAINS_AT = 768
-CHUNK = 48
+CHUNK = 96
 GRANT = 40
 ROWS = 40
 
@@ -93,12 +93,10 @@
 def phase_kernel(width, t, reach, me_ref, *refs):
     anchor = me_ref[0].astype(F32) * float(width)
     if t == 0:
-        delay_ref, flag_ref, wave_ref, mix_ref, own_ref = refs
+        delay_ref, _, wave_ref, mix_ref = refs
     else:
         delay_ref, win_ref, wave_ref, mix_ref, apart_ref, *mask_refs = refs
-    if t == 0:
-        own_ref[...] = flag_ref[...]
-    else:
+    if t == 1:
         window_masks(width, reach, me_ref[0], win_ref, *mask_refs)
         apart = blocks_apart(me_ref[0], reach, apart_ref.shape[2])
         for time in range(2):
@@ -237,7 +235,7 @@
                 return tuple(new)
 
             zero = jnp.zeros((8, count), F32)
-            sums = lax.fori_loop(0, width // 16, step, (zero,) * 24, unroll=4)
+            sums = lax.fori_loop(0, width // 16, step, (zero,) * 24, unroll=6)
             for s in range(2):
                 owner = lax.bitwise_xor(lax.bitwise_and(me, 3), t + 2 * s)
                 found = []
@@ -265,6 +263,10 @@
     partner_of = baseline + 1.0 + jnp.sum(first * (station - offset), axis=0, keepdims=True)
     second = jnp.where(partner_of == station, 1.0, 0.0)
     return first.astype(BF16), second.astype(BF16)
+
+
+def own_kernel(flag_ref, own_ref):
+    own_ref[...] = flag_ref[...]
 
 
 def hots_kernel(hot_ref):
@@ -403,44 +405,47 @@
     reach = count // 4
     remote_rows = 16 * pl.cdiv(4 * reach, 16)
 
+    cost = pl.CostEstimate(flops=10 ** 7, bytes_accessed=6 * 2 ** 20, transcendentals=0)
     hots = pl.pallas_call(
         hots_kernel,
         out_specs=vmem_ref,
         out_shape=jax.ShapeDtypeStruct((2, ROWS, pairs), BF16),
         compiler_params=params,
-        cost_estimate=pl.CostEstimate(flops=10 ** 7, bytes_accessed=6 * 2 ** 20, transcendentals=0),
+        cost_estimate=cost,
         name="station_hots",
     )()
+    beside = [partner(flags, d) for d in range(1, 4)]
+    own = pl.pallas_call(
+        own_kernel,
+        in_specs=[vmem_ref],
+        out_specs=vmem_ref,
+        out_shape=jax.ShapeDtypeStruct(flags.shape, flags.dtype),
+        compiler_params=params,
+        cost_estimate=cost,
+        name="own_flags",
+    )(flags)
+    stack = jnp.concatenate([own] + beside, axis=0)
+    while stack.shape[0] < reach:
+        stride = stack.shape[0]
+        stack = jnp.concatenate([stack] + [partner(stack, stride * d) for d in range(1, 4)], axis=0)
+    gathered = [stack] + [partner(stack, d * reach) for d in (1, 3)]
     made = []
-    beside = [partner(flags, d) for d in range(1, 4)]
     for t in range(2):
         shape = lambda *dims: jax.ShapeDtypeStruct(dims, F32)
-        out_shape = [
-            shape(2, 2, width, pairs),
-            jax.ShapeDtypeStruct((2, 2, width, pairs), BF16),
-        ]
-        if t == 0:
-            operands = (me, delays, flags)
-            out_shape += [jax.ShapeDtypeStruct(flags.shape, flags.dtype)]
-        else:
-            operands = (me, delays, windows.reshape(1, window_count))
+        out_shape = [shape(2, 2, width, pairs), jax.ShapeDtypeStruct((2, 2, width, pairs), BF16)]
+        operands = (me, delays, windows.reshape(1, window_count) if t else stack)
+        if t:
             out_shape += [shape(2, 2, remote_rows, pairs), shape(window_count, width), shape(width, window_count),
                           shape(remote_rows, width), shape(2, window_count, 128)]
         made.append(pl.pallas_call(
             lambda *refs: phase_kernel(width, t, reach, *refs),
-            in_specs=[smem()] + [vmem_ref] * (len(operands) - 1),
+            in_specs=[smem()] + [vmem_ref] * 2,
             out_specs=[vmem_ref] * len(out_shape),
             out_shape=out_shape,
             compiler_params=params,
-            cost_estimate=pl.CostEstimate(flops=10 ** 7, bytes_accessed=6 * 2 ** 20, transcendentals=0),
+            cost_estimate=cost,
             name="phases",
         )(*operands))
-        if t == 0:
-            gathered = jnp.concatenate([made[0][2]] + beside, axis=0)
-            while gathered.shape[0] < reach:
-                stride = gathered.shape[0]
-                gathered = jnp.concatenate([gathered] + [partner(gathered, stride * d) for d in range(1, 4)], axis=0)
-            gathered = [gathered] + [partner(gathered, d * reach) for d in (1, 3)]
     waves, mixing = ([part[i] for part in made] for i in range(2))
     masks = made[1][2:]
     *quarters, held = pl.pallas_call(

time: 42.5 us -> 42.7 us (level)
    unnamed x11 -> x8, local copies, waits for them, and re-layouts: 2.07 us -> 2.08 us
  transfers between devices with their start and end apart: 14 -> 14, of which waited for: 9 -> 10; matrix products, arithmetic and copies ran while one was open for 0% -> 0% of each run, Pallas kernels for 5% -> 5%
where the time goes in v9:
time: 42.7 us; the launch traced here: 42.4 us
  starting transfers between devices  15.1 us (35%)
  Pallas kernels  14.7 us (34%)
  waiting for transfers between devices  9.85 us (23%)
  local copies, waits for them, and re-layouts  2.08 us (5%)
  between operations  0.71 us (2%)
    ppermute x14, starting transfers between devices, partner(): return lax.ppermute(value, 'sub', [(i, i ^ bits) for i in range(count)])  15.1 us
    ppermute x14, waiting for transfers between devices, partner(): return lax.ppermute(value, 'sub', [(i, i ^ bits) for i in range(count)])  9.85 us
    pallas_call x1, Pallas kernels, local(): pl.pallas_call(lambda *refs: sums_kernel(width, reach, *refs), in_specs=[...  5.88 us
    pallas_call x1, Pallas kernels, local(): pl.pallas_call(lambda *refs: clean_kernel(width, *refs), in_specs=[smem()...  4.81 us
    unnamed x8, local copies, waits for them, and re-layouts  2.08 us
    pallas_call x1, Pallas kernels, local(): pl.pallas_call(lambda *refs: solve_kernel(float(window_count), *refs), in...  2.07 us
    pallas_call x2, Pallas kernels, local(): pl.pallas_call(lambda *refs: phase_kernel(width, t, reach, *refs), in_spe...  1.86 us
  transfers between devices with their start and end apart: 14, of which 10 were waited for; matrix products, arithmetic and copies ran while one was open for 0% of the time, Pallas kernels for 5%

profile of v9, /device:TPU:0, one launch (start us, length us, event | category | flops | bytes accessed | tf_op | source)
XLA Modules:
  0.0 42.4 jit_solution(14022088328380510852)
XLA Ops:
  0.6 2.5 %collective-permute-start.2 = (s32[1,2,192]{2,1,0:T(2,128)}, s32[1,2,192]{2,1,0:T(2,128)S(1)}, u32[]{:S(2)}, u32[]{:S(2)}) collective-permute-start(s32[1,2,192]{2,1,0:T(2,128)} %bitcast.15), channel_id=1, source_target_pairs={{0,3},{1,2},{2,1},{3,0},{4,7},{5,6},{6,5},{7,4},{8,11},{9,10},{10,... | collective-permute-start | bytes 4616 | tf_op jit(solution)/shard_map/ppermute | solution.py:385
  3.1 0.6 %collective-permute-start.1 = (s32[1,2,192]{2,1,0:T(2,128)}, s32[1,2,192]{2,1,0:T(2,128)S(1)}, u32[]{:S(2)}, u32[]{:S(2)}) collective-permute-start(s32[1,2,192]{2,1,0:T(2,128)} %bitcast.16), channel_id=1, source_target_pairs={{0,2},{1,3},{2,0},{3,1},{4,6},{5,7},{6,4},{7,5},{8,10},{9,11},{10,... | collective-permute-start | bytes 4616 | tf_op jit(solution)/shard_map/ppermute | solution.py:385
  3.7 0.0 collective-permute-start
  3.8 0.0 copy-start.2
  3.8 0.7 %copy-done.2 = s32[2,192]{1,0:T(2,128)S(1)} copy-done((s32[2,192]{1,0:T(2,128)S(1)}, s32[2,192]{1,0:T(2,128)}, u32[]{:S(2)}) %copy-start.2) | copy-done | bytes 1560
  4.5 0.1 collective-permute-done.2
  4.6 2.3 %collective-permute-done.1 = s32[1,2,192]{2,1,0:T(2,128)S(1)} collective-permute-done((s32[1,2,192]{2,1,0:T(2,128)}, s32[1,2,192]{2,1,0:T(2,128)S(1)}, u32[]{:S(2)}, u32[]{:S(2)}) %collective-permute-start.1) | collective-permute-done | bytes 1568 | tf_op jit(solution)/shard_map/ppermute | solution.py:385
  6.9 0.0 collective-permute-done
  6.9 3.7 %collective-permute-start.4 = (s32[4,2,192]{2,1,0:T(2,128)S(1)}, s32[4,2,192]{2,1,0:T(2,128)S(1)}, u32[]{:S(2)}, u32[]{:S(2)}) collective-permute-start(s32[4,2,192]{2,1,0:T(2,128)S(1)} %pad_add_fusion.refs_2_.refs_1_), channel_id=1, source_target_pairs={{0,12},{1,13},{2,14},{3,15},{4,8},{5,9},{6,10},{7,11},{8,4},{9,5},... | collective-permute-start | bytes 18440 | tf_op jit(solution)/shard_map/ppermute | solution.py:385
  10.6 0.0 collective-permute-start.3
  10.6 0.0 copy-start.1
  10.6 0.7 %copy-done.1 = f32[2,2,703]{2,1,0:T(2,128)S(1)} copy-done((f32[2,2,703]{2,1,0:T(2,128)S(1)}, f32[2,2,703]{2,1,0:T(2,128)}, u32[]{:S(2)}) %copy-start.1) | copy-done | bytes 11272
  11.3 0.0 copy-start.3
  11.3 0.7 %copy-done.3 = s32[32]{0:T(128)S(1)} copy-done((s32[32]{0:T(128)S(1)}, s32[32]{0:T(128)}, u32[]{:S(2)}) %copy-start.3) | copy-done | bytes 152
  11.9 1.0 %phases.2 = (f32[2,2,192,703]{3,2,1,0:T(8,128)S(1)}, bf16[2,2,192,703]{3,2,1,0:T(8,128)(2,1)S(1)}, f32[2,2,16,703]{3,2,1,0:T(8,128)S(1)}, f32[32,192]{1,0:T(8,12...) custom-call(s32[1]{0:T(128)} %bitcast.refs_0_, f32[2,2,703]{2,1,0:T(2,128)S(1)} %copy-done.1, ...), custom_call_target="tpu_custom_call" | custom-call | flops 10000000 | bytes 6291456 | tf_op jit(solution)/shard_map/phases/pallas_call | solution.py:440
  13.0 0.8 %phases.3 = (f32[2,2,192,703]{3,2,1,0:T(8,128)S(1)}, bf16[2,2,192,703]{3,2,1,0:T(8,128)(2,1)S(1)}) custom-call(s32[1]{0:T(128)} %bitcast.refs_0_, f32[2,2,703]{2,1,0:T(2,128)S(1)} %copy-done.1, s32[4,2,192]{2,1,0:T(2,128)S(1)} %pad_add_fusion.refs_2_.refs_1_), custom_call_target="tpu_custom_call" | custom-call | flops 10000000 | bytes 6291456 | tf_op jit(solution)/shard_map/phases/pallas_call | solution.py:440
  13.8 0.0 collective-permute-done.4.refs_3_
  13.8 0.4 collective-permute-done.3.refs_2_
  14.2 0.0 copy-start
  14.2 5.9 %window_sums.1 = (f32[4,2,703]{2,1,0:T(2,128)S(1)}, f32[4,2,703]{2,1,0:T(2,128)S(1)}, f32[4,2,703]{2,1,0:T(2,128)S(1)}, f32[4,2,703]{2,1,0:T(2,128)S(1)}, bf16[2,2,4,192,703]{4,3,2,1,0:T(8,128)(2,1)S(1)}) custom-call(s32[1]{0:T(128)} %bitcast.refs_0_, s32[4,2,192]{2,1,0:T(2,128)S(1)} %pad_add_fusion.refs_2_.refs_1_, ...), custom_call_target="tpu_custom_call" | custom-call | tf_op jit(solution)/shard_map/window_sums/pallas_call | solution.py:451
  20.1 0.1 collective-permute-start.5
  20.2 0.7 %collective-permute-start.6 = (f32[4,2,703]{2,1,0:T(2,128)S(1)}, f32[4,2,703]{2,1,0:T(2,128)S(1)}, u32[]{:S(2)}, u32[]{:S(2)}) collective-permute-start(f32[4,2,703]{2,1,0:T(2,128)S(1)} %get-tuple-element.30), channel_id=1, source_target_pairs={{0,2},{1,3},{2,0},{3,1},{4,6},{5,7},{6,4},{7,5},{8,10},{9,11},{10,... | collective-permute-start | bytes 67496 | tf_op jit(solution)/shard_map/ppermute | solution.py:385
  20.9 1.2 %collective-permute-start.7 = (f32[4,2,703]{2,1,0:T(2,128)S(1)}, f32[4,2,703]{2,1,0:T(2,128)S(1)}, u32[]{:S(2)}, u32[]{:S(2)}) collective-permute-start(f32[4,2,703]{2,1,0:T(2,128)S(1)} %get-tuple-element.31), channel_id=1, source_target_pairs={{0,3},{1,2},{2,1},{3,0},{4,7},{5,6},{6,5},{7,4},{8,11},{9,10},{10,... | collective-permute-start | bytes 67496 | tf_op jit(solution)/shard_map/ppermute | solution.py:385
  22.1 0.0 collective-permute-done.5
  22.1 2.2 %collective-permute-done.6 = f32[4,2,703]{2,1,0:T(2,128)S(1)} collective-permute-done((f32[4,2,703]{2,1,0:T(2,128)S(1)}, f32[4,2,703]{2,1,0:T(2,128)S(1)}, u32[]{:S(2)}, u32[]{:S(2)}) %collective-permute-start.6) | collective-permute-done | bytes 22528 | tf_op jit(solution)/shard_map/ppermute | solution.py:385
  24.3 0.1 collective-permute-done.7
  24.4 1.9 %collective-permute-start.10 = (f32[4,2,703]{2,1,0:T(2,128)S(1)}, f32[4,2,703]{2,1,0:T(2,128)S(1)}, u32[]{:S(2)}, u32[]{:S(2)}) collective-permute-start(f32[4,2,703]{2,1,0:T(2,128)S(1)} %bitcast.10), channel_id=1, source_target_pairs={{0,12},{1,13},{2,14},{3,15},{4,8},{5,9},{6,10},{7,11},{8,4},{9,5},... | collective-permute-start | bytes 67496 | tf_op jit(solution)/shard_map/ppermute | solution.py:385
  26.3 1.3 %collective-permute-start.9 = (f32[4,2,703]{2,1,0:T(2,128)S(1)}, f32[4,2,703]{2,1,0:T(2,128)S(1)}, u32[]{:S(2)}, u32[]{:S(2)}) collective-permute-start(f32[4,2,703]{2,1,0:T(2,128)S(1)} %bitcast.11), channel_id=1, source_target_pairs={{0,8},{1,9},{2,10},{3,11},{4,12},{5,13},{6,14},{7,15},{8,0},{9,1},... | collective-permute-start | bytes 67496 | tf_op jit(solution)/shard_map/ppermute | solution.py:385
  27.6 1.3 %collective-permute-start.8 = (f32[4,2,703]{2,1,0:T(2,128)S(1)}, f32[4,2,703]{2,1,0:T(2,128)S(1)}, u32[]{:S(2)}, u32[]{:S(2)}) collective-permute-start(f32[4,2,703]{2,1,0:T(2,128)S(1)} %bitcast.12), channel_id=1, source_target_pairs={{0,4},{1,5},{2,6},{3,7},{4,0},{5,1},{6,2},{7,3},{8,12},{9,13},{10,... | collective-permute-start | bytes 67496 | tf_op jit(solution)/shard_map/ppermute | solution.py:385
  28.9 0.1 station_hots.1.refs_2_
  28.9 1.3 %collective-permute-done.10.refs_6_ = f32[4,2,703]{2,1,0:T(2,128)S(1)} collective-permute-done((f32[4,2,703]{2,1,0:T(2,128)S(1)}, f32[4,2,703]{2,1,0:T(2,128)S(1)}, u32[]{:S(2)}, u32[]{:S(2)}) %collective-permute-start.10) | collective-permute-done | bytes 22528 | tf_op jit(solution)/shard_map/ppermute | solution.py:385
  30.2 0.8 %collective-permute-done.9.refs_5_ = f32[4,2,703]{2,1,0:T(2,128)S(1)} collective-permute-done((f32[4,2,703]{2,1,0:T(2,128)S(1)}, f32[4,2,703]{2,1,0:T(2,128)S(1)}, u32[]{:S(2)}, u32[]{:S(2)}) %collective-permute-start.9) | collective-permute-done | bytes 22528 | tf_op jit(solution)/shard_map/ppermute | solution.py:385
  31.0 0.4 collective-permute-done.8.refs_4_
  31.4 0.0 copy-done
  31.4 2.1 %gain_solve.1.refs_4_ = f32[4,2,806]{2,1,0:T(2,128)S(1)} custom-call(s32[1]{0:T(128)} %bitcast.refs_0_, s32[2,2]{1,0:T(2,128)S(1)} %copy-done, bf16[2,40,703]{2,1,0:T(8,128)(2,1)S(1)} %station_hots.1.refs_2_, f32[4,2,703]{2,1,0:T(2,128)S(1)} %bitcast.13, f32[4,2,703]{2,1,0:T(2,128)S(1)} %collective-permute-done.8.refs_4_, ...), custom_call_target="tpu_custom_call" | custom-call | tf_op jit(solution)/shard_map/gain_solve/pallas_call | solution.py:468
  33.5 0.1 collective-permute-start.13
  33.6 1.2 %collective-permute-start.12 = (f32[4,2,806]{2,1,0:T(2,128)S(1)}, f32[4,2,806]{2,1,0:T(2,128)S(1)}, u32[]{:S(2)}, u32[]{:S(2)}) collective-permute-start(f32[4,2,806]{2,1,0:T(2,128)S(1)} %gain_solve.1.refs_4_), channel_id=1, source_target_pairs={{0,2},{1,3},{2,0},{3,1},{4,6},{5,7},{6,4},{7,5},{8,10},{9,11},{10,... | collective-permute-start | bytes 77384 | tf_op jit(solution)/shard_map/ppermute | solution.py:385
  34.8 0.7 %collective-permute-start.11 = (f32[4,2,806]{2,1,0:T(2,128)S(1)}, f32[4,2,806]{2,1,0:T(2,128)S(1)}, u32[]{:S(2)}, u32[]{:S(2)}) collective-permute-start(f32[4,2,806]{2,1,0:T(2,128)S(1)} %gain_solve.1.refs_4_), channel_id=1, source_target_pairs={{0,1},{1,0},{2,3},{3,2},{4,5},{5,4},{6,7},{7,6},{8,9},{9,8},{10,11... | collective-permute-start | bytes 77384 | tf_op jit(solution)/shard_map/ppermute | solution.py:385
  35.4 1.4 %collective-permute-done.13.refs_7_ = f32[4,2,806]{2,1,0:T(2,128)S(1)} collective-permute-done((f32[4,2,806]{2,1,0:T(2,128)S(1)}, f32[4,2,806]{2,1,0:T(2,128)S(1)}, u32[]{:S(2)}, u32[]{:S(2)}) %collective-permute-start.13) | collective-permute-done | bytes 25824 | tf_op jit(solution)/shard_map/ppermute | solution.py:385
  36.9 0.8 %collective-permute-done.12.refs_6_ = f32[4,2,806]{2,1,0:T(2,128)S(1)} collective-permute-done((f32[4,2,806]{2,1,0:T(2,128)S(1)}, f32[4,2,806]{2,1,0:T(2,128)S(1)}, u32[]{:S(2)}, u32[]{:S(2)}) %collective-permute-start.12) | collective-permute-done | bytes 25824 | tf_op jit(solution)/shard_map/ppermute | solution.py:385
  37.6 0.0 collective-permute-done.11.refs_5_
  37.6 4.8 %clean.1 = (bf16[2,2,4,192,703]{4,3,2,1,0:T(8,128)(2,1)}, f32[2,2,2,4,38]{4,3,2,1,0:T(4,128)}) custom-call(s32[1]{0:T(128)} %bitcast.refs_0_, bf16[2,2,4,192,703]{4,3,2,1,0:T(8,128)(2,1)S(1)} %get-tuple-element.27.refs_1_, f32[2,2,192,703]{3,2,1,0:T(8,128)S(1)} %get-tuple-element.23.refs_10_.refs_2_, ...), custom_call_target="tpu_custom_call" | custom-call | tf_op jit(solution)/shard_map/clean/pallas_call | solution.py:477
  (3 shorter events, 0.0 us)
Async XLA Ops:
  0.6 4.0 %collective-permute-start.2 = (s32[1,2,192]{2,1,0:T(2,128)}, s32[1,2,192]{2,1,0:T(2,128)S(1)}, u32[]{:S(2)}, u32[]{:S(2)}) collective-permute-start(s32[1,2,192]{2,1,0:T(2,128)} %bitcast.15), channel_id=1, source_target_pairs={{0,3},{1,2},{2,1},{3,0},{4,7},{5,6},{6,5},{7,4},{8,11},{9,10},{10,... | collective-permute-start | bytes 4616 | tf_op jit(solution)/shard_map/ppermute | solution.py:385
  3.1 3.8 %collective-permute-start.1 = (s32[1,2,192]{2,1,0:T(2,128)}, s32[1,2,192]{2,1,0:T(2,128)S(1)}, u32[]{:S(2)}, u32[]{:S(2)}) collective-permute-start(s32[1,2,192]{2,1,0:T(2,128)} %bitcast.16), channel_id=1, source_target_pairs={{0,2},{1,3},{2,0},{3,1},{4,6},{5,7},{6,4},{7,5},{8,10},{9,11},{10,... | collective-permute-start | bytes 4616 | tf_op jit(solution)/shard_map/ppermute | solution.py:385
  3.7 3.2 %collective-permute-start = (s32[1,2,192]{2,1,0:T(2,128)}, s32[1,2,192]{2,1,0:T(2,128)S(1)}, u32[]{:S(2)}, u32[]{:S(2)}) collective-permute-start(s32[1,2,192]{2,1,0:T(2,128)} %bitcast.17), channel_id=1, source_target_pairs={{0,1},{1,0},{2,3},{3,2},{4,5},{5,4},{6,7},{7,6},{8,9},{9,8},{10,11... | collective-permute-start | bytes 4616 | tf_op jit(solution)/shard_map/ppermute | solution.py:385
  3.8 0.7 %copy-start.2 = (s32[2,192]{1,0:T(2,128)S(1)}, s32[2,192]{1,0:T(2,128)}, u32[]{:S(2)}) copy-start(s32[2,192]{1,0:T(2,128)} %param.7) | copy-start | bytes 4612
  6.9 6.9 %collective-permute-start.4 = (s32[4,2,192]{2,1,0:T(2,128)S(1)}, s32[4,2,192]{2,1,0:T(2,128)S(1)}, u32[]{:S(2)}, u32[]{:S(2)}) collective-permute-start(s32[4,2,192]{2,1,0:T(2,128)S(1)} %pad_add_fusion.refs_2_.refs_1_), channel_id=1, source_target_pairs={{0,12},{1,13},{2,14},{3,15},{4,8},{5,9},{6,10},{7,11},{8,4},{9,5},... | collective-permute-start | bytes 18440 | tf_op jit(solution)/shard_map/ppermute | solution.py:385
  10.6 3.7 %collective-permute-start.3 = (s32[4,2,192]{2,1,0:T(2,128)S(1)}, s32[4,2,192]{2,1,0:T(2,128)S(1)}, u32[]{:S(2)}, u32[]{:S(2)}) collective-permute-start(s32[4,2,192]{2,1,0:T(2,128)S(1)} %pad_add_fusion.refs_2_.refs_1_), channel_id=1, source_target_pairs={{0,4},{1,5},{2,6},{3,7},{4,0},{5,1},{6,2},{7,3},{8,12},{9,13},{10,... | collective-permute-start | bytes 18440 | tf_op jit(solution)/shard_map/ppermute | solution.py:385
  10.6 0.7 %copy-start.1 = (f32[2,2,703]{2,1,0:T(2,128)S(1)}, f32[2,2,703]{2,1,0:T(2,128)}, u32[]{:S(2)}) copy-start(f32[2,2,703]{2,1,0:T(2,128)} %refs_1_.4) | copy-start | bytes 33748
  11.3 0.7 %copy-start.3 = (s32[32]{0:T(128)S(1)}, s32[32]{0:T(128)}, u32[]{:S(2)}) copy-start(s32[32]{0:T(128)} %param.8) | copy-start | bytes 388
  14.2 17.2 %copy-start = (s32[2,2]{1,0:T(2,128)S(1)}, s32[2,2]{1,0:T(2,128)}, u32[]{:S(2)}) copy-start(s32[2,2]{1,0:T(2,128)} %refs_1_.5) | copy-start | bytes 52
  20.1 1.9 %collective-permute-start.5 = (f32[4,2,703]{2,1,0:T(2,128)S(1)}, f32[4,2,703]{2,1,0:T(2,128)S(1)}, u32[]{:S(2)}, u32[]{:S(2)}) collective-permute-start(f32[4,2,703]{2,1,0:T(2,128)S(1)} %get-tuple-element.29), channel_id=1, source_target_pairs={{0,1},{1,0},{2,3},{3,2},{4,5},{5,4},{6,7},{7,6},{8,9},{9,8},{10,11... | collective-permute-start | bytes 67496 | tf_op jit(solution)/shard_map/ppermute | solution.py:385
  20.2 4.1 %collective-permute-start.6 = (f32[4,2,703]{2,1,0:T(2,128)S(1)}, f32[4,2,703]{2,1,0:T(2,128)S(1)}, u32[]{:S(2)}, u32[]{:S(2)}) collective-permute-start(f32[4,2,703]{2,1,0:T(2,128)S(1)} %get-tuple-element.30), channel_id=1, source_target_pairs={{0,2},{1,3},{2,0},{3,1},{4,6},{5,7},{6,4},{7,5},{8,10},{9,11},{10,... | collective-permute-start | bytes 67496 | tf_op jit(solution)/shard_map/ppermute | solution.py:385
  20.9 3.5 %collective-permute-start.7 = (f32[4,2,703]{2,1,0:T(2,128)S(1)}, f32[4,2,703]{2,1,0:T(2,128)S(1)}, u32[]{:S(2)}, u32[]{:S(2)}) collective-permute-start(f32[4,2,703]{2,1,0:T(2,128)S(1)} %get-tuple-element.31), channel_id=1, source_target_pairs={{0,3},{1,2},{2,1},{3,0},{4,7},{5,6},{6,5},{7,4},{8,11},{9,10},{10,... | collective-permute-start | bytes 67496 | tf_op jit(solution)/shard_map/ppermute | solution.py:385
  24.4 5.8 %collective-permute-start.10 = (f32[4,2,703]{2,1,0:T(2,128)S(1)}, f32[4,2,703]{2,1,0:T(2,128)S(1)}, u32[]{:S(2)}, u32[]{:S(2)}) collective-permute-start(f32[4,2,703]{2,1,0:T(2,128)S(1)} %bitcast.10), channel_id=1, source_target_pairs={{0,12},{1,13},{2,14},{3,15},{4,8},{5,9},{6,10},{7,11},{8,4},{9,5},... | collective-permute-start | bytes 67496 | tf_op jit(solution)/shard_map/ppermute | solution.py:385
  26.3 4.7 %collective-permute-start.9 = (f32[4,2,703]{2,1,0:T(2,128)S(1)}, f32[4,2,703]{2,1,0:T(2,128)S(1)}, u32[]{:S(2)}, u32[]{:S(2)}) collective-permute-start(f32[4,2,703]{2,1,0:T(2,128)S(1)} %bitcast.11), channel_id=1, source_target_pairs={{0,8},{1,9},{2,10},{3,11},{4,12},{5,13},{6,14},{7,15},{8,0},{9,1},... | collective-permute-start | bytes 67496 | tf_op jit(solution)/shard_map/ppermute | solution.py:385
  27.6 3.8 %collective-permute-start.8 = (f32[4,2,703]{2,1,0:T(2,128)S(1)}, f32[4,2,703]{2,1,0:T(2,128)S(1)}, u32[]{:S(2)}, u32[]{:S(2)}) collective-permute-start(f32[4,2,703]{2,1,0:T(2,128)S(1)} %bitcast.12), channel_id=1, source_target_pairs={{0,4},{1,5},{2,6},{3,7},{4,0},{5,1},{6,2},{7,3},{8,12},{9,13},{10,... | collective-permute-start | bytes 67496 | tf_op jit(solution)/shard_map/ppermute | solution.py:385
  33.5 3.4 %collective-permute-start.13 = (f32[4,2,806]{2,1,0:T(2,128)S(1)}, f32[4,2,806]{2,1,0:T(2,128)S(1)}, u32[]{:S(2)}, u32[]{:S(2)}) collective-permute-start(f32[4,2,806]{2,1,0:T(2,128)S(1)} %gain_solve.1.refs_4_), channel_id=1, source_target_pairs={{0,3},{1,2},{2,1},{3,0},{4,7},{5,6},{6,5},{7,4},{8,11},{9,10},{10,... | collective-permute-start | bytes 77384 | tf_op jit(solution)/shard_map/ppermute | solution.py:385
  33.6 4.0 %collective-permute-start.12 = (f32[4,2,806]{2,1,0:T(2,128)S(1)}, f32[4,2,806]{2,1,0:T(2,128)S(1)}, u32[]{:S(2)}, u32[]{:S(2)}) collective-permute-start(f32[4,2,806]{2,1,0:T(2,128)S(1)} %gain_solve.1.refs_4_), channel_id=1, source_target_pairs={{0,2},{1,3},{2,0},{3,1},{4,6},{5,7},{6,4},{7,5},{8,10},{9,11},{10,... | collective-permute-start | bytes 77384 | tf_op jit(solution)/shard_map/ppermute | solution.py:385
  34.8 2.9 %collective-permute-start.11 = (f32[4,2,806]{2,1,0:T(2,128)S(1)}, f32[4,2,806]{2,1,0:T(2,128)S(1)}, u32[]{:S(2)}, u32[]{:S(2)}) collective-permute-start(f32[4,2,806]{2,1,0:T(2,128)S(1)} %gain_solve.1.refs_4_), channel_id=1, source_target_pairs={{0,1},{1,0},{2,3},{3,2},{4,5},{5,4},{6,7},{7,6},{8,9},{9,8},{10,11... | collective-permute-start | bytes 77384 | tf_op jit(solution)/shard_map/ppermute | solution.py:385

commit v10 on v8

--- a/solution.py
+++ b/solution.py
@@ -11,8 +11,8 @@
 DAMPING = 1.0
 STEPS_PER_TURN = 64
 GAINS_AT = 768
-CHUNK = 48
-GRANT = 40
+GRANT = 42
+GRANTS = (50, 45)
 ROWS = 40
 
 F32 = jnp.float32
@@ -95,7 +95,9 @@
     if t == 0:
         delay_ref, flag_ref, wave_ref, mix_ref, own_ref = refs
     else:
-        delay_ref, win_ref, wave_ref, mix_ref, apart_ref, *mask_refs = refs
+        vis_hbm, delay_ref, win_ref, wave_ref, mix_ref, vis_ref, apart_ref, *mask_refs, sem = refs
+        copy = pltpu.make_async_copy(vis_hbm.at[:, 0], vis_ref, sem)
+        copy.start()
     if t == 0:
         own_ref[...] = flag_ref[...]
     else:
@@ -129,6 +131,8 @@
                 mix_ref[slot, 1, rows, lanes] = low
 
     tiles(pairs, waves)
+    if t == 1:
+        copy.wait()
 
 
 def blocks_apart(me, reach, rows):
@@ -166,10 +170,11 @@
 def sums_kernel(width, reach, me_ref, *refs):
     flag_refs, refs = refs[:3], refs[3:]
     apart_ref, inside_ref, chosen_ref, outside_ref, ends_ref = refs[:5]
-    vis_hbm, wave_refs, mix_refs, refs = refs[5], refs[6:8], refs[8:10], refs[10:]
-    out_refs, (vis_ref, alpha_s, mexp_s, wt_s, sems) = refs[:4], refs[4:]
-    copies = [pltpu.make_async_copy(vis_hbm.at[:, t], vis_ref.at[:, t], sems.at[t]) for t in range(2)]
-    copies[0].start()
+    vis_hbm, first_ref, wave_refs, mix_refs, refs = refs[5], refs[6], refs[7:9], refs[9:11], refs[11:]
+    out_refs, (second_ref, alpha_s, mexp_s, wt_s, sem) = refs[:4], refs[4:]
+    vis_refs = (first_ref, second_ref)
+    copy = pltpu.make_async_copy(vis_hbm.at[:, 1], second_ref, sem)
+    copy.start()
     me = me_ref[0]
     place = lax.rem(me, reach)
     windows = inside_ref.shape[0]
@@ -227,8 +232,8 @@
                     factors.append((fr, fi - fr, fr + fi))
                 new = []
                 for k in range(4):
-                    vr = vis_ref[0, t, k, rows, lanes].astype(F32)
-                    vi = vis_ref[1, t, k, rows, lanes].astype(F32)
+                    vr = vis_refs[t][0, k, rows, lanes].astype(F32)
+                    vi = vis_refs[t][1, k, rows, lanes].astype(F32)
                     vs = vr + vi
                     for s in range(2):
                         for v, f in zip((vs, vr, vi), factors[s]):
@@ -237,7 +242,7 @@
                 return tuple(new)
 
             zero = jnp.zeros((8, count), F32)
-            sums = lax.fori_loop(0, width // 16, step, (zero,) * 24, unroll=4)
+            sums = lax.fori_loop(0, width // 16, step, (zero,) * 24, unroll=6)
             for s in range(2):
                 owner = lax.bitwise_xor(lax.bitwise_and(me, 3), t + 2 * s)
                 found = []
@@ -251,9 +256,8 @@
                             for ri in range(2):
                                 out_refs[d][k, ri:ri + 1, lanes] = found[k][ri]
 
-        copies[t].wait()
-        if t == 0:
-            copies[1].start()
+        if t == 1:
+            copy.wait()
         tiles(pairs, main)
 
 
@@ -329,8 +333,8 @@
 
 
 def clean_kernel(width, me_ref, *refs):
-    vis_ref, wave_refs, piece_refs = refs[0], refs[1:3], refs[3:7]
-    out_hbm, gain_out_ref, out_s, model_s, sems = refs[7:]
+    vis_refs, wave_refs, piece_refs = refs[:2], refs[2:4], refs[4:8]
+    out_hbm, gain_out_ref, out_s, model_s, sems = refs[8:]
     pairs = wave_refs[0].shape[3]
     mine = lax.bitwise_and(me_ref[0], 3)
     for d, piece in enumerate(piece_refs):
@@ -343,39 +347,37 @@
             for slot, value in enumerate((re, im - re, re + im)):
                 model_s[owner, 3 * k + slot:3 * k + slot + 1, :] = value
 
-    def copy_out(t, index):
-        rows = pl.ds(pl.multiple_of(index * CHUNK, CHUNK), CHUNK)
-        return pltpu.make_async_copy(out_s.at[:, t, :, rows], out_hbm.at[:, t, :, rows], sems.at[t, index])
-
-    chunks = width // CHUNK
-    for t in range(2):
-        def chunk(index, carry):
-            def main(lanes, count):
-                for block in range(CHUNK // 16):
-                    rows = pl.ds(pl.multiple_of(index * CHUNK + block * 16, 16), 16)
-                    waves = []
-                    for s in range(2):
-                        re, im = (wave_refs[t][s, ri, rows, lanes] for ri in range(2))
-                        waves.append((re + im, re, im))
-                    for k in range(4):
-                        sums = []
-                        for slot in range(3):
-                            one, two = (waves[s][slot] * model_s[t + 2 * s, 3 * k + slot:3 * k + slot + 1, lanes]
-                                        for s in range(2))
-                            sums.append(one + two)
-                        vr = vis_ref[0, t, k, rows, lanes].astype(F32)
-                        vi = vis_ref[1, t, k, rows, lanes].astype(F32)
-                        out_s[0, t, k, rows, lanes] = (vr - (sums[0] - sums[2])).astype(BF16)
-                        out_s[1, t, k, rows, lanes] = (vi - (sums[0] + sums[1])).astype(BF16)
-
-            tiles(pairs, main)
-            copy_out(t, index).start()
-            return carry
-
-        lax.fori_loop(0, chunks, chunk, 0)
-    for t in range(2):
-        for index in range(chunks):
-            copy_out(t, index).wait()
+    half = width // 32 * 16
+    quarter = half // 32 * 16
+    pieces = [(0, 0, half), (0, half, width - half),
+              (1, 0, half), (1, half, half - quarter), (1, 2 * half - quarter, width - 2 * half + quarter)]
+    copies = []
+    for t, start, length in pieces:
+        def main(lanes, count):
+            for block in range(length // 16):
+                rows = slice(start + block * 16, start + block * 16 + 16)
+                waves = []
+                for s in range(2):
+                    re, im = (wave_refs[t][s, ri, rows, lanes] for ri in range(2))
+                    waves.append((re + im, re, im))
+                for k in range(4):
+                    sums = []
+                    for slot in range(3):
+                        one, two = (waves[s][slot] * model_s[t + 2 * s, 3 * k + slot:3 * k + slot + 1, lanes]
+                                    for s in range(2))
+                        sums.append(one + two)
+                    vr = vis_refs[t][0, k, rows, lanes].astype(F32)
+                    vi = vis_refs[t][1, k, rows, lanes].astype(F32)
+                    out_s[0, t, k, rows, lanes] = (vr - (sums[0] - sums[2])).astype(BF16)
+                    out_s[1, t, k, rows, lanes] = (vi - (sums[0] + sums[1])).astype(BF16)
+
+        tiles(pairs, main)
+        rows = pl.ds(start, length)
+        copies.append(pltpu.make_async_copy(
+            out_s.at[:, t, :, rows], out_hbm.at[:, t, :, rows], sems.at[len(copies)]))
+        copies[-1].start()
+    for copy in copies:
+        copy.wait()
 
 
 def partner(value, bits):
@@ -421,17 +423,21 @@
         ]
         if t == 0:
             operands = (me, delays, flags)
+            in_specs = [smem()] + [vmem_ref] * 2
             out_shape += [jax.ShapeDtypeStruct(flags.shape, flags.dtype)]
         else:
-            operands = (me, delays, windows.reshape(1, window_count))
-            out_shape += [shape(2, 2, remote_rows, pairs), shape(window_count, width), shape(width, window_count),
+            operands = (me, turned, delays, windows.reshape(1, window_count))
+            in_specs = [smem(), hbm_ref] + [vmem_ref] * 2
+            out_shape += [jax.ShapeDtypeStruct((2, 4, width, pairs), BF16),
+                          shape(2, 2, remote_rows, pairs), shape(window_count, width), shape(width, window_count),
                           shape(remote_rows, width), shape(2, window_count, 128)]
         made.append(pl.pallas_call(
             lambda *refs: phase_kernel(width, t, reach, *refs),
-            in_specs=[smem()] + [vmem_ref] * (len(operands) - 1),
+            in_specs=in_specs,
             out_specs=[vmem_ref] * len(out_shape),
             out_shape=out_shape,
-            compiler_params=params,
+            scratch_shapes=[pltpu.SemaphoreType.DMA] * t,
+            compiler_params=pltpu.CompilerParams(vmem_limit_bytes=GRANTS[t] * 2 ** 20),
             cost_estimate=pl.CostEstimate(flops=10 ** 7, bytes_accessed=6 * 2 ** 20, transcendentals=0),
             name="phases",
         )(*operands))
@@ -442,17 +448,17 @@
                 gathered = jnp.concatenate([gathered] + [partner(gathered, stride * d) for d in range(1, 4)], axis=0)
             gathered = [gathered] + [partner(gathered, d * reach) for d in (1, 3)]
     waves, mixing = ([part[i] for part in made] for i in range(2))
-    masks = made[1][2:]
-    *quarters, held = pl.pallas_call(
+    held, *masks = made[1][2:]
+    *quarters, held_too = pl.pallas_call(
         lambda *refs: sums_kernel(width, reach, *refs),
-        in_specs=[smem()] + [vmem_ref] * 8 + [hbm_ref] + [vmem_ref] * 4,
+        in_specs=[smem()] + [vmem_ref] * 8 + [hbm_ref] + [vmem_ref] * 5,
         out_specs=[vmem_ref] * 5,
-        out_shape=[jax.ShapeDtypeStruct((4, 2, pairs), F32)] * 4 + [jax.ShapeDtypeStruct(turned.shape, BF16)],
+        out_shape=[jax.ShapeDtypeStruct((4, 2, pairs), F32)] * 4 + [jax.ShapeDtypeStruct(held.shape, BF16)],
         scratch_shapes=[vmem(2, width, 128), vmem(2, 2, width, pairs), vmem(2, remote_rows, width),
-                        pltpu.SemaphoreType.DMA((2,))],
+                        pltpu.SemaphoreType.DMA],
         compiler_params=pltpu.CompilerParams(vmem_limit_bytes=GRANT * 2 ** 20),
         name="window_sums",
-    )(me, *gathered, *masks, turned, *waves, *mixing)
+    )(me, *gathered, *masks, turned, held, *waves, *mixing)
     pieces = [quarters[0]] + [partner(quarters[d], d) for d in range(1, 4)]
     stride = 4
     while stride < count:
@@ -471,7 +477,7 @@
     model = [model] + [partner(model, d) for d in range(1, 4)]
     cleaned, gains = pl.pallas_call(
         lambda *refs: clean_kernel(width, *refs),
-        in_specs=[smem()] + [vmem_ref] * 7,
+        in_specs=[smem()] + [vmem_ref] * 8,
         out_specs=[hbm_ref, vmem_ref],
         out_shape=[
             jax.ShapeDtypeStruct(turned.shape, BF16),
@@ -480,11 +486,11 @@
         scratch_shapes=[
             pltpu.VMEM(turned.shape, BF16),
             vmem(4, 16, pairs),
-            pltpu.SemaphoreType.DMA((2, width // CHUNK)),
+            pltpu.SemaphoreType.DMA((5,)),
         ],
         compiler_params=params,
         name="clean",
-    )(me, held, *waves, *model)
+    )(me, held, held_too, *waves, *model)
     return jnp.transpose(cleaned, (0, 1, 2, 4, 3)), gains
 
 

time: 42.5 us -> 41.6 us (0.979)
  waiting for transfers between devices: 9.52 us -> 8.83 us
    ppermute x14, waiting for transfers between devices: 9.52 us -> 8.83 us  [partner(): return lax.ppermute(value, 'sub', [(i, i ^ bits) for i in range(count)])]
    pallas_call x2, Pallas kernels: 1.85 us -> 2.51 us  [local(): pl.pallas_call(lambda *refs: phase_kernel(width, t, reach, *refs), in_spe...]
    pallas_call x1, Pallas kernels: 4.82 us -> 4.39 us  [local(): pl.pallas_call(lambda *refs: clean_kernel(width, *refs), in_specs=[smem()...]
  transfers between devices with their start and end apart: 14 -> 14, of which waited for: 9 -> 8; matrix products, arithmetic and copies ran while one was open for 0% -> 0% of each run, Pallas kernels for 5% -> 6%
where the time goes in v10:
time: 41.6 us; the launch traced here: 41.3 us
  starting transfers between devices  15.1 us (36%)
  Pallas kernels  14.6 us (35%)
  waiting for transfers between devices  8.83 us (21%)
  local copies, waits for them, and re-layouts  2.07 us (5%)
  between operations  0.72 us (2%)
    ppermute x14, starting transfers between devices, partner(): return lax.ppermute(value, 'sub', [(i, i ^ bits) for i in range(count)])  15.1 us
    ppermute x14, waiting for transfers between devices, partner(): return lax.ppermute(value, 'sub', [(i, i ^ bits) for i in range(count)])  8.83 us
    pallas_call x1, Pallas kernels, local(): pl.pallas_call(lambda *refs: sums_kernel(width, reach, *refs), in_specs=[...  5.56 us
    pallas_call x1, Pallas kernels, local(): pl.pallas_call(lambda *refs: clean_kernel(width, *refs), in_specs=[smem()...  4.39 us
    pallas_call x2, Pallas kernels, local(): pl.pallas_call(lambda *refs: phase_kernel(width, t, reach, *refs), in_spe...  2.51 us
    pallas_call x1, Pallas kernels, local(): pl.pallas_call(lambda *refs: solve_kernel(float(window_count), *refs), in...  2.07 us
    unnamed x11, local copies, waits for them, and re-layouts  2.07 us
  transfers between devices with their start and end apart: 14, of which 8 were waited for; matrix products, arithmetic and copies ran while one was open for 0% of the time, Pallas kernels for 6%

profile of v10, /device:TPU:0, one launch (start us, length us, event | category | flops | bytes accessed | tf_op | source)
XLA Modules:
  0.0 41.3 jit_solution(12467661685992976264)
XLA Ops:
  0.6 2.5 %collective-permute-start.2 = (s32[1,2,192]{2,1,0:T(2,128)}, s32[1,2,192]{2,1,0:T(2,128)S(1)}, u32[]{:S(2)}, u32[]{:S(2)}) collective-permute-start(s32[1,2,192]{2,1,0:T(2,128)} %bitcast.16), channel_id=1, source_target_pairs={{0,3},{1,2},{2,1},{3,0},{4,7},{5,6},{6,5},{7,4},{8,11},{9,10},{10,... | collective-permute-start | bytes 4616 | tf_op jit(solution)/shard_map/ppermute | solution.py:385
  3.1 0.6 %collective-permute-start.1 = (s32[1,2,192]{2,1,0:T(2,128)}, s32[1,2,192]{2,1,0:T(2,128)S(1)}, u32[]{:S(2)}, u32[]{:S(2)}) collective-permute-start(s32[1,2,192]{2,1,0:T(2,128)} %bitcast.17), channel_id=1, source_target_pairs={{0,2},{1,3},{2,0},{3,1},{4,6},{5,7},{6,4},{7,5},{8,10},{9,11},{10,... | collective-permute-start | bytes 4616 | tf_op jit(solution)/shard_map/ppermute | solution.py:385
  3.7 0.0 collective-permute-start
  3.8 0.0 copy-start
  3.8 0.7 %copy-done = f32[2,2,703]{2,1,0:T(2,128)S(1)} copy-done((f32[2,2,703]{2,1,0:T(2,128)S(1)}, f32[2,2,703]{2,1,0:T(2,128)}, u32[]{:S(2)}) %copy-start) | copy-done | bytes 11272
  4.5 0.0 copy-start.3
  4.5 0.7 %copy-done.3 = s32[2,192]{1,0:T(2,128)S(1)} copy-done((s32[2,192]{1,0:T(2,128)S(1)}, s32[2,192]{1,0:T(2,128)}, u32[]{:S(2)}) %copy-start.3) | copy-done | bytes 1560
  5.2 0.8 %phases.3 = (f32[2,2,192,703]{3,2,1,0:T(8,128)S(1)}, bf16[2,2,192,703]{3,2,1,0:T(8,128)(2,1)S(1)}, s32[1,2,192]{2,1,0:T(2,128)S(1)}) custom-call(s32[1]{0:T(128)} %bitcast.refs_0_, f32[2,2,703]{2,1,0:T(2,128)S(1)} %copy-done, s32[1,2,192]{2,1,0:T(2,128)S(1)} %bitcast.19), custom_call_target="tpu_custom_call" | custom-call | flops 10000000 | bytes 6291456 | tf_op jit(solution)/shard_map/phases/pallas_call | solution.py:434
  6.0 0.0 collective-permute-done
  6.0 0.9 %collective-permute-done.1 = s32[1,2,192]{2,1,0:T(2,128)S(1)} collective-permute-done((s32[1,2,192]{2,1,0:T(2,128)}, s32[1,2,192]{2,1,0:T(2,128)S(1)}, u32[]{:S(2)}, u32[]{:S(2)}) %collective-permute-start.1) | collective-permute-done | bytes 1568 | tf_op jit(solution)/shard_map/ppermute | solution.py:385
  6.9 0.0 collective-permute-done.2
  6.9 3.7 %collective-permute-start.4 = (s32[4,2,192]{2,1,0:T(2,128)S(1)}, s32[4,2,192]{2,1,0:T(2,128)S(1)}, u32[]{:S(2)}, u32[]{:S(2)}) collective-permute-start(s32[4,2,192]{2,1,0:T(2,128)S(1)} %constant_dynamic-update-slice_fusion.refs_1_), channel_id=1, source_target_pairs={{0,12},{1,13},{2,14},{3,15},{4,8},{5,9},{6,10},{7,11},{8,4},{9,5},... | collective-permute-start | bytes 18440 | tf_op jit(solution)/shard_map/ppermute | solution.py:385
  10.6 0.0 collective-permute-start.3
  10.6 0.0 copy-start.2
  10.6 0.7 %copy-done.2 = s32[32]{0:T(128)S(1)} copy-done((s32[32]{0:T(128)S(1)}, s32[32]{0:T(128)}, u32[]{:S(2)}) %copy-start.2) | copy-done | bytes 152
  11.2 1.7 %phases.2 = (f32[2,2,192,703]{3,2,1,0:T(8,128)S(1)}, bf16[2,2,192,703]{3,2,1,0:T(8,128)(2,1)S(1)}, bf16[2,4,192,703]{3,2,1,0:T(8,128)(2,1)S(1)}, f32[2,2,16,703]...) custom-call(s32[1]{0:T(128)} %bitcast.refs_0_, ...), custom_call_target="tpu_custom_call" | custom-call | flops 10000000 | bytes 6291456 | tf_op jit(solution)/shard_map/phases/pallas_call | solution.py:434
  12.9 0.0 collective-permute-done.4.refs_3_
  12.9 1.3 %collective-permute-done.3.refs_2_ = s32[4,2,192]{2,1,0:T(2,128)S(1)} collective-permute-done((s32[4,2,192]{2,1,0:T(2,128)S(1)}, s32[4,2,192]{2,1,0:T(2,128)S(1)}, u32[]{:S(2)}, u32[]{:S(2)}) %collective-permute-start.3) | collective-permute-done | bytes 6176 | tf_op jit(solution)/shard_map/ppermute | solution.py:385
  14.2 0.0 copy-start.1
  14.2 5.6 %window_sums.1 = (f32[4,2,703]{2,1,0:T(2,128)S(1)}, f32[4,2,703]{2,1,0:T(2,128)S(1)}, f32[4,2,703]{2,1,0:T(2,128)S(1)}, f32[4,2,703]{2,1,0:T(2,128)S(1)}, bf16[2,4,192,703]{3,2,1,0:T(8,128)(2,1)S(1)}) custom-call(s32[1]{0:T(128)} %bitcast.refs_0_, s32[4,2,192]{2,1,0:T(2,128)S(1)} %constant_dynamic-update-slice_fusion.refs_1_, ...), custom_call_target="tpu_custom_call" | custom-call | tf_op jit(solution)/shard_map/window_sums/pallas_call | solution.py:452
  19.8 0.1 collective-permute-start.5
  19.9 1.0 %collective-permute-start.6 = (f32[4,2,703]{2,1,0:T(2,128)S(1)}, f32[4,2,703]{2,1,0:T(2,128)S(1)}, u32[]{:S(2)}, u32[]{:S(2)}) collective-permute-start(f32[4,2,703]{2,1,0:T(2,128)S(1)} %get-tuple-element.34), channel_id=1, source_target_pairs={{0,2},{1,3},{2,0},{3,1},{4,6},{5,7},{6,4},{7,5},{8,10},{9,11},{10,... | collective-permute-start | bytes 67496 | tf_op jit(solution)/shard_map/ppermute | solution.py:385
  20.9 0.9 %collective-permute-start.7 = (f32[4,2,703]{2,1,0:T(2,128)S(1)}, f32[4,2,703]{2,1,0:T(2,128)S(1)}, u32[]{:S(2)}, u32[]{:S(2)}) collective-permute-start(f32[4,2,703]{2,1,0:T(2,128)S(1)} %get-tuple-element.35), channel_id=1, source_target_pairs={{0,3},{1,2},{2,1},{3,0},{4,7},{5,6},{6,5},{7,4},{8,11},{9,10},{10,... | collective-permute-start | bytes 67496 | tf_op jit(solution)/shard_map/ppermute | solution.py:385
  21.7 0.0 collective-permute-done.5
  21.7 2.0 %collective-permute-done.6 = f32[4,2,703]{2,1,0:T(2,128)S(1)} collective-permute-done((f32[4,2,703]{2,1,0:T(2,128)S(1)}, f32[4,2,703]{2,1,0:T(2,128)S(1)}, u32[]{:S(2)}, u32[]{:S(2)}) %collective-permute-start.6) | collective-permute-done | bytes 22528 | tf_op jit(solution)/shard_map/ppermute | solution.py:385
  23.8 0.3 collective-permute-done.7
  24.1 1.9 %collective-permute-start.10 = (f32[4,2,703]{2,1,0:T(2,128)S(1)}, f32[4,2,703]{2,1,0:T(2,128)S(1)}, u32[]{:S(2)}, u32[]{:S(2)}) collective-permute-start(f32[4,2,703]{2,1,0:T(2,128)S(1)} %bitcast.10), channel_id=1, source_target_pairs={{0,12},{1,13},{2,14},{3,15},{4,8},{5,9},{6,10},{7,11},{8,4},{9,5},... | collective-permute-start | bytes 67496 | tf_op jit(solution)/shard_map/ppermute | solution.py:385
  26.0 0.4 collective-permute-start.9
  26.4 2.2 %collective-permute-start.8 = (f32[4,2,703]{2,1,0:T(2,128)S(1)}, f32[4,2,703]{2,1,0:T(2,128)S(1)}, u32[]{:S(2)}, u32[]{:S(2)}) collective-permute-start(f32[4,2,703]{2,1,0:T(2,128)S(1)} %bitcast.12), channel_id=1, source_target_pairs={{0,4},{1,5},{2,6},{3,7},{4,0},{5,1},{6,2},{7,3},{8,12},{9,13},{10,... | collective-permute-start | bytes 67496 | tf_op jit(solution)/shard_map/ppermute | solution.py:385
  28.6 0.1 station_hots.1.refs_2_
  28.6 1.3 %collective-permute-done.10.refs_6_ = f32[4,2,703]{2,1,0:T(2,128)S(1)} collective-permute-done((f32[4,2,703]{2,1,0:T(2,128)S(1)}, f32[4,2,703]{2,1,0:T(2,128)S(1)}, u32[]{:S(2)}, u32[]{:S(2)}) %collective-permute-start.10) | collective-permute-done | bytes 22528 | tf_op jit(solution)/shard_map/ppermute | solution.py:385
  29.9 0.8 %collective-permute-done.9.refs_5_ = f32[4,2,703]{2,1,0:T(2,128)S(1)} collective-permute-done((f32[4,2,703]{2,1,0:T(2,128)S(1)}, f32[4,2,703]{2,1,0:T(2,128)S(1)}, u32[]{:S(2)}, u32[]{:S(2)}) %collective-permute-start.9) | collective-permute-done | bytes 22528 | tf_op jit(solution)/shard_map/ppermute | solution.py:385
  30.7 0.0 collective-permute-done.8.refs_4_
  30.7 0.0 copy-done.1
  30.7 2.1 %gain_solve.1.refs_5_ = f32[4,2,806]{2,1,0:T(2,128)S(1)} custom-call(s32[1]{0:T(128)} %bitcast.refs_0_, s32[2,2]{1,0:T(2,128)S(1)} %copy-done.1, bf16[2,40,703]{2,1,0:T(8,128)(2,1)S(1)} %station_hots.1.refs_2_, f32[4,2,703]{2,1,0:T(2,128)S(1)} %bitcast.13, f32[4,2,703]{2,1,0:T(2,128)S(1)} %collective-permute-done.8.refs_4_, ...), custom_call_target="tpu_custom_call" | custom-call | tf_op jit(solution)/shard_map/gain_solve/pallas_call | solution.py:469
  32.8 0.1 collective-permute-start.13
  32.9 1.2 %collective-permute-start.12 = (f32[4,2,806]{2,1,0:T(2,128)S(1)}, f32[4,2,806]{2,1,0:T(2,128)S(1)}, u32[]{:S(2)}, u32[]{:S(2)}) collective-permute-start(f32[4,2,806]{2,1,0:T(2,128)S(1)} %gain_solve.1.refs_5_), channel_id=1, source_target_pairs={{0,2},{1,3},{2,0},{3,1},{4,6},{5,7},{6,4},{7,5},{8,10},{9,11},{10,... | collective-permute-start | bytes 77384 | tf_op jit(solution)/shard_map/ppermute | solution.py:385
  34.0 0.7 %collective-permute-start.11 = (f32[4,2,806]{2,1,0:T(2,128)S(1)}, f32[4,2,806]{2,1,0:T(2,128)S(1)}, u32[]{:S(2)}, u32[]{:S(2)}) collective-permute-start(f32[4,2,806]{2,1,0:T(2,128)S(1)} %gain_solve.1.refs_5_), channel_id=1, source_target_pairs={{0,1},{1,0},{2,3},{3,2},{4,5},{5,4},{6,7},{7,6},{8,9},{9,8},{10,11... | collective-permute-start | bytes 77384 | tf_op jit(solution)/shard_map/ppermute | solution.py:385
  34.7 1.4 %collective-permute-done.13.refs_8_ = f32[4,2,806]{2,1,0:T(2,128)S(1)} collective-permute-done((f32[4,2,806]{2,1,0:T(2,128)S(1)}, f32[4,2,806]{2,1,0:T(2,128)S(1)}, u32[]{:S(2)}, u32[]{:S(2)}) %collective-permute-start.13) | collective-permute-done | bytes 25824 | tf_op jit(solution)/shard_map/ppermute | solution.py:385
  36.2 0.8 %collective-permute-done.12.refs_7_ = f32[4,2,806]{2,1,0:T(2,128)S(1)} collective-permute-done((f32[4,2,806]{2,1,0:T(2,128)S(1)}, f32[4,2,806]{2,1,0:T(2,128)S(1)}, u32[]{:S(2)}, u32[]{:S(2)}) %collective-permute-start.12) | collective-permute-done | bytes 25824 | tf_op jit(solution)/shard_map/ppermute | solution.py:385
  36.9 0.0 collective-permute-done.11.refs_6_
  36.9 4.4 %clean.1 = (bf16[2,2,4,192,703]{4,3,2,1,0:T(8,128)(2,1)}, f32[2,2,2,4,38]{4,3,2,1,0:T(4,128)}) custom-call(s32[1]{0:T(128)} %bitcast.refs_0_, bf16[2,4,192,703]{3,2,1,0:T(8,128)(2,1)S(1)} %get-tuple-element.20.refs_10_.refs_1_, bf16[2,4,192,703]{3,2,1,0:T(8,128)(2,1)S(1)} %get-tuple-element.31.refs_2_, ...), custom_call_target="tpu_custom_call" | custom-call | tf_op jit(solution)/shard_map/clean/pallas_call | solution.py:478
  (5 shorter events, 0.0 us)
Async XLA Ops:
  0.6 6.3 %collective-permute-start.2 = (s32[1,2,192]{2,1,0:T(2,128)}, s32[1,2,192]{2,1,0:T(2,128)S(1)}, u32[]{:S(2)}, u32[]{:S(2)}) collective-permute-start(s32[1,2,192]{2,1,0:T(2,128)} %bitcast.16), channel_id=1, source_target_pairs={{0,3},{1,2},{2,1},{3,0},{4,7},{5,6},{6,5},{7,4},{8,11},{9,10},{10,... | collective-permute-start | bytes 4616 | tf_op jit(solution)/shard_map/ppermute | solution.py:385
  3.1 3.8 %collective-permute-start.1 = (s32[1,2,192]{2,1,0:T(2,128)}, s32[1,2,192]{2,1,0:T(2,128)S(1)}, u32[]{:S(2)}, u32[]{:S(2)}) collective-permute-start(s32[1,2,192]{2,1,0:T(2,128)} %bitcast.17), channel_id=1, source_target_pairs={{0,2},{1,3},{2,0},{3,1},{4,6},{5,7},{6,4},{7,5},{8,10},{9,11},{10,... | collective-permute-start | bytes 4616 | tf_op jit(solution)/shard_map/ppermute | solution.py:385
  3.7 2.3 %collective-permute-start = (s32[1,2,192]{2,1,0:T(2,128)}, s32[1,2,192]{2,1,0:T(2,128)S(1)}, u32[]{:S(2)}, u32[]{:S(2)}) collective-permute-start(s32[1,2,192]{2,1,0:T(2,128)} %bitcast.18), channel_id=1, source_target_pairs={{0,1},{1,0},{2,3},{3,2},{4,5},{5,4},{6,7},{7,6},{8,9},{9,8},{10,11... | collective-permute-start | bytes 4616 | tf_op jit(solution)/shard_map/ppermute | solution.py:385
  3.8 0.7 %copy-start = (f32[2,2,703]{2,1,0:T(2,128)S(1)}, f32[2,2,703]{2,1,0:T(2,128)}, u32[]{:S(2)}) copy-start(f32[2,2,703]{2,1,0:T(2,128)} %refs_1_.2) | copy-start | bytes 33748
  4.5 0.7 %copy-start.3 = (s32[2,192]{1,0:T(2,128)S(1)}, s32[2,192]{1,0:T(2,128)}, u32[]{:S(2)}) copy-start(s32[2,192]{1,0:T(2,128)} %param.7) | copy-start | bytes 4612
  6.9 6.0 %collective-permute-start.4 = (s32[4,2,192]{2,1,0:T(2,128)S(1)}, s32[4,2,192]{2,1,0:T(2,128)S(1)}, u32[]{:S(2)}, u32[]{:S(2)}) collective-permute-start(s32[4,2,192]{2,1,0:T(2,128)S(1)} %constant_dynamic-update-slice_fusion.refs_1_), channel_id=1, source_target_pairs={{0,12},{1,13},{2,14},{3,15},{4,8},{5,9},{6,10},{7,11},{8,4},{9,5},... | collective-permute-start | bytes 18440 | tf_op jit(solution)/shard_map/ppermute | solution.py:385
  10.6 3.7 %collective-permute-start.3 = (s32[4,2,192]{2,1,0:T(2,128)S(1)}, s32[4,2,192]{2,1,0:T(2,128)S(1)}, u32[]{:S(2)}, u32[]{:S(2)}) collective-permute-start(s32[4,2,192]{2,1,0:T(2,128)S(1)} %constant_dynamic-update-slice_fusion.refs_1_), channel_id=1, source_target_pairs={{0,4},{1,5},{2,6},{3,7},{4,0},{5,1},{6,2},{7,3},{8,12},{9,13},{10,... | collective-permute-start | bytes 18440 | tf_op jit(solution)/shard_map/ppermute | solution.py:385
  10.6 0.7 %copy-start.2 = (s32[32]{0:T(128)S(1)}, s32[32]{0:T(128)}, u32[]{:S(2)}) copy-start(s32[32]{0:T(128)} %param.8) | copy-start | bytes 388
  14.2 16.5 %copy-start.1 = (s32[2,2]{1,0:T(2,128)S(1)}, s32[2,2]{1,0:T(2,128)}, u32[]{:S(2)}) copy-start(s32[2,2]{1,0:T(2,128)} %refs_1_.3) | copy-start | bytes 52
  19.8 1.9 %collective-permute-start.5 = (f32[4,2,703]{2,1,0:T(2,128)S(1)}, f32[4,2,703]{2,1,0:T(2,128)S(1)}, u32[]{:S(2)}, u32[]{:S(2)}) collective-permute-start(f32[4,2,703]{2,1,0:T(2,128)S(1)} %get-tuple-element.33), channel_id=1, source_target_pairs={{0,1},{1,0},{2,3},{3,2},{4,5},{5,4},{6,7},{7,6},{8,9},{9,8},{10,11... | collective-permute-start | bytes 67496 | tf_op jit(solution)/shard_map/ppermute | solution.py:385
  19.9 3.9 %collective-permute-start.6 = (f32[4,2,703]{2,1,0:T(2,128)S(1)}, f32[4,2,703]{2,1,0:T(2,128)S(1)}, u32[]{:S(2)}, u32[]{:S(2)}) collective-permute-start(f32[4,2,703]{2,1,0:T(2,128)S(1)} %get-tuple-element.34), channel_id=1, source_target_pairs={{0,2},{1,3},{2,0},{3,1},{4,6},{5,7},{6,4},{7,5},{8,10},{9,11},{10,... | collective-permute-start | bytes 67496 | tf_op jit(solution)/shard_map/ppermute | solution.py:385
  20.9 3.3 %collective-permute-start.7 = (f32[4,2,703]{2,1,0:T(2,128)S(1)}, f32[4,2,703]{2,1,0:T(2,128)S(1)}, u32[]{:S(2)}, u32[]{:S(2)}) collective-permute-start(f32[4,2,703]{2,1,0:T(2,128)S(1)} %get-tuple-element.35), channel_id=1, source_target_pairs={{0,3},{1,2},{2,1},{3,0},{4,7},{5,6},{6,5},{7,4},{8,11},{9,10},{10,... | collective-permute-start | bytes 67496 | tf_op jit(solution)/shard_map/ppermute | solution.py:385
  24.1 5.8 %collective-permute-start.10 = (f32[4,2,703]{2,1,0:T(2,128)S(1)}, f32[4,2,703]{2,1,0:T(2,128)S(1)}, u32[]{:S(2)}, u32[]{:S(2)}) collective-permute-start(f32[4,2,703]{2,1,0:T(2,128)S(1)} %bitcast.10), channel_id=1, source_target_pairs={{0,12},{1,13},{2,14},{3,15},{4,8},{5,9},{6,10},{7,11},{8,4},{9,5},... | collective-permute-start | bytes 67496 | tf_op jit(solution)/shard_map/ppermute | solution.py:385
  26.0 4.7 %collective-permute-start.9 = (f32[4,2,703]{2,1,0:T(2,128)S(1)}, f32[4,2,703]{2,1,0:T(2,128)S(1)}, u32[]{:S(2)}, u32[]{:S(2)}) collective-permute-start(f32[4,2,703]{2,1,0:T(2,128)S(1)} %bitcast.11), channel_id=1, source_target_pairs={{0,8},{1,9},{2,10},{3,11},{4,12},{5,13},{6,14},{7,15},{8,0},{9,1},... | collective-permute-start | bytes 67496 | tf_op jit(solution)/shard_map/ppermute | solution.py:385
  26.4 4.3 %collective-permute-start.8 = (f32[4,2,703]{2,1,0:T(2,128)S(1)}, f32[4,2,703]{2,1,0:T(2,128)S(1)}, u32[]{:S(2)}, u32[]{:S(2)}) collective-permute-start(f32[4,2,703]{2,1,0:T(2,128)S(1)} %bitcast.12), channel_id=1, source_target_pairs={{0,4},{1,5},{2,6},{3,7},{4,0},{5,1},{6,2},{7,3},{8,12},{9,13},{10,... | collective-permute-start | bytes 67496 | tf_op jit(solution)/shard_map/ppermute | solution.py:385
  32.8 3.4 %collective-permute-start.13 = (f32[4,2,806]{2,1,0:T(2,128)S(1)}, f32[4,2,806]{2,1,0:T(2,128)S(1)}, u32[]{:S(2)}, u32[]{:S(2)}) collective-permute-start(f32[4,2,806]{2,1,0:T(2,128)S(1)} %gain_solve.1.refs_5_), channel_id=1, source_target_pairs={{0,3},{1,2},{2,1},{3,0},{4,7},{5,6},{6,5},{7,4},{8,11},{9,10},{10,... | collective-permute-start | bytes 77384 | tf_op jit(solution)/shard_map/ppermute | solution.py:385
  32.9 4.1 %collective-permute-start.12 = (f32[4,2,806]{2,1,0:T(2,128)S(1)}, f32[4,2,806]{2,1,0:T(2,128)S(1)}, u32[]{:S(2)}, u32[]{:S(2)}) collective-permute-start(f32[4,2,806]{2,1,0:T(2,128)S(1)} %gain_solve.1.refs_5_), channel_id=1, source_target_pairs={{0,2},{1,3},{2,0},{3,1},{4,6},{5,7},{6,4},{7,5},{8,10},{9,11},{10,... | collective-permute-start | bytes 77384 | tf_op jit(solution)/shard_map/ppermute | solution.py:385
  34.0 2.9 %collective-permute-start.11 = (f32[4,2,806]{2,1,0:T(2,128)S(1)}, f32[4,2,806]{2,1,0:T(2,128)S(1)}, u32[]{:S(2)}, u32[]{:S(2)}) collective-permute-start(f32[4,2,806]{2,1,0:T(2,128)S(1)} %gain_solve.1.refs_5_), channel_id=1, source_target_pairs={{0,1},{1,0},{2,3},{3,2},{4,5},{5,4},{6,7},{7,6},{8,9},{9,8},{10,11... | collective-permute-start | bytes 77384 | tf_op jit(solution)/shard_map/ppermute | solution.py:385

commit v11 on v10

--- a/solution.py
+++ b/solution.py
@@ -12,8 +12,8 @@
 STEPS_PER_TURN = 64
 GAINS_AT = 768
 GRANT = 42
-GRANTS = (50, 45)
-ROWS = 40
+GRANTS = (47, 45)
+ROWS = 48
 
 F32 = jnp.float32
 BF16 = jnp.bfloat16
@@ -78,6 +78,11 @@
     return fine, coarse
 
 
+def visibility(vis_refs, ri, t, k, rows, lanes):
+    ref, at = (vis_refs[2], k) if t else (vis_refs[k // 2], k % 2)
+    return ref[ri, at, rows, lanes].astype(F32)
+
+
 def tiles(pairs, body):
     full = pairs // 128
 
@@ -93,13 +98,14 @@
 def phase_kernel(width, t, reach, me_ref, *refs):
     anchor = me_ref[0].astype(F32) * float(width)
     if t == 0:
-        delay_ref, flag_ref, wave_ref, mix_ref, own_ref = refs
+        vis_hbm, delay_ref, flag_ref, win_ref, wave_ref, mix_ref, vis_ref, own_ref, win_out_ref, sem = refs
     else:
         vis_hbm, delay_ref, win_ref, wave_ref, mix_ref, vis_ref, apart_ref, *mask_refs, sem = refs
-        copy = pltpu.make_async_copy(vis_hbm.at[:, 0], vis_ref, sem)
-        copy.start()
+    copy = pltpu.make_async_copy(vis_hbm.at[:, 0, 2 * t:2 * t + 2], vis_ref, sem)
+    copy.start()
     if t == 0:
         own_ref[...] = flag_ref[...]
+        win_out_ref[...] = win_ref[...]
     else:
         window_masks(width, reach, me_ref[0], win_ref, *mask_refs)
         apart = blocks_apart(me_ref[0], reach, apart_ref.shape[2])
@@ -131,8 +137,7 @@
                 mix_ref[slot, 1, rows, lanes] = low
 
     tiles(pairs, waves)
-    if t == 1:
-        copy.wait()
+    copy.wait()
 
 
 def blocks_apart(me, reach, rows):
@@ -170,9 +175,9 @@
 def sums_kernel(width, reach, me_ref, *refs):
     flag_refs, refs = refs[:3], refs[3:]
     apart_ref, inside_ref, chosen_ref, outside_ref, ends_ref = refs[:5]
-    vis_hbm, first_ref, wave_refs, mix_refs, refs = refs[5], refs[6], refs[7:9], refs[9:11], refs[11:]
+    vis_hbm, first_refs, wave_refs, mix_refs, refs = refs[5], refs[6:8], refs[8:10], refs[10:12], refs[12:]
     out_refs, (second_ref, alpha_s, mexp_s, wt_s, sem) = refs[:4], refs[4:]
-    vis_refs = (first_ref, second_ref)
+    vis_refs = (*first_refs, second_ref)
     copy = pltpu.make_async_copy(vis_hbm.at[:, 1], second_ref, sem)
     copy.start()
     me = me_ref[0]
@@ -232,8 +237,8 @@
                     factors.append((fr, fi - fr, fr + fi))
                 new = []
                 for k in range(4):
-                    vr = vis_refs[t][0, k, rows, lanes].astype(F32)
-                    vi = vis_refs[t][1, k, rows, lanes].astype(F32)
+                    vr = visibility(vis_refs, 0, t, k, rows, lanes)
+                    vi = visibility(vis_refs, 1, t, k, rows, lanes)
                     vs = vr + vi
                     for s in range(2):
                         for v, f in zip((vs, vr, vi), factors[s]):
@@ -333,8 +338,8 @@
 
 
 def clean_kernel(width, me_ref, *refs):
-    vis_refs, wave_refs, piece_refs = refs[:2], refs[2:4], refs[4:8]
-    out_hbm, gain_out_ref, out_s, model_s, sems = refs[8:]
+    vis_refs, wave_refs, piece_refs = refs[:3], refs[3:5], refs[5:9]
+    out_hbm, gain_out_ref, out_s, model_s, sems = refs[9:]
     pairs = wave_refs[0].shape[3]
     mine = lax.bitwise_and(me_ref[0], 3)
     for d, piece in enumerate(piece_refs):
@@ -366,8 +371,8 @@
                         one, two = (waves[s][slot] * model_s[t + 2 * s, 3 * k + slot:3 * k + slot + 1, lanes]
                                     for s in range(2))
                         sums.append(one + two)
-                    vr = vis_refs[t][0, k, rows, lanes].astype(F32)
-                    vi = vis_refs[t][1, k, rows, lanes].astype(F32)
+                    vr = visibility(vis_refs, 0, t, k, rows, lanes)
+                    vi = visibility(vis_refs, 1, t, k, rows, lanes)
                     out_s[0, t, k, rows, lanes] = (vr - (sums[0] - sums[2])).astype(BF16)
                     out_s[1, t, k, rows, lanes] = (vi - (sums[0] + sums[1])).astype(BF16)
 
@@ -401,6 +406,7 @@
     vmem = lambda *shape: pltpu.VMEM(shape, F32)
     params = pltpu.CompilerParams(vmem_limit_bytes=24 * 2 ** 20)
     flags = flags[None]
+    windows = windows.reshape(1, window_count)
 
     reach = count // 4
     remote_rows = 16 * pl.cdiv(4 * reach, 16)
@@ -421,44 +427,43 @@
             shape(2, 2, width, pairs),
             jax.ShapeDtypeStruct((2, 2, width, pairs), BF16),
         ]
+        out_shape += [jax.ShapeDtypeStruct((2, 2, width, pairs), BF16)]
         if t == 0:
-            operands = (me, delays, flags)
-            in_specs = [smem()] + [vmem_ref] * 2
-            out_shape += [jax.ShapeDtypeStruct(flags.shape, flags.dtype)]
+            operands = (me, turned, delays, flags, windows)
+            out_shape += [jax.ShapeDtypeStruct(flags.shape, flags.dtype),
+                          jax.ShapeDtypeStruct(windows.shape, windows.dtype)]
         else:
-            operands = (me, turned, delays, windows.reshape(1, window_count))
-            in_specs = [smem(), hbm_ref] + [vmem_ref] * 2
-            out_shape += [jax.ShapeDtypeStruct((2, 4, width, pairs), BF16),
-                          shape(2, 2, remote_rows, pairs), shape(window_count, width), shape(width, window_count),
+            operands = (me, turned, delays, made[0][4])
+            out_shape += [shape(2, 2, remote_rows, pairs), shape(window_count, width), shape(width, window_count),
                           shape(remote_rows, width), shape(2, window_count, 128)]
         made.append(pl.pallas_call(
             lambda *refs: phase_kernel(width, t, reach, *refs),
-            in_specs=in_specs,
+            in_specs=[smem(), hbm_ref] + [vmem_ref] * (len(operands) - 2),
             out_specs=[vmem_ref] * len(out_shape),
             out_shape=out_shape,
-            scratch_shapes=[pltpu.SemaphoreType.DMA] * t,
+            scratch_shapes=[pltpu.SemaphoreType.DMA],
             compiler_params=pltpu.CompilerParams(vmem_limit_bytes=GRANTS[t] * 2 ** 20),
             cost_estimate=pl.CostEstimate(flops=10 ** 7, bytes_accessed=6 * 2 ** 20, transcendentals=0),
             name="phases",
         )(*operands))
         if t == 0:
-            gathered = jnp.concatenate([made[0][2]] + beside, axis=0)
+            gathered = jnp.concatenate([made[0][3]] + beside, axis=0)
             while gathered.shape[0] < reach:
                 stride = gathered.shape[0]
                 gathered = jnp.concatenate([gathered] + [partner(gathered, stride * d) for d in range(1, 4)], axis=0)
             gathered = [gathered] + [partner(gathered, d * reach) for d in (1, 3)]
-    waves, mixing = ([part[i] for part in made] for i in range(2))
-    held, *masks = made[1][2:]
+    waves, mixing, held = ([part[i] for part in made] for i in range(3))
+    masks = made[1][3:]
     *quarters, held_too = pl.pallas_call(
         lambda *refs: sums_kernel(width, reach, *refs),
-        in_specs=[smem()] + [vmem_ref] * 8 + [hbm_ref] + [vmem_ref] * 5,
+        in_specs=[smem()] + [vmem_ref] * 8 + [hbm_ref] + [vmem_ref] * 6,
         out_specs=[vmem_ref] * 5,
-        out_shape=[jax.ShapeDtypeStruct((4, 2, pairs), F32)] * 4 + [jax.ShapeDtypeStruct(held.shape, BF16)],
+        out_shape=[jax.ShapeDtypeStruct((4, 2, pairs), F32)] * 4 + [jax.ShapeDtypeStruct((2, 4, width, pairs), BF16)],
         scratch_shapes=[vmem(2, width, 128), vmem(2, 2, width, pairs), vmem(2, remote_rows, width),
                         pltpu.SemaphoreType.DMA],
         compiler_params=pltpu.CompilerParams(vmem_limit_bytes=GRANT * 2 ** 20),
         name="window_sums",
-    )(me, *gathered, *masks, turned, held, *waves, *mixing)
+    )(me, *gathered, *masks, turned, *held, *waves, *mixing)
     pieces = [quarters[0]] + [partner(quarters[d], d) for d in range(1, 4)]
     stride = 4
     while stride < count:
@@ -477,7 +482,7 @@
     model = [model] + [partner(model, d) for d in range(1, 4)]
     cleaned, gains = pl.pallas_call(
         lambda *refs: clean_kernel(width, *refs),
-        in_specs=[smem()] + [vmem_ref] * 8,
+        in_specs=[smem()] + [vmem_ref] * 9,
         out_specs=[hbm_ref, vmem_ref],
         out_shape=[
             jax.ShapeDtypeStruct(turned.shape, BF16),
@@ -490,7 +495,7 @@
         ],
         compiler_params=params,
         name="clean",
-    )(me, held, held_too, *waves, *model)
+    )(me, *held, held_too, *waves, *model)
     return jnp.transpose(cleaned, (0, 1, 2, 4, 3)), gains
 
 

time: 41.6 us -> 43 us (1.034)
  waiting for transfers between devices: 8.83 us -> 9.66 us
    ppermute x14, waiting for transfers between devices: 8.83 us -> 9.66 us  [partner(): return lax.ppermute(value, 'sub', [(i, i ^ bits) for i in range(count)])]
where the time goes in v11:
time: 43 us; the launch traced here: 42.7 us
  starting transfers between devices  15.3 us (36%)
  Pallas kernels  14.9 us (35%)
  waiting for transfers between devices  9.66 us (22%)
  local copies, waits for them, and re-layouts  2.08 us (5%)
  between operations  0.74 us (2%)
    ppermute x14, starting transfers between devices, partner(): return lax.ppermute(value, 'sub', [(i, i ^ bits) for i in range(count)])  15.3 us
    ppermute x14, waiting for transfers between devices, partner(): return lax.ppermute(value, 'sub', [(i, i ^ bits) for i in range(count)])  9.66 us
    pallas_call x1, Pallas kernels, local(): pl.pallas_call(lambda *refs: sums_kernel(width, reach, *refs), in_specs=[...  5.56 us
    pallas_call x1, Pallas kernels, local(): pl.pallas_call(lambda *refs: clean_kernel(width, *refs), in_specs=[smem()...  4.39 us
    pallas_call x2, Pallas kernels, local(): pl.pallas_call(lambda *refs: phase_kernel(width, t, reach, *refs), in_spe...  2.56 us
    pallas_call x1, Pallas kernels, local(): pl.pallas_call(lambda *refs: solve_kernel(float(window_count), *refs), in...  2.31 us
    unnamed x11, local copies, waits for them, and re-layouts  2.07 us
  transfers between devices with their start and end apart: 14, of which 8 were waited for; matrix products, arithmetic and copies ran while one was open for 0% of the time, Pallas kernels for 6%

profile of v11, /device:TPU:0, one launch (start us, length us, event | category | flops | bytes accessed | tf_op | source)
XLA Modules:
  0.0 42.7 jit_solution(5826933091678546611)
XLA Ops:
  0.6 2.5 %collective-permute-start.2 = (s32[1,2,192]{2,1,0:T(2,128)}, s32[1,2,192]{2,1,0:T(2,128)S(1)}, u32[]{:S(2)}, u32[]{:S(2)}) collective-permute-start(s32[1,2,192]{2,1,0:T(2,128)} %bitcast.15), channel_id=1, source_target_pairs={{0,3},{1,2},{2,1},{3,0},{4,7},{5,6},{6,5},{7,4},{8,11},{9,10},{10,... | collective-permute-start | bytes 4616 | tf_op jit(solution)/shard_map/ppermute | solution.py:390
  3.1 0.6 %collective-permute-start.1 = (s32[1,2,192]{2,1,0:T(2,128)}, s32[1,2,192]{2,1,0:T(2,128)S(1)}, u32[]{:S(2)}, u32[]{:S(2)}) collective-permute-start(s32[1,2,192]{2,1,0:T(2,128)} %bitcast.16), channel_id=1, source_target_pairs={{0,2},{1,3},{2,0},{3,1},{4,6},{5,7},{6,4},{7,5},{8,10},{9,11},{10,... | collective-permute-start | bytes 4616 | tf_op jit(solution)/shard_map/ppermute | solution.py:390
  3.7 0.0 collective-permute-start
  3.8 0.0 copy-start
  3.8 0.7 %copy-done = f32[2,2,703]{2,1,0:T(2,128)S(1)} copy-done((f32[2,2,703]{2,1,0:T(2,128)S(1)}, f32[2,2,703]{2,1,0:T(2,128)}, u32[]{:S(2)}) %copy-start) | copy-done | bytes 11272
  4.5 0.0 copy-start.1
  4.5 0.7 %copy-done.1 = s32[2,192]{1,0:T(2,128)S(1)} copy-done((s32[2,192]{1,0:T(2,128)S(1)}, s32[2,192]{1,0:T(2,128)}, u32[]{:S(2)}) %copy-start.1) | copy-done | bytes 1560
  5.2 0.0 copy-start.3
  5.2 0.7 %copy-done.3 = s32[32]{0:T(128)S(1)} copy-done((s32[32]{0:T(128)S(1)}, s32[32]{0:T(128)}, u32[]{:S(2)}) %copy-start.3) | copy-done | bytes 152
  5.8 1.3 %phases.2 = (f32[2,2,192,703]{3,2,1,0:T(8,128)S(1)}, bf16[2,2,192,703]{3,2,1,0:T(8,128)(2,1)S(1)}, bf16[2,2,192,703]{3,2,1,0:T(8,128)(2,1)S(1)}, s32[1,2,192]{2,1,0:T(2,128)S(1)}, s32[1,32]{1,0:T(1,128)S(1)}) custom-call(s32[1]{0:T(128)} %bitcast.refs_0_, bf16[2,2,4,192,703]{4,3,2,1,0:T(8,128)(2,1)} %bitcast.20, f32[2,2,703]{2,1,0:T(2,128)S(1)} %copy-done, ...), custom_call_target="tpu_custom_call" | custom-call | flops 10000000 | bytes 6291456 | tf_op jit(solution)/shard_map/phases/pallas_call | solution.py:439
  7.1 0.0 collective-permute-done
  7.1 0.0 collective-permute-done.1
  7.2 0.0 collective-permute-done.2
  7.2 3.9 %collective-permute-start.4 = (s32[4,2,192]{2,1,0:T(2,128)S(1)}, s32[4,2,192]{2,1,0:T(2,128)S(1)}, u32[]{:S(2)}, u32[]{:S(2)}) collective-permute-start(s32[4,2,192]{2,1,0:T(2,128)S(1)} %constant_dynamic-update-slice_fusion.refs_1_), channel_id=1, source_target_pairs={{0,12},{1,13},{2,14},{3,15},{4,8},{5,9},{6,10},{7,11},{8,4},{9,5},... | collective-permute-start | bytes 18440 | tf_op jit(solution)/shard_map/ppermute | solution.py:390
  11.1 0.0 collective-permute-start.3
  11.1 1.3 %phases.3 = (f32[2,2,192,703]{3,2,1,0:T(8,128)S(1)}, bf16[2,2,192,703]{3,2,1,0:T(8,128)(2,1)S(1)}, bf16[2,2,192,703]{3,2,1,0:T(8,128)(2,1)S(1)}, f32[2,2,16,703]...) custom-call(s32[1]{0:T(128)} %bitcast.refs_0_, ...), custom_call_target="tpu_custom_call" | custom-call | flops 10000000 | bytes 6291456 | tf_op jit(solution)/shard_map/phases/pallas_call | solution.py:439
  12.4 0.3 collective-permute-done.4.refs_3_
  12.7 2.0 %collective-permute-done.3.refs_2_ = s32[4,2,192]{2,1,0:T(2,128)S(1)} collective-permute-done((s32[4,2,192]{2,1,0:T(2,128)S(1)}, s32[4,2,192]{2,1,0:T(2,128)S(1)}, u32[]{:S(2)}, u32[]{:S(2)}) %collective-permute-start.3) | collective-permute-done | bytes 6176 | tf_op jit(solution)/shard_map/ppermute | solution.py:390
  14.7 0.0 copy-start.2
  14.7 5.6 %window_sums.1 = (f32[4,2,703]{2,1,0:T(2,128)S(1)}, f32[4,2,703]{2,1,0:T(2,128)S(1)}, f32[4,2,703]{2,1,0:T(2,128)S(1)}, f32[4,2,703]{2,1,0:T(2,128)S(1)}, bf16[2,4,192,703]{3,2,1,0:T(8,128)(2,1)S(1)}) custom-call(s32[1]{0:T(128)} %bitcast.refs_0_, s32[4,2,192]{2,1,0:T(2,128)S(1)} %constant_dynamic-update-slice_fusion.refs_1_, ...), custom_call_target="tpu_custom_call" | custom-call | tf_op jit(solution)/shard_map/window_sums/pallas_call | solution.py:457
  20.3 0.1 collective-permute-start.5
  20.4 1.6 %collective-permute-start.6 = (f32[4,2,703]{2,1,0:T(2,128)S(1)}, f32[4,2,703]{2,1,0:T(2,128)S(1)}, u32[]{:S(2)}, u32[]{:S(2)}) collective-permute-start(f32[4,2,703]{2,1,0:T(2,128)S(1)} %get-tuple-element.38), channel_id=1, source_target_pairs={{0,2},{1,3},{2,0},{3,1},{4,6},{5,7},{6,4},{7,5},{8,10},{9,11},{10,... | collective-permute-start | bytes 67496 | tf_op jit(solution)/shard_map/ppermute | solution.py:390
  22.0 0.3 collective-permute-start.7
  22.2 0.0 collective-permute-done.5
  22.2 2.0 %collective-permute-done.6 = f32[4,2,703]{2,1,0:T(2,128)S(1)} collective-permute-done((f32[4,2,703]{2,1,0:T(2,128)S(1)}, f32[4,2,703]{2,1,0:T(2,128)S(1)}, u32[]{:S(2)}, u32[]{:S(2)}) %collective-permute-start.6) | collective-permute-done | bytes 22528 | tf_op jit(solution)/shard_map/ppermute | solution.py:390
  24.3 0.9 %collective-permute-done.7 = f32[4,2,703]{2,1,0:T(2,128)S(1)} collective-permute-done((f32[4,2,703]{2,1,0:T(2,128)S(1)}, f32[4,2,703]{2,1,0:T(2,128)S(1)}, u32[]{:S(2)}, u32[]{:S(2)}) %collective-permute-start.7) | collective-permute-done | bytes 22528 | tf_op jit(solution)/shard_map/ppermute | solution.py:390
  25.2 1.9 %collective-permute-start.10 = (f32[4,2,703]{2,1,0:T(2,128)S(1)}, f32[4,2,703]{2,1,0:T(2,128)S(1)}, u32[]{:S(2)}, u32[]{:S(2)}) collective-permute-start(f32[4,2,703]{2,1,0:T(2,128)S(1)} %bitcast.10), channel_id=1, source_target_pairs={{0,12},{1,13},{2,14},{3,15},{4,8},{5,9},{6,10},{7,11},{8,4},{9,5},... | collective-permute-start | bytes 67496 | tf_op jit(solution)/shard_map/ppermute | solution.py:390
  27.1 0.0 collective-permute-start.9
  27.1 2.6 %collective-permute-start.8 = (f32[4,2,703]{2,1,0:T(2,128)S(1)}, f32[4,2,703]{2,1,0:T(2,128)S(1)}, u32[]{:S(2)}, u32[]{:S(2)}) collective-permute-start(f32[4,2,703]{2,1,0:T(2,128)S(1)} %bitcast.12), channel_id=1, source_target_pairs={{0,4},{1,5},{2,6},{3,7},{4,0},{5,1},{6,2},{7,3},{8,12},{9,13},{10,... | collective-permute-start | bytes 67496 | tf_op jit(solution)/shard_map/ppermute | solution.py:390
  29.7 0.1 station_hots.1.refs_2_
  29.7 1.3 %collective-permute-done.10.refs_6_ = f32[4,2,703]{2,1,0:T(2,128)S(1)} collective-permute-done((f32[4,2,703]{2,1,0:T(2,128)S(1)}, f32[4,2,703]{2,1,0:T(2,128)S(1)}, u32[]{:S(2)}, u32[]{:S(2)}) %collective-permute-start.10) | collective-permute-done | bytes 22528 | tf_op jit(solution)/shard_map/ppermute | solution.py:390
  31.0 0.8 %collective-permute-done.9.refs_5_ = f32[4,2,703]{2,1,0:T(2,128)S(1)} collective-permute-done((f32[4,2,703]{2,1,0:T(2,128)S(1)}, f32[4,2,703]{2,1,0:T(2,128)S(1)}, u32[]{:S(2)}, u32[]{:S(2)}) %collective-permute-start.9) | collective-permute-done | bytes 22528 | tf_op jit(solution)/shard_map/ppermute | solution.py:390
  31.8 0.0 collective-permute-done.8.refs_4_
  31.8 0.0 copy-done.2
  31.8 2.3 %gain_solve.1.refs_6_ = f32[4,2,806]{2,1,0:T(2,128)S(1)} custom-call(s32[1]{0:T(128)} %bitcast.refs_0_, s32[2,2]{1,0:T(2,128)S(1)} %copy-done.2, bf16[2,48,703]{2,1,0:T(8,128)(2,1)S(1)} %station_hots.1.refs_2_, f32[4,2,703]{2,1,0:T(2,128)S(1)} %bitcast.13, f32[4,2,703]{2,1,0:T(2,128)S(1)} %collective-permute-done.8.refs_4_, ...), custom_call_target="tpu_custom_call" | custom-call | tf_op jit(solution)/shard_map/gain_solve/pallas_call | solution.py:474
  34.1 0.1 collective-permute-start.13
  34.2 0.8 %collective-permute-start.12 = (f32[4,2,806]{2,1,0:T(2,128)S(1)}, f32[4,2,806]{2,1,0:T(2,128)S(1)}, u32[]{:S(2)}, u32[]{:S(2)}) collective-permute-start(f32[4,2,806]{2,1,0:T(2,128)S(1)} %gain_solve.1.refs_6_), channel_id=1, source_target_pairs={{0,2},{1,3},{2,0},{3,1},{4,6},{5,7},{6,4},{7,5},{8,10},{9,11},{10,... | collective-permute-start | bytes 77384 | tf_op jit(solution)/shard_map/ppermute | solution.py:390
  35.1 1.0 %collective-permute-start.11 = (f32[4,2,806]{2,1,0:T(2,128)S(1)}, f32[4,2,806]{2,1,0:T(2,128)S(1)}, u32[]{:S(2)}, u32[]{:S(2)}) collective-permute-start(f32[4,2,806]{2,1,0:T(2,128)S(1)} %gain_solve.1.refs_6_), channel_id=1, source_target_pairs={{0,1},{1,0},{2,3},{3,2},{4,5},{5,4},{6,7},{7,6},{8,9},{9,8},{10,11... | collective-permute-start | bytes 77384 | tf_op jit(solution)/shard_map/ppermute | solution.py:390
  36.1 1.4 %collective-permute-done.13.refs_9_ = f32[4,2,806]{2,1,0:T(2,128)S(1)} collective-permute-done((f32[4,2,806]{2,1,0:T(2,128)S(1)}, f32[4,2,806]{2,1,0:T(2,128)S(1)}, u32[]{:S(2)}, u32[]{:S(2)}) %collective-permute-start.13) | collective-permute-done | bytes 25824 | tf_op jit(solution)/shard_map/ppermute | solution.py:390
  37.5 0.8 %collective-permute-done.12.refs_8_ = f32[4,2,806]{2,1,0:T(2,128)S(1)} collective-permute-done((f32[4,2,806]{2,1,0:T(2,128)S(1)}, f32[4,2,806]{2,1,0:T(2,128)S(1)}, u32[]{:S(2)}, u32[]{:S(2)}) %collective-permute-start.12) | collective-permute-done | bytes 25824 | tf_op jit(solution)/shard_map/ppermute | solution.py:390
  38.3 0.0 collective-permute-done.11.refs_7_
  38.3 4.4 %clean.1 = (bf16[2,2,4,192,703]{4,3,2,1,0:T(8,128)(2,1)}, f32[2,2,2,4,38]{4,3,2,1,0:T(4,128)}) custom-call(s32[1]{0:T(128)} %bitcast.refs_0_, bf16[2,2,192,703]{3,2,1,0:T(8,128)(2,1)S(1)} %get-tuple-element.22.refs_10_.refs_1_, bf16[2,2,192,703]{3,2,1,0:T(8,128)(2,1)S(1)} %get-tuple-element.24.refs_11_.refs_2_, ...), custom_call_target="tpu_custom_call" | custom-call | tf_op jit(solution)/shard_map/clean/pallas_call | solution.py:483
  (5 shorter events, 0.0 us)
Async XLA Ops:
  0.6 6.5 %collective-permute-start.2 = (s32[1,2,192]{2,1,0:T(2,128)}, s32[1,2,192]{2,1,0:T(2,128)S(1)}, u32[]{:S(2)}, u32[]{:S(2)}) collective-permute-start(s32[1,2,192]{2,1,0:T(2,128)} %bitcast.15), channel_id=1, source_target_pairs={{0,3},{1,2},{2,1},{3,0},{4,7},{5,6},{6,5},{7,4},{8,11},{9,10},{10,... | collective-permute-start | bytes 4616 | tf_op jit(solution)/shard_map/ppermute | solution.py:390
  3.1 4.0 %collective-permute-start.1 = (s32[1,2,192]{2,1,0:T(2,128)}, s32[1,2,192]{2,1,0:T(2,128)S(1)}, u32[]{:S(2)}, u32[]{:S(2)}) collective-permute-start(s32[1,2,192]{2,1,0:T(2,128)} %bitcast.16), channel_id=1, source_target_pairs={{0,2},{1,3},{2,0},{3,1},{4,6},{5,7},{6,4},{7,5},{8,10},{9,11},{10,... | collective-permute-start | bytes 4616 | tf_op jit(solution)/shard_map/ppermute | solution.py:390
  3.7 3.4 %collective-permute-start = (s32[1,2,192]{2,1,0:T(2,128)}, s32[1,2,192]{2,1,0:T(2,128)S(1)}, u32[]{:S(2)}, u32[]{:S(2)}) collective-permute-start(s32[1,2,192]{2,1,0:T(2,128)} %bitcast.17), channel_id=1, source_target_pairs={{0,1},{1,0},{2,3},{3,2},{4,5},{5,4},{6,7},{7,6},{8,9},{9,8},{10,11... | collective-permute-start | bytes 4616 | tf_op jit(solution)/shard_map/ppermute | solution.py:390
  3.8 0.7 %copy-start = (f32[2,2,703]{2,1,0:T(2,128)S(1)}, f32[2,2,703]{2,1,0:T(2,128)}, u32[]{:S(2)}) copy-start(f32[2,2,703]{2,1,0:T(2,128)} %refs_2_.3) | copy-start | bytes 33748
  4.5 0.7 %copy-start.1 = (s32[2,192]{1,0:T(2,128)S(1)}, s32[2,192]{1,0:T(2,128)}, u32[]{:S(2)}) copy-start(s32[2,192]{1,0:T(2,128)} %param.7) | copy-start | bytes 4612
  5.2 0.7 %copy-start.3 = (s32[32]{0:T(128)S(1)}, s32[32]{0:T(128)}, u32[]{:S(2)}) copy-start(s32[32]{0:T(128)} %param.8) | copy-start | bytes 388
  7.2 5.5 %collective-permute-start.4 = (s32[4,2,192]{2,1,0:T(2,128)S(1)}, s32[4,2,192]{2,1,0:T(2,128)S(1)}, u32[]{:S(2)}, u32[]{:S(2)}) collective-permute-start(s32[4,2,192]{2,1,0:T(2,128)S(1)} %constant_dynamic-update-slice_fusion.refs_1_), channel_id=1, source_target_pairs={{0,12},{1,13},{2,14},{3,15},{4,8},{5,9},{6,10},{7,11},{8,4},{9,5},... | collective-permute-start | bytes 18440 | tf_op jit(solution)/shard_map/ppermute | solution.py:390
  11.1 3.7 %collective-permute-start.3 = (s32[4,2,192]{2,1,0:T(2,128)S(1)}, s32[4,2,192]{2,1,0:T(2,128)S(1)}, u32[]{:S(2)}, u32[]{:S(2)}) collective-permute-start(s32[4,2,192]{2,1,0:T(2,128)S(1)} %constant_dynamic-update-slice_fusion.refs_1_), channel_id=1, source_target_pairs={{0,4},{1,5},{2,6},{3,7},{4,0},{5,1},{6,2},{7,3},{8,12},{9,13},{10,... | collective-permute-start | bytes 18440 | tf_op jit(solution)/shard_map/ppermute | solution.py:390
  14.7 17.1 %copy-start.2 = (s32[2,2]{1,0:T(2,128)S(1)}, s32[2,2]{1,0:T(2,128)}, u32[]{:S(2)}) copy-start(s32[2,2]{1,0:T(2,128)} %refs_1_.1) | copy-start | bytes 52
  20.3 1.9 %collective-permute-start.5 = (f32[4,2,703]{2,1,0:T(2,128)S(1)}, f32[4,2,703]{2,1,0:T(2,128)S(1)}, u32[]{:S(2)}, u32[]{:S(2)}) collective-permute-start(f32[4,2,703]{2,1,0:T(2,128)S(1)} %get-tuple-element.37), channel_id=1, source_target_pairs={{0,1},{1,0},{2,3},{3,2},{4,5},{5,4},{6,7},{7,6},{8,9},{9,8},{10,11... | collective-permute-start | bytes 67496 | tf_op jit(solution)/shard_map/ppermute | solution.py:390
  20.4 3.9 %collective-permute-start.6 = (f32[4,2,703]{2,1,0:T(2,128)S(1)}, f32[4,2,703]{2,1,0:T(2,128)S(1)}, u32[]{:S(2)}, u32[]{:S(2)}) collective-permute-start(f32[4,2,703]{2,1,0:T(2,128)S(1)} %get-tuple-element.38), channel_id=1, source_target_pairs={{0,2},{1,3},{2,0},{3,1},{4,6},{5,7},{6,4},{7,5},{8,10},{9,11},{10,... | collective-permute-start | bytes 67496 | tf_op jit(solution)/shard_map/ppermute | solution.py:390
  22.0 3.3 %collective-permute-start.7 = (f32[4,2,703]{2,1,0:T(2,128)S(1)}, f32[4,2,703]{2,1,0:T(2,128)S(1)}, u32[]{:S(2)}, u32[]{:S(2)}) collective-permute-start(f32[4,2,703]{2,1,0:T(2,128)S(1)} %get-tuple-element.39), channel_id=1, source_target_pairs={{0,3},{1,2},{2,1},{3,0},{4,7},{5,6},{6,5},{7,4},{8,11},{9,10},{10,... | collective-permute-start | bytes 67496 | tf_op jit(solution)/shard_map/ppermute | solution.py:390
  25.2 5.8 %collective-permute-start.10 = (f32[4,2,703]{2,1,0:T(2,128)S(1)}, f32[4,2,703]{2,1,0:T(2,128)S(1)}, u32[]{:S(2)}, u32[]{:S(2)}) collective-permute-start(f32[4,2,703]{2,1,0:T(2,128)S(1)} %bitcast.10), channel_id=1, source_target_pairs={{0,12},{1,13},{2,14},{3,15},{4,8},{5,9},{6,10},{7,11},{8,4},{9,5},... | collective-permute-start | bytes 67496 | tf_op jit(solution)/shard_map/ppermute | solution.py:390
  27.1 4.7 %collective-permute-start.9 = (f32[4,2,703]{2,1,0:T(2,128)S(1)}, f32[4,2,703]{2,1,0:T(2,128)S(1)}, u32[]{:S(2)}, u32[]{:S(2)}) collective-permute-start(f32[4,2,703]{2,1,0:T(2,128)S(1)} %bitcast.11), channel_id=1, source_target_pairs={{0,8},{1,9},{2,10},{3,11},{4,12},{5,13},{6,14},{7,15},{8,0},{9,1},... | collective-permute-start | bytes 67496 | tf_op jit(solution)/shard_map/ppermute | solution.py:390
  27.1 4.7 %collective-permute-start.8 = (f32[4,2,703]{2,1,0:T(2,128)S(1)}, f32[4,2,703]{2,1,0:T(2,128)S(1)}, u32[]{:S(2)}, u32[]{:S(2)}) collective-permute-start(f32[4,2,703]{2,1,0:T(2,128)S(1)} %bitcast.12), channel_id=1, source_target_pairs={{0,4},{1,5},{2,6},{3,7},{4,0},{5,1},{6,2},{7,3},{8,12},{9,13},{10,... | collective-permute-start | bytes 67496 | tf_op jit(solution)/shard_map/ppermute | solution.py:390
  34.1 3.4 %collective-permute-start.13 = (f32[4,2,806]{2,1,0:T(2,128)S(1)}, f32[4,2,806]{2,1,0:T(2,128)S(1)}, u32[]{:S(2)}, u32[]{:S(2)}) collective-permute-start(f32[4,2,806]{2,1,0:T(2,128)S(1)} %gain_solve.1.refs_6_), channel_id=1, source_target_pairs={{0,3},{1,2},{2,1},{3,0},{4,7},{5,6},{6,5},{7,4},{8,11},{9,10},{10,... | collective-permute-start | bytes 77384 | tf_op jit(solution)/shard_map/ppermute | solution.py:390
  34.2 4.1 %collective-permute-start.12 = (f32[4,2,806]{2,1,0:T(2,128)S(1)}, f32[4,2,806]{2,1,0:T(2,128)S(1)}, u32[]{:S(2)}, u32[]{:S(2)}) collective-permute-start(f32[4,2,806]{2,1,0:T(2,128)S(1)} %gain_solve.1.refs_6_), channel_id=1, source_target_pairs={{0,2},{1,3},{2,0},{3,1},{4,6},{5,7},{6,4},{7,5},{8,10},{9,11},{10,... | collective-permute-start | bytes 77384 | tf_op jit(solution)/shard_map/ppermute | solution.py:390
  35.1 3.2 %collective-permute-start.11 = (f32[4,2,806]{2,1,0:T(2,128)S(1)}, f32[4,2,806]{2,1,0:T(2,128)S(1)}, u32[]{:S(2)}, u32[]{:S(2)}) collective-permute-start(f32[4,2,806]{2,1,0:T(2,128)S(1)} %gain_solve.1.refs_6_), channel_id=1, source_target_pairs={{0,1},{1,0},{2,3},{3,2},{4,5},{5,4},{6,7},{7,6},{8,9},{9,8},{10,11... | collective-permute-start | bytes 77384 | tf_op jit(solution)/shard_map/ppermute | solution.py:390

commit v12 on v10

--- a/solution.py
+++ b/solution.py
@@ -12,7 +12,7 @@
 STEPS_PER_TURN = 64
 GAINS_AT = 768
 GRANT = 42
-GRANTS = (50, 45)
+GRANTS = (47, 45)
 ROWS = 40
 
 F32 = jnp.float32
@@ -93,13 +93,14 @@
 def phase_kernel(width, t, reach, me_ref, *refs):
     anchor = me_ref[0].astype(F32) * float(width)
     if t == 0:
-        delay_ref, flag_ref, wave_ref, mix_ref, own_ref = refs
+        delay_ref, small_ref, wave_ref, mix_ref, own_ref, win_out_ref = refs
     else:
         vis_hbm, delay_ref, win_ref, wave_ref, mix_ref, vis_ref, apart_ref, *mask_refs, sem = refs
         copy = pltpu.make_async_copy(vis_hbm.at[:, 0], vis_ref, sem)
         copy.start()
     if t == 0:
-        own_ref[...] = flag_ref[...]
+        own_ref[0] = small_ref[:2]
+        win_out_ref[...] = small_ref[2:3, :win_out_ref.shape[1]]
     else:
         window_masks(width, reach, me_ref[0], win_ref, *mask_refs)
         apart = blocks_apart(me_ref[0], reach, apart_ref.shape[2])
@@ -413,6 +414,7 @@
         cost_estimate=pl.CostEstimate(flops=10 ** 7, bytes_accessed=6 * 2 ** 20, transcendentals=0),
         name="station_hots",
     )()
+    small = jnp.pad(flags[0], ((0, 1), (0, 0))) + jnp.pad(windows[None], ((2, 0), (0, width - window_count)))
     made = []
     beside = [partner(flags, d) for d in range(1, 4)]
     for t in range(2):
@@ -422,11 +424,12 @@
             jax.ShapeDtypeStruct((2, 2, width, pairs), BF16),
         ]
         if t == 0:
-            operands = (me, delays, flags)
+            operands = (me, delays, small)
             in_specs = [smem()] + [vmem_ref] * 2
-            out_shape += [jax.ShapeDtypeStruct(flags.shape, flags.dtype)]
+            out_shape += [jax.ShapeDtypeStruct(flags.shape, flags.dtype),
+                          jax.ShapeDtypeStruct((1, window_count), windows.dtype)]
         else:
-            operands = (me, turned, delays, windows.reshape(1, window_count))
+            operands = (me, turned, delays, made[0][3])
             in_specs = [smem(), hbm_ref] + [vmem_ref] * 2
             out_shape += [jax.ShapeDtypeStruct((2, 4, width, pairs), BF16),
                           shape(2, 2, remote_rows, pairs), shape(window_count, width), shape(width, window_count),

time: 41.6 us -> 41.6 us (level)
  local copies, waits for them, and re-layouts: 2.07 us -> 0.74 us
  other arithmetic: 0.01 us -> 0.73 us
  waiting for transfers between devices: 8.83 us -> 9.51 us
    unnamed x11 -> x7, local copies, waits for them, and re-layouts: 2.07 us -> 0.73 us
    add x0 -> x1, other arithmetic: none -> 0.72 us  [local(): jnp.pad(flags[0], ((0, 1), (0, 0)))]
    ppermute x14, waiting for transfers between devices: 8.83 us -> 9.51 us  [partner(): return lax.ppermute(value, 'sub', [(i, i ^ bits) for i in range(count)])]
  transfers between devices with their start and end apart: 14 -> 14, of which waited for: 8 -> 9; matrix products, arithmetic and copies ran while one was open for 0% -> 2% of each run, Pallas kernels for 6% -> 6%
where the time goes in v12:
time: 41.6 us; the launch traced here: 41.4 us
  starting transfers between devices  15.1 us (36%)
  Pallas kernels  14.6 us (35%)
  waiting for transfers between devices  9.51 us (23%)
  local copies, waits for them, and re-layouts  0.74 us (2%)
  other arithmetic  0.73 us (2%)
  between operations  0.71 us (2%)
    ppermute x14, starting transfers between devices, partner(): return lax.ppermute(value, 'sub', [(i, i ^ bits) for i in range(count)])  15.1 us
    ppermute x14, waiting for transfers between devices, partner(): return lax.ppermute(value, 'sub', [(i, i ^ bits) for i in range(count)])  9.51 us
    pallas_call x1, Pallas kernels, local(): pl.pallas_call(lambda *refs: sums_kernel(width, reach, *refs), in_specs=[...  5.55 us
    pallas_call x1, Pallas kernels, local(): pl.pallas_call(lambda *refs: clean_kernel(width, *refs), in_specs=[smem()...  4.39 us
    pallas_call x2, Pallas kernels, local(): pl.pallas_call(lambda *refs: phase_kernel(width, t, reach, *refs), in_spe...  2.51 us
    pallas_call x1, Pallas kernels, local(): pl.pallas_call(lambda *refs: solve_kernel(float(window_count), *refs), in...  2.07 us
  transfers between devices with their start and end apart: 14, of which 9 were waited for; matrix products, arithmetic and copies ran while one was open for 2% of the time, Pallas kernels for 6%

profile of v12, /device:TPU:0, one launch (start us, length us, event | category | flops | bytes accessed | tf_op | source)
XLA Modules:
  0.0 41.4 jit_solution(8384886393508647214)
XLA Ops:
  0.6 2.5 %collective-permute-start.2 = (s32[1,2,192]{2,1,0:T(2,128)}, s32[1,2,192]{2,1,0:T(2,128)S(1)}, u32[]{:S(2)}, u32[]{:S(2)}) collective-permute-start(s32[1,2,192]{2,1,0:T(2,128)} %bitcast.20), channel_id=1, source_target_pairs={{0,3},{1,2},{2,1},{3,0},{4,7},{5,6},{6,5},{7,4},{8,11},{9,10},{10,... | collective-permute-start | bytes 4616 | tf_op jit(solution)/shard_map/ppermute | solution.py:386
  3.1 0.6 %collective-permute-start.1 = (s32[1,2,192]{2,1,0:T(2,128)}, s32[1,2,192]{2,1,0:T(2,128)S(1)}, u32[]{:S(2)}, u32[]{:S(2)}) collective-permute-start(s32[1,2,192]{2,1,0:T(2,128)} %bitcast.21), channel_id=1, source_target_pairs={{0,2},{1,3},{2,0},{3,1},{4,6},{5,7},{6,4},{7,5},{8,10},{9,11},{10,... | collective-permute-start | bytes 4616 | tf_op jit(solution)/shard_map/ppermute | solution.py:386
  3.7 0.0 collective-permute-start
  3.8 0.7 %pad_add_fusion.refs_2_ = s32[3,192]{1,0:T(4,128)S(1)} fusion(s32[1,32]{1,0:T(1,128)} %bitcast.23, s32[2,192]{1,0:T(2,128)} %param.7), kind=kLoop, calls=%fused_computation.5 | loop fusion | flops 576 | bytes 3968 | tf_op jit(solution)/shard_map/add | solution.py:417
  4.5 0.0 copy-start
  4.5 0.7 %copy-done = f32[2,2,703]{2,1,0:T(2,128)S(1)} copy-done((f32[2,2,703]{2,1,0:T(2,128)S(1)}, f32[2,2,703]{2,1,0:T(2,128)}, u32[]{:S(2)}) %copy-start) | copy-done | bytes 11272
  5.2 0.8 %phases.2 = (f32[2,2,192,703]{3,2,1,0:T(8,128)S(1)}, bf16[2,2,192,703]{3,2,1,0:T(8,128)(2,1)S(1)}, s32[1,2,192]{2,1,0:T(2,128)S(1)}, s32[1,32]{1,0:T(1,128)S(1)}) custom-call(s32[1]{0:T(128)} %bitcast.refs_0_, f32[2,2,703]{2,1,0:T(2,128)S(1)} %copy-done, s32[3,192]{1,0:T(4,128)S(1)} %pad_add_fusion.refs_2_), custom_call_target="tpu_custom_call" | custom-call | flops 10000000 | bytes 6291456 | tf_op jit(solution)/shard_map/phases/pallas_call | solution.py:437
  6.1 0.0 collective-permute-done
  6.1 0.8 %collective-permute-done.1 = s32[1,2,192]{2,1,0:T(2,128)S(1)} collective-permute-done((s32[1,2,192]{2,1,0:T(2,128)}, s32[1,2,192]{2,1,0:T(2,128)S(1)}, u32[]{:S(2)}, u32[]{:S(2)}) %collective-permute-start.1) | collective-permute-done | bytes 1568 | tf_op jit(solution)/shard_map/ppermute | solution.py:386
  6.9 0.0 collective-permute-done.2
  6.9 3.7 %collective-permute-start.4 = (s32[4,2,192]{2,1,0:T(2,128)S(1)}, s32[4,2,192]{2,1,0:T(2,128)S(1)}, u32[]{:S(2)}, u32[]{:S(2)}) collective-permute-start(s32[4,2,192]{2,1,0:T(2,128)S(1)} %constant_dynamic-update-slice_fusion.refs_1_), channel_id=1, source_target_pairs={{0,12},{1,13},{2,14},{3,15},{4,8},{5,9},{6,10},{7,11},{8,4},{9,5},... | collective-permute-start | bytes 18440 | tf_op jit(solution)/shard_map/ppermute | solution.py:386
  10.6 0.0 collective-permute-start.3
  10.6 1.7 %phases.3 = (f32[2,2,192,703]{3,2,1,0:T(8,128)S(1)}, bf16[2,2,192,703]{3,2,1,0:T(8,128)(2,1)S(1)}, bf16[2,4,192,703]{3,2,1,0:T(8,128)(2,1)S(1)}, f32[2,2,16,703]...) custom-call(s32[1]{0:T(128)} %bitcast.refs_0_, ...), custom_call_target="tpu_custom_call" | custom-call | flops 10000000 | bytes 6291456 | tf_op jit(solution)/shard_map/phases/pallas_call | solution.py:437
  12.3 0.2 collective-permute-done.4.refs_3_
  12.4 1.8 %collective-permute-done.3.refs_2_ = s32[4,2,192]{2,1,0:T(2,128)S(1)} collective-permute-done((s32[4,2,192]{2,1,0:T(2,128)S(1)}, s32[4,2,192]{2,1,0:T(2,128)S(1)}, u32[]{:S(2)}, u32[]{:S(2)}) %collective-permute-start.3) | collective-permute-done | bytes 6176 | tf_op jit(solution)/shard_map/ppermute | solution.py:386
  14.2 0.0 copy-start.1
  14.2 5.6 %window_sums.1 = (f32[4,2,703]{2,1,0:T(2,128)S(1)}, f32[4,2,703]{2,1,0:T(2,128)S(1)}, f32[4,2,703]{2,1,0:T(2,128)S(1)}, f32[4,2,703]{2,1,0:T(2,128)S(1)}, bf16[2,4,192,703]{3,2,1,0:T(8,128)(2,1)S(1)}) custom-call(s32[1]{0:T(128)} %bitcast.refs_0_, s32[4,2,192]{2,1,0:T(2,128)S(1)} %constant_dynamic-update-slice_fusion.refs_1_, ...), custom_call_target="tpu_custom_call" | custom-call | tf_op jit(solution)/shard_map/window_sums/pallas_call | solution.py:455
  19.8 0.1 collective-permute-start.5
  19.9 1.0 %collective-permute-start.6 = (f32[4,2,703]{2,1,0:T(2,128)S(1)}, f32[4,2,703]{2,1,0:T(2,128)S(1)}, u32[]{:S(2)}, u32[]{:S(2)}) collective-permute-start(f32[4,2,703]{2,1,0:T(2,128)S(1)} %get-tuple-element.36), channel_id=1, source_target_pairs={{0,2},{1,3},{2,0},{3,1},{4,6},{5,7},{6,4},{7,5},{8,10},{9,11},{10,... | collective-permute-start | bytes 67496 | tf_op jit(solution)/shard_map/ppermute | solution.py:386
  20.9 0.8 %collective-permute-start.7 = (f32[4,2,703]{2,1,0:T(2,128)S(1)}, f32[4,2,703]{2,1,0:T(2,128)S(1)}, u32[]{:S(2)}, u32[]{:S(2)}) collective-permute-start(f32[4,2,703]{2,1,0:T(2,128)S(1)} %get-tuple-element.37), channel_id=1, source_target_pairs={{0,3},{1,2},{2,1},{3,0},{4,7},{5,6},{6,5},{7,4},{8,11},{9,10},{10,... | collective-permute-start | bytes 67496 | tf_op jit(solution)/shard_map/ppermute | solution.py:386
  21.7 0.0 collective-permute-done.5
  21.7 2.0 %collective-permute-done.6 = f32[4,2,703]{2,1,0:T(2,128)S(1)} collective-permute-done((f32[4,2,703]{2,1,0:T(2,128)S(1)}, f32[4,2,703]{2,1,0:T(2,128)S(1)}, u32[]{:S(2)}, u32[]{:S(2)}) %collective-permute-start.6) | collective-permute-done | bytes 22528 | tf_op jit(solution)/shard_map/ppermute | solution.py:386
  23.8 0.4 collective-permute-done.7
  24.2 1.9 %collective-permute-start.10 = (f32[4,2,703]{2,1,0:T(2,128)S(1)}, f32[4,2,703]{2,1,0:T(2,128)S(1)}, u32[]{:S(2)}, u32[]{:S(2)}) collective-permute-start(f32[4,2,703]{2,1,0:T(2,128)S(1)} %bitcast.10), channel_id=1, source_target_pairs={{0,12},{1,13},{2,14},{3,15},{4,8},{5,9},{6,10},{7,11},{8,4},{9,5},... | collective-permute-start | bytes 67496 | tf_op jit(solution)/shard_map/ppermute | solution.py:386
  26.0 0.0 collective-permute-start.9
  26.0 2.6 %collective-permute-start.8 = (f32[4,2,703]{2,1,0:T(2,128)S(1)}, f32[4,2,703]{2,1,0:T(2,128)S(1)}, u32[]{:S(2)}, u32[]{:S(2)}) collective-permute-start(f32[4,2,703]{2,1,0:T(2,128)S(1)} %bitcast.12), channel_id=1, source_target_pairs={{0,4},{1,5},{2,6},{3,7},{4,0},{5,1},{6,2},{7,3},{8,12},{9,13},{10,... | collective-permute-start | bytes 67496 | tf_op jit(solution)/shard_map/ppermute | solution.py:386
  28.6 0.1 station_hots.1.refs_2_
  28.7 1.3 %collective-permute-done.10.refs_6_ = f32[4,2,703]{2,1,0:T(2,128)S(1)} collective-permute-done((f32[4,2,703]{2,1,0:T(2,128)S(1)}, f32[4,2,703]{2,1,0:T(2,128)S(1)}, u32[]{:S(2)}, u32[]{:S(2)}) %collective-permute-start.10) | collective-permute-done | bytes 22528 | tf_op jit(solution)/shard_map/ppermute | solution.py:386
  29.9 0.8 %collective-permute-done.9.refs_5_ = f32[4,2,703]{2,1,0:T(2,128)S(1)} collective-permute-done((f32[4,2,703]{2,1,0:T(2,128)S(1)}, f32[4,2,703]{2,1,0:T(2,128)S(1)}, u32[]{:S(2)}, u32[]{:S(2)}) %collective-permute-start.9) | collective-permute-done | bytes 22528 | tf_op jit(solution)/shard_map/ppermute | solution.py:386
  30.7 0.0 collective-permute-done.8.refs_4_
  30.7 0.0 copy-done.1
  30.7 2.1 %gain_solve.1.refs_5_ = f32[4,2,806]{2,1,0:T(2,128)S(1)} custom-call(s32[1]{0:T(128)} %bitcast.refs_0_, s32[2,2]{1,0:T(2,128)S(1)} %copy-done.1, bf16[2,40,703]{2,1,0:T(8,128)(2,1)S(1)} %station_hots.1.refs_2_, f32[4,2,703]{2,1,0:T(2,128)S(1)} %bitcast.13, f32[4,2,703]{2,1,0:T(2,128)S(1)} %collective-permute-done.8.refs_4_, ...), custom_call_target="tpu_custom_call" | custom-call | tf_op jit(solution)/shard_map/gain_solve/pallas_call | solution.py:472
  32.8 0.1 collective-permute-start.13
  32.9 1.1 %collective-permute-start.12 = (f32[4,2,806]{2,1,0:T(2,128)S(1)}, f32[4,2,806]{2,1,0:T(2,128)S(1)}, u32[]{:S(2)}, u32[]{:S(2)}) collective-permute-start(f32[4,2,806]{2,1,0:T(2,128)S(1)} %gain_solve.1.refs_5_), channel_id=1, source_target_pairs={{0,2},{1,3},{2,0},{3,1},{4,6},{5,7},{6,4},{7,5},{8,10},{9,11},{10,... | collective-permute-start | bytes 77384 | tf_op jit(solution)/shard_map/ppermute | solution.py:386
  34.0 0.7 %collective-permute-start.11 = (f32[4,2,806]{2,1,0:T(2,128)S(1)}, f32[4,2,806]{2,1,0:T(2,128)S(1)}, u32[]{:S(2)}, u32[]{:S(2)}) collective-permute-start(f32[4,2,806]{2,1,0:T(2,128)S(1)} %gain_solve.1.refs_5_), channel_id=1, source_target_pairs={{0,1},{1,0},{2,3},{3,2},{4,5},{5,4},{6,7},{7,6},{8,9},{9,8},{10,11... | collective-permute-start | bytes 77384 | tf_op jit(solution)/shard_map/ppermute | solution.py:386
  34.8 1.4 %collective-permute-done.13.refs_8_ = f32[4,2,806]{2,1,0:T(2,128)S(1)} collective-permute-done((f32[4,2,806]{2,1,0:T(2,128)S(1)}, f32[4,2,806]{2,1,0:T(2,128)S(1)}, u32[]{:S(2)}, u32[]{:S(2)}) %collective-permute-start.13) | collective-permute-done | bytes 25824 | tf_op jit(solution)/shard_map/ppermute | solution.py:386
  36.2 0.8 %collective-permute-done.12.refs_7_ = f32[4,2,806]{2,1,0:T(2,128)S(1)} collective-permute-done((f32[4,2,806]{2,1,0:T(2,128)S(1)}, f32[4,2,806]{2,1,0:T(2,128)S(1)}, u32[]{:S(2)}, u32[]{:S(2)}) %collective-permute-start.12) | collective-permute-done | bytes 25824 | tf_op jit(solution)/shard_map/ppermute | solution.py:386
  37.0 0.0 collective-permute-done.11.refs_6_
  37.0 4.4 %clean.1 = (bf16[2,2,4,192,703]{4,3,2,1,0:T(8,128)(2,1)}, f32[2,2,2,4,38]{4,3,2,1,0:T(4,128)}) custom-call(s32[1]{0:T(128)} %bitcast.refs_0_, bf16[2,4,192,703]{3,2,1,0:T(8,128)(2,1)S(1)} %get-tuple-element.22.refs_10_.refs_1_, bf16[2,4,192,703]{3,2,1,0:T(8,128)(2,1)S(1)} %get-tuple-element.33.refs_2_, ...), custom_call_target="tpu_custom_call" | custom-call | tf_op jit(solution)/shard_map/clean/pallas_call | solution.py:481
  (5 shorter events, 0.0 us)
Async XLA Ops:
  0.6 6.3 %collective-permute-start.2 = (s32[1,2,192]{2,1,0:T(2,128)}, s32[1,2,192]{2,1,0:T(2,128)S(1)}, u32[]{:S(2)}, u32[]{:S(2)}) collective-permute-start(s32[1,2,192]{2,1,0:T(2,128)} %bitcast.20), channel_id=1, source_target_pairs={{0,3},{1,2},{2,1},{3,0},{4,7},{5,6},{6,5},{7,4},{8,11},{9,10},{10,... | collective-permute-start | bytes 4616 | tf_op jit(solution)/shard_map/ppermute | solution.py:386
  3.1 3.8 %collective-permute-start.1 = (s32[1,2,192]{2,1,0:T(2,128)}, s32[1,2,192]{2,1,0:T(2,128)S(1)}, u32[]{:S(2)}, u32[]{:S(2)}) collective-permute-start(s32[1,2,192]{2,1,0:T(2,128)} %bitcast.21), channel_id=1, source_target_pairs={{0,2},{1,3},{2,0},{3,1},{4,6},{5,7},{6,4},{7,5},{8,10},{9,11},{10,... | collective-permute-start | bytes 4616 | tf_op jit(solution)/shard_map/ppermute | solution.py:386
  3.7 2.3 %collective-permute-start = (s32[1,2,192]{2,1,0:T(2,128)}, s32[1,2,192]{2,1,0:T(2,128)S(1)}, u32[]{:S(2)}, u32[]{:S(2)}) collective-permute-start(s32[1,2,192]{2,1,0:T(2,128)} %bitcast.22), channel_id=1, source_target_pairs={{0,1},{1,0},{2,3},{3,2},{4,5},{5,4},{6,7},{7,6},{8,9},{9,8},{10,11... | collective-permute-start | bytes 4616 | tf_op jit(solution)/shard_map/ppermute | solution.py:386
  4.5 0.7 %copy-start = (f32[2,2,703]{2,1,0:T(2,128)S(1)}, f32[2,2,703]{2,1,0:T(2,128)}, u32[]{:S(2)}) copy-start(f32[2,2,703]{2,1,0:T(2,128)} %refs_2_.1) | copy-start | bytes 33748
  6.9 5.5 %collective-permute-start.4 = (s32[4,2,192]{2,1,0:T(2,128)S(1)}, s32[4,2,192]{2,1,0:T(2,128)S(1)}, u32[]{:S(2)}, u32[]{:S(2)}) collective-permute-start(s32[4,2,192]{2,1,0:T(2,128)S(1)} %constant_dynamic-update-slice_fusion.refs_1_), channel_id=1, source_target_pairs={{0,12},{1,13},{2,14},{3,15},{4,8},{5,9},{6,10},{7,11},{8,4},{9,5},... | collective-permute-start | bytes 18440 | tf_op jit(solution)/shard_map/ppermute | solution.py:386
  10.6 3.7 %collective-permute-start.3 = (s32[4,2,192]{2,1,0:T(2,128)S(1)}, s32[4,2,192]{2,1,0:T(2,128)S(1)}, u32[]{:S(2)}, u32[]{:S(2)}) collective-permute-start(s32[4,2,192]{2,1,0:T(2,128)S(1)} %constant_dynamic-update-slice_fusion.refs_1_), channel_id=1, source_target_pairs={{0,4},{1,5},{2,6},{3,7},{4,0},{5,1},{6,2},{7,3},{8,12},{9,13},{10,... | collective-permute-start | bytes 18440 | tf_op jit(solution)/shard_map/ppermute | solution.py:386
  14.2 16.5 %copy-start.1 = (s32[2,2]{1,0:T(2,128)S(1)}, s32[2,2]{1,0:T(2,128)}, u32[]{:S(2)}) copy-start(s32[2,2]{1,0:T(2,128)} %refs_1_.3) | copy-start | bytes 52
  19.8 1.9 %collective-permute-start.5 = (f32[4,2,703]{2,1,0:T(2,128)S(1)}, f32[4,2,703]{2,1,0:T(2,128)S(1)}, u32[]{:S(2)}, u32[]{:S(2)}) collective-permute-start(f32[4,2,703]{2,1,0:T(2,128)S(1)} %get-tuple-element.35), channel_id=1, source_target_pairs={{0,1},{1,0},{2,3},{3,2},{4,5},{5,4},{6,7},{7,6},{8,9},{9,8},{10,11... | collective-permute-start | bytes 67496 | tf_op jit(solution)/shard_map/ppermute | solution.py:386
  19.9 3.9 %collective-permute-start.6 = (f32[4,2,703]{2,1,0:T(2,128)S(1)}, f32[4,2,703]{2,1,0:T(2,128)S(1)}, u32[]{:S(2)}, u32[]{:S(2)}) collective-permute-start(f32[4,2,703]{2,1,0:T(2,128)S(1)} %get-tuple-element.36), channel_id=1, source_target_pairs={{0,2},{1,3},{2,0},{3,1},{4,6},{5,7},{6,4},{7,5},{8,10},{9,11},{10,... | collective-permute-start | bytes 67496 | tf_op jit(solution)/shard_map/ppermute | solution.py:386
  20.9 3.3 %collective-permute-start.7 = (f32[4,2,703]{2,1,0:T(2,128)S(1)}, f32[4,2,703]{2,1,0:T(2,128)S(1)}, u32[]{:S(2)}, u32[]{:S(2)}) collective-permute-start(f32[4,2,703]{2,1,0:T(2,128)S(1)} %get-tuple-element.37), channel_id=1, source_target_pairs={{0,3},{1,2},{2,1},{3,0},{4,7},{5,6},{6,5},{7,4},{8,11},{9,10},{10,... | collective-permute-start | bytes 67496 | tf_op jit(solution)/shard_map/ppermute | solution.py:386
  24.2 5.8 %collective-permute-start.10 = (f32[4,2,703]{2,1,0:T(2,128)S(1)}, f32[4,2,703]{2,1,0:T(2,128)S(1)}, u32[]{:S(2)}, u32[]{:S(2)}) collective-permute-start(f32[4,2,703]{2,1,0:T(2,128)S(1)} %bitcast.10), channel_id=1, source_target_pairs={{0,12},{1,13},{2,14},{3,15},{4,8},{5,9},{6,10},{7,11},{8,4},{9,5},... | collective-permute-start | bytes 67496 | tf_op jit(solution)/shard_map/ppermute | solution.py:386
  26.0 4.7 %collective-permute-start.9 = (f32[4,2,703]{2,1,0:T(2,128)S(1)}, f32[4,2,703]{2,1,0:T(2,128)S(1)}, u32[]{:S(2)}, u32[]{:S(2)}) collective-permute-start(f32[4,2,703]{2,1,0:T(2,128)S(1)} %bitcast.11), channel_id=1, source_target_pairs={{0,8},{1,9},{2,10},{3,11},{4,12},{5,13},{6,14},{7,15},{8,0},{9,1},... | collective-permute-start | bytes 67496 | tf_op jit(solution)/shard_map/ppermute | solution.py:386
  26.0 4.7 %collective-permute-start.8 = (f32[4,2,703]{2,1,0:T(2,128)S(1)}, f32[4,2,703]{2,1,0:T(2,128)S(1)}, u32[]{:S(2)}, u32[]{:S(2)}) collective-permute-start(f32[4,2,703]{2,1,0:T(2,128)S(1)} %bitcast.12), channel_id=1, source_target_pairs={{0,4},{1,5},{2,6},{3,7},{4,0},{5,1},{6,2},{7,3},{8,12},{9,13},{10,... | collective-permute-start | bytes 67496 | tf_op jit(solution)/shard_map/ppermute | solution.py:386
  32.8 3.4 %collective-permute-start.13 = (f32[4,2,806]{2,1,0:T(2,128)S(1)}, f32[4,2,806]{2,1,0:T(2,128)S(1)}, u32[]{:S(2)}, u32[]{:S(2)}) collective-permute-start(f32[4,2,806]{2,1,0:T(2,128)S(1)} %gain_solve.1.refs_5_), channel_id=1, source_target_pairs={{0,3},{1,2},{2,1},{3,0},{4,7},{5,6},{6,5},{7,4},{8,11},{9,10},{10,... | collective-permute-start | bytes 77384 | tf_op jit(solution)/shard_map/ppermute | solution.py:386
  32.9 4.1 %collective-permute-start.12 = (f32[4,2,806]{2,1,0:T(2,128)S(1)}, f32[4,2,806]{2,1,0:T(2,128)S(1)}, u32[]{:S(2)}, u32[]{:S(2)}) collective-permute-start(f32[4,2,806]{2,1,0:T(2,128)S(1)} %gain_solve.1.refs_5_), channel_id=1, source_target_pairs={{0,2},{1,3},{2,0},{3,1},{4,6},{5,7},{6,4},{7,5},{8,10},{9,11},{10,... | collective-permute-start | bytes 77384 | tf_op jit(solution)/shard_map/ppermute | solution.py:386
  34.0 3.0 %collective-permute-start.11 = (f32[4,2,806]{2,1,0:T(2,128)S(1)}, f32[4,2,806]{2,1,0:T(2,128)S(1)}, u32[]{:S(2)}, u32[]{:S(2)}) collective-permute-start(f32[4,2,806]{2,1,0:T(2,128)S(1)} %gain_solve.1.refs_5_), channel_id=1, source_target_pairs={{0,1},{1,0},{2,3},{3,2},{4,5},{5,4},{6,7},{7,6},{8,9},{9,8},{10,11... | collective-permute-start | bytes 77384 | tf_op jit(solution)/shard_map/ppermute | solution.py:386

commit v13 on v12

--- a/solution.py
+++ b/solution.py
@@ -192,7 +192,7 @@
 
     for t in range(2):
         mine = lax.div(me, reach)
-        for group, other in enumerate((mine, lax.bitwise_xor(mine, 1), lax.bitwise_xor(mine, 3))):
+        for group, other in enumerate((mine, lax.bitwise_xor(mine, 3), lax.bitwise_xor(mine, 1))):
             side = jnp.where(jnp.abs(other - mine) > 1, 3, other - mine + 1)
             for slot in range(reach):
                 row = flag_refs[group][slot, t:t + 1, :].astype(F32)
@@ -449,7 +449,9 @@
             while gathered.shape[0] < reach:
                 stride = gathered.shape[0]
                 gathered = jnp.concatenate([gathered] + [partner(gathered, stride * d) for d in range(1, 4)], axis=0)
-            gathered = [gathered] + [partner(gathered, d * reach) for d in (1, 3)]
+            middle = [(i, i ^ (3 * reach)) for i in range(count) if reach <= i < 3 * reach]
+            beyond = lax.ppermute(gathered, "sub", middle)
+            gathered = [gathered, beyond, partner(gathered, reach)]
     waves, mixing = ([part[i] for part in made] for i in range(2))
     held, *masks = made[1][2:]
     *quarters, held_too = pl.pallas_call(

time: 41.6 us -> 41.5 us (level)
  waiting for transfers between devices: 9.51 us -> 8.8 us
  starting transfers between devices: 15.1 us -> 15.6 us
    ppermute x14 -> x13, waiting for transfers between devices: 9.51 us -> 8.8 us  [partner(): return lax.ppermute(value, 'sub', [(i, i ^ bits) for i in range(count)])]
    ppermute x0 -> x1, starting transfers between devices: none -> 0.65 us  [local(): beyond = lax.ppermute(gathered, 'sub', middle)]
    ppermute x14 -> x13, starting transfers between devices: 15.1 us -> 15 us  [partner(): return lax.ppermute(value, 'sub', [(i, i ^ bits) for i in range(count)])]
  transfers between devices with their start and end apart: 14 -> 14, of which waited for: 9 -> 7; matrix products, arithmetic and copies ran while one was open for 2% -> 2% of each run, Pallas kernels for 6% -> 6%
where the time goes in v13:
time: 41.5 us; the launch traced here: 41.3 us
  starting transfers between devices  15.6 us (38%)
  Pallas kernels  14.6 us (35%)
  waiting for transfers between devices  8.8 us (21%)
  between operations  0.75 us (2%)
  local copies, waits for them, and re-layouts  0.74 us (2%)
  other arithmetic  0.73 us (2%)
    ppermute x13, starting transfers between devices, partner(): return lax.ppermute(value, 'sub', [(i, i ^ bits) for i in range(count)])  15 us
    ppermute x13, waiting for transfers between devices, partner(): return lax.ppermute(value, 'sub', [(i, i ^ bits) for i in range(count)])  8.8 us
    pallas_call x1, Pallas kernels, local(): pl.pallas_call(lambda *refs: sums_kernel(width, reach, *refs), in_specs=[...  5.56 us
    pallas_call x1, Pallas kernels, local(): pl.pallas_call(lambda *refs: clean_kernel(width, *refs), in_specs=[smem()...  4.39 us
    pallas_call x2, Pallas kernels, local(): pl.pallas_call(lambda *refs: phase_kernel(width, t, reach, *refs), in_spe...  2.52 us
    pallas_call x1, Pallas kernels, local(): pl.pallas_call(lambda *refs: solve_kernel(float(window_count), *refs), in...  2.07 us
  transfers between devices with their start and end apart: 14, of which 7 were waited for; matrix products, arithmetic and copies ran while one was open for 2% of the time, Pallas kernels for 6%

profile of v13, /device:TPU:0, one launch (start us, length us, event | category | flops | bytes accessed | tf_op | source)
XLA Modules:
  0.0 41.3 jit_solution(4586310148415919017)
XLA Ops:
  0.6 2.5 %collective-permute-start.2 = (s32[1,2,192]{2,1,0:T(2,128)}, s32[1,2,192]{2,1,0:T(2,128)S(1)}, u32[]{:S(2)}, u32[]{:S(2)}) collective-permute-start(s32[1,2,192]{2,1,0:T(2,128)} %bitcast.20), channel_id=1, source_target_pairs={{0,3},{1,2},{2,1},{3,0},{4,7},{5,6},{6,5},{7,4},{8,11},{9,10},{10,... | collective-permute-start | bytes 4616 | tf_op jit(solution)/shard_map/ppermute | solution.py:386
  3.1 0.6 %collective-permute-start.1 = (s32[1,2,192]{2,1,0:T(2,128)}, s32[1,2,192]{2,1,0:T(2,128)S(1)}, u32[]{:S(2)}, u32[]{:S(2)}) collective-permute-start(s32[1,2,192]{2,1,0:T(2,128)} %bitcast.21), channel_id=1, source_target_pairs={{0,2},{1,3},{2,0},{3,1},{4,6},{5,7},{6,4},{7,5},{8,10},{9,11},{10,... | collective-permute-start | bytes 4616 | tf_op jit(solution)/shard_map/ppermute | solution.py:386
  3.7 0.0 collective-permute-start
  3.8 0.7 %pad_add_fusion.refs_2_ = s32[3,192]{1,0:T(4,128)S(1)} fusion(s32[1,32]{1,0:T(1,128)} %bitcast.23, s32[2,192]{1,0:T(2,128)} %param.7), kind=kLoop, calls=%fused_computation.5 | loop fusion | flops 576 | bytes 3968 | tf_op jit(solution)/shard_map/add | solution.py:417
  4.5 0.0 copy-start
  4.5 0.7 %copy-done = f32[2,2,703]{2,1,0:T(2,128)S(1)} copy-done((f32[2,2,703]{2,1,0:T(2,128)S(1)}, f32[2,2,703]{2,1,0:T(2,128)}, u32[]{:S(2)}) %copy-start) | copy-done | bytes 11272
  5.2 0.8 %phases.2 = (f32[2,2,192,703]{3,2,1,0:T(8,128)S(1)}, bf16[2,2,192,703]{3,2,1,0:T(8,128)(2,1)S(1)}, s32[1,2,192]{2,1,0:T(2,128)S(1)}, s32[1,32]{1,0:T(1,128)S(1)}) custom-call(s32[1]{0:T(128)} %bitcast.refs_0_, f32[2,2,703]{2,1,0:T(2,128)S(1)} %copy-done, s32[3,192]{1,0:T(4,128)S(1)} %pad_add_fusion.refs_2_), custom_call_target="tpu_custom_call" | custom-call | flops 10000000 | bytes 6291456 | tf_op jit(solution)/shard_map/phases/pallas_call | solution.py:437
  6.1 0.0 collective-permute-done
  6.1 0.8 %collective-permute-done.1 = s32[1,2,192]{2,1,0:T(2,128)S(1)} collective-permute-done((s32[1,2,192]{2,1,0:T(2,128)}, s32[1,2,192]{2,1,0:T(2,128)S(1)}, u32[]{:S(2)}, u32[]{:S(2)}) %collective-permute-start.1) | collective-permute-done | bytes 1568 | tf_op jit(solution)/shard_map/ppermute | solution.py:386
  6.9 0.0 collective-permute-done.2
  6.9 1.6 %collective-permute-start.4 = (s32[4,2,192]{2,1,0:T(2,128)S(1)}, s32[4,2,192]{2,1,0:T(2,128)S(1)}, u32[]{:S(2)}, u32[]{:S(2)}) collective-permute-start(s32[4,2,192]{2,1,0:T(2,128)S(1)} %constant_dynamic-update-slice_fusion.refs_1_), channel_id=1, source_target_pairs={{0,4},{1,5},{2,6},{3,7},{4,0},{5,1},{6,2},{7,3},{8,12},{9,13},{10,... | collective-permute-start | bytes 18440 | tf_op jit(solution)/shard_map/ppermute | solution.py:386
  8.6 0.6 %collective-permute-start.3 = (s32[4,2,192]{2,1,0:T(2,128)S(1)}, s32[4,2,192]{2,1,0:T(2,128)S(1)}, u32[]{:S(2)}, u32[]{:S(2)}) collective-permute-start(s32[4,2,192]{2,1,0:T(2,128)S(1)} %constant_dynamic-update-slice_fusion.refs_1_), channel_id=1, source_target_pairs={{4,8},{5,9},{6,10},{7,11},{8,4},{9,5},{10,6},{11,7},{20,24},{21,25... | collective-permute-start | bytes 18440 | tf_op jit(solution)/shard_map/ppermute | solution.py:453
  9.2 1.7 %phases.3 = (f32[2,2,192,703]{3,2,1,0:T(8,128)S(1)}, bf16[2,2,192,703]{3,2,1,0:T(8,128)(2,1)S(1)}, bf16[2,4,192,703]{3,2,1,0:T(8,128)(2,1)S(1)}, f32[2,2,16,703]...) custom-call(s32[1]{0:T(128)} %bitcast.refs_0_, ...), custom_call_target="tpu_custom_call" | custom-call | flops 10000000 | bytes 6291456 | tf_op jit(solution)/shard_map/phases/pallas_call | solution.py:437
  10.9 0.0 collective-permute-done.4.refs_3_
  10.9 0.0 collective-permute-done.3.refs_2_
  10.9 0.0 copy-start.1
  10.9 5.6 %window_sums.1 = (f32[4,2,703]{2,1,0:T(2,128)S(1)}, f32[4,2,703]{2,1,0:T(2,128)S(1)}, f32[4,2,703]{2,1,0:T(2,128)S(1)}, f32[4,2,703]{2,1,0:T(2,128)S(1)}, bf16[2,4,192,703]{3,2,1,0:T(8,128)(2,1)S(1)}) custom-call(s32[1]{0:T(128)} %bitcast.refs_0_, s32[4,2,192]{2,1,0:T(2,128)S(1)} %constant_dynamic-update-slice_fusion.refs_1_, ...), custom_call_target="tpu_custom_call" | custom-call | tf_op jit(solution)/shard_map/window_sums/pallas_call | solution.py:457
  16.5 0.1 collective-permute-start.5
  16.6 1.0 %collective-permute-start.6 = (f32[4,2,703]{2,1,0:T(2,128)S(1)}, f32[4,2,703]{2,1,0:T(2,128)S(1)}, u32[]{:S(2)}, u32[]{:S(2)}) collective-permute-start(f32[4,2,703]{2,1,0:T(2,128)S(1)} %get-tuple-element.36), channel_id=1, source_target_pairs={{0,2},{1,3},{2,0},{3,1},{4,6},{5,7},{6,4},{7,5},{8,10},{9,11},{10,... | collective-permute-start | bytes 67496 | tf_op jit(solution)/shard_map/ppermute | solution.py:386
  17.6 0.9 %collective-permute-start.7 = (f32[4,2,703]{2,1,0:T(2,128)S(1)}, f32[4,2,703]{2,1,0:T(2,128)S(1)}, u32[]{:S(2)}, u32[]{:S(2)}) collective-permute-start(f32[4,2,703]{2,1,0:T(2,128)S(1)} %get-tuple-element.37), channel_id=1, source_target_pairs={{0,3},{1,2},{2,1},{3,0},{4,7},{5,6},{6,5},{7,4},{8,11},{9,10},{10,... | collective-permute-start | bytes 67496 | tf_op jit(solution)/shard_map/ppermute | solution.py:386
  18.4 0.0 collective-permute-done.5
  18.4 2.0 %collective-permute-done.6 = f32[4,2,703]{2,1,0:T(2,128)S(1)} collective-permute-done((f32[4,2,703]{2,1,0:T(2,128)S(1)}, f32[4,2,703]{2,1,0:T(2,128)S(1)}, u32[]{:S(2)}, u32[]{:S(2)}) %collective-permute-start.6) | collective-permute-done | bytes 22528 | tf_op jit(solution)/shard_map/ppermute | solution.py:386
  20.5 0.4 collective-permute-done.7
  20.9 3.4 %collective-permute-start.10 = (f32[4,2,703]{2,1,0:T(2,128)S(1)}, f32[4,2,703]{2,1,0:T(2,128)S(1)}, u32[]{:S(2)}, u32[]{:S(2)}) collective-permute-start(f32[4,2,703]{2,1,0:T(2,128)S(1)} %bitcast.10), channel_id=1, source_target_pairs={{0,12},{1,13},{2,14},{3,15},{4,8},{5,9},{6,10},{7,11},{8,4},{9,5},... | collective-permute-start | bytes 67496 | tf_op jit(solution)/shard_map/ppermute | solution.py:386
  24.2 2.6 %collective-permute-start.9 = (f32[4,2,703]{2,1,0:T(2,128)S(1)}, f32[4,2,703]{2,1,0:T(2,128)S(1)}, u32[]{:S(2)}, u32[]{:S(2)}) collective-permute-start(f32[4,2,703]{2,1,0:T(2,128)S(1)} %bitcast.11), channel_id=1, source_target_pairs={{0,8},{1,9},{2,10},{3,11},{4,12},{5,13},{6,14},{7,15},{8,0},{9,1},... | collective-permute-start | bytes 67496 | tf_op jit(solution)/shard_map/ppermute | solution.py:386
  26.8 0.4 %collective-permute-start.8 = (f32[4,2,703]{2,1,0:T(2,128)S(1)}, f32[4,2,703]{2,1,0:T(2,128)S(1)}, u32[]{:S(2)}, u32[]{:S(2)}) collective-permute-start(f32[4,2,703]{2,1,0:T(2,128)S(1)} %bitcast.12), channel_id=1, source_target_pairs={{0,4},{1,5},{2,6},{3,7},{4,0},{5,1},{6,2},{7,3},{8,12},{9,13},{10,... | collective-permute-start | bytes 67496 | tf_op jit(solution)/shard_map/ppermute | solution.py:386
  27.2 0.1 station_hots.1.refs_2_
  27.3 0.0 collective-permute-done.10.refs_6_
  27.3 1.7 %collective-permute-done.9.refs_5_ = f32[4,2,703]{2,1,0:T(2,128)S(1)} collective-permute-done((f32[4,2,703]{2,1,0:T(2,128)S(1)}, f32[4,2,703]{2,1,0:T(2,128)S(1)}, u32[]{:S(2)}, u32[]{:S(2)}) %collective-permute-start.9) | collective-permute-done | bytes 22528 | tf_op jit(solution)/shard_map/ppermute | solution.py:386
  28.9 1.7 %collective-permute-done.8.refs_4_ = f32[4,2,703]{2,1,0:T(2,128)S(1)} collective-permute-done((f32[4,2,703]{2,1,0:T(2,128)S(1)}, f32[4,2,703]{2,1,0:T(2,128)S(1)}, u32[]{:S(2)}, u32[]{:S(2)}) %collective-permute-start.8) | collective-permute-done | bytes 22528 | tf_op jit(solution)/shard_map/ppermute | solution.py:386
  30.6 0.0 copy-done.1
  30.6 2.1 %gain_solve.1.refs_5_ = f32[4,2,806]{2,1,0:T(2,128)S(1)} custom-call(s32[1]{0:T(128)} %bitcast.refs_0_, s32[2,2]{1,0:T(2,128)S(1)} %copy-done.1, bf16[2,40,703]{2,1,0:T(8,128)(2,1)S(1)} %station_hots.1.refs_2_, f32[4,2,703]{2,1,0:T(2,128)S(1)} %bitcast.13, f32[4,2,703]{2,1,0:T(2,128)S(1)} %collective-permute-done.8.refs_4_, ...), custom_call_target="tpu_custom_call" | custom-call | tf_op jit(solution)/shard_map/gain_solve/pallas_call | solution.py:474
  32.7 0.1 collective-permute-start.13
  32.8 1.1 %collective-permute-start.12 = (f32[4,2,806]{2,1,0:T(2,128)S(1)}, f32[4,2,806]{2,1,0:T(2,128)S(1)}, u32[]{:S(2)}, u32[]{:S(2)}) collective-permute-start(f32[4,2,806]{2,1,0:T(2,128)S(1)} %gain_solve.1.refs_5_), channel_id=1, source_target_pairs={{0,2},{1,3},{2,0},{3,1},{4,6},{5,7},{6,4},{7,5},{8,10},{9,11},{10,... | collective-permute-start | bytes 77384 | tf_op jit(solution)/shard_map/ppermute | solution.py:386
  33.9 0.7 %collective-permute-start.11 = (f32[4,2,806]{2,1,0:T(2,128)S(1)}, f32[4,2,806]{2,1,0:T(2,128)S(1)}, u32[]{:S(2)}, u32[]{:S(2)}) collective-permute-start(f32[4,2,806]{2,1,0:T(2,128)S(1)} %gain_solve.1.refs_5_), channel_id=1, source_target_pairs={{0,1},{1,0},{2,3},{3,2},{4,5},{5,4},{6,7},{7,6},{8,9},{9,8},{10,11... | collective-permute-start | bytes 77384 | tf_op jit(solution)/shard_map/ppermute | solution.py:386
  34.6 1.4 %collective-permute-done.13.refs_8_ = f32[4,2,806]{2,1,0:T(2,128)S(1)} collective-permute-done((f32[4,2,806]{2,1,0:T(2,128)S(1)}, f32[4,2,806]{2,1,0:T(2,128)S(1)}, u32[]{:S(2)}, u32[]{:S(2)}) %collective-permute-start.13) | collective-permute-done | bytes 25824 | tf_op jit(solution)/shard_map/ppermute | solution.py:386
  36.0 0.8 %collective-permute-done.12.refs_7_ = f32[4,2,806]{2,1,0:T(2,128)S(1)} collective-permute-done((f32[4,2,806]{2,1,0:T(2,128)S(1)}, f32[4,2,806]{2,1,0:T(2,128)S(1)}, u32[]{:S(2)}, u32[]{:S(2)}) %collective-permute-start.12) | collective-permute-done | bytes 25824 | tf_op jit(solution)/shard_map/ppermute | solution.py:386
  36.9 0.0 collective-permute-done.11.refs_6_
  36.9 4.4 %clean.1 = (bf16[2,2,4,192,703]{4,3,2,1,0:T(8,128)(2,1)}, f32[2,2,2,4,38]{4,3,2,1,0:T(4,128)}) custom-call(s32[1]{0:T(128)} %bitcast.refs_0_, bf16[2,4,192,703]{3,2,1,0:T(8,128)(2,1)S(1)} %get-tuple-element.22.refs_10_.refs_1_, bf16[2,4,192,703]{3,2,1,0:T(8,128)(2,1)S(1)} %get-tuple-element.33.refs_2_, ...), custom_call_target="tpu_custom_call" | custom-call | tf_op jit(solution)/shard_map/clean/pallas_call | solution.py:483
  (5 shorter events, 0.0 us)
Async XLA Ops:
  0.6 6.3 %collective-permute-start.2 = (s32[1,2,192]{2,1,0:T(2,128)}, s32[1,2,192]{2,1,0:T(2,128)S(1)}, u32[]{:S(2)}, u32[]{:S(2)}) collective-permute-start(s32[1,2,192]{2,1,0:T(2,128)} %bitcast.20), channel_id=1, source_target_pairs={{0,3},{1,2},{2,1},{3,0},{4,7},{5,6},{6,5},{7,4},{8,11},{9,10},{10,... | collective-permute-start | bytes 4616 | tf_op jit(solution)/shard_map/ppermute | solution.py:386
  3.1 3.8 %collective-permute-start.1 = (s32[1,2,192]{2,1,0:T(2,128)}, s32[1,2,192]{2,1,0:T(2,128)S(1)}, u32[]{:S(2)}, u32[]{:S(2)}) collective-permute-start(s32[1,2,192]{2,1,0:T(2,128)} %bitcast.21), channel_id=1, source_target_pairs={{0,2},{1,3},{2,0},{3,1},{4,6},{5,7},{6,4},{7,5},{8,10},{9,11},{10,... | collective-permute-start | bytes 4616 | tf_op jit(solution)/shard_map/ppermute | solution.py:386
  3.7 2.3 %collective-permute-start = (s32[1,2,192]{2,1,0:T(2,128)}, s32[1,2,192]{2,1,0:T(2,128)S(1)}, u32[]{:S(2)}, u32[]{:S(2)}) collective-permute-start(s32[1,2,192]{2,1,0:T(2,128)} %bitcast.22), channel_id=1, source_target_pairs={{0,1},{1,0},{2,3},{3,2},{4,5},{5,4},{6,7},{7,6},{8,9},{9,8},{10,11... | collective-permute-start | bytes 4616 | tf_op jit(solution)/shard_map/ppermute | solution.py:386
  4.5 0.7 %copy-start = (f32[2,2,703]{2,1,0:T(2,128)S(1)}, f32[2,2,703]{2,1,0:T(2,128)}, u32[]{:S(2)}) copy-start(f32[2,2,703]{2,1,0:T(2,128)} %refs_2_.1) | copy-start | bytes 33748
  6.9 4.0 %collective-permute-start.4 = (s32[4,2,192]{2,1,0:T(2,128)S(1)}, s32[4,2,192]{2,1,0:T(2,128)S(1)}, u32[]{:S(2)}, u32[]{:S(2)}) collective-permute-start(s32[4,2,192]{2,1,0:T(2,128)S(1)} %constant_dynamic-update-slice_fusion.refs_1_), channel_id=1, source_target_pairs={{0,4},{1,5},{2,6},{3,7},{4,0},{5,1},{6,2},{7,3},{8,12},{9,13},{10,... | collective-permute-start | bytes 18440 | tf_op jit(solution)/shard_map/ppermute | solution.py:386
  8.6 2.4 %collective-permute-start.3 = (s32[4,2,192]{2,1,0:T(2,128)S(1)}, s32[4,2,192]{2,1,0:T(2,128)S(1)}, u32[]{:S(2)}, u32[]{:S(2)}) collective-permute-start(s32[4,2,192]{2,1,0:T(2,128)S(1)} %constant_dynamic-update-slice_fusion.refs_1_), channel_id=1, source_target_pairs={{4,8},{5,9},{6,10},{7,11},{8,4},{9,5},{10,6},{11,7},{20,24},{21,25... | collective-permute-start | bytes 18440 | tf_op jit(solution)/shard_map/ppermute | solution.py:453
  10.9 19.7 %copy-start.1 = (s32[2,2]{1,0:T(2,128)S(1)}, s32[2,2]{1,0:T(2,128)}, u32[]{:S(2)}) copy-start(s32[2,2]{1,0:T(2,128)} %refs_1_.3) | copy-start | bytes 52
  16.5 1.9 %collective-permute-start.5 = (f32[4,2,703]{2,1,0:T(2,128)S(1)}, f32[4,2,703]{2,1,0:T(2,128)S(1)}, u32[]{:S(2)}, u32[]{:S(2)}) collective-permute-start(f32[4,2,703]{2,1,0:T(2,128)S(1)} %get-tuple-element.35), channel_id=1, source_target_pairs={{0,1},{1,0},{2,3},{3,2},{4,5},{5,4},{6,7},{7,6},{8,9},{9,8},{10,11... | collective-permute-start | bytes 67496 | tf_op jit(solution)/shard_map/ppermute | solution.py:386
  16.6 3.9 %collective-permute-start.6 = (f32[4,2,703]{2,1,0:T(2,128)S(1)}, f32[4,2,703]{2,1,0:T(2,128)S(1)}, u32[]{:S(2)}, u32[]{:S(2)}) collective-permute-start(f32[4,2,703]{2,1,0:T(2,128)S(1)} %get-tuple-element.36), channel_id=1, source_target_pairs={{0,2},{1,3},{2,0},{3,1},{4,6},{5,7},{6,4},{7,5},{8,10},{9,11},{10,... | collective-permute-start | bytes 67496 | tf_op jit(solution)/shard_map/ppermute | solution.py:386
  17.6 3.3 %collective-permute-start.7 = (f32[4,2,703]{2,1,0:T(2,128)S(1)}, f32[4,2,703]{2,1,0:T(2,128)S(1)}, u32[]{:S(2)}, u32[]{:S(2)}) collective-permute-start(f32[4,2,703]{2,1,0:T(2,128)S(1)} %get-tuple-element.37), channel_id=1, source_target_pairs={{0,3},{1,2},{2,1},{3,0},{4,7},{5,6},{6,5},{7,4},{8,11},{9,10},{10,... | collective-permute-start | bytes 67496 | tf_op jit(solution)/shard_map/ppermute | solution.py:386
  20.9 6.4 %collective-permute-start.10 = (f32[4,2,703]{2,1,0:T(2,128)S(1)}, f32[4,2,703]{2,1,0:T(2,128)S(1)}, u32[]{:S(2)}, u32[]{:S(2)}) collective-permute-start(f32[4,2,703]{2,1,0:T(2,128)S(1)} %bitcast.10), channel_id=1, source_target_pairs={{0,12},{1,13},{2,14},{3,15},{4,8},{5,9},{6,10},{7,11},{8,4},{9,5},... | collective-permute-start | bytes 67496 | tf_op jit(solution)/shard_map/ppermute | solution.py:386
  24.2 4.7 %collective-permute-start.9 = (f32[4,2,703]{2,1,0:T(2,128)S(1)}, f32[4,2,703]{2,1,0:T(2,128)S(1)}, u32[]{:S(2)}, u32[]{:S(2)}) collective-permute-start(f32[4,2,703]{2,1,0:T(2,128)S(1)} %bitcast.11), channel_id=1, source_target_pairs={{0,8},{1,9},{2,10},{3,11},{4,12},{5,13},{6,14},{7,15},{8,0},{9,1},... | collective-permute-start | bytes 67496 | tf_op jit(solution)/shard_map/ppermute | solution.py:386
  26.8 3.8 %collective-permute-start.8 = (f32[4,2,703]{2,1,0:T(2,128)S(1)}, f32[4,2,703]{2,1,0:T(2,128)S(1)}, u32[]{:S(2)}, u32[]{:S(2)}) collective-permute-start(f32[4,2,703]{2,1,0:T(2,128)S(1)} %bitcast.12), channel_id=1, source_target_pairs={{0,4},{1,5},{2,6},{3,7},{4,0},{5,1},{6,2},{7,3},{8,12},{9,13},{10,... | collective-permute-start | bytes 67496 | tf_op jit(solution)/shard_map/ppermute | solution.py:386
  32.7 3.4 %collective-permute-start.13 = (f32[4,2,806]{2,1,0:T(2,128)S(1)}, f32[4,2,806]{2,1,0:T(2,128)S(1)}, u32[]{:S(2)}, u32[]{:S(2)}) collective-permute-start(f32[4,2,806]{2,1,0:T(2,128)S(1)} %gain_solve.1.refs_5_), channel_id=1, source_target_pairs={{0,3},{1,2},{2,1},{3,0},{4,7},{5,6},{6,5},{7,4},{8,11},{9,10},{10,... | collective-permute-start | bytes 77384 | tf_op jit(solution)/shard_map/ppermute | solution.py:386
  32.8 4.1 %collective-permute-start.12 = (f32[4,2,806]{2,1,0:T(2,128)S(1)}, f32[4,2,806]{2,1,0:T(2,128)S(1)}, u32[]{:S(2)}, u32[]{:S(2)}) collective-permute-start(f32[4,2,806]{2,1,0:T(2,128)S(1)} %gain_solve.1.refs_5_), channel_id=1, source_target_pairs={{0,2},{1,3},{2,0},{3,1},{4,6},{5,7},{6,4},{7,5},{8,10},{9,11},{10,... | collective-permute-start | bytes 77384 | tf_op jit(solution)/shard_map/ppermute | solution.py:386
  33.9 3.0 %collective-permute-start.11 = (f32[4,2,806]{2,1,0:T(2,128)S(1)}, f32[4,2,806]{2,1,0:T(2,128)S(1)}, u32[]{:S(2)}, u32[]{:S(2)}) collective-permute-start(f32[4,2,806]{2,1,0:T(2,128)S(1)} %gain_solve.1.refs_5_), channel_id=1, source_target_pairs={{0,1},{1,0},{2,3},{3,2},{4,5},{5,4},{6,7},{7,6},{8,9},{9,8},{10,11... | collective-permute-start | bytes 77384 | tf_op jit(solution)/shard_map/ppermute | solution.py:386

commit v14 on v13

--- a/solution.py
+++ b/solution.py
@@ -192,7 +192,7 @@
 
     for t in range(2):
         mine = lax.div(me, reach)
-        for group, other in enumerate((mine, lax.bitwise_xor(mine, 3), lax.bitwise_xor(mine, 1))):
+        for group, other in enumerate((mine, lax.bitwise_xor(mine, 1), lax.bitwise_xor(mine, 3))):
             side = jnp.where(jnp.abs(other - mine) > 1, 3, other - mine + 1)
             for slot in range(reach):
                 row = flag_refs[group][slot, t:t + 1, :].astype(F32)
@@ -451,7 +451,7 @@
                 gathered = jnp.concatenate([gathered] + [partner(gathered, stride * d) for d in range(1, 4)], axis=0)
             middle = [(i, i ^ (3 * reach)) for i in range(count) if reach <= i < 3 * reach]
             beyond = lax.ppermute(gathered, "sub", middle)
-            gathered = [gathered, beyond, partner(gathered, reach)]
+            gathered = [gathered, partner(gathered, reach), beyond]
     waves, mixing = ([part[i] for part in made] for i in range(2))
     held, *masks = made[1][2:]
     *quarters, held_too = pl.pallas_call(

time: 41.5 us -> 41.9 us (level)
  starting transfers between devices: 15.6 us -> 16.6 us
  waiting for transfers between devices: 8.8 us -> 8.24 us
    ppermute x13, starting transfers between devices: 15 us -> 15.9 us  [partner(): return lax.ppermute(value, 'sub', [(i, i ^ bits) for i in range(count)])]
    ppermute x13, waiting for transfers between devices: 8.8 us -> 8.23 us  [partner(): return lax.ppermute(value, 'sub', [(i, i ^ bits) for i in range(count)])]
  transfers between devices with their start and end apart: 14 -> 14, of which waited for: 7 -> 8; matrix products, arithmetic and copies ran while one was open for 2% -> 2% of each run, Pallas kernels for 6% -> 6%
where the time goes in v14:
time: 41.9 us; the launch traced here: 41.6 us
  starting transfers between devices  16.6 us (40%)
  Pallas kernels  14.6 us (35%)
  waiting for transfers between devices  8.24 us (20%)
  local copies, waits for them, and re-layouts  0.74 us (2%)
  between operations  0.74 us (2%)
  other arithmetic  0.73 us (2%)
    ppermute x13, starting transfers between devices, partner(): return lax.ppermute(value, 'sub', [(i, i ^ bits) for i in range(count)])  15.9 us
    ppermute x13, waiting for transfers between devices, partner(): return lax.ppermute(value, 'sub', [(i, i ^ bits) for i in range(count)])  8.23 us
    pallas_call x1, Pallas kernels, local(): pl.pallas_call(lambda *refs: sums_kernel(width, reach, *refs), in_specs=[...  5.57 us
    pallas_call x1, Pallas kernels, local(): pl.pallas_call(lambda *refs: clean_kernel(width, *refs), in_specs=[smem()...  4.39 us
    pallas_call x2, Pallas kernels, local(): pl.pallas_call(lambda *refs: phase_kernel(width, t, reach, *refs), in_spe...  2.51 us
    pallas_call x1, Pallas kernels, local(): pl.pallas_call(lambda *refs: solve_kernel(float(window_count), *refs), in...  2.06 us
  transfers between devices with their start and end apart: 14, of which 8 were waited for; matrix products, arithmetic and copies ran while one was open for 2% of the time, Pallas kernels for 6%

profile of v14, /device:TPU:0, one launch (start us, length us, event | category | flops | bytes accessed | tf_op | source)
XLA Modules:
  0.0 41.6 jit_solution(14039578161657823370)
XLA Ops:
  0.6 2.5 %collective-permute-start.2 = (s32[1,2,192]{2,1,0:T(2,128)}, s32[1,2,192]{2,1,0:T(2,128)S(1)}, u32[]{:S(2)}, u32[]{:S(2)}) collective-permute-start(s32[1,2,192]{2,1,0:T(2,128)} %bitcast.20), channel_id=1, source_target_pairs={{0,3},{1,2},{2,1},{3,0},{4,7},{5,6},{6,5},{7,4},{8,11},{9,10},{10,... | collective-permute-start | bytes 4616 | tf_op jit(solution)/shard_map/ppermute | solution.py:386
  3.1 0.6 %collective-permute-start.1 = (s32[1,2,192]{2,1,0:T(2,128)}, s32[1,2,192]{2,1,0:T(2,128)S(1)}, u32[]{:S(2)}, u32[]{:S(2)}) collective-permute-start(s32[1,2,192]{2,1,0:T(2,128)} %bitcast.21), channel_id=1, source_target_pairs={{0,2},{1,3},{2,0},{3,1},{4,6},{5,7},{6,4},{7,5},{8,10},{9,11},{10,... | collective-permute-start | bytes 4616 | tf_op jit(solution)/shard_map/ppermute | solution.py:386
  3.7 0.0 collective-permute-start
  3.8 0.7 %pad_add_fusion.refs_2_ = s32[3,192]{1,0:T(4,128)S(1)} fusion(s32[1,32]{1,0:T(1,128)} %bitcast.23, s32[2,192]{1,0:T(2,128)} %param.7), kind=kLoop, calls=%fused_computation.5 | loop fusion | flops 576 | bytes 3968 | tf_op jit(solution)/shard_map/add | solution.py:417
  4.5 0.0 copy-start
  4.5 0.7 %copy-done = f32[2,2,703]{2,1,0:T(2,128)S(1)} copy-done((f32[2,2,703]{2,1,0:T(2,128)S(1)}, f32[2,2,703]{2,1,0:T(2,128)}, u32[]{:S(2)}) %copy-start) | copy-done | bytes 11272
  5.2 0.8 %phases.2 = (f32[2,2,192,703]{3,2,1,0:T(8,128)S(1)}, bf16[2,2,192,703]{3,2,1,0:T(8,128)(2,1)S(1)}, s32[1,2,192]{2,1,0:T(2,128)S(1)}, s32[1,32]{1,0:T(1,128)S(1)}) custom-call(s32[1]{0:T(128)} %bitcast.refs_0_, f32[2,2,703]{2,1,0:T(2,128)S(1)} %copy-done, s32[3,192]{1,0:T(4,128)S(1)} %pad_add_fusion.refs_2_), custom_call_target="tpu_custom_call" | custom-call | flops 10000000 | bytes 6291456 | tf_op jit(solution)/shard_map/phases/pallas_call | solution.py:437
  6.1 0.0 collective-permute-done
  6.1 0.8 %collective-permute-done.1 = s32[1,2,192]{2,1,0:T(2,128)S(1)} collective-permute-done((s32[1,2,192]{2,1,0:T(2,128)}, s32[1,2,192]{2,1,0:T(2,128)S(1)}, u32[]{:S(2)}, u32[]{:S(2)}) %collective-permute-start.1) | collective-permute-done | bytes 1568 | tf_op jit(solution)/shard_map/ppermute | solution.py:386
  6.9 0.0 collective-permute-done.2
  6.9 0.7 %collective-permute-start.4 = (s32[4,2,192]{2,1,0:T(2,128)S(1)}, s32[4,2,192]{2,1,0:T(2,128)S(1)}, u32[]{:S(2)}, u32[]{:S(2)}) collective-permute-start(s32[4,2,192]{2,1,0:T(2,128)S(1)} %constant_dynamic-update-slice_fusion.refs_1_), channel_id=1, source_target_pairs={{4,8},{5,9},{6,10},{7,11},{8,4},{9,5},{10,6},{11,7},{20,24},{21,25... | collective-permute-start | bytes 18440 | tf_op jit(solution)/shard_map/ppermute | solution.py:453
  7.6 4.5 %collective-permute-start.3 = (s32[4,2,192]{2,1,0:T(2,128)S(1)}, s32[4,2,192]{2,1,0:T(2,128)S(1)}, u32[]{:S(2)}, u32[]{:S(2)}) collective-permute-start(s32[4,2,192]{2,1,0:T(2,128)S(1)} %constant_dynamic-update-slice_fusion.refs_1_), channel_id=1, source_target_pairs={{0,4},{1,5},{2,6},{3,7},{4,0},{5,1},{6,2},{7,3},{8,12},{9,13},{10,... | collective-permute-start | bytes 18440 | tf_op jit(solution)/shard_map/ppermute | solution.py:386
  12.0 1.7 %phases.3 = (f32[2,2,192,703]{3,2,1,0:T(8,128)S(1)}, bf16[2,2,192,703]{3,2,1,0:T(8,128)(2,1)S(1)}, bf16[2,4,192,703]{3,2,1,0:T(8,128)(2,1)S(1)}, f32[2,2,16,703]...) custom-call(s32[1]{0:T(128)} %bitcast.refs_0_, ...), custom_call_target="tpu_custom_call" | custom-call | flops 10000000 | bytes 6291456 | tf_op jit(solution)/shard_map/phases/pallas_call | solution.py:437
  13.7 0.0 collective-permute-done.4.refs_3_
  13.7 0.0 collective-permute-done.3.refs_2_
  13.7 0.0 copy-start.1
  13.8 5.6 %window_sums.1 = (f32[4,2,703]{2,1,0:T(2,128)S(1)}, f32[4,2,703]{2,1,0:T(2,128)S(1)}, f32[4,2,703]{2,1,0:T(2,128)S(1)}, f32[4,2,703]{2,1,0:T(2,128)S(1)}, bf16[2,4,192,703]{3,2,1,0:T(8,128)(2,1)S(1)}) custom-call(s32[1]{0:T(128)} %bitcast.refs_0_, s32[4,2,192]{2,1,0:T(2,128)S(1)} %constant_dynamic-update-slice_fusion.refs_1_, ...), custom_call_target="tpu_custom_call" | custom-call | tf_op jit(solution)/shard_map/window_sums/pallas_call | solution.py:457
  19.3 0.1 collective-permute-start.5
  19.4 1.0 %collective-permute-start.6 = (f32[4,2,703]{2,1,0:T(2,128)S(1)}, f32[4,2,703]{2,1,0:T(2,128)S(1)}, u32[]{:S(2)}, u32[]{:S(2)}) collective-permute-start(f32[4,2,703]{2,1,0:T(2,128)S(1)} %get-tuple-element.36), channel_id=1, source_target_pairs={{0,2},{1,3},{2,0},{3,1},{4,6},{5,7},{6,4},{7,5},{8,10},{9,11},{10,... | collective-permute-start | bytes 67496 | tf_op jit(solution)/shard_map/ppermute | solution.py:386
  20.4 0.9 %collective-permute-start.7 = (f32[4,2,703]{2,1,0:T(2,128)S(1)}, f32[4,2,703]{2,1,0:T(2,128)S(1)}, u32[]{:S(2)}, u32[]{:S(2)}) collective-permute-start(f32[4,2,703]{2,1,0:T(2,128)S(1)} %get-tuple-element.37), channel_id=1, source_target_pairs={{0,3},{1,2},{2,1},{3,0},{4,7},{5,6},{6,5},{7,4},{8,11},{9,10},{10,... | collective-permute-start | bytes 67496 | tf_op jit(solution)/shard_map/ppermute | solution.py:386
  21.3 0.0 collective-permute-done.5
  21.3 2.0 %collective-permute-done.6 = f32[4,2,703]{2,1,0:T(2,128)S(1)} collective-permute-done((f32[4,2,703]{2,1,0:T(2,128)S(1)}, f32[4,2,703]{2,1,0:T(2,128)S(1)}, u32[]{:S(2)}, u32[]{:S(2)}) %collective-permute-start.6) | collective-permute-done | bytes 22528 | tf_op jit(solution)/shard_map/ppermute | solution.py:386
  23.3 0.4 collective-permute-done.7
  23.7 1.4 %collective-permute-start.10 = (f32[4,2,703]{2,1,0:T(2,128)S(1)}, f32[4,2,703]{2,1,0:T(2,128)S(1)}, u32[]{:S(2)}, u32[]{:S(2)}) collective-permute-start(f32[4,2,703]{2,1,0:T(2,128)S(1)} %bitcast.10), channel_id=1, source_target_pairs={{0,12},{1,13},{2,14},{3,15},{4,8},{5,9},{6,10},{7,11},{8,4},{9,5},... | collective-permute-start | bytes 67496 | tf_op jit(solution)/shard_map/ppermute | solution.py:386
  25.1 2.0 %collective-permute-start.9 = (f32[4,2,703]{2,1,0:T(2,128)S(1)}, f32[4,2,703]{2,1,0:T(2,128)S(1)}, u32[]{:S(2)}, u32[]{:S(2)}) collective-permute-start(f32[4,2,703]{2,1,0:T(2,128)S(1)} %bitcast.11), channel_id=1, source_target_pairs={{0,8},{1,9},{2,10},{3,11},{4,12},{5,13},{6,14},{7,15},{8,0},{9,1},... | collective-permute-start | bytes 67496 | tf_op jit(solution)/shard_map/ppermute | solution.py:386
  27.1 1.0 %collective-permute-start.8 = (f32[4,2,703]{2,1,0:T(2,128)S(1)}, f32[4,2,703]{2,1,0:T(2,128)S(1)}, u32[]{:S(2)}, u32[]{:S(2)}) collective-permute-start(f32[4,2,703]{2,1,0:T(2,128)S(1)} %bitcast.12), channel_id=1, source_target_pairs={{0,4},{1,5},{2,6},{3,7},{4,0},{5,1},{6,2},{7,3},{8,12},{9,13},{10,... | collective-permute-start | bytes 67496 | tf_op jit(solution)/shard_map/ppermute | solution.py:386
  28.1 0.1 station_hots.1.refs_2_
  28.2 1.3 %collective-permute-done.10.refs_6_ = f32[4,2,703]{2,1,0:T(2,128)S(1)} collective-permute-done((f32[4,2,703]{2,1,0:T(2,128)S(1)}, f32[4,2,703]{2,1,0:T(2,128)S(1)}, u32[]{:S(2)}, u32[]{:S(2)}) %collective-permute-start.10) | collective-permute-done | bytes 22528 | tf_op jit(solution)/shard_map/ppermute | solution.py:386
  29.5 0.4 %collective-permute-done.9.refs_5_ = f32[4,2,703]{2,1,0:T(2,128)S(1)} collective-permute-done((f32[4,2,703]{2,1,0:T(2,128)S(1)}, f32[4,2,703]{2,1,0:T(2,128)S(1)}, u32[]{:S(2)}, u32[]{:S(2)}) %collective-permute-start.9) | collective-permute-done | bytes 22528 | tf_op jit(solution)/shard_map/ppermute | solution.py:386
  29.9 1.1 %collective-permute-done.8.refs_4_ = f32[4,2,703]{2,1,0:T(2,128)S(1)} collective-permute-done((f32[4,2,703]{2,1,0:T(2,128)S(1)}, f32[4,2,703]{2,1,0:T(2,128)S(1)}, u32[]{:S(2)}, u32[]{:S(2)}) %collective-permute-start.8) | collective-permute-done | bytes 22528 | tf_op jit(solution)/shard_map/ppermute | solution.py:386
  31.0 0.0 copy-done.1
  31.0 2.1 %gain_solve.1.refs_5_ = f32[4,2,806]{2,1,0:T(2,128)S(1)} custom-call(s32[1]{0:T(128)} %bitcast.refs_0_, s32[2,2]{1,0:T(2,128)S(1)} %copy-done.1, bf16[2,40,703]{2,1,0:T(8,128)(2,1)S(1)} %station_hots.1.refs_2_, f32[4,2,703]{2,1,0:T(2,128)S(1)} %bitcast.13, f32[4,2,703]{2,1,0:T(2,128)S(1)} %collective-permute-done.8.refs_4_, ...), custom_call_target="tpu_custom_call" | custom-call | tf_op jit(solution)/shard_map/gain_solve/pallas_call | solution.py:474
  33.0 0.1 collective-permute-start.13
  33.1 1.1 %collective-permute-start.12 = (f32[4,2,806]{2,1,0:T(2,128)S(1)}, f32[4,2,806]{2,1,0:T(2,128)S(1)}, u32[]{:S(2)}, u32[]{:S(2)}) collective-permute-start(f32[4,2,806]{2,1,0:T(2,128)S(1)} %gain_solve.1.refs_5_), channel_id=1, source_target_pairs={{0,2},{1,3},{2,0},{3,1},{4,6},{5,7},{6,4},{7,5},{8,10},{9,11},{10,... | collective-permute-start | bytes 77384 | tf_op jit(solution)/shard_map/ppermute | solution.py:386
  34.3 0.7 %collective-permute-start.11 = (f32[4,2,806]{2,1,0:T(2,128)S(1)}, f32[4,2,806]{2,1,0:T(2,128)S(1)}, u32[]{:S(2)}, u32[]{:S(2)}) collective-permute-start(f32[4,2,806]{2,1,0:T(2,128)S(1)} %gain_solve.1.refs_5_), channel_id=1, source_target_pairs={{0,1},{1,0},{2,3},{3,2},{4,5},{5,4},{6,7},{7,6},{8,9},{9,8},{10,11... | collective-permute-start | bytes 77384 | tf_op jit(solution)/shard_map/ppermute | solution.py:386
  35.0 1.4 %collective-permute-done.13.refs_8_ = f32[4,2,806]{2,1,0:T(2,128)S(1)} collective-permute-done((f32[4,2,806]{2,1,0:T(2,128)S(1)}, f32[4,2,806]{2,1,0:T(2,128)S(1)}, u32[]{:S(2)}, u32[]{:S(2)}) %collective-permute-start.13) | collective-permute-done | bytes 25824 | tf_op jit(solution)/shard_map/ppermute | solution.py:386
  36.4 0.8 %collective-permute-done.12.refs_7_ = f32[4,2,806]{2,1,0:T(2,128)S(1)} collective-permute-done((f32[4,2,806]{2,1,0:T(2,128)S(1)}, f32[4,2,806]{2,1,0:T(2,128)S(1)}, u32[]{:S(2)}, u32[]{:S(2)}) %collective-permute-start.12) | collective-permute-done | bytes 25824 | tf_op jit(solution)/shard_map/ppermute | solution.py:386
  37.2 0.0 collective-permute-done.11.refs_6_
  37.2 4.4 %clean.1 = (bf16[2,2,4,192,703]{4,3,2,1,0:T(8,128)(2,1)}, f32[2,2,2,4,38]{4,3,2,1,0:T(4,128)}) custom-call(s32[1]{0:T(128)} %bitcast.refs_0_, bf16[2,4,192,703]{3,2,1,0:T(8,128)(2,1)S(1)} %get-tuple-element.22.refs_10_.refs_1_, bf16[2,4,192,703]{3,2,1,0:T(8,128)(2,1)S(1)} %get-tuple-element.33.refs_2_, ...), custom_call_target="tpu_custom_call" | custom-call | tf_op jit(solution)/shard_map/clean/pallas_call | solution.py:483
  (5 shorter events, 0.0 us)
Async XLA Ops:
  0.6 6.3 %collective-permute-start.2 = (s32[1,2,192]{2,1,0:T(2,128)}, s32[1,2,192]{2,1,0:T(2,128)S(1)}, u32[]{:S(2)}, u32[]{:S(2)}) collective-permute-start(s32[1,2,192]{2,1,0:T(2,128)} %bitcast.20), channel_id=1, source_target_pairs={{0,3},{1,2},{2,1},{3,0},{4,7},{5,6},{6,5},{7,4},{8,11},{9,10},{10,... | collective-permute-start | bytes 4616 | tf_op jit(solution)/shard_map/ppermute | solution.py:386
  3.1 3.8 %collective-permute-start.1 = (s32[1,2,192]{2,1,0:T(2,128)}, s32[1,2,192]{2,1,0:T(2,128)S(1)}, u32[]{:S(2)}, u32[]{:S(2)}) collective-permute-start(s32[1,2,192]{2,1,0:T(2,128)} %bitcast.21), channel_id=1, source_target_pairs={{0,2},{1,3},{2,0},{3,1},{4,6},{5,7},{6,4},{7,5},{8,10},{9,11},{10,... | collective-permute-start | bytes 4616 | tf_op jit(solution)/shard_map/ppermute | solution.py:386
  3.7 2.3 %collective-permute-start = (s32[1,2,192]{2,1,0:T(2,128)}, s32[1,2,192]{2,1,0:T(2,128)S(1)}, u32[]{:S(2)}, u32[]{:S(2)}) collective-permute-start(s32[1,2,192]{2,1,0:T(2,128)} %bitcast.22), channel_id=1, source_target_pairs={{0,1},{1,0},{2,3},{3,2},{4,5},{5,4},{6,7},{7,6},{8,9},{9,8},{10,11... | collective-permute-start | bytes 4616 | tf_op jit(solution)/shard_map/ppermute | solution.py:386
  4.5 0.7 %copy-start = (f32[2,2,703]{2,1,0:T(2,128)S(1)}, f32[2,2,703]{2,1,0:T(2,128)}, u32[]{:S(2)}) copy-start(f32[2,2,703]{2,1,0:T(2,128)} %refs_2_.1) | copy-start | bytes 33748
  6.9 6.8 %collective-permute-start.4 = (s32[4,2,192]{2,1,0:T(2,128)S(1)}, s32[4,2,192]{2,1,0:T(2,128)S(1)}, u32[]{:S(2)}, u32[]{:S(2)}) collective-permute-start(s32[4,2,192]{2,1,0:T(2,128)S(1)} %constant_dynamic-update-slice_fusion.refs_1_), channel_id=1, source_target_pairs={{4,8},{5,9},{6,10},{7,11},{8,4},{9,5},{10,6},{11,7},{20,24},{21,25... | collective-permute-start | bytes 18440 | tf_op jit(solution)/shard_map/ppermute | solution.py:453
  7.6 6.2 %collective-permute-start.3 = (s32[4,2,192]{2,1,0:T(2,128)S(1)}, s32[4,2,192]{2,1,0:T(2,128)S(1)}, u32[]{:S(2)}, u32[]{:S(2)}) collective-permute-start(s32[4,2,192]{2,1,0:T(2,128)S(1)} %constant_dynamic-update-slice_fusion.refs_1_), channel_id=1, source_target_pairs={{0,4},{1,5},{2,6},{3,7},{4,0},{5,1},{6,2},{7,3},{8,12},{9,13},{10,... | collective-permute-start | bytes 18440 | tf_op jit(solution)/shard_map/ppermute | solution.py:386
  13.7 17.2 %copy-start.1 = (s32[2,2]{1,0:T(2,128)S(1)}, s32[2,2]{1,0:T(2,128)}, u32[]{:S(2)}) copy-start(s32[2,2]{1,0:T(2,128)} %refs_1_.3) | copy-start | bytes 52
  19.3 1.9 %collective-permute-start.5 = (f32[4,2,703]{2,1,0:T(2,128)S(1)}, f32[4,2,703]{2,1,0:T(2,128)S(1)}, u32[]{:S(2)}, u32[]{:S(2)}) collective-permute-start(f32[4,2,703]{2,1,0:T(2,128)S(1)} %get-tuple-element.35), channel_id=1, source_target_pairs={{0,1},{1,0},{2,3},{3,2},{4,5},{5,4},{6,7},{7,6},{8,9},{9,8},{10,11... | collective-permute-start | bytes 67496 | tf_op jit(solution)/shard_map/ppermute | solution.py:386
  19.4 3.9 %collective-permute-start.6 = (f32[4,2,703]{2,1,0:T(2,128)S(1)}, f32[4,2,703]{2,1,0:T(2,128)S(1)}, u32[]{:S(2)}, u32[]{:S(2)}) collective-permute-start(f32[4,2,703]{2,1,0:T(2,128)S(1)} %get-tuple-element.36), channel_id=1, source_target_pairs={{0,2},{1,3},{2,0},{3,1},{4,6},{5,7},{6,4},{7,5},{8,10},{9,11},{10,... | collective-permute-start | bytes 67496 | tf_op jit(solution)/shard_map/ppermute | solution.py:386
  20.4 3.3 %collective-permute-start.7 = (f32[4,2,703]{2,1,0:T(2,128)S(1)}, f32[4,2,703]{2,1,0:T(2,128)S(1)}, u32[]{:S(2)}, u32[]{:S(2)}) collective-permute-start(f32[4,2,703]{2,1,0:T(2,128)S(1)} %get-tuple-element.37), channel_id=1, source_target_pairs={{0,3},{1,2},{2,1},{3,0},{4,7},{5,6},{6,5},{7,4},{8,11},{9,10},{10,... | collective-permute-start | bytes 67496 | tf_op jit(solution)/shard_map/ppermute | solution.py:386
  23.7 5.8 %collective-permute-start.10 = (f32[4,2,703]{2,1,0:T(2,128)S(1)}, f32[4,2,703]{2,1,0:T(2,128)S(1)}, u32[]{:S(2)}, u32[]{:S(2)}) collective-permute-start(f32[4,2,703]{2,1,0:T(2,128)S(1)} %bitcast.10), channel_id=1, source_target_pairs={{0,12},{1,13},{2,14},{3,15},{4,8},{5,9},{6,10},{7,11},{8,4},{9,5},... | collective-permute-start | bytes 67496 | tf_op jit(solution)/shard_map/ppermute | solution.py:386
  25.1 4.8 %collective-permute-start.9 = (f32[4,2,703]{2,1,0:T(2,128)S(1)}, f32[4,2,703]{2,1,0:T(2,128)S(1)}, u32[]{:S(2)}, u32[]{:S(2)}) collective-permute-start(f32[4,2,703]{2,1,0:T(2,128)S(1)} %bitcast.11), channel_id=1, source_target_pairs={{0,8},{1,9},{2,10},{3,11},{4,12},{5,13},{6,14},{7,15},{8,0},{9,1},... | collective-permute-start | bytes 67496 | tf_op jit(solution)/shard_map/ppermute | solution.py:386
  27.1 3.8 %collective-permute-start.8 = (f32[4,2,703]{2,1,0:T(2,128)S(1)}, f32[4,2,703]{2,1,0:T(2,128)S(1)}, u32[]{:S(2)}, u32[]{:S(2)}) collective-permute-start(f32[4,2,703]{2,1,0:T(2,128)S(1)} %bitcast.12), channel_id=1, source_target_pairs={{0,4},{1,5},{2,6},{3,7},{4,0},{5,1},{6,2},{7,3},{8,12},{9,13},{10,... | collective-permute-start | bytes 67496 | tf_op jit(solution)/shard_map/ppermute | solution.py:386
  33.0 3.4 %collective-permute-start.13 = (f32[4,2,806]{2,1,0:T(2,128)S(1)}, f32[4,2,806]{2,1,0:T(2,128)S(1)}, u32[]{:S(2)}, u32[]{:S(2)}) collective-permute-start(f32[4,2,806]{2,1,0:T(2,128)S(1)} %gain_solve.1.refs_5_), channel_id=1, source_target_pairs={{0,3},{1,2},{2,1},{3,0},{4,7},{5,6},{6,5},{7,4},{8,11},{9,10},{10,... | collective-permute-start | bytes 77384 | tf_op jit(solution)/shard_map/ppermute | solution.py:386
  33.1 4.1 %collective-permute-start.12 = (f32[4,2,806]{2,1,0:T(2,128)S(1)}, f32[4,2,806]{2,1,0:T(2,128)S(1)}, u32[]{:S(2)}, u32[]{:S(2)}) collective-permute-start(f32[4,2,806]{2,1,0:T(2,128)S(1)} %gain_solve.1.refs_5_), channel_id=1, source_target_pairs={{0,2},{1,3},{2,0},{3,1},{4,6},{5,7},{6,4},{7,5},{8,10},{9,11},{10,... | collective-permute-start | bytes 77384 | tf_op jit(solution)/shard_map/ppermute | solution.py:386
  34.3 3.0 %collective-permute-start.11 = (f32[4,2,806]{2,1,0:T(2,128)S(1)}, f32[4,2,806]{2,1,0:T(2,128)S(1)}, u32[]{:S(2)}, u32[]{:S(2)}) collective-permute-start(f32[4,2,806]{2,1,0:T(2,128)S(1)} %gain_solve.1.refs_5_), channel_id=1, source_target_pairs={{0,1},{1,0},{2,3},{3,2},{4,5},{5,4},{6,7},{7,6},{8,9},{9,8},{10,11... | collective-permute-start | bytes 77384 | tf_op jit(solution)/shard_map/ppermute | solution.py:386

commit v15 on v13

--- a/solution.py
+++ b/solution.py
@@ -243,7 +243,7 @@
                 return tuple(new)
 
             zero = jnp.zeros((8, count), F32)
-            sums = lax.fori_loop(0, width // 16, step, (zero,) * 24, unroll=6)
+            sums = lax.fori_loop(0, width // 16, step, (zero,) * 24, unroll=12)
             for s in range(2):
                 owner = lax.bitwise_xor(lax.bitwise_and(me, 3), t + 2 * s)
                 found = []

time: 41.5 us -> 41.3 us (level)
  no operation moved by 1% of the time
where the time goes in v15:
time: 41.3 us; the launch traced here: 41 us
  starting transfers between devices  15.7 us (38%)
  Pallas kernels  14.3 us (35%)
  waiting for transfers between devices  8.8 us (21%)
  between operations  0.75 us (2%)
  local copies, waits for them, and re-layouts  0.74 us (2%)
  other arithmetic  0.73 us (2%)
    ppermute x13, starting transfers between devices, partner(): return lax.ppermute(value, 'sub', [(i, i ^ bits) for i in range(count)])  15 us
    ppermute x13, waiting for transfers between devices, partner(): return lax.ppermute(value, 'sub', [(i, i ^ bits) for i in range(count)])  8.8 us
    pallas_call x1, Pallas kernels, local(): pl.pallas_call(lambda *refs: sums_kernel(width, reach, *refs), in_specs=[...  5.3 us
    pallas_call x1, Pallas kernels, local(): pl.pallas_call(lambda *refs: clean_kernel(width, *refs), in_specs=[smem()...  4.39 us
    pallas_call x2, Pallas kernels, local(): pl.pallas_call(lambda *refs: phase_kernel(width, t, reach, *refs), in_spe...  2.52 us
    pallas_call x1, Pallas kernels, local(): pl.pallas_call(lambda *refs: solve_kernel(float(window_count), *refs), in...  2.07 us
  transfers between devices with their start and end apart: 14, of which 7 were waited for; matrix products, arithmetic and copies ran while one was open for 2% of the time, Pallas kernels for 6%

profile of v15, /device:TPU:0, one launch (start us, length us, event | category | flops | bytes accessed | tf_op | source)
XLA Modules:
  0.0 41.0 jit_solution(11553424843726754343)
XLA Ops:
  0.6 2.5 %collective-permute-start.2 = (s32[1,2,192]{2,1,0:T(2,128)}, s32[1,2,192]{2,1,0:T(2,128)S(1)}, u32[]{:S(2)}, u32[]{:S(2)}) collective-permute-start(s32[1,2,192]{2,1,0:T(2,128)} %bitcast.20), channel_id=1, source_target_pairs={{0,3},{1,2},{2,1},{3,0},{4,7},{5,6},{6,5},{7,4},{8,11},{9,10},{10,... | collective-permute-start | bytes 4616 | tf_op jit(solution)/shard_map/ppermute | solution.py:386
  3.1 0.6 %collective-permute-start.1 = (s32[1,2,192]{2,1,0:T(2,128)}, s32[1,2,192]{2,1,0:T(2,128)S(1)}, u32[]{:S(2)}, u32[]{:S(2)}) collective-permute-start(s32[1,2,192]{2,1,0:T(2,128)} %bitcast.21), channel_id=1, source_target_pairs={{0,2},{1,3},{2,0},{3,1},{4,6},{5,7},{6,4},{7,5},{8,10},{9,11},{10,... | collective-permute-start | bytes 4616 | tf_op jit(solution)/shard_map/ppermute | solution.py:386
  3.7 0.0 collective-permute-start
  3.8 0.7 %pad_add_fusion.refs_2_ = s32[3,192]{1,0:T(4,128)S(1)} fusion(s32[1,32]{1,0:T(1,128)} %bitcast.23, s32[2,192]{1,0:T(2,128)} %param.7), kind=kLoop, calls=%fused_computation.5 | loop fusion | flops 576 | bytes 3968 | tf_op jit(solution)/shard_map/add | solution.py:417
  4.5 0.0 copy-start
  4.5 0.7 %copy-done = f32[2,2,703]{2,1,0:T(2,128)S(1)} copy-done((f32[2,2,703]{2,1,0:T(2,128)S(1)}, f32[2,2,703]{2,1,0:T(2,128)}, u32[]{:S(2)}) %copy-start) | copy-done | bytes 11272
  5.2 0.8 %phases.2 = (f32[2,2,192,703]{3,2,1,0:T(8,128)S(1)}, bf16[2,2,192,703]{3,2,1,0:T(8,128)(2,1)S(1)}, s32[1,2,192]{2,1,0:T(2,128)S(1)}, s32[1,32]{1,0:T(1,128)S(1)}) custom-call(s32[1]{0:T(128)} %bitcast.refs_0_, f32[2,2,703]{2,1,0:T(2,128)S(1)} %copy-done, s32[3,192]{1,0:T(4,128)S(1)} %pad_add_fusion.refs_2_), custom_call_target="tpu_custom_call" | custom-call | flops 10000000 | bytes 6291456 | tf_op jit(solution)/shard_map/phases/pallas_call | solution.py:437
  6.1 0.0 collective-permute-done
  6.1 0.8 %collective-permute-done.1 = s32[1,2,192]{2,1,0:T(2,128)S(1)} collective-permute-done((s32[1,2,192]{2,1,0:T(2,128)}, s32[1,2,192]{2,1,0:T(2,128)S(1)}, u32[]{:S(2)}, u32[]{:S(2)}) %collective-permute-start.1) | collective-permute-done | bytes 1568 | tf_op jit(solution)/shard_map/ppermute | solution.py:386
  6.9 0.0 collective-permute-done.2
  6.9 1.6 %collective-permute-start.4 = (s32[4,2,192]{2,1,0:T(2,128)S(1)}, s32[4,2,192]{2,1,0:T(2,128)S(1)}, u32[]{:S(2)}, u32[]{:S(2)}) collective-permute-start(s32[4,2,192]{2,1,0:T(2,128)S(1)} %constant_dynamic-update-slice_fusion.refs_1_), channel_id=1, source_target_pairs={{0,4},{1,5},{2,6},{3,7},{4,0},{5,1},{6,2},{7,3},{8,12},{9,13},{10,... | collective-permute-start | bytes 18440 | tf_op jit(solution)/shard_map/ppermute | solution.py:386
  8.6 0.6 %collective-permute-start.3 = (s32[4,2,192]{2,1,0:T(2,128)S(1)}, s32[4,2,192]{2,1,0:T(2,128)S(1)}, u32[]{:S(2)}, u32[]{:S(2)}) collective-permute-start(s32[4,2,192]{2,1,0:T(2,128)S(1)} %constant_dynamic-update-slice_fusion.refs_1_), channel_id=1, source_target_pairs={{4,8},{5,9},{6,10},{7,11},{8,4},{9,5},{10,6},{11,7},{20,24},{21,25... | collective-permute-start | bytes 18440 | tf_op jit(solution)/shard_map/ppermute | solution.py:453
  9.2 1.7 %phases.3 = (f32[2,2,192,703]{3,2,1,0:T(8,128)S(1)}, bf16[2,2,192,703]{3,2,1,0:T(8,128)(2,1)S(1)}, bf16[2,4,192,703]{3,2,1,0:T(8,128)(2,1)S(1)}, f32[2,2,16,703]...) custom-call(s32[1]{0:T(128)} %bitcast.refs_0_, ...), custom_call_target="tpu_custom_call" | custom-call | flops 10000000 | bytes 6291456 | tf_op jit(solution)/shard_map/phases/pallas_call | solution.py:437
  10.9 0.0 collective-permute-done.4.refs_3_
  10.9 0.0 collective-permute-done.3.refs_2_
  10.9 0.0 copy-start.1
  10.9 5.3 %window_sums.1 = (f32[4,2,703]{2,1,0:T(2,128)S(1)}, f32[4,2,703]{2,1,0:T(2,128)S(1)}, f32[4,2,703]{2,1,0:T(2,128)S(1)}, f32[4,2,703]{2,1,0:T(2,128)S(1)}, bf16[2,4,192,703]{3,2,1,0:T(8,128)(2,1)S(1)}) custom-call(s32[1]{0:T(128)} %bitcast.refs_0_, s32[4,2,192]{2,1,0:T(2,128)S(1)} %constant_dynamic-update-slice_fusion.refs_1_, ...), custom_call_target="tpu_custom_call" | custom-call | tf_op jit(solution)/shard_map/window_sums/pallas_call | solution.py:457
  16.2 0.1 collective-permute-start.5
  16.3 1.0 %collective-permute-start.6 = (f32[4,2,703]{2,1,0:T(2,128)S(1)}, f32[4,2,703]{2,1,0:T(2,128)S(1)}, u32[]{:S(2)}, u32[]{:S(2)}) collective-permute-start(f32[4,2,703]{2,1,0:T(2,128)S(1)} %get-tuple-element.36), channel_id=1, source_target_pairs={{0,2},{1,3},{2,0},{3,1},{4,6},{5,7},{6,4},{7,5},{8,10},{9,11},{10,... | collective-permute-start | bytes 67496 | tf_op jit(solution)/shard_map/ppermute | solution.py:386
  17.3 0.8 %collective-permute-start.7 = (f32[4,2,703]{2,1,0:T(2,128)S(1)}, f32[4,2,703]{2,1,0:T(2,128)S(1)}, u32[]{:S(2)}, u32[]{:S(2)}) collective-permute-start(f32[4,2,703]{2,1,0:T(2,128)S(1)} %get-tuple-element.37), channel_id=1, source_target_pairs={{0,3},{1,2},{2,1},{3,0},{4,7},{5,6},{6,5},{7,4},{8,11},{9,10},{10,... | collective-permute-start | bytes 67496 | tf_op jit(solution)/shard_map/ppermute | solution.py:386
  18.2 0.0 collective-permute-done.5
  18.2 2.0 %collective-permute-done.6 = f32[4,2,703]{2,1,0:T(2,128)S(1)} collective-permute-done((f32[4,2,703]{2,1,0:T(2,128)S(1)}, f32[4,2,703]{2,1,0:T(2,128)S(1)}, u32[]{:S(2)}, u32[]{:S(2)}) %collective-permute-start.6) | collective-permute-done | bytes 22528 | tf_op jit(solution)/shard_map/ppermute | solution.py:386
  20.2 0.4 collective-permute-done.7
  20.6 3.4 %collective-permute-start.10 = (f32[4,2,703]{2,1,0:T(2,128)S(1)}, f32[4,2,703]{2,1,0:T(2,128)S(1)}, u32[]{:S(2)}, u32[]{:S(2)}) collective-permute-start(f32[4,2,703]{2,1,0:T(2,128)S(1)} %bitcast.10), channel_id=1, source_target_pairs={{0,12},{1,13},{2,14},{3,15},{4,8},{5,9},{6,10},{7,11},{8,4},{9,5},... | collective-permute-start | bytes 67496 | tf_op jit(solution)/shard_map/ppermute | solution.py:386
  24.0 2.6 %collective-permute-start.9 = (f32[4,2,703]{2,1,0:T(2,128)S(1)}, f32[4,2,703]{2,1,0:T(2,128)S(1)}, u32[]{:S(2)}, u32[]{:S(2)}) collective-permute-start(f32[4,2,703]{2,1,0:T(2,128)S(1)} %bitcast.11), channel_id=1, source_target_pairs={{0,8},{1,9},{2,10},{3,11},{4,12},{5,13},{6,14},{7,15},{8,0},{9,1},... | collective-permute-start | bytes 67496 | tf_op jit(solution)/shard_map/ppermute | solution.py:386
  26.5 0.4 %collective-permute-start.8 = (f32[4,2,703]{2,1,0:T(2,128)S(1)}, f32[4,2,703]{2,1,0:T(2,128)S(1)}, u32[]{:S(2)}, u32[]{:S(2)}) collective-permute-start(f32[4,2,703]{2,1,0:T(2,128)S(1)} %bitcast.12), channel_id=1, source_target_pairs={{0,4},{1,5},{2,6},{3,7},{4,0},{5,1},{6,2},{7,3},{8,12},{9,13},{10,... | collective-permute-start | bytes 67496 | tf_op jit(solution)/shard_map/ppermute | solution.py:386
  27.0 0.1 station_hots.1.refs_2_
  27.0 0.0 collective-permute-done.10.refs_6_
  27.0 1.6 %collective-permute-done.9.refs_5_ = f32[4,2,703]{2,1,0:T(2,128)S(1)} collective-permute-done((f32[4,2,703]{2,1,0:T(2,128)S(1)}, f32[4,2,703]{2,1,0:T(2,128)S(1)}, u32[]{:S(2)}, u32[]{:S(2)}) %collective-permute-start.9) | collective-permute-done | bytes 22528 | tf_op jit(solution)/shard_map/ppermute | solution.py:386
  28.7 1.7 %collective-permute-done.8.refs_4_ = f32[4,2,703]{2,1,0:T(2,128)S(1)} collective-permute-done((f32[4,2,703]{2,1,0:T(2,128)S(1)}, f32[4,2,703]{2,1,0:T(2,128)S(1)}, u32[]{:S(2)}, u32[]{:S(2)}) %collective-permute-start.8) | collective-permute-done | bytes 22528 | tf_op jit(solution)/shard_map/ppermute | solution.py:386
  30.4 0.0 copy-done.1
  30.4 2.1 %gain_solve.1.refs_5_ = f32[4,2,806]{2,1,0:T(2,128)S(1)} custom-call(s32[1]{0:T(128)} %bitcast.refs_0_, s32[2,2]{1,0:T(2,128)S(1)} %copy-done.1, bf16[2,40,703]{2,1,0:T(8,128)(2,1)S(1)} %station_hots.1.refs_2_, f32[4,2,703]{2,1,0:T(2,128)S(1)} %bitcast.13, f32[4,2,703]{2,1,0:T(2,128)S(1)} %collective-permute-done.8.refs_4_, ...), custom_call_target="tpu_custom_call" | custom-call | tf_op jit(solution)/shard_map/gain_solve/pallas_call | solution.py:474
  32.4 0.1 collective-permute-start.13
  32.5 1.1 %collective-permute-start.12 = (f32[4,2,806]{2,1,0:T(2,128)S(1)}, f32[4,2,806]{2,1,0:T(2,128)S(1)}, u32[]{:S(2)}, u32[]{:S(2)}) collective-permute-start(f32[4,2,806]{2,1,0:T(2,128)S(1)} %gain_solve.1.refs_5_), channel_id=1, source_target_pairs={{0,2},{1,3},{2,0},{3,1},{4,6},{5,7},{6,4},{7,5},{8,10},{9,11},{10,... | collective-permute-start | bytes 77384 | tf_op jit(solution)/shard_map/ppermute | solution.py:386
  33.6 0.7 %collective-permute-start.11 = (f32[4,2,806]{2,1,0:T(2,128)S(1)}, f32[4,2,806]{2,1,0:T(2,128)S(1)}, u32[]{:S(2)}, u32[]{:S(2)}) collective-permute-start(f32[4,2,806]{2,1,0:T(2,128)S(1)} %gain_solve.1.refs_5_), channel_id=1, source_target_pairs={{0,1},{1,0},{2,3},{3,2},{4,5},{5,4},{6,7},{7,6},{8,9},{9,8},{10,11... | collective-permute-start | bytes 77384 | tf_op jit(solution)/shard_map/ppermute | solution.py:386
  34.4 1.4 %collective-permute-done.13.refs_8_ = f32[4,2,806]{2,1,0:T(2,128)S(1)} collective-permute-done((f32[4,2,806]{2,1,0:T(2,128)S(1)}, f32[4,2,806]{2,1,0:T(2,128)S(1)}, u32[]{:S(2)}, u32[]{:S(2)}) %collective-permute-start.13) | collective-permute-done | bytes 25824 | tf_op jit(solution)/shard_map/ppermute | solution.py:386
  35.8 0.8 %collective-permute-done.12.refs_7_ = f32[4,2,806]{2,1,0:T(2,128)S(1)} collective-permute-done((f32[4,2,806]{2,1,0:T(2,128)S(1)}, f32[4,2,806]{2,1,0:T(2,128)S(1)}, u32[]{:S(2)}, u32[]{:S(2)}) %collective-permute-start.12) | collective-permute-done | bytes 25824 | tf_op jit(solution)/shard_map/ppermute | solution.py:386
  36.6 0.0 collective-permute-done.11.refs_6_
  36.6 4.4 %clean.1 = (bf16[2,2,4,192,703]{4,3,2,1,0:T(8,128)(2,1)}, f32[2,2,2,4,38]{4,3,2,1,0:T(4,128)}) custom-call(s32[1]{0:T(128)} %bitcast.refs_0_, bf16[2,4,192,703]{3,2,1,0:T(8,128)(2,1)S(1)} %get-tuple-element.22.refs_10_.refs_1_, bf16[2,4,192,703]{3,2,1,0:T(8,128)(2,1)S(1)} %get-tuple-element.33.refs_2_, ...), custom_call_target="tpu_custom_call" | custom-call | tf_op jit(solution)/shard_map/clean/pallas_call | solution.py:483
  (5 shorter events, 0.0 us)
Async XLA Ops:
  0.6 6.3 %collective-permute-start.2 = (s32[1,2,192]{2,1,0:T(2,128)}, s32[1,2,192]{2,1,0:T(2,128)S(1)}, u32[]{:S(2)}, u32[]{:S(2)}) collective-permute-start(s32[1,2,192]{2,1,0:T(2,128)} %bitcast.20), channel_id=1, source_target_pairs={{0,3},{1,2},{2,1},{3,0},{4,7},{5,6},{6,5},{7,4},{8,11},{9,10},{10,... | collective-permute-start | bytes 4616 | tf_op jit(solution)/shard_map/ppermute | solution.py:386
  3.1 3.8 %collective-permute-start.1 = (s32[1,2,192]{2,1,0:T(2,128)}, s32[1,2,192]{2,1,0:T(2,128)S(1)}, u32[]{:S(2)}, u32[]{:S(2)}) collective-permute-start(s32[1,2,192]{2,1,0:T(2,128)} %bitcast.21), channel_id=1, source_target_pairs={{0,2},{1,3},{2,0},{3,1},{4,6},{5,7},{6,4},{7,5},{8,10},{9,11},{10,... | collective-permute-start | bytes 4616 | tf_op jit(solution)/shard_map/ppermute | solution.py:386
  3.7 2.3 %collective-permute-start = (s32[1,2,192]{2,1,0:T(2,128)}, s32[1,2,192]{2,1,0:T(2,128)S(1)}, u32[]{:S(2)}, u32[]{:S(2)}) collective-permute-start(s32[1,2,192]{2,1,0:T(2,128)} %bitcast.22), channel_id=1, source_target_pairs={{0,1},{1,0},{2,3},{3,2},{4,5},{5,4},{6,7},{7,6},{8,9},{9,8},{10,11... | collective-permute-start | bytes 4616 | tf_op jit(solution)/shard_map/ppermute | solution.py:386
  4.5 0.7 %copy-start = (f32[2,2,703]{2,1,0:T(2,128)S(1)}, f32[2,2,703]{2,1,0:T(2,128)}, u32[]{:S(2)}) copy-start(f32[2,2,703]{2,1,0:T(2,128)} %refs_2_.1) | copy-start | bytes 33748
  6.9 4.0 %collective-permute-start.4 = (s32[4,2,192]{2,1,0:T(2,128)S(1)}, s32[4,2,192]{2,1,0:T(2,128)S(1)}, u32[]{:S(2)}, u32[]{:S(2)}) collective-permute-start(s32[4,2,192]{2,1,0:T(2,128)S(1)} %constant_dynamic-update-slice_fusion.refs_1_), channel_id=1, source_target_pairs={{0,4},{1,5},{2,6},{3,7},{4,0},{5,1},{6,2},{7,3},{8,12},{9,13},{10,... | collective-permute-start | bytes 18440 | tf_op jit(solution)/shard_map/ppermute | solution.py:386
  8.6 2.4 %collective-permute-start.3 = (s32[4,2,192]{2,1,0:T(2,128)S(1)}, s32[4,2,192]{2,1,0:T(2,128)S(1)}, u32[]{:S(2)}, u32[]{:S(2)}) collective-permute-start(s32[4,2,192]{2,1,0:T(2,128)S(1)} %constant_dynamic-update-slice_fusion.refs_1_), channel_id=1, source_target_pairs={{4,8},{5,9},{6,10},{7,11},{8,4},{9,5},{10,6},{11,7},{20,24},{21,25... | collective-permute-start | bytes 18440 | tf_op jit(solution)/shard_map/ppermute | solution.py:453
  10.9 19.4 %copy-start.1 = (s32[2,2]{1,0:T(2,128)S(1)}, s32[2,2]{1,0:T(2,128)}, u32[]{:S(2)}) copy-start(s32[2,2]{1,0:T(2,128)} %refs_1_.3) | copy-start | bytes 52
  16.2 1.9 %collective-permute-start.5 = (f32[4,2,703]{2,1,0:T(2,128)S(1)}, f32[4,2,703]{2,1,0:T(2,128)S(1)}, u32[]{:S(2)}, u32[]{:S(2)}) collective-permute-start(f32[4,2,703]{2,1,0:T(2,128)S(1)} %get-tuple-element.35), channel_id=1, source_target_pairs={{0,1},{1,0},{2,3},{3,2},{4,5},{5,4},{6,7},{7,6},{8,9},{9,8},{10,11... | collective-permute-start | bytes 67496 | tf_op jit(solution)/shard_map/ppermute | solution.py:386
  16.3 3.9 %collective-permute-start.6 = (f32[4,2,703]{2,1,0:T(2,128)S(1)}, f32[4,2,703]{2,1,0:T(2,128)S(1)}, u32[]{:S(2)}, u32[]{:S(2)}) collective-permute-start(f32[4,2,703]{2,1,0:T(2,128)S(1)} %get-tuple-element.36), channel_id=1, source_target_pairs={{0,2},{1,3},{2,0},{3,1},{4,6},{5,7},{6,4},{7,5},{8,10},{9,11},{10,... | collective-permute-start | bytes 67496 | tf_op jit(solution)/shard_map/ppermute | solution.py:386
  17.3 3.3 %collective-permute-start.7 = (f32[4,2,703]{2,1,0:T(2,128)S(1)}, f32[4,2,703]{2,1,0:T(2,128)S(1)}, u32[]{:S(2)}, u32[]{:S(2)}) collective-permute-start(f32[4,2,703]{2,1,0:T(2,128)S(1)} %get-tuple-element.37), channel_id=1, source_target_pairs={{0,3},{1,2},{2,1},{3,0},{4,7},{5,6},{6,5},{7,4},{8,11},{9,10},{10,... | collective-permute-start | bytes 67496 | tf_op jit(solution)/shard_map/ppermute | solution.py:386
  20.6 6.4 %collective-permute-start.10 = (f32[4,2,703]{2,1,0:T(2,128)S(1)}, f32[4,2,703]{2,1,0:T(2,128)S(1)}, u32[]{:S(2)}, u32[]{:S(2)}) collective-permute-start(f32[4,2,703]{2,1,0:T(2,128)S(1)} %bitcast.10), channel_id=1, source_target_pairs={{0,12},{1,13},{2,14},{3,15},{4,8},{5,9},{6,10},{7,11},{8,4},{9,5},... | collective-permute-start | bytes 67496 | tf_op jit(solution)/shard_map/ppermute | solution.py:386
  24.0 4.7 %collective-permute-start.9 = (f32[4,2,703]{2,1,0:T(2,128)S(1)}, f32[4,2,703]{2,1,0:T(2,128)S(1)}, u32[]{:S(2)}, u32[]{:S(2)}) collective-permute-start(f32[4,2,703]{2,1,0:T(2,128)S(1)} %bitcast.11), channel_id=1, source_target_pairs={{0,8},{1,9},{2,10},{3,11},{4,12},{5,13},{6,14},{7,15},{8,0},{9,1},... | collective-permute-start | bytes 67496 | tf_op jit(solution)/shard_map/ppermute | solution.py:386
  26.5 3.8 %collective-permute-start.8 = (f32[4,2,703]{2,1,0:T(2,128)S(1)}, f32[4,2,703]{2,1,0:T(2,128)S(1)}, u32[]{:S(2)}, u32[]{:S(2)}) collective-permute-start(f32[4,2,703]{2,1,0:T(2,128)S(1)} %bitcast.12), channel_id=1, source_target_pairs={{0,4},{1,5},{2,6},{3,7},{4,0},{5,1},{6,2},{7,3},{8,12},{9,13},{10,... | collective-permute-start | bytes 67496 | tf_op jit(solution)/shard_map/ppermute | solution.py:386
  32.4 3.4 %collective-permute-start.13 = (f32[4,2,806]{2,1,0:T(2,128)S(1)}, f32[4,2,806]{2,1,0:T(2,128)S(1)}, u32[]{:S(2)}, u32[]{:S(2)}) collective-permute-start(f32[4,2,806]{2,1,0:T(2,128)S(1)} %gain_solve.1.refs_5_), channel_id=1, source_target_pairs={{0,3},{1,2},{2,1},{3,0},{4,7},{5,6},{6,5},{7,4},{8,11},{9,10},{10,... | collective-permute-start | bytes 77384 | tf_op jit(solution)/shard_map/ppermute | solution.py:386
  32.5 4.1 %collective-permute-start.12 = (f32[4,2,806]{2,1,0:T(2,128)S(1)}, f32[4,2,806]{2,1,0:T(2,128)S(1)}, u32[]{:S(2)}, u32[]{:S(2)}) collective-permute-start(f32[4,2,806]{2,1,0:T(2,128)S(1)} %gain_solve.1.refs_5_), channel_id=1, source_target_pairs={{0,2},{1,3},{2,0},{3,1},{4,6},{5,7},{6,4},{7,5},{8,10},{9,11},{10,... | collective-permute-start | bytes 77384 | tf_op jit(solution)/shard_map/ppermute | solution.py:386
  33.6 3.0 %collective-permute-start.11 = (f32[4,2,806]{2,1,0:T(2,128)S(1)}, f32[4,2,806]{2,1,0:T(2,128)S(1)}, u32[]{:S(2)}, u32[]{:S(2)}) collective-permute-start(f32[4,2,806]{2,1,0:T(2,128)S(1)} %gain_solve.1.refs_5_), channel_id=1, source_target_pairs={{0,1},{1,0},{2,3},{3,2},{4,5},{5,4},{6,7},{7,6},{8,9},{9,8},{10,11... | collective-permute-start | bytes 77384 | tf_op jit(solution)/shard_map/ppermute | solution.py:386

commit v16 on v15

--- a/solution.py
+++ b/solution.py
@@ -478,7 +478,7 @@
         out_shape=jax.ShapeDtypeStruct((4, 2, GAINS_AT + STATIONS), F32),
         compiler_params=params,
         name="gain_solve",
-    )(me, tracks, hots, *pieces)
+    )(me, tracks, hots, pieces[0], *pieces[:0:-1])
     model = [model] + [partner(model, d) for d in range(1, 4)]
     cleaned, gains = pl.pallas_call(
         lambda *refs: clean_kernel(width, *refs),

time: 41.3 us -> 43 us (1.041)
  starting transfers between devices: 15.7 us -> 16.6 us
  waiting for transfers between devices: 8.8 us -> 9.67 us
    ppermute x13, starting transfers between devices: 15 us -> 15.9 us  [partner(): return lax.ppermute(value, 'sub', [(i, i ^ bits) for i in range(count)])]
    ppermute x13, waiting for transfers between devices: 8.8 us -> 9.67 us  [partner(): return lax.ppermute(value, 'sub', [(i, i ^ bits) for i in range(count)])]
where the time goes in v16:
time: 43 us; the launch traced here: 42.8 us
  starting transfers between devices  16.6 us (39%)
  Pallas kernels  14.3 us (33%)
  waiting for transfers between devices  9.67 us (22%)
  between operations  0.75 us (2%)
  local copies, waits for them, and re-layouts  0.74 us (2%)
  other arithmetic  0.73 us (2%)
    ppermute x13, starting transfers between devices, partner(): return lax.ppermute(value, 'sub', [(i, i ^ bits) for i in range(count)])  15.9 us
    ppermute x13, waiting for transfers between devices, partner(): return lax.ppermute(value, 'sub', [(i, i ^ bits) for i in range(count)])  9.67 us
    pallas_call x1, Pallas kernels, local(): pl.pallas_call(lambda *refs: sums_kernel(width, reach, *refs), in_specs=[...  5.3 us
    pallas_call x1, Pallas kernels, local(): pl.pallas_call(lambda *refs: clean_kernel(width, *refs), in_specs=[smem()...  4.39 us
    pallas_call x2, Pallas kernels, local(): pl.pallas_call(lambda *refs: phase_kernel(width, t, reach, *refs), in_spe...  2.52 us
    pallas_call x1, Pallas kernels, local(): pl.pallas_call(lambda *refs: solve_kernel(float(window_count), *refs), in...  2.07 us
  transfers between devices with their start and end apart: 14, of which 7 were waited for; matrix products, arithmetic and copies ran while one was open for 2% of the time, Pallas kernels for 6%

profile of v16, /device:TPU:0, one launch (start us, length us, event | category | flops | bytes accessed | tf_op | source)
XLA Modules:
  0.0 42.8 jit_solution(11310170840167329133)
XLA Ops:
  0.6 2.5 %collective-permute-start.2 = (s32[1,2,192]{2,1,0:T(2,128)}, s32[1,2,192]{2,1,0:T(2,128)S(1)}, u32[]{:S(2)}, u32[]{:S(2)}) collective-permute-start(s32[1,2,192]{2,1,0:T(2,128)} %bitcast.20), channel_id=1, source_target_pairs={{0,3},{1,2},{2,1},{3,0},{4,7},{5,6},{6,5},{7,4},{8,11},{9,10},{10,... | collective-permute-start | bytes 4616 | tf_op jit(solution)/shard_map/ppermute | solution.py:386
  3.1 0.6 %collective-permute-start.1 = (s32[1,2,192]{2,1,0:T(2,128)}, s32[1,2,192]{2,1,0:T(2,128)S(1)}, u32[]{:S(2)}, u32[]{:S(2)}) collective-permute-start(s32[1,2,192]{2,1,0:T(2,128)} %bitcast.21), channel_id=1, source_target_pairs={{0,2},{1,3},{2,0},{3,1},{4,6},{5,7},{6,4},{7,5},{8,10},{9,11},{10,... | collective-permute-start | bytes 4616 | tf_op jit(solution)/shard_map/ppermute | solution.py:386
  3.7 0.0 collective-permute-start
  3.8 0.7 %pad_add_fusion.refs_2_ = s32[3,192]{1,0:T(4,128)S(1)} fusion(s32[1,32]{1,0:T(1,128)} %bitcast.23, s32[2,192]{1,0:T(2,128)} %param.7), kind=kLoop, calls=%fused_computation.5 | loop fusion | flops 576 | bytes 3968 | tf_op jit(solution)/shard_map/add | solution.py:417
  4.5 0.0 copy-start
  4.5 0.7 %copy-done = f32[2,2,703]{2,1,0:T(2,128)S(1)} copy-done((f32[2,2,703]{2,1,0:T(2,128)S(1)}, f32[2,2,703]{2,1,0:T(2,128)}, u32[]{:S(2)}) %copy-start) | copy-done | bytes 11272
  5.2 0.8 %phases.2 = (f32[2,2,192,703]{3,2,1,0:T(8,128)S(1)}, bf16[2,2,192,703]{3,2,1,0:T(8,128)(2,1)S(1)}, s32[1,2,192]{2,1,0:T(2,128)S(1)}, s32[1,32]{1,0:T(1,128)S(1)}) custom-call(s32[1]{0:T(128)} %bitcast.refs_0_, f32[2,2,703]{2,1,0:T(2,128)S(1)} %copy-done, s32[3,192]{1,0:T(4,128)S(1)} %pad_add_fusion.refs_2_), custom_call_target="tpu_custom_call" | custom-call | flops 10000000 | bytes 6291456 | tf_op jit(solution)/shard_map/phases/pallas_call | solution.py:437
  6.1 0.0 collective-permute-done
  6.1 0.8 %collective-permute-done.1 = s32[1,2,192]{2,1,0:T(2,128)S(1)} collective-permute-done((s32[1,2,192]{2,1,0:T(2,128)}, s32[1,2,192]{2,1,0:T(2,128)S(1)}, u32[]{:S(2)}, u32[]{:S(2)}) %collective-permute-start.1) | collective-permute-done | bytes 1568 | tf_op jit(solution)/shard_map/ppermute | solution.py:386
  6.9 0.0 collective-permute-done.2
  6.9 1.6 %collective-permute-start.4 = (s32[4,2,192]{2,1,0:T(2,128)S(1)}, s32[4,2,192]{2,1,0:T(2,128)S(1)}, u32[]{:S(2)}, u32[]{:S(2)}) collective-permute-start(s32[4,2,192]{2,1,0:T(2,128)S(1)} %constant_dynamic-update-slice_fusion.refs_1_), channel_id=1, source_target_pairs={{0,4},{1,5},{2,6},{3,7},{4,0},{5,1},{6,2},{7,3},{8,12},{9,13},{10,... | collective-permute-start | bytes 18440 | tf_op jit(solution)/shard_map/ppermute | solution.py:386
  8.6 0.6 %collective-permute-start.3 = (s32[4,2,192]{2,1,0:T(2,128)S(1)}, s32[4,2,192]{2,1,0:T(2,128)S(1)}, u32[]{:S(2)}, u32[]{:S(2)}) collective-permute-start(s32[4,2,192]{2,1,0:T(2,128)S(1)} %constant_dynamic-update-slice_fusion.refs_1_), channel_id=1, source_target_pairs={{4,8},{5,9},{6,10},{7,11},{8,4},{9,5},{10,6},{11,7},{20,24},{21,25... | collective-permute-start | bytes 18440 | tf_op jit(solution)/shard_map/ppermute | solution.py:453
  9.2 1.7 %phases.3 = (f32[2,2,192,703]{3,2,1,0:T(8,128)S(1)}, bf16[2,2,192,703]{3,2,1,0:T(8,128)(2,1)S(1)}, bf16[2,4,192,703]{3,2,1,0:T(8,128)(2,1)S(1)}, f32[2,2,16,703]...) custom-call(s32[1]{0:T(128)} %bitcast.refs_0_, ...), custom_call_target="tpu_custom_call" | custom-call | flops 10000000 | bytes 6291456 | tf_op jit(solution)/shard_map/phases/pallas_call | solution.py:437
  10.9 0.0 collective-permute-done.4.refs_3_
  10.9 0.0 collective-permute-done.3.refs_2_
  10.9 0.0 copy-start.1
  10.9 5.3 %window_sums.1 = (f32[4,2,703]{2,1,0:T(2,128)S(1)}, f32[4,2,703]{2,1,0:T(2,128)S(1)}, f32[4,2,703]{2,1,0:T(2,128)S(1)}, f32[4,2,703]{2,1,0:T(2,128)S(1)}, bf16[2,4,192,703]{3,2,1,0:T(8,128)(2,1)S(1)}) custom-call(s32[1]{0:T(128)} %bitcast.refs_0_, s32[4,2,192]{2,1,0:T(2,128)S(1)} %constant_dynamic-update-slice_fusion.refs_1_, ...), custom_call_target="tpu_custom_call" | custom-call | tf_op jit(solution)/shard_map/window_sums/pallas_call | solution.py:457
  16.2 0.1 collective-permute-start.5
  16.3 1.0 %collective-permute-start.6 = (f32[4,2,703]{2,1,0:T(2,128)S(1)}, f32[4,2,703]{2,1,0:T(2,128)S(1)}, u32[]{:S(2)}, u32[]{:S(2)}) collective-permute-start(f32[4,2,703]{2,1,0:T(2,128)S(1)} %get-tuple-element.36), channel_id=1, source_target_pairs={{0,2},{1,3},{2,0},{3,1},{4,6},{5,7},{6,4},{7,5},{8,10},{9,11},{10,... | collective-permute-start | bytes 67496 | tf_op jit(solution)/shard_map/ppermute | solution.py:386
  17.3 0.8 %collective-permute-start.7 = (f32[4,2,703]{2,1,0:T(2,128)S(1)}, f32[4,2,703]{2,1,0:T(2,128)S(1)}, u32[]{:S(2)}, u32[]{:S(2)}) collective-permute-start(f32[4,2,703]{2,1,0:T(2,128)S(1)} %get-tuple-element.37), channel_id=1, source_target_pairs={{0,3},{1,2},{2,1},{3,0},{4,7},{5,6},{6,5},{7,4},{8,11},{9,10},{10,... | collective-permute-start | bytes 67496 | tf_op jit(solution)/shard_map/ppermute | solution.py:386
  18.2 0.0 collective-permute-done.5
  18.2 2.0 %collective-permute-done.6 = f32[4,2,703]{2,1,0:T(2,128)S(1)} collective-permute-done((f32[4,2,703]{2,1,0:T(2,128)S(1)}, f32[4,2,703]{2,1,0:T(2,128)S(1)}, u32[]{:S(2)}, u32[]{:S(2)}) %collective-permute-start.6) | collective-permute-done | bytes 22528 | tf_op jit(solution)/shard_map/ppermute | solution.py:386
  20.2 0.4 collective-permute-done.7
  20.6 4.5 %collective-permute-start.10 = (f32[4,2,703]{2,1,0:T(2,128)S(1)}, f32[4,2,703]{2,1,0:T(2,128)S(1)}, u32[]{:S(2)}, u32[]{:S(2)}) collective-permute-start(f32[4,2,703]{2,1,0:T(2,128)S(1)} %bitcast.10), channel_id=1, source_target_pairs={{0,4},{1,5},{2,6},{3,7},{4,0},{5,1},{6,2},{7,3},{8,12},{9,13},{10,... | collective-permute-start | bytes 67496 | tf_op jit(solution)/shard_map/ppermute | solution.py:386
  25.1 1.4 %collective-permute-start.9 = (f32[4,2,703]{2,1,0:T(2,128)S(1)}, f32[4,2,703]{2,1,0:T(2,128)S(1)}, u32[]{:S(2)}, u32[]{:S(2)}) collective-permute-start(f32[4,2,703]{2,1,0:T(2,128)S(1)} %bitcast.11), channel_id=1, source_target_pairs={{0,8},{1,9},{2,10},{3,11},{4,12},{5,13},{6,14},{7,15},{8,0},{9,1},... | collective-permute-start | bytes 67496 | tf_op jit(solution)/shard_map/ppermute | solution.py:386
  26.5 1.4 %collective-permute-start.8 = (f32[4,2,703]{2,1,0:T(2,128)S(1)}, f32[4,2,703]{2,1,0:T(2,128)S(1)}, u32[]{:S(2)}, u32[]{:S(2)}) collective-permute-start(f32[4,2,703]{2,1,0:T(2,128)S(1)} %bitcast.12), channel_id=1, source_target_pairs={{0,12},{1,13},{2,14},{3,15},{4,8},{5,9},{6,10},{7,11},{8,4},{9,5},... | collective-permute-start | bytes 67496 | tf_op jit(solution)/shard_map/ppermute | solution.py:386
  27.9 0.1 station_hots.1.refs_2_
  27.9 0.0 collective-permute-done.10.refs_6_
  27.9 2.1 %collective-permute-done.9.refs_5_ = f32[4,2,703]{2,1,0:T(2,128)S(1)} collective-permute-done((f32[4,2,703]{2,1,0:T(2,128)S(1)}, f32[4,2,703]{2,1,0:T(2,128)S(1)}, u32[]{:S(2)}, u32[]{:S(2)}) %collective-permute-start.9) | collective-permute-done | bytes 22528 | tf_op jit(solution)/shard_map/ppermute | solution.py:386
  30.1 2.1 %collective-permute-done.8.refs_4_ = f32[4,2,703]{2,1,0:T(2,128)S(1)} collective-permute-done((f32[4,2,703]{2,1,0:T(2,128)S(1)}, f32[4,2,703]{2,1,0:T(2,128)S(1)}, u32[]{:S(2)}, u32[]{:S(2)}) %collective-permute-start.8) | collective-permute-done | bytes 22528 | tf_op jit(solution)/shard_map/ppermute | solution.py:386
  32.1 0.0 copy-done.1
  32.1 2.1 %gain_solve.1.refs_5_ = f32[4,2,806]{2,1,0:T(2,128)S(1)} custom-call(s32[1]{0:T(128)} %bitcast.refs_0_, s32[2,2]{1,0:T(2,128)S(1)} %copy-done.1, bf16[2,40,703]{2,1,0:T(8,128)(2,1)S(1)} %station_hots.1.refs_2_, f32[4,2,703]{2,1,0:T(2,128)S(1)} %bitcast.13, f32[4,2,703]{2,1,0:T(2,128)S(1)} %collective-permute-done.8.refs_4_, ...), custom_call_target="tpu_custom_call" | custom-call | tf_op jit(solution)/shard_map/gain_solve/pallas_call | solution.py:474
  34.2 0.1 collective-permute-start.13
  34.3 1.1 %collective-permute-start.12 = (f32[4,2,806]{2,1,0:T(2,128)S(1)}, f32[4,2,806]{2,1,0:T(2,128)S(1)}, u32[]{:S(2)}, u32[]{:S(2)}) collective-permute-start(f32[4,2,806]{2,1,0:T(2,128)S(1)} %gain_solve.1.refs_5_), channel_id=1, source_target_pairs={{0,2},{1,3},{2,0},{3,1},{4,6},{5,7},{6,4},{7,5},{8,10},{9,11},{10,... | collective-permute-start | bytes 77384 | tf_op jit(solution)/shard_map/ppermute | solution.py:386
  35.4 0.7 %collective-permute-start.11 = (f32[4,2,806]{2,1,0:T(2,128)S(1)}, f32[4,2,806]{2,1,0:T(2,128)S(1)}, u32[]{:S(2)}, u32[]{:S(2)}) collective-permute-start(f32[4,2,806]{2,1,0:T(2,128)S(1)} %gain_solve.1.refs_5_), channel_id=1, source_target_pairs={{0,1},{1,0},{2,3},{3,2},{4,5},{5,4},{6,7},{7,6},{8,9},{9,8},{10,11... | collective-permute-start | bytes 77384 | tf_op jit(solution)/shard_map/ppermute | solution.py:386
  36.1 1.4 %collective-permute-done.13.refs_8_ = f32[4,2,806]{2,1,0:T(2,128)S(1)} collective-permute-done((f32[4,2,806]{2,1,0:T(2,128)S(1)}, f32[4,2,806]{2,1,0:T(2,128)S(1)}, u32[]{:S(2)}, u32[]{:S(2)}) %collective-permute-start.13) | collective-permute-done | bytes 25824 | tf_op jit(solution)/shard_map/ppermute | solution.py:386
  37.5 0.8 %collective-permute-done.12.refs_7_ = f32[4,2,806]{2,1,0:T(2,128)S(1)} collective-permute-done((f32[4,2,806]{2,1,0:T(2,128)S(1)}, f32[4,2,806]{2,1,0:T(2,128)S(1)}, u32[]{:S(2)}, u32[]{:S(2)}) %collective-permute-start.12) | collective-permute-done | bytes 25824 | tf_op jit(solution)/shard_map/ppermute | solution.py:386
  38.4 0.0 collective-permute-done.11.refs_6_
  38.4 4.4 %clean.1 = (bf16[2,2,4,192,703]{4,3,2,1,0:T(8,128)(2,1)}, f32[2,2,2,4,38]{4,3,2,1,0:T(4,128)}) custom-call(s32[1]{0:T(128)} %bitcast.refs_0_, bf16[2,4,192,703]{3,2,1,0:T(8,128)(2,1)S(1)} %get-tuple-element.22.refs_10_.refs_1_, bf16[2,4,192,703]{3,2,1,0:T(8,128)(2,1)S(1)} %get-tuple-element.33.refs_2_, ...), custom_call_target="tpu_custom_call" | custom-call | tf_op jit(solution)/shard_map/clean/pallas_call | solution.py:483
  (5 shorter events, 0.0 us)
Async XLA Ops:
  0.6 6.3 %collective-permute-start.2 = (s32[1,2,192]{2,1,0:T(2,128)}, s32[1,2,192]{2,1,0:T(2,128)S(1)}, u32[]{:S(2)}, u32[]{:S(2)}) collective-permute-start(s32[1,2,192]{2,1,0:T(2,128)} %bitcast.20), channel_id=1, source_target_pairs={{0,3},{1,2},{2,1},{3,0},{4,7},{5,6},{6,5},{7,4},{8,11},{9,10},{10,... | collective-permute-start | bytes 4616 | tf_op jit(solution)/shard_map/ppermute | solution.py:386
  3.1 3.8 %collective-permute-start.1 = (s32[1,2,192]{2,1,0:T(2,128)}, s32[1,2,192]{2,1,0:T(2,128)S(1)}, u32[]{:S(2)}, u32[]{:S(2)}) collective-permute-start(s32[1,2,192]{2,1,0:T(2,128)} %bitcast.21), channel_id=1, source_target_pairs={{0,2},{1,3},{2,0},{3,1},{4,6},{5,7},{6,4},{7,5},{8,10},{9,11},{10,... | collective-permute-start | bytes 4616 | tf_op jit(solution)/shard_map/ppermute | solution.py:386
  3.7 2.3 %collective-permute-start = (s32[1,2,192]{2,1,0:T(2,128)}, s32[1,2,192]{2,1,0:T(2,128)S(1)}, u32[]{:S(2)}, u32[]{:S(2)}) collective-permute-start(s32[1,2,192]{2,1,0:T(2,128)} %bitcast.22), channel_id=1, source_target_pairs={{0,1},{1,0},{2,3},{3,2},{4,5},{5,4},{6,7},{7,6},{8,9},{9,8},{10,11... | collective-permute-start | bytes 4616 | tf_op jit(solution)/shard_map/ppermute | solution.py:386
  4.5 0.7 %copy-start = (f32[2,2,703]{2,1,0:T(2,128)S(1)}, f32[2,2,703]{2,1,0:T(2,128)}, u32[]{:S(2)}) copy-start(f32[2,2,703]{2,1,0:T(2,128)} %refs_2_.1) | copy-start | bytes 33748
  6.9 4.0 %collective-permute-start.4 = (s32[4,2,192]{2,1,0:T(2,128)S(1)}, s32[4,2,192]{2,1,0:T(2,128)S(1)}, u32[]{:S(2)}, u32[]{:S(2)}) collective-permute-start(s32[4,2,192]{2,1,0:T(2,128)S(1)} %constant_dynamic-update-slice_fusion.refs_1_), channel_id=1, source_target_pairs={{0,4},{1,5},{2,6},{3,7},{4,0},{5,1},{6,2},{7,3},{8,12},{9,13},{10,... | collective-permute-start | bytes 18440 | tf_op jit(solution)/shard_map/ppermute | solution.py:386
  8.6 2.4 %collective-permute-start.3 = (s32[4,2,192]{2,1,0:T(2,128)S(1)}, s32[4,2,192]{2,1,0:T(2,128)S(1)}, u32[]{:S(2)}, u32[]{:S(2)}) collective-permute-start(s32[4,2,192]{2,1,0:T(2,128)S(1)} %constant_dynamic-update-slice_fusion.refs_1_), channel_id=1, source_target_pairs={{4,8},{5,9},{6,10},{7,11},{8,4},{9,5},{10,6},{11,7},{20,24},{21,25... | collective-permute-start | bytes 18440 | tf_op jit(solution)/shard_map/ppermute | solution.py:453
  10.9 21.2 %copy-start.1 = (s32[2,2]{1,0:T(2,128)S(1)}, s32[2,2]{1,0:T(2,128)}, u32[]{:S(2)}) copy-start(s32[2,2]{1,0:T(2,128)} %refs_1_.3) | copy-start | bytes 52
  16.2 1.9 %collective-permute-start.5 = (f32[4,2,703]{2,1,0:T(2,128)S(1)}, f32[4,2,703]{2,1,0:T(2,128)S(1)}, u32[]{:S(2)}, u32[]{:S(2)}) collective-permute-start(f32[4,2,703]{2,1,0:T(2,128)S(1)} %get-tuple-element.35), channel_id=1, source_target_pairs={{0,1},{1,0},{2,3},{3,2},{4,5},{5,4},{6,7},{7,6},{8,9},{9,8},{10,11... | collective-permute-start | bytes 67496 | tf_op jit(solution)/shard_map/ppermute | solution.py:386
  16.3 3.9 %collective-permute-start.6 = (f32[4,2,703]{2,1,0:T(2,128)S(1)}, f32[4,2,703]{2,1,0:T(2,128)S(1)}, u32[]{:S(2)}, u32[]{:S(2)}) collective-permute-start(f32[4,2,703]{2,1,0:T(2,128)S(1)} %get-tuple-element.36), channel_id=1, source_target_pairs={{0,2},{1,3},{2,0},{3,1},{4,6},{5,7},{6,4},{7,5},{8,10},{9,11},{10,... | collective-permute-start | bytes 67496 | tf_op jit(solution)/shard_map/ppermute | solution.py:386
  17.3 3.3 %collective-permute-start.7 = (f32[4,2,703]{2,1,0:T(2,128)S(1)}, f32[4,2,703]{2,1,0:T(2,128)S(1)}, u32[]{:S(2)}, u32[]{:S(2)}) collective-permute-start(f32[4,2,703]{2,1,0:T(2,128)S(1)} %get-tuple-element.37), channel_id=1, source_target_pairs={{0,3},{1,2},{2,1},{3,0},{4,7},{5,6},{6,5},{7,4},{8,11},{9,10},{10,... | collective-permute-start | bytes 67496 | tf_op jit(solution)/shard_map/ppermute | solution.py:386
  20.6 7.3 %collective-permute-start.10 = (f32[4,2,703]{2,1,0:T(2,128)S(1)}, f32[4,2,703]{2,1,0:T(2,128)S(1)}, u32[]{:S(2)}, u32[]{:S(2)}) collective-permute-start(f32[4,2,703]{2,1,0:T(2,128)S(1)} %bitcast.10), channel_id=1, source_target_pairs={{0,4},{1,5},{2,6},{3,7},{4,0},{5,1},{6,2},{7,3},{8,12},{9,13},{10,... | collective-permute-start | bytes 67496 | tf_op jit(solution)/shard_map/ppermute | solution.py:386
  25.1 5.0 %collective-permute-start.9 = (f32[4,2,703]{2,1,0:T(2,128)S(1)}, f32[4,2,703]{2,1,0:T(2,128)S(1)}, u32[]{:S(2)}, u32[]{:S(2)}) collective-permute-start(f32[4,2,703]{2,1,0:T(2,128)S(1)} %bitcast.11), channel_id=1, source_target_pairs={{0,8},{1,9},{2,10},{3,11},{4,12},{5,13},{6,14},{7,15},{8,0},{9,1},... | collective-permute-start | bytes 67496 | tf_op jit(solution)/shard_map/ppermute | solution.py:386
  26.5 5.6 %collective-permute-start.8 = (f32[4,2,703]{2,1,0:T(2,128)S(1)}, f32[4,2,703]{2,1,0:T(2,128)S(1)}, u32[]{:S(2)}, u32[]{:S(2)}) collective-permute-start(f32[4,2,703]{2,1,0:T(2,128)S(1)} %bitcast.12), channel_id=1, source_target_pairs={{0,12},{1,13},{2,14},{3,15},{4,8},{5,9},{6,10},{7,11},{8,4},{9,5},... | collective-permute-start | bytes 67496 | tf_op jit(solution)/shard_map/ppermute | solution.py:386
  34.2 3.4 %collective-permute-start.13 = (f32[4,2,806]{2,1,0:T(2,128)S(1)}, f32[4,2,806]{2,1,0:T(2,128)S(1)}, u32[]{:S(2)}, u32[]{:S(2)}) collective-permute-start(f32[4,2,806]{2,1,0:T(2,128)S(1)} %gain_solve.1.refs_5_), channel_id=1, source_target_pairs={{0,3},{1,2},{2,1},{3,0},{4,7},{5,6},{6,5},{7,4},{8,11},{9,10},{10,... | collective-permute-start | bytes 77384 | tf_op jit(solution)/shard_map/ppermute | solution.py:386
  34.3 4.1 %collective-permute-start.12 = (f32[4,2,806]{2,1,0:T(2,128)S(1)}, f32[4,2,806]{2,1,0:T(2,128)S(1)}, u32[]{:S(2)}, u32[]{:S(2)}) collective-permute-start(f32[4,2,806]{2,1,0:T(2,128)S(1)} %gain_solve.1.refs_5_), channel_id=1, source_target_pairs={{0,2},{1,3},{2,0},{3,1},{4,6},{5,7},{6,4},{7,5},{8,10},{9,11},{10,... | collective-permute-start | bytes 77384 | tf_op jit(solution)/shard_map/ppermute | solution.py:386
  35.4 3.0 %collective-permute-start.11 = (f32[4,2,806]{2,1,0:T(2,128)S(1)}, f32[4,2,806]{2,1,0:T(2,128)S(1)}, u32[]{:S(2)}, u32[]{:S(2)}) collective-permute-start(f32[4,2,806]{2,1,0:T(2,128)S(1)} %gain_solve.1.refs_5_), channel_id=1, source_target_pairs={{0,1},{1,0},{2,3},{3,2},{4,5},{5,4},{6,7},{7,6},{8,9},{9,8},{10,11... | collective-permute-start | bytes 77384 | tf_op jit(solution)/shard_map/ppermute | solution.py:386
